TPU v7x, 32 devices: a whole 2x2x4 slice. The times are simulated.
32 devices in a mesh: section: 2 (over x), dp: 2 (over core), ctx: 8 (over z, y).
Axes of the slice: x: 2, y: 2, z: 4, core: 2. Of those that a mesh axis runs over, the one named last changes fastest.
Arguments:
- inputs: bfloat16 [2, 2, 1024, 1600], P(None, 'dp', 'ctx'), may hold values from -6 to 6
- cotangent: bfloat16 [2, 2, 1024, 1600], P(None, 'dp', 'ctx'), may hold values from -6 to 6
- positions: int32 [2, 1024], P(None, 'ctx'), may hold values from 0 to 1023, each once within a row
- w_qkv: bfloat16 [2, 1600, 4800], P('section', ('dp', 'ctx')), may hold values from -0.15625 to 0.15625
- w_attn_out: bfloat16 [2, 1600, 1600], P('section', ('dp', 'ctx')), may hold values from -0.625 to 0.625
- w_fc: bfloat16 [2, 1600, 6400], P('section', ('dp', 'ctx')), may hold values from -0.15625 to 0.15625
- w_proj: bfloat16 [2, 6400, 1600], P('section', ('dp', 'ctx')), may hold values from -0.078125 to 0.078125
- norm_gains: bfloat16 [2, 1600, 2], P('section', ('dp', 'ctx')), may hold values from 0.5 to 1.5
- biases: bfloat16 [2, 1600, 6], P('section', ('dp', 'ctx')), may hold values from -3 to 3
- fc_bias: bfloat16 [2, 6400], P('section', ('dp', 'ctx')), may hold values from -3 to 3
Outputs:
- section_out: bfloat16 [2, 2, 2, 1024, 1600], P('section', None, 'dp', 'ctx')
- section_grad: bfloat16 [2, 2, 2, 1024, 1600], P('section', None, 'dp', 'ctx')
- grad_qkv: float32 [2, 1600, 4800], P('section', ('dp', 'ctx'))
- grad_attn_out: float32 [2, 1600, 1600], P('section', ('dp', 'ctx'))
- grad_fc: float32 [2, 1600, 6400], P('section', ('dp', 'ctx'))
- grad_proj: float32 [2, 6400, 1600], P('section', ('dp', 'ctx'))
- grad_gains: float32 [2, 1600, 2], P('section', ('dp', 'ctx'))
- grad_biases: float32 [2, 1600, 6], P('section', ('dp', 'ctx'))
- grad_fc_bias: float32 [2, 6400], P('section', ('dp', 'ctx'))
Inputs may be any that keep to these rules, and one draw needn't show every extreme that they name: `positions`: each row of a micro-batch holds every position from 0 to 1023 once, in any order over the slots.
All inputs are finite; a program needn't handle non-finite values.
Results may differ from a plain program's by a relative error of at most 0.02.
Values may be sent and summed in bfloat16 or wider, within the bound.
A program may use at most 576 MiB of HBM per device.

v0:
```python
import jax
import jax.numpy as jnp
from jax import lax
from jax.sharding import PartitionSpec as P

HEADS = 25


EPSILON = 1e-05


def shifted(block, axis, distance):
    devices = range(lax.axis_size(axis))
    route = [(i - distance, i) for i in devices if i - distance in devices]
    return lax.ppermute(block, axis, route)


def normalize(rows_in, gain_col, shift_col):
    centred = rows_in - jnp.mean(rows_in, axis=-1, keepdims=True)
    spread = jnp.mean(centred * centred, axis=-1, keepdims=True)
    return centred * lax.rsqrt(spread + EPSILON) * gain_col + shift_col


def smooth(values_in):
    return jax.nn.gelu(values_in, approximate=True)


def contract_rows(left_side, right_side):
    return lax.dot_general(
        left_side, right_side, (((0,), (0,)), ((), ())), preferred_element_type=jnp.float32
    )


def contract_cols(left_side, right_side):
    return lax.dot_general(
        left_side, right_side, (((1,), (1,)), ((), ())), preferred_element_type=jnp.float32
    )


def attend(queries, key_rows, value_rows, place_query, place_keys):
    seq_count, row_count, model_width = queries.shape
    head_size = model_width // HEADS
    score_scale = head_size ** (-0.5)
    query_heads = queries.reshape(seq_count, row_count, HEADS, head_size)
    running_max = jnp.full((seq_count, HEADS, row_count), -1e30, jnp.float32)
    key_piece = lax.all_gather(key_rows, "ctx", axis=1, tiled=True)
    value_piece = lax.all_gather(value_rows, "ctx", axis=1, tiled=True)
    row_span = key_piece.shape[1]
    key_heads = key_piece.reshape(seq_count, row_span, HEADS, head_size)
    value_heads = value_piece.reshape(seq_count, row_span, HEADS, head_size)
    scores = (
        jnp.einsum("sqhd,snhd->shqn", query_heads, key_heads, preferred_element_type=jnp.float32)
        * score_scale
    )
    allowed = (place_query[:, None] >= place_keys[None, :])[None, None]
    scores = jnp.where(allowed, scores, -1e30)
    new_max = jnp.maximum(running_max, jnp.max(scores, axis=-1))
    weights = jnp.where(allowed, jnp.exp(scores - new_max[..., None]), 0.0)
    running_sum = jnp.sum(weights, axis=-1)
    weighted = jnp.einsum(
        "shqn,snhd->shqd",
        weights.astype(jnp.bfloat16),
        value_heads,
        preferred_element_type=jnp.float32,
    )
    running_max, running_sum, weighted = (new_max, running_sum, weighted)
    attended = weighted / running_sum[..., None]
    attended = jnp.transpose(attended, (0, 2, 1, 3)).reshape(seq_count, row_count, model_width)
    return (attended.astype(jnp.bfloat16), running_max + jnp.log(running_sum))


def attend_back(queries, key_rows, value_rows, grad_attended, log_totals, place_query, place_keys):
    seq_count, row_count, model_width = queries.shape
    head_size = model_width // HEADS
    score_scale = head_size ** (-0.5)

    def one_sequence(carried, element):
        query_one, key_one, value_one, grad_one, totals_one = element
        key_all, value_all = (
            lax.all_gather(key_one, "ctx", axis=0, tiled=True),
            lax.all_gather(value_one, "ctx", axis=0, tiled=True),
        )
        token_count = key_all.shape[0]
        query_heads = query_one.reshape(row_count, HEADS, head_size)
        key_heads = key_all.reshape(token_count, HEADS, head_size)
        value_heads = value_all.reshape(token_count, HEADS, head_size)
        grad_heads = grad_one.reshape(row_count, HEADS, head_size)
        scores = (
            jnp.einsum("qhd,nhd->hqn", query_heads, key_heads, preferred_element_type=jnp.float32)
            * score_scale
        )
        allowed = (place_query[:, None] >= place_keys[None, :])[None]
        scores = jnp.where(allowed, scores, -1e30)
        probs = jnp.where(allowed, jnp.exp(scores - totals_one[..., None]), 0.0)
        grad_probs = jnp.einsum(
            "qhd,nhd->hqn", grad_heads, value_heads, preferred_element_type=jnp.float32
        )
        centre = jnp.sum(probs * grad_probs, axis=-1)
        grad_scores = (probs * (grad_probs - centre[..., None])).astype(jnp.bfloat16)
        grad_query = (
            jnp.einsum("hqn,nhd->qhd", grad_scores, key_heads, preferred_element_type=jnp.float32)
            * score_scale
        )
        key_term = (
            jnp.einsum("hqn,qhd->nhd", grad_scores, query_heads, preferred_element_type=jnp.float32)
            * score_scale
        )
        value_term = jnp.einsum(
            "hqn,qhd->nhd",
            probs.astype(jnp.bfloat16),
            grad_heads,
            preferred_element_type=jnp.float32,
        )
        grad_key, grad_value = (
            lax.psum_scatter(
                key_term.reshape(token_count, model_width).astype(jnp.bfloat16),
                "ctx",
                scatter_dimension=0,
                tiled=True,
            ).astype(jnp.float32),
            lax.psum_scatter(
                value_term.reshape(token_count, model_width).astype(jnp.bfloat16),
                "ctx",
                scatter_dimension=0,
                tiled=True,
            ).astype(jnp.float32),
        )
        return (
            carried,
            (
                grad_query.reshape(row_count, model_width).astype(jnp.bfloat16),
                grad_key.astype(jnp.bfloat16),
                grad_value.astype(jnp.bfloat16),
            ),
        )

    unused, (grad_query, grad_key, grad_value) = lax.scan(
        one_sequence,
        jnp.zeros((), jnp.float32),
        (queries, key_rows, value_rows, grad_attended, log_totals),
    )
    return (grad_query, grad_key, grad_value)


def layer_forward(layer_in, place_query, place_keys, params):
    w_joint, w_output, w_hidden, w_back, gain_cols, shift_cols, unit_shift = params
    seq_count, row_count, model_width = layer_in.shape
    gain_cols = gain_cols.astype(jnp.float32)
    shift_cols = shift_cols.astype(jnp.float32)
    rows_in = layer_in.reshape(seq_count * row_count, model_width).astype(jnp.float32)
    normed = normalize(rows_in, gain_cols[:, 0], shift_cols[:, 0]).astype(jnp.bfloat16)
    projected = jnp.dot(normed, w_joint, preferred_element_type=jnp.float32)
    queries = (projected[:, :model_width] + shift_cols[:, 1]).astype(jnp.bfloat16)
    key_rows = projected[:, model_width : 2 * model_width].astype(jnp.bfloat16)
    value_rows = (projected[:, 2 * model_width :] + shift_cols[:, 2]).astype(jnp.bfloat16)
    block_shape = (seq_count, row_count, model_width)
    attended, log_totals = attend(
        queries.reshape(block_shape),
        key_rows.reshape(block_shape),
        value_rows.reshape(block_shape),
        place_query,
        place_keys,
    )
    attended_rows = attended.reshape(seq_count * row_count, model_width)
    residual_mid = rows_in + (
        jnp.dot(attended_rows, w_output, preferred_element_type=jnp.float32) + shift_cols[:, 3]
    )
    normed_two = normalize(residual_mid, gain_cols[:, 1], shift_cols[:, 4]).astype(jnp.bfloat16)
    hidden = jnp.dot(normed_two, w_hidden, preferred_element_type=jnp.float32) + unit_shift.astype(
        jnp.float32
    )
    activated = smooth(hidden).astype(jnp.bfloat16)
    result = residual_mid + (
        jnp.dot(activated, w_back, preferred_element_type=jnp.float32) + shift_cols[:, 5]
    )
    kept = (
        rows_in,
        residual_mid,
        normed,
        queries.reshape(block_shape),
        key_rows.reshape(block_shape),
        value_rows.reshape(block_shape),
        attended_rows,
        log_totals,
        normed_two,
        hidden,
        activated,
    )
    return (result.astype(jnp.bfloat16).reshape(block_shape), kept)


def layer_backward(grad_out, kept, place_query, place_keys, params):
    w_joint, w_output, w_hidden, w_back, gain_cols, shift_cols, unit_shift = params
    (
        rows_in,
        residual_mid,
        normed,
        queries,
        key_rows,
        value_rows,
        attended_rows,
        log_totals,
        normed_two,
        hidden,
        activated,
    ) = kept
    seq_count, row_count, model_width = queries.shape
    gain_cols = gain_cols.astype(jnp.float32)
    shift_cols = shift_cols.astype(jnp.float32)
    grad_rows = grad_out.reshape(seq_count * row_count, model_width).astype(jnp.float32)
    grad_branch = grad_rows.astype(jnp.bfloat16)
    grad_activated = contract_cols(grad_branch, w_back)
    unused_value, smooth_back = jax.vjp(smooth, hidden)
    grad_hidden = smooth_back(grad_activated)[0].astype(jnp.bfloat16)
    grad_normed_two = contract_cols(grad_hidden, w_hidden)
    unused_norm, second_back = jax.vjp(normalize, residual_mid, gain_cols[:, 1], shift_cols[:, 4])
    mid_part, gain_two, shift_two = second_back(grad_normed_two)
    grad_mid = grad_rows + mid_part
    grad_attn = grad_mid.astype(jnp.bfloat16)
    grad_attended = contract_cols(grad_attn, w_output).astype(jnp.bfloat16)
    grad_query, grad_key, grad_value = attend_back(
        queries,
        key_rows,
        value_rows,
        grad_attended.reshape(seq_count, row_count, model_width),
        log_totals,
        place_query,
        place_keys,
    )
    grad_joint = jnp.concatenate([grad_query, grad_key, grad_value], axis=-1).reshape(
        seq_count * row_count, 3 * model_width
    )
    grad_normed = contract_cols(grad_joint, w_joint)
    unused_first, first_back = jax.vjp(normalize, rows_in, gain_cols[:, 0], shift_cols[:, 0])
    in_part, gain_one, shift_one = first_back(grad_normed)
    grad_in = grad_mid + in_part
    small_cols = jnp.stack(
        [
            gain_one,
            gain_two,
            shift_one,
            jnp.sum(grad_query.astype(jnp.float32), axis=(0, 1)),
            jnp.sum(grad_value.astype(jnp.float32), axis=(0, 1)),
            jnp.sum(grad_attn.astype(jnp.float32), axis=0),
            shift_two,
            jnp.sum(grad_branch.astype(jnp.float32), axis=0),
        ],
        axis=1,
    )
    unit_sums = jnp.sum(grad_hidden.astype(jnp.float32), axis=0)
    factors = (
        normed,
        grad_joint,
        attended_rows,
        grad_attn,
        normed_two,
        grad_hidden,
        activated,
        grad_branch,
    )
    return (grad_in.reshape(seq_count, row_count, model_width), factors, small_cols, unit_sums)


def on_device(
    inputs, cotangent, positions, w_qkv, w_attn_out, w_fc, w_proj, norm_gains, biases, fc_bias
):
    micro_count, seq_count, row_count, model_width = inputs.shape
    unit_count = w_fc.shape[2]
    shard_count = lax.axis_size(("dp", "ctx"))
    section_index = lax.axis_index("section")
    places_all = lax.all_gather(positions, "ctx", axis=1, tiled=True)
    params = (
        lax.all_gather(w_qkv[0], ("dp", "ctx"), axis=0, tiled=True),
        lax.all_gather(w_attn_out[0], ("dp", "ctx"), axis=0, tiled=True),
        lax.all_gather(w_fc[0], ("dp", "ctx"), axis=0, tiled=True),
        lax.all_gather(w_proj[0], ("dp", "ctx"), axis=0, tiled=True),
        lax.all_gather(norm_gains[0], ("dp", "ctx"), axis=0, tiled=True),
        lax.all_gather(biases[0], ("dp", "ctx"), axis=0, tiled=True),
        lax.all_gather(fc_bias[0], ("dp", "ctx"), axis=0, tiled=True),
    )
    outs_forward = jnp.zeros_like(inputs)
    outs_backward = jnp.zeros_like(inputs)
    arrived = jnp.zeros((seq_count, row_count, model_width), jnp.bfloat16)
    returned = jnp.zeros((seq_count, row_count, model_width), jnp.bfloat16)
    history = []
    factor_list = []
    small_total = jnp.zeros((model_width, 8), jnp.float32)
    unit_total = jnp.zeros((unit_count,), jnp.float32)

    def by_section(late_value, early_value):
        return jnp.where(section_index == 1, late_value, early_value)

    for step_index in range(micro_count + 2):
        forward_index = step_index - section_index
        forward_valid = (forward_index >= 0) & (forward_index < micro_count)
        forward_pick = jnp.clip(forward_index, 0, micro_count - 1)
        source = lax.dynamic_index_in_dim(inputs, forward_pick, 0, keepdims=False)
        layer_in = jnp.where(section_index == 0, source, arrived)
        place_query = lax.dynamic_index_in_dim(positions, forward_pick, 0, keepdims=False)
        place_keys = lax.dynamic_index_in_dim(places_all, forward_pick, 0, keepdims=False)
        result, kept = layer_forward(layer_in, place_query, place_keys, params)
        earlier = lax.dynamic_index_in_dim(outs_forward, forward_pick, 0, keepdims=False)
        outs_forward = lax.dynamic_update_index_in_dim(
            outs_forward, jnp.where(forward_valid, result, earlier), forward_pick, 0
        )
        arrived = shifted(result, "section", 1)
        history.append((kept, place_query, place_keys))
        older = history[step_index - 2] if step_index >= 2 else history[step_index]
        chosen, back_query, back_keys = jax.tree.map(by_section, history[step_index], older)
        back_index = step_index - 2 + section_index
        back_valid = (back_index >= 0) & (back_index < micro_count)
        back_pick = jnp.clip(back_index, 0, micro_count - 1)
        seed_grad = jnp.where(
            section_index == 1,
            lax.dynamic_index_in_dim(cotangent, back_pick, 0, keepdims=False),
            returned,
        )
        seed_grad = jnp.where(back_valid, seed_grad, jnp.zeros_like(seed_grad))
        grad_in, factors, small_cols, unit_sums = layer_backward(
            seed_grad, chosen, back_query, back_keys, params
        )
        factor_list.append(factors)
        small_total = small_total + small_cols
        unit_total = unit_total + unit_sums
        grad_low = grad_in.astype(jnp.bfloat16)
        previous = lax.dynamic_index_in_dim(outs_backward, back_pick, 0, keepdims=False)
        outs_backward = lax.dynamic_update_index_in_dim(
            outs_backward, jnp.where(back_valid, grad_low, previous), back_pick, 0
        )
        returned = shifted(grad_low, "section", -1)
    joined = [jnp.concatenate(parts, axis=0) for parts in zip(*factor_list)]
    (
        normed_all,
        joint_all,
        attended_all,
        attn_all,
        normed_two_all,
        hidden_all,
        activated_all,
        branch_all,
    ) = joined
    wide_full = jnp.concatenate(
        [
            contract_rows(normed_all, joint_all),
            contract_rows(attended_all, attn_all),
            contract_rows(normed_two_all, hidden_all),
            small_total,
        ],
        axis=1,
    )
    tall_full = jnp.concatenate(
        [contract_rows(activated_all, branch_all), unit_total[:, None]], axis=1
    )
    wide_parts = wide_full.reshape(shard_count, model_width // shard_count, wide_full.shape[1])
    tall_parts = tall_full.reshape(shard_count, unit_count // shard_count, tall_full.shape[1])
    got_wide, got_tall = (
        lax.all_to_all(
            wide_parts.astype(jnp.bfloat16), ("dp", "ctx"), split_axis=0, concat_axis=0, tiled=True
        ).astype(wide_parts.dtype),
        lax.all_to_all(
            tall_parts.astype(jnp.bfloat16), ("dp", "ctx"), split_axis=0, concat_axis=0, tiled=True
        ).astype(tall_parts.dtype),
    )
    sums_wide = jnp.sum(got_wide, axis=0)
    sums_tall = jnp.sum(got_tall, axis=0)
    cut_one = 3 * model_width
    cut_two = 4 * model_width
    cut_three = cut_two + unit_count
    grad_joint = sums_wide[:, :cut_one]
    grad_output = sums_wide[:, cut_one:cut_two]
    grad_hidden = sums_wide[:, cut_two:cut_three]
    grad_gain_cols = sums_wide[:, cut_three : cut_three + 2]
    grad_shift_cols = sums_wide[:, cut_three + 2 : cut_three + 8]
    grad_back = sums_tall[:, :model_width]
    grad_units = sums_tall[:, model_width]
    return (
        outs_forward[None],
        outs_backward[None],
        grad_joint[None],
        grad_output[None],
        grad_hidden[None],
        grad_back[None],
        grad_gain_cols[None],
        grad_shift_cols[None],
        grad_units[None],
    )


def solution(mesh):
    in_specs = (
        P(None, "dp", "ctx", None),
        P(None, "dp", "ctx", None),
        P(None, "ctx"),
        P("section", ("dp", "ctx"), None),
        P("section", ("dp", "ctx"), None),
        P("section", ("dp", "ctx"), None),
        P("section", ("dp", "ctx"), None),
        P("section", ("dp", "ctx"), None),
        P("section", ("dp", "ctx"), None),
        P("section", ("dp", "ctx")),
    )
    out_specs = (
        P("section", None, "dp", "ctx", None),
        P("section", None, "dp", "ctx", None),
        P("section", ("dp", "ctx"), None),
        P("section", ("dp", "ctx"), None),
        P("section", ("dp", "ctx"), None),
        P("section", ("dp", "ctx"), None),
        P("section", ("dp", "ctx"), None),
        P("section", ("dp", "ctx"), None),
        P("section", ("dp", "ctx")),
    )
    return jax.shard_map(
        on_device, mesh=mesh, in_specs=in_specs, out_specs=out_specs, check_vma=False
    )
```

profile of v0, /device:TPU:3, one launch (start us, length us, event | category | flops | bytes accessed | tf_op | source)
XLA Modules:
  0.0 3682.4 jit_solution(10339652002548080763)
XLA Ops:
  13.0 50.3 %all-gather = bf16[1,1600,2]{2,0,1:T(2,128)(2,1)S(1)} all-gather(bf16[1,100,2]{2,0,1:T(2,128)(2,1)S(1)} %copy.168), channel_id=2, replica_groups=mesh['section'=2,'dp'=2,'ctx'=8] {'dp','ctx'}, dimensions={1}, use_global_device_ids=true | all-gather | bytes 6800 | tf_op jit(solution)/shard_map/all_gather | solution.py:277
  64.3 46.1 %all-gather.1 = bf16[1,1600,6]{2,0,1:T(2,128)(2,1)S(1)} all-gather(bf16[1,100,6]{2,0,1:T(2,128)(2,1)S(1)} %copy.169), channel_id=3, replica_groups=mesh['section'=2,'dp'=2,'ctx'=8] {'dp','ctx'}, dimensions={1}, use_global_device_ids=true | all-gather | bytes 20400 | tf_op jit(solution)/shard_map/all_gather | solution.py:278
  115.4 84.7 %all-gather.40.cloned.1.call-done = bf16[1,1600,4800]{2,0,1:T(2,128)(2,1)} async-done(((bf16[1,100,4800]{2,0,1:T(2,128)(2,1)}), bf16[1,1600,4800]{2,0,1:T(2,128)(2,1)}) %all-gather.40.cloned.1.call-update) | async-done | bytes 15360016 | tf_op jit(solution)/shard_map/all_gather | solution.py:273
  200.1 20.1 copy.205
  241.0 62.6 %all-reduce = bf16[6400]{0:T(1024)(128)(2,1)S(1)} all-reduce(bf16[6400]{0:T(1024)(128)(2,1)S(1)} %dynamic-update-slice), channel_id=9, replica_groups=mesh['section'=2,'dp'=2,'ctx'=8] {'dp','ctx'}, use_global_device_ids=true, to_apply=%add | all-reduce | flops 6400 | bytes 25600
  325.2 33.0 all-gather.42.cloned.1.call-done
  375.1 47.8 %all-gather.44.cloned.1.call-done = bf16[1024,1600]{0,1:T(8,128)(2,1)} async-done(((bf16[128,1600]{0,1:T(8,128)(2,1)}), bf16[1024,1600]{0,1:T(8,128)(2,1)}) %all-gather.44.cloned.1.call-update) | async-done | bytes 3276816 | tf_op jit(solution)/shard_map/all_gather | solution.py:47
  434.4 192.5 %all-gather.48.cloned.1.call-done = bf16[1,1600,6400]{2,0,1:T(2,128)(2,1)} async-done(((bf16[1,100,6400]{2,0,1:T(2,128)(2,1)}), bf16[1,1600,6400]{2,0,1:T(2,128)(2,1)}) %all-gather.48.cloned.1.call-update) | async-done | bytes 20480016 | tf_op jit(solution)/shard_map/all_gather | solution.py:275
  626.8 31.7 copy.207
  671.4 67.3 %all-gather.50.cloned.1.call-done = bf16[1,6400,1600]{2,1,0:T(8,128)(2,1)} async-done(((bf16[1,400,1600]{2,1,0:T(8,128)(2,1)}), bf16[1,6400,1600]{2,1,0:T(8,128)(2,1)}) %all-gather.50.cloned.1.call-update) | async-done | bytes 20480016 | tf_op jit(solution)/shard_map/all_gather | solution.py:276
  806.6 34.9 all-gather.52.cloned.1.call-done
  859.0 47.4 %all-gather.54.cloned.1.call-done = bf16[1024,1600]{0,1:T(8,128)(2,1)} async-done(((bf16[128,1600]{0,1:T(8,128)(2,1)}), bf16[1024,1600]{0,1:T(8,128)(2,1)}) %all-gather.54.cloned.1.call-update) | async-done | bytes 3276816 | tf_op jit(solution)/shard_map/all_gather | solution.py:47
  1010.2 19.3 reduce-scatter.25.cloned.1.call-done
  1031.5 78.8 %reduce-scatter.27.cloned.1.call-done = bf16[128,1600]{1,0:T(8,128)(2,1)} async-done(((bf16[1024,1600]{1,0:T(8,128)(2,1)}), bf16[128,1600]{1,0:T(8,128)(2,1)}) %reduce-scatter.27.cloned.1.call-update) | async-done | bytes 409616
  1250.6 17.7 all-gather.58.cloned.1.call-done
  1322.5 25.1 reduce-scatter.29.cloned.1.call-done
  1349.6 78.7 %reduce-scatter.31.cloned.1.call-done = bf16[128,1600]{1,0:T(8,128)(2,1)} async-done(((bf16[1024,1600]{1,0:T(8,128)(2,1)}), bf16[128,1600]{1,0:T(8,128)(2,1)}) %reduce-scatter.31.cloned.1.call-update) | async-done | bytes 409616
  1513.4 45.3 %all-gather.32.cloned.1.call-done = bf16[1024,1600]{0,1:T(8,128)(2,1)} async-done(((bf16[128,1600]{0,1:T(8,128)(2,1)}), bf16[1024,1600]{0,1:T(8,128)(2,1)}) %all-gather.32.cloned.1.call-update) | async-done | bytes 3276816 | tf_op jit(solution)/shard_map/while/body/eval_jaxpr/all_gather | solution.py:80
  1641.0 47.1 %all-gather.62.cloned.1.call-done = bf16[1024,1600]{0,1:T(8,128)(2,1)} async-done(((bf16[128,1600]{0,1:T(8,128)(2,1)}), bf16[1024,1600]{0,1:T(8,128)(2,1)}) %all-gather.62.cloned.1.call-update) | async-done | bytes 3276816 | tf_op jit(solution)/shard_map/all_gather | solution.py:47
  1700.9 66.4 %reduce-scatter.33.cloned.1.call-done = bf16[128,1600]{1,0:T(8,128)(2,1)} async-done(((bf16[1024,1600]{1,0:T(8,128)(2,1)}), bf16[128,1600]{1,0:T(8,128)(2,1)}) %reduce-scatter.33.cloned.1.call-update) | async-done | bytes 409616
  1769.3 78.7 %reduce-scatter.35.cloned.1.call-done = bf16[128,1600]{1,0:T(8,128)(2,1)} async-done(((bf16[1024,1600]{1,0:T(8,128)(2,1)}), bf16[128,1600]{1,0:T(8,128)(2,1)}) %reduce-scatter.35.cloned.1.call-update) | async-done | bytes 409616
  1878.5 16.6 convolution_convert_fusion
  1895.1 29.8 copy.181
  1941.8 21.5 pad_maximum_fusion
  1988.7 162.5 %all-gather.38.cloned.1.call-done = bf16[1024,1600]{0,1:T(8,128)(2,1)} async-done(((bf16[128,1600]{0,1:T(8,128)(2,1)}), bf16[1024,1600]{0,1:T(8,128)(2,1)}) %all-gather.38.cloned.1.call-update) | async-done | bytes 3276816 | tf_op jit(solution)/shard_map/while/body/eval_jaxpr/all_gather | solution.py:81
  2159.8 202.1 %all-gather.36.cloned.1.call-done = bf16[1024,1600]{0,1:T(8,128)(2,1)} async-done(((bf16[128,1600]{0,1:T(8,128)(2,1)}), bf16[1024,1600]{0,1:T(8,128)(2,1)}) %all-gather.36.cloned.1.call-update) | async-done | bytes 3276816 | tf_op jit(solution)/shard_map/while/body/eval_jaxpr/all_gather | solution.py:80
  2454.4 71.4 %reduce-scatter.37.cloned.1.call-done = bf16[128,1600]{1,0:T(8,128)(2,1)} async-done(((bf16[1024,1600]{1,0:T(8,128)(2,1)}), bf16[128,1600]{1,0:T(8,128)(2,1)}) %reduce-scatter.37.cloned.1.call-update) | async-done | bytes 409616
  2527.1 91.1 %reduce-scatter.39.cloned.1.call-done = bf16[128,1600]{1,0:T(8,128)(2,1)} async-done(((bf16[1024,1600]{1,0:T(8,128)(2,1)}), bf16[128,1600]{1,0:T(8,128)(2,1)}) %reduce-scatter.39.cloned.1.call-update) | async-done | bytes 409616
  2648.6 67.7 %concatenate.57 = bf16[1600,12808]{1,0:T(8,128)(2,1)} concatenate(bf16[1600,4800]{1,0:T(8,128)(2,1)} %convolution_convert_fusion.2, bf16[1600,1600]{1,0:T(8,128)(2,1)} %convolution_convert_fusion.3, bf16[1600,6400]{1,0:T(8,128)(2,1)} %convolution_convert_fusion.1, bf16[1600,8]{1,0:T(8,128)(2,1)S(1)} %copy-done.101), dimensions={1} | concatenate | bytes 81971200 | tf_op jit(solution)/shard_map/concatenate | solution.py:342
  2716.4 48.1 %convert_element_type.713 = bf16[16,100,12808]{2,1,0:T(8,128)(2,1)} reshape(bf16[1600,12808]{1,0:T(8,128)(2,1)} %concatenate.57) | data formatting | bytes 81971200 | tf_op jit(solution)/shard_map/convert_element_type | solution.py:358
  2801.3 839.5 %all-to-all-done = bf16[16,100,12808]{2,1,0:T(8,128)(2,1)} async-done(((bf16[16,100,12808]{2,1,0:T(8,128)(2,1)}), bf16[16,100,12808]{2,1,0:T(8,128)(2,1)}, u32[]{:S(2)}, u32[]{:S(2)}) %all-to-all-start) | async-done | bytes 40985632 | tf_op jit(solution)/shard_map/all_to_all | solution.py:357
  3640.8 17.6 convert_reduce_fusion
  (839 shorter events, 920.4 us)
Async XLA Ops:
  7.2 192.9 %all-gather.40.cloned.1.call-start = ((), (), s32[]{:S(2)}) async-start(), calls=%async_computation.14 | async-start | bytes 33075200 | tf_op jit(solution)/shard_map/all_gather | solution.py:273
  11.3 306.6 %all-gather.46.cloned.1.call-start = ((), (), s32[]{:S(2)}) async-start(), calls=%async_computation.17 | async-start | bytes 11315200 | tf_op jit(solution)/shard_map/all_gather | solution.py:274
  12.7 345.4 %all-gather.42.cloned.1.call-start = ((), (), s32[]{:S(2)}) async-start(), calls=%async_computation.15 | async-start | bytes 3686400 | tf_op jit(solution)/shard_map/all_gather | solution.py:46
  232.3 190.6 %all-gather.44.cloned.1.call-start = ((), (), s32[]{:S(2)}) async-start(), calls=%async_computation.16 | async-start | bytes 3686400 | tf_op jit(solution)/shard_map/all_gather | solution.py:47
  235.2 391.6 %all-gather.48.cloned.1.call-start = ((), (), s32[]{:S(2)}) async-start(), calls=%async_computation.18 | async-start | bytes 43520000 | tf_op jit(solution)/shard_map/all_gather | solution.py:275
  238.8 499.9 %all-gather.50.cloned.1.call-start = ((), (), s32[]{:S(2)}) async-start(), calls=%async_computation.19 | async-start | bytes 22630400 | tf_op jit(solution)/shard_map/all_gather | solution.py:276
  239.4 602.2 %all-gather.52.cloned.1.call-start = ((), (), s32[]{:S(2)}) async-start(), calls=%async_computation.20 | async-start | bytes 3686400 | tf_op jit(solution)/shard_map/all_gather | solution.py:46
  750.9 12.7 collective-permute-start
  776.8 129.5 %all-gather.54.cloned.1.call-start = ((), (), s32[]{:S(2)}) async-start(), calls=%async_computation.21 | async-start | bytes 3686400 | tf_op jit(solution)/shard_map/all_gather | solution.py:47
  779.6 250.0 %reduce-scatter.25.cloned.1.call-start = ((), (), s32[]{:S(2)}) async-start(), calls=%async_computation.26 | async-start | bytes 3833856
  953.7 156.5 %reduce-scatter.27.cloned.1.call-start = ((), (), s32[]{:S(2)}) async-start(), calls=%async_computation.27 | async-start | bytes 3833856
  969.4 263.7 %all-gather.56.cloned.1.call-start = ((), (), s32[]{:S(2)}) async-start(), calls=%async_computation.22 | async-start | bytes 3686400 | tf_op jit(solution)/shard_map/all_gather | solution.py:46
  998.1 11.9 collective-permute-start.1
  1139.6 128.7 %all-gather.58.cloned.1.call-start = ((), (), s32[]{:S(2)}) async-start(), calls=%async_computation.23 | async-start | bytes 3686400 | tf_op jit(solution)/shard_map/all_gather | solution.py:47
  1145.8 10.2 collective-permute-start.3
  1148.1 199.5 %reduce-scatter.29.cloned.1.call-start = ((), (), s32[]{:S(2)}) async-start(), calls=%async_computation.28 | async-start | bytes 3833856
  1216.4 211.8 %reduce-scatter.31.cloned.1.call-start = ((), (), s32[]{:S(2)}) async-start(), calls=%async_computation.29 | async-start | bytes 3833856
  1231.1 273.8 %all-gather.34.cloned.1.call-start = ((), (), s32[]{:S(2)}) async-start(), calls=%async_computation.11 | async-start | bytes 3686400 | tf_op jit(solution)/shard_map/while/body/eval_jaxpr/all_gather | solution.py:81
  1231.7 327.0 %all-gather.32.cloned.1.call-start = ((), (), s32[]{:S(2)}) async-start(), calls=%async_computation.10 | async-start | bytes 3686400 | tf_op jit(solution)/shard_map/while/body/eval_jaxpr/all_gather | solution.py:80
  1233.0 390.4 %all-gather.60.cloned.1.call-start = ((), (), s32[]{:S(2)}) async-start(), calls=%async_computation.24 | async-start | bytes 3686400 | tf_op jit(solution)/shard_map/all_gather | solution.py:46
  1310.3 11.9 collective-permute-start.2
  1457.7 230.3 %all-gather.62.cloned.1.call-start = ((), (), s32[]{:S(2)}) async-start(), calls=%async_computation.25 | async-start | bytes 3686400 | tf_op jit(solution)/shard_map/all_gather | solution.py:47
  1463.1 10.2 collective-permute-start.4
  1466.1 301.2 %reduce-scatter.33.cloned.1.call-start = ((), (), s32[]{:S(2)}) async-start(), calls=%async_computation.30 | async-start | bytes 3833856
  1588.5 259.5 %reduce-scatter.35.cloned.1.call-start = ((), (), s32[]{:S(2)}) async-start(), calls=%async_computation.31 | async-start | bytes 3833856
  1861.4 16.1 collective-permute-start.5
  1963.4 801.1 %all-to-all-start.1 = ((bf16[16,400,1601]{2,1,0:T(8,128)(2,1)}), bf16[16,400,1601]{2,1,0:T(8,128)(2,1)}, u32[]{:S(2)}, u32[]{:S(2)}) async-start(bf16[16,400,1601]{2,1,0:T(8,128)(2,1)} %pad_maximum_fusion), calls=%async_computation.1 | async-start | bytes 42598400 | tf_op jit(solution)/shard_map/all_to_all | solution.py:360
  1969.9 181.3 %all-gather.38.cloned.1.call-start = ((), (), s32[]{:S(2)}) async-start(), calls=%async_computation.13 | async-start | bytes 3686400 | tf_op jit(solution)/shard_map/while/body/eval_jaxpr/all_gather | solution.py:81
  1970.7 391.2 %all-gather.36.cloned.1.call-start = ((), (), s32[]{:S(2)}) async-start(), calls=%async_computation.12 | async-start | bytes 3686400 | tf_op jit(solution)/shard_map/while/body/eval_jaxpr/all_gather | solution.py:80
  1971.4 554.5 %reduce-scatter.37.cloned.1.call-start = ((), (), s32[]{:S(2)}) async-start(), calls=%async_computation.32 | async-start | bytes 3833856
  2391.7 226.6 %reduce-scatter.39.cloned.1.call-start = ((), (), s32[]{:S(2)}) async-start(), calls=%async_computation.33 | async-start | bytes 3833856
  2764.5 876.3 %all-to-all-start = ((bf16[16,100,12808]{2,1,0:T(8,128)(2,1)}), bf16[16,100,12808]{2,1,0:T(8,128)(2,1)}, u32[]{:S(2)}, u32[]{:S(2)}) async-start(bf16[16,100,12808]{2,1,0:T(8,128)(2,1)} %convert_element_type.713), calls=%async_computation | async-start | bytes 86048768 | tf_op jit(solution)/shard_map/all_to_all | solution.py:357
  (248 other events, 12282.6 us)
Sparse Core Ops, SparseCore 0:
  11.4 188.6 all-gather.39
  202.9 90.4 all-gather.45
  296.1 62.0 all-gather.41
  360.1 62.7 all-gather.43
  424.9 201.9 all-gather.47
  628.3 110.3 all-gather.49
  776.9 64.5 all-gather.51
  843.6 62.7 all-gather.53
  953.9 75.6 reduce-scatter.24
  1033.4 76.7 reduce-scatter.26
  1139.8 63.8 all-gather.55
  1205.5 62.7 all-gather.57
  1271.9 75.6 reduce-scatter.28
  1351.5 76.7 reduce-scatter.30
  1430.2 63.8 all-gather.33
  1495.9 62.7 all-gather.31
  1560.6 62.7 all-gather.59
  1625.3 62.7 all-gather.61
  1691.7 75.6 reduce-scatter.32
  1771.2 76.7 reduce-scatter.34
  1972.8 178.3 all-gather.37
  2153.2 208.6 all-gather.35
  2391.8 134.0 reduce-scatter.36
  2529.8 88.4 reduce-scatter.38
where the time goes:
time: 3750 us; the launch traced here: 3680 us
  waiting for transfers between devices  2380 us (63%)
  matrix products  568 us (15%)
  local copies, waits for them, and re-layouts  337 us (9%)
  other arithmetic  181 us (5%)
  blocking collectives  172 us (5%)
    all_to_all x1, waiting for transfers between devices, on_device(): lax.all_to_all(wide_parts.astype(jnp.bfloat16), ('dp', 'ctx'), split_axis...  840 us
    unnamed x32, waiting for transfers between devices  512 us
    all_gather x2, waiting for transfers between devices, one_sequence(): lax.all_gather(key_one, 'ctx', axis=0, tiled=True)  247 us
    all_gather x1, waiting for transfers between devices, on_device(): lax.all_gather(w_fc[0], ('dp', 'ctx'), axis=0, tiled=True)  192 us
    unnamed x530, local copies, waits for them, and re-layouts  164 us
    all_gather x2, waiting for transfers between devices, one_sequence(): lax.all_gather(value_one, 'ctx', axis=0, tiled=True)  162 us
    all_gather x4, waiting for transfers between devices, attend(): value_piece = lax.all_gather(value_rows, 'ctx', axis=1, tiled=True)  160 us
    dot_general x16, matrix products, contract_cols(): lax.dot_general(left_side, right_side, (((1,), (1,)), ((), ())), preferre...  154 us
  transfers between devices with their start and end apart: 32, of which 27 were waited for; matrix products, arithmetic and copies ran while one was open for 22% of the time, Pallas kernels for 0%

commit v1 on v0

v1 whole, which is shorter than its diff:
```python
import jax
import jax.numpy as jnp
from jax import lax
from jax.sharding import Mesh
from jax.sharding import PartitionSpec as P

HEADS = 25
EPSILON = 1e-05

SLAB = ("section", "dp", "r")
ALL = ("section", "dp", "z", "r")


def normalize(rows_in, gain_col, shift_col):
    centred = rows_in - jnp.mean(rows_in, axis=-1, keepdims=True)
    spread = jnp.mean(centred * centred, axis=-1, keepdims=True)
    return centred * lax.rsqrt(spread + EPSILON) * gain_col + shift_col


def smooth(values_in):
    return jax.nn.gelu(values_in, approximate=True)


def dot(a, b, ca, cb):
    return lax.dot_general(a, b, (((ca,), (cb,)), ((), ())), preferred_element_type=jnp.float32)


class Layout:
    def __init__(self, inputs, w_fc):
        self.micros, _, self.rows, self.width = inputs.shape
        self.sections = lax.axis_size("section")
        self.cores = lax.axis_size("dp")
        self.zs = lax.axis_size("z")
        self.rest = lax.axis_size("r")
        self.slab = self.sections * self.cores * self.rest
        self.shards = self.cores * self.zs * self.rest
        self.units = w_fc.shape[2]
        self.tokens = self.rows * self.slab
        self.seqs = self.cores
        self.head = self.width // HEADS
        self.slots = -(-HEADS // self.slab)
        self.block = self.width // self.shards
        self.unit_block = self.units // self.shards
        self.half = self.unit_block // self.sections
        self.cols = self.width // self.slab
        self.x = lax.axis_index("section")
        self.c = lax.axis_index("dp")
        self.z = lax.axis_index("z")
        self.r = lax.axis_index("r")
        self.t = (self.x * self.cores + self.c) * self.rest + self.r

    def number(self, x, c, z, r):
        return ((x * self.cores + c) * self.zs + z) * self.rest + r

    def order(self, a):
        lead = a.shape[:-1]
        a = a.reshape(*lead, self.cores, self.zs, self.rest * self.block)
        return jnp.swapaxes(a, -3, -2).reshape(*lead, self.width)

    def restore(self, a):
        lead = a.shape[:-1]
        a = a.reshape(*lead, self.zs, self.cores, self.rest * self.block)
        return jnp.swapaxes(a, -3, -2).reshape(*lead, self.width)

    def routes(self, micro):
        pairs = []
        for x in range(self.sections):
            for c in range(self.cores):
                for s in range(self.seqs):
                    for r in range(self.rest):
                        place = x * self.cores + c
                        pairs.append(((x, s, place, r), (x, c, micro * self.seqs + s, r)))
        return pairs

    def tokens_in(self, a):
        got = []
        for micro in range(self.micros):
            route = [(self.number(*f), self.number(*g)) for f, g in self.routes(micro)]
            got.append(lax.ppermute(a[micro, 0], ALL, route))
        out = got[0]
        for micro in range(1, self.micros):
            out = jnp.where(self.z // self.seqs == micro, got[micro], out)
        return out

    def tokens_out(self, parts):
        result = []
        for micro in range(self.micros):
            got = []
            for layer, part in enumerate(parts):
                route = [
                    (self.number(*g), self.number(layer, *f[1:])) for f, g in self.routes(micro)
                ]
                got.append(lax.ppermute(part, ALL, route))
            out = got[0]
            for layer in range(1, len(parts)):
                out = jnp.where(self.x == layer, got[layer], out)
            result.append(out)
        return jnp.stack(result)[None, :, None]


def slab_gather(a):
    return lax.all_gather(a, SLAB, axis=0, tiled=True)


def slab_sum(a, lay):
    parts = a.astype(jnp.bfloat16).reshape(lay.slab, lay.rows, a.shape[1])
    got = lax.all_to_all(parts, SLAB, 0, 0, tiled=True)
    return jnp.sum(got.astype(jnp.float32), axis=0)


def ring_sum(part, lay):
    ring = [(i, (i + 1) % lay.zs) for i in range(lay.zs)]

    def own(step):
        return lax.dynamic_index_in_dim(part, (lay.z - 1 - step) % lay.zs, 0, keepdims=False)

    acc = own(0).astype(jnp.bfloat16)
    for step in range(1, lay.zs):
        acc = lax.ppermute(acc, "z", ring)
        acc = (acc.astype(jnp.float32) + own(step).astype(jnp.float32)).astype(jnp.bfloat16)
    return acc


def spread_weights(lay, w_qkv, w_attn_out, w_fc, w_proj):
    n = lay.slab
    width, block = lay.width, lay.block
    slot_cols = lay.slots * lay.head
    qkv = w_qkv[0].reshape(block, 3, width)
    qkv = jnp.pad(qkv, ((0, 0), (0, 0), (0, n * slot_cols - width)))
    qkv = qkv.reshape(block, 3, n, slot_cols).transpose(2, 0, 1, 3).reshape(n, block, 3 * slot_cols)
    out = lay.order(w_attn_out[0]).reshape(block, n, lay.cols).transpose(1, 0, 2)
    fc = w_fc[0].reshape(block, lay.cores, lay.zs, lay.rest, lay.sections, lay.half)
    fc = fc.transpose(4, 1, 3, 0, 2, 5).reshape(n, block, lay.zs * lay.half)
    proj = lay.order(w_proj[0]).reshape(lay.sections, lay.half, width)

    def move(a):
        got = lax.all_to_all(a, SLAB, 0, 0, tiled=True)
        got = got.reshape(lay.sections, lay.cores * lay.rest * block, a.shape[2])
        return [got[layer] for layer in range(lay.sections)]

    qkv, out, fc = move(qkv), move(out), move(fc)
    proj = lax.all_to_all(proj, ("section",), 0, 0, tiled=True)
    params = []
    for layer in range(lay.sections):
        full = [
            lax.all_gather(a, "z", axis=0, tiled=True)
            for a in (qkv[layer], out[layer], fc[layer], proj[layer])
        ]
        wo = full[1].reshape(lay.zs, lay.cores, lay.rest * block, lay.cols)
        wo = jnp.swapaxes(wo, 0, 1).reshape(width, lay.cols)
        wo = jnp.pad(wo, ((0, n * slot_cols - width), (0, 0))).reshape(n, slot_cols, lay.cols)
        wo = lax.all_to_all(wo, SLAB, 0, 0, tiled=True)
        wo = wo.transpose(1, 0, 2).reshape(slot_cols, width)
        params.append((full[0], wo, full[2], full[3]))
    return params


def attend(q, k, v, places, lay):
    tokens = q.shape[0]
    scale = lay.head ** (-0.5)
    qh = q.reshape(tokens, lay.slots, lay.head)
    kh = k.reshape(tokens, lay.slots, lay.head)
    vh = v.reshape(tokens, lay.slots, lay.head)
    scores = jnp.einsum("qhd,nhd->hqn", qh, kh, preferred_element_type=jnp.float32) * scale
    allowed = (places[:, None] >= places[None, :])[None]
    scores = jnp.where(allowed, scores, -1e30)
    top = jnp.max(scores, axis=-1)
    weights = jnp.exp(scores - top[..., None])
    total = jnp.sum(weights, axis=-1)
    mixed = jnp.einsum(
        "hqn,nhd->hqd", weights.astype(jnp.bfloat16), vh, preferred_element_type=jnp.float32
    )
    mixed = (mixed / total[..., None]).transpose(1, 0, 2).reshape(tokens, -1)
    return mixed.astype(jnp.bfloat16), top + jnp.log(total)


def attend_back(q, k, v, g, logs, places, lay):
    tokens = q.shape[0]
    scale = lay.head ** (-0.5)
    qh = q.reshape(tokens, lay.slots, lay.head)
    kh = k.reshape(tokens, lay.slots, lay.head)
    vh = v.reshape(tokens, lay.slots, lay.head)
    gh = g.reshape(tokens, lay.slots, lay.head)
    scores = jnp.einsum("qhd,nhd->hqn", qh, kh, preferred_element_type=jnp.float32) * scale
    allowed = (places[:, None] >= places[None, :])[None]
    probs = jnp.where(allowed, jnp.exp(scores - logs[..., None]), 0.0)
    g_probs = jnp.einsum("qhd,nhd->hqn", gh, vh, preferred_element_type=jnp.float32)
    centre = jnp.sum(probs * g_probs, axis=-1, keepdims=True)
    g_scores = (probs * (g_probs - centre)).astype(jnp.bfloat16)
    gq = jnp.einsum("hqn,nhd->qhd", g_scores, kh, preferred_element_type=jnp.float32) * scale
    gk = jnp.einsum("hqn,qhd->nhd", g_scores, qh, preferred_element_type=jnp.float32) * scale
    gv = jnp.einsum(
        "hqn,qhd->nhd", probs.astype(jnp.bfloat16), gh, preferred_element_type=jnp.float32
    )
    return [a.reshape(tokens, -1).astype(jnp.bfloat16) for a in (gq, gk, gv)]


def forward(h, params, small, places, lay):
    w_qkv, w_out, w_fc, w_proj = params
    gains, shifts, q_bias, v_bias, unit_bias = small
    span = lay.slots * lay.head
    normed = slab_gather(normalize(h, gains[0], shifts[0]).astype(jnp.bfloat16))
    qkv = dot(normed, w_qkv, 1, 0)
    q = (qkv[:, :span] + q_bias).astype(jnp.bfloat16)
    k = qkv[:, span : 2 * span].astype(jnp.bfloat16)
    v = (qkv[:, 2 * span :] + v_bias).astype(jnp.bfloat16)
    attended, logs = attend(q, k, v, places, lay)
    mid = h + (slab_sum(dot(attended, w_out, 1, 0), lay) + shifts[3])
    normed_two = slab_gather(normalize(mid, gains[1], shifts[4]).astype(jnp.bfloat16))
    hidden = dot(normed_two, w_fc, 1, 0) + unit_bias
    activated = smooth(hidden).astype(jnp.bfloat16)
    result = mid + (slab_sum(dot(activated, w_proj, 1, 0), lay) + shifts[5])
    kept = (h, mid, normed, q, k, v, attended, logs, normed_two, hidden, activated)
    return result.astype(jnp.bfloat16), kept


def backward(g_rows, kept, params, small, places, lay):
    w_qkv, w_out, w_fc, w_proj = params
    gains, shifts, q_bias, v_bias, unit_bias = small
    h, mid, normed, q, k, v, attended, logs, normed_two, hidden, activated = kept
    branch_rows = g_rows.astype(jnp.bfloat16)
    branch = slab_gather(branch_rows)
    g_activated = dot(branch, w_proj, 1, 1)
    _, smooth_back = jax.vjp(smooth, hidden)
    g_hidden = smooth_back(g_activated)[0].astype(jnp.bfloat16)
    grad_proj = dot(activated, branch, 0, 0)
    g_normed_two = slab_sum(dot(g_hidden, w_fc, 1, 1), lay)
    grad_fc = dot(normed_two, g_hidden, 0, 0)
    _, second_back = jax.vjp(normalize, mid, gains[1], shifts[4])
    mid_part, gain_two, shift_two = second_back(g_normed_two)
    g_mid = g_rows + mid_part
    g_attn_rows = g_mid.astype(jnp.bfloat16)
    g_attn = slab_gather(g_attn_rows)
    g_attended = dot(g_attn, w_out, 1, 1).astype(jnp.bfloat16)
    grad_out = dot(attended, g_attn, 0, 0)
    gq, gk, gv = attend_back(q, k, v, g_attended, logs, places, lay)
    joint = jnp.concatenate([gq, gk, gv], axis=1)
    g_normed = slab_sum(dot(joint, w_qkv, 1, 1), lay)
    grad_qkv = dot(normed, joint, 0, 0)
    _, first_back = jax.vjp(normalize, h, gains[0], shifts[0])
    in_part, gain_one, shift_one = first_back(g_normed)
    g_in = g_mid + in_part

    def total(a):
        return jnp.sum(a.astype(jnp.float32), axis=0)

    local = (gain_one, gain_two, shift_one, total(g_attn_rows), shift_two, total(branch_rows))
    shard = (total(gq), total(gv), total(g_hidden))
    return g_in, (grad_qkv, grad_out, grad_fc, grad_proj), local, shard


def on_device(
    inputs, cotangent, positions, w_qkv, w_attn_out, w_fc, w_proj, norm_gains, biases, fc_bias
):
    lay = Layout(inputs, w_fc)
    n, block, width = lay.slab, lay.block, lay.width
    span = lay.slots * lay.head
    micro = lay.z // lay.seqs

    params = spread_weights(lay, w_qkv, w_attn_out, w_fc, w_proj)

    per_row = lay.unit_block // block
    thin = jnp.concatenate([norm_gains[0], biases[0], fc_bias[0].reshape(block, per_row)], axis=1)
    thin = lax.all_gather(thin, ALL, axis=0, tiled=True).astype(jnp.float32)
    thin = thin.reshape(lay.sections, width, 8 + per_row)
    smalls = []
    for layer in range(lay.sections):
        gains = [lay.order(thin[layer, :, i]) for i in range(2)]
        shifts = [lay.order(thin[layer, :, 2 + i]) for i in range(6)]
        heads = [
            lax.dynamic_slice_in_dim(
                jnp.pad(thin[layer, :, 2 + i], (0, n * span - width)), lay.t * span, span
            )
            for i in (1, 2)
        ]
        unit = thin[layer, :, 8:].reshape(lay.cores, lay.zs, lay.rest, lay.sections, lay.half)
        unit = unit.transpose(3, 0, 2, 1, 4).reshape(n, lay.zs * lay.half)
        unit = lax.dynamic_index_in_dim(unit, lay.t, 0, keepdims=False)
        smalls.append((gains, shifts, heads[0], heads[1], unit))

    places = lax.all_gather(positions, ("z", "r"), axis=1, tiled=True)
    places = lax.dynamic_index_in_dim(places, micro, 0, keepdims=False)

    h = lay.order(lay.tokens_in(inputs))
    g = lay.order(lay.tokens_in(cotangent))

    outs, keeps = [], []
    for layer in range(lay.sections):
        h, kept = forward(h.astype(jnp.float32), params[layer], smalls[layer], places, lay)
        outs.append(h)
        keeps.append(kept)

    grads = [None] * lay.sections
    grad_rows = [None] * lay.sections
    locals_, shards = [None] * lay.sections, [None] * lay.sections
    for layer in reversed(range(lay.sections)):
        g, grads[layer], locals_[layer], shards[layer] = backward(
            g.astype(jnp.float32), keeps[layer], params[layer], smalls[layer], places, lay
        )
        g = g.astype(jnp.bfloat16)
        grad_rows[layer] = g

    section_out = lay.tokens_out([lay.restore(a) for a in outs])
    section_grad = lay.tokens_out([lay.restore(a) for a in grad_rows])

    def by_z(a):
        return a.reshape(lay.zs, a.shape[0] // lay.zs, a.shape[1])

    sums = []
    for layer in range(lay.sections):
        grad_qkv, grad_out, grad_fc, grad_proj = grads[layer]
        wo = grad_out.astype(jnp.bfloat16).reshape(span, n, lay.cols).transpose(1, 0, 2)
        wo = lax.all_to_all(wo, SLAB, 0, 0, tiled=True).reshape(n * span, lay.cols)[:width]
        wo = wo.reshape(lay.cores, lay.zs, lay.rest * block, lay.cols)
        wo = jnp.swapaxes(wo, 0, 1).reshape(width, lay.cols)
        sums.append([ring_sum(by_z(a), lay) for a in (grad_qkv, wo, grad_fc, grad_proj)])

    def back(i):
        both = jnp.stack([sums[layer][i] for layer in range(lay.sections)])
        return lax.all_to_all(
            both.reshape(n, block, both.shape[2]), SLAB, 0, 0, tiled=True
        )

    got = back(0).reshape(n, block, 3, span).transpose(1, 2, 0, 3).reshape(block, 3, n * span)
    out_qkv = got[:, :, :width].reshape(block, 3 * width).astype(jnp.float32)
    got = back(1).transpose(1, 0, 2).reshape(block, width)
    out_attn = lay.restore(got).astype(jnp.float32)
    got = back(2).reshape(lay.sections, lay.cores, lay.rest, block, lay.zs, lay.half)
    out_fc = got.transpose(3, 1, 4, 2, 0, 5).reshape(block, lay.units).astype(jnp.float32)
    both = jnp.stack([sums[layer][3] for layer in range(lay.sections)])
    got = lax.all_to_all(both, ("section",), 0, 0, tiled=True)
    out_proj = lay.restore(got.reshape(lay.unit_block, width)).astype(jnp.float32)

    rows = []
    for layer in range(lay.sections):
        gain_one, gain_two, shift_one, s_attn, shift_two, s_branch = [
            lay.restore(a) for a in locals_[layer]
        ]
        gq, gv, units = shards[layer]
        zero = jnp.zeros((n * span,), jnp.float32)
        s_q = lax.dynamic_update_slice_in_dim(zero, gq, lay.t * span, 0)[:width]
        s_v = lax.dynamic_update_slice_in_dim(zero, gv, lay.t * span, 0)[:width]
        cols = [gain_one, gain_two, shift_one, s_q, s_v, s_attn, shift_two, s_branch]
        cols = jnp.stack(cols, axis=1).reshape(lay.shards, block * 8)
        spots = jnp.zeros((n, lay.zs, lay.half), jnp.float32)
        spots = lax.dynamic_update_index_in_dim(
            spots, units.reshape(lay.zs, lay.half), lay.t, 0
        )
        spots = spots.reshape(lay.sections, lay.cores, lay.rest, lay.zs, lay.half)
        spots = spots.transpose(1, 3, 2, 0, 4).reshape(lay.shards, lay.unit_block)
        rows.append(jnp.concatenate([cols, spots], axis=1))
    rows = jnp.concatenate(rows, axis=0)
    rows = jnp.sum(lax.all_to_all(rows, ALL, 0, 0, tiled=True), axis=0)
    cols = rows[: block * 8].reshape(block, 8)
    return (
        section_out,
        section_grad,
        out_qkv[None],
        out_attn[None],
        out_fc[None],
        out_proj[None],
        cols[None, :, :2],
        cols[None, :, 2:],
        rows[None, block * 8 :],
    )


def solution(mesh):
    sections, cores, contexts = (mesh.shape[a] for a in ("section", "dp", "ctx"))
    zs = sections * cores
    shape = (sections, cores, zs, contexts // zs)
    inner = Mesh(mesh.devices.reshape(shape), ALL)
    tokens = P(None, "dp", ("z", "r"), None)
    rows = P("section", ("dp", "z", "r"), None)
    units = P("section", ("dp", "z", "r"))
    out_tokens = P("section", None, "dp", ("z", "r"), None)
    return jax.shard_map(
        on_device,
        mesh=inner,
        in_specs=(tokens, tokens, P(None, ("z", "r"))) + (rows,) * 6 + (units,),
        out_specs=(out_tokens, out_tokens) + (rows,) * 6 + (units,),
        check_vma=False,
    )
```

time: 3750 us -> 1580 us (0.42); the launches traced: 3680 us -> 1570 us
  waiting for transfers between devices: 2380 us -> 628 us
  matrix products: 568 us -> 209 us
  starting transfers between devices: 28 us -> 206 us
  local copies, waits for them, and re-layouts: 337 us -> 192 us
  other arithmetic: 181 us -> 126 us
    all_gather x16 -> x14, waiting for transfers between devices: 994 us -> 241 us  [the longest x8 138 us: slab_gather(): return lax.all_gather(a, SLAB, axis=0, tiled=True)]
    all_to_all x2 -> x19, waiting for transfers between devices: 840 us -> 216 us  [the longest x8 203 us: slab_sum(): got = lax.all_to_all(parts, SLAB, 0, 0, tiled=True)]
    unnamed x32 -> x14, waiting for transfers between devices: 512 us -> 0.75 us
    dot_general x62 -> x36, matrix products: 568 us -> 209 us  [the longest x24 121 us: dot(): lax.dot_general(a, b, (((ca,), (cb,)), ((), ())), preferred_element_type=...]
    unnamed x530 -> x340, local copies, waits for them, and re-layouts: 164 us -> 22.1 us
    ppermute x6 -> x36, waiting for transfers between devices: 31.5 us -> 170 us  [the longest x24 143 us: ring_sum(): acc = lax.ppermute(acc, 'z', ring)]
    all_to_all x2 -> x19, starting transfers between devices: 14.3 us -> 139 us  [the longest x2 41.3 us: on_device(): lax.all_to_all(wo, SLAB, 0, 0, tiled=True).reshape(n * span, lay.cols)]
    concatenate x1 -> x0, local copies, waits for them, and re-layouts: 67.7 us -> none  [on_device(): jnp.concatenate([contract_rows(normed_all, joint_all), contract_rows(atte...]
  transfers between devices with their start and end apart: 32 -> 69, of which waited for: 27 -> 34; matrix products, arithmetic and copies ran while one was open for 22% -> 26% of each run, Pallas kernels for 0% -> 0%
where the time goes in v1:
time: 1580 us; the launch traced here: 1570 us
  waiting for transfers between devices  628 us (40%)
  matrix products  209 us (13%)
  starting transfers between devices  206 us (13%)
  local copies, waits for them, and re-layouts  192 us (12%)
  blocking collectives  189 us (12%)
  other arithmetic  126 us (8%)
  between operations  17.4 us (1%)
    all_to_all x8, waiting for transfers between devices, slab_sum(): got = lax.all_to_all(parts, SLAB, 0, 0, tiled=True)  203 us
    ppermute x24, waiting for transfers between devices, ring_sum(): acc = lax.ppermute(acc, 'z', ring)  143 us
    all_gather x8, waiting for transfers between devices, slab_gather(): return lax.all_gather(a, SLAB, axis=0, tiled=True)  138 us
    dot_general x24, matrix products, dot(): lax.dot_general(a, b, (((ca,), (cb,)), ((), ())), preferred_element_type=...  121 us
    all_gather x6, waiting for transfers between devices, spread_weights(): lax.all_gather(a, 'z', axis=0, tiled=True)  103 us
    all_gather x1, blocking collectives, on_device(): thin = lax.all_gather(thin, ALL, axis=0, tiled=True).astype(jnp.float32)  93.1 us
    all_to_all x2, starting transfers between devices, on_device(): lax.all_to_all(wo, SLAB, 0, 0, tiled=True).reshape(n * span, lay.cols)  41.3 us
    all_to_all x8, starting transfers between devices, slab_sum(): got = lax.all_to_all(parts, SLAB, 0, 0, tiled=True)  40.2 us
  transfers between devices with their start and end apart: 69, of which 34 were waited for; matrix products, arithmetic and copies ran while one was open for 26% of the time, Pallas kernels for 0%

profile of v1, /device:TPU:3, one launch (start us, length us, event | category | flops | bytes accessed | tf_op | source)
XLA Modules:
  0.0 1568.0 jit_solution(13514269569582266094)
XLA Ops:
  16.4 20.8 %all_to_all.109 = bf16[8,100,768]{2,1,0:T(8,128)(2,1)S(1)} all-to-all(bf16[8,100,768]{2,1,0:T(8,128)(2,1)} %reshape.1446), channel_id=1, replica_groups=mesh['section'=2,'dp'=2,'z'=4,'r'=2] {'section','dp','r'}, dimensions={0} | all-to-all | bytes 2457600 | tf_op jit(solution)/shard_map/all_to_all | solution.py:137
  41.6 93.1 %all-gather.2 = bf16[32,100,12]{1,2,0:T(8,128)(2,1)S(1)} all-gather(bf16[1,100,12]{1,2,0:T(8,128)(2,1)S(1)} %maximum_bitcast_fusion.2), channel_id=1, replica_groups=mesh['section'=2,'dp'=2,'z'=4,'r'=2] {'section','dp','z','r'}, dimensions={0}, use_global_device_ids=true | all-gather | bytes 79200 | tf_op jit(solution)/shard_map/all_gather | solution.py:264
  168.2 14.0 all_gather.54
  184.5 16.3 %all_gather.58 = bf16[1600,200]{1,0:T(8,128)(2,1)} all-gather(bf16[400,200]{1,0:T(8,128)(2,1)S(1)} %squeeze.142), channel_id=1, replica_groups=mesh['section'=2,'dp'=2,'z'=4,'r'=2] {'z'}, dimensions={0}, use_global_device_ids=true | all-gather | bytes 800000 | tf_op jit(solution)/shard_map/all_gather | solution.py:146
  268.0 33.4 %all-to-all-done.3 = bf16[8,128,1600]{1,2,0:T(8,128)(2,1)} async-done(((bf16[8,128,1600]{1,2,0:T(8,128)(2,1)}), bf16[8,128,1600]{1,2,0:T(8,128)(2,1)}, u32[]{:S(2)}, u32[]{:S(2)}) %all-to-all-start.3) | async-done | bytes 3276832 | tf_op jit(solution)/shard_map/all_to_all | solution.py:107
  324.4 23.8 %all_to_all.110 = bf16[2,200,1600]{2,1,0:T(8,128)(2,1)S(1)} all-to-all(bf16[2,200,1600]{2,1,0:T(8,128)(2,1)} %reshape_reshape.15), channel_id=1, replica_groups=mesh['section'=2,'dp'=2,'z'=4,'r'=2] {'section'}, dimensions={0} | all-to-all | bytes 2560000 | tf_op jit(solution)/shard_map/all_to_all | solution.py:142
  351.8 11.8 all-gather.22.cloned.1.call-done
  371.3 49.4 %all-gather.42.cloned.1.call-done = bf16[1,800,1600]{2,1,0:T(8,128)(2,1)} async-done(((bf16[1,200,1600]{2,1,0:T(8,128)(2,1)}), bf16[1,800,1600]{2,1,0:T(8,128)(2,1)}) %all-gather.42.cloned.1.call-update) | async-done | bytes 2560016 | tf_op jit(solution)/shard_map/all_gather | solution.py:146
  437.1 36.2 %all-to-all-done.6 = bf16[8,128,1600]{1,2,0:T(8,128)(2,1)} async-done(((bf16[8,128,1600]{1,2,0:T(8,128)(2,1)}), bf16[8,128,1600]{1,2,0:T(8,128)(2,1)}, u32[]{:S(2)}, u32[]{:S(2)}) %all-to-all-start.6) | async-done | bytes 3276832 | tf_op jit(solution)/shard_map/all_to_all | solution.py:107
  480.2 21.0 %all_gather.64 = bf16[1600,200]{1,0:T(8,128)(2,1)S(1)} all-gather(bf16[400,200]{1,0:T(8,128)(2,1)S(1)} %squeeze.148), channel_id=1, replica_groups=mesh['section'=2,'dp'=2,'z'=4,'r'=2] {'z'}, dimensions={0}, use_global_device_ids=true | all-gather | bytes 800000 | tf_op jit(solution)/shard_map/all_gather | solution.py:146
  509.0 23.2 %all-gather.26.cloned.1.call-done = bf16[1024,1600]{0,1:T(8,128)(2,1)} async-done(((bf16[128,1600]{0,1:T(8,128)(2,1)}), bf16[1024,1600]{0,1:T(8,128)(2,1)}) %all-gather.26.cloned.1.call-update) | async-done | bytes 3276816 | tf_op jit(solution)/shard_map/all_gather | solution.py:102
  562.5 35.7 %all-to-all-done.8 = bf16[8,128,1600]{1,2,0:T(8,128)(2,1)} async-done(((bf16[8,128,1600]{1,2,0:T(8,128)(2,1)}), bf16[8,128,1600]{1,2,0:T(8,128)(2,1)}, u32[]{:S(2)}, u32[]{:S(2)}) %all-to-all-start.8) | async-done | bytes 3276832 | tf_op jit(solution)/shard_map/all_to_all | solution.py:107
  607.9 22.1 %collective-permute-done.7 = bf16[128,1600]{0,1:T(8,128)(2,1)S(1)} collective-permute-done((bf16[128,1600]{0,1:T(8,128)(2,1)S(1)}, bf16[128,1600]{0,1:T(8,128)(2,1)S(1)}, u32[]{:S(2)}, u32[]{:S(2)}) %collective-permute-start.7) | collective-permute-done | bytes 409632 | tf_op jit(solution)/shard_map/ppermute | solution.py:79
  636.6 35.4 %all-gather.30.cloned.1.call-done = bf16[1024,1600]{0,1:T(8,128)(2,1)} async-done(((bf16[128,1600]{0,1:T(8,128)(2,1)}), bf16[1024,1600]{0,1:T(8,128)(2,1)}) %all-gather.30.cloned.1.call-update) | async-done | bytes 3276816 | tf_op jit(solution)/shard_map/all_gather | solution.py:102
  679.7 49.4 %all-gather.44.cloned.1.call-done = bf16[1,800,1600]{2,1,0:T(8,128)(2,1)} async-done(((bf16[1,200,1600]{2,1,0:T(8,128)(2,1)}), bf16[1,800,1600]{2,1,0:T(8,128)(2,1)}) %all-gather.44.cloned.1.call-update) | async-done | bytes 2560016 | tf_op jit(solution)/shard_map/all_gather | solution.py:146
  729.1 34.5 %all-gather.34.cloned.1.call-done = bf16[1024,1600]{0,1:T(8,128)(2,1)} async-done(((bf16[128,1600]{0,1:T(8,128)(2,1)}), bf16[1024,1600]{0,1:T(8,128)(2,1)}) %all-gather.34.cloned.1.call-update) | async-done | bytes 3276816 | tf_op jit(solution)/shard_map/all_gather | solution.py:102
  793.2 28.4 %all-to-all-done.10 = bf16[8,128,1600]{1,2,0:T(8,128)(2,1)} async-done(((bf16[8,128,1600]{1,2,0:T(8,128)(2,1)}), bf16[8,128,1600]{1,2,0:T(8,128)(2,1)}, u32[]{:S(2)}, u32[]{:S(2)}) %all-to-all-start.10) | async-done | bytes 3276832 | tf_op jit(solution)/shard_map/all_to_all | solution.py:107
  833.1 31.5 %all-to-all-done.9 = bf16[8,128,1600]{1,2,0:T(8,128)(2,1)} async-done(((bf16[8,128,1600]{1,2,0:T(8,128)(2,1)}), bf16[8,128,1600]{1,2,0:T(8,128)(2,1)}, u32[]{:S(2)}, u32[]{:S(2)}) %all-to-all-start.9) | async-done | bytes 3276832 | tf_op jit(solution)/shard_map/all_to_all | solution.py:107
  871.0 33.2 %all-gather.36.cloned.1.call-done = bf16[1024,1600]{0,1:T(8,128)(2,1)} async-done(((bf16[128,1600]{0,1:T(8,128)(2,1)}), bf16[1024,1600]{0,1:T(8,128)(2,1)}) %all-gather.36.cloned.1.call-update) | async-done | bytes 3276816 | tf_op jit(solution)/shard_map/all_gather | solution.py:102
  917.7 15.4 multiply_reduce_fusion.1
  957.0 37.4 %all-to-all-done.11 = bf16[8,128,1600]{1,2,0:T(8,128)(2,1)} async-done(((bf16[8,128,1600]{1,2,0:T(8,128)(2,1)}), bf16[8,128,1600]{1,2,0:T(8,128)(2,1)}, u32[]{:S(2)}, u32[]{:S(2)}) %all-to-all-start.11) | async-done | bytes 3276832 | tf_op jit(solution)/shard_map/all_to_all | solution.py:107
  1016.4 11.7 collective-permute-done.27
  1062.7 14.7 collective-permute-done.34
  1154.0 11.1 collective-permute-done.24
  1183.6 13.0 collective-permute-done.25
  1199.0 11.9 collective-permute-done.31
  1214.1 14.4 collective-permute-done.23
  1231.4 12.4 collective-permute-done.26
  1245.5 12.7 collective-permute-done.32
  1264.9 34.9 %all-to-all-start.15 = ((bf16[8,256,200]{1,2,0:T(8,128)(2,1)}), bf16[8,256,200]{1,2,0:T(8,128)(2,1)}, u32[]{:S(2)}, u32[]{:S(2)}) async-start(bf16[8,256,200]{1,2,0:T(8,128)(2,1)} %bitcast.120), calls=%async_computation.15 | async-start | bytes 1638400 | tf_op jit(solution)/shard_map/all_to_all | solution.py:313
  1303.9 16.1 %multiply_reduce_fusion = (f32[4,1024]{1,0:T(4,128)}, f32[4,1024,1024]{1,2,0:T(8,128)}) fusion(f32[4,1024,1024]{1,2,0:T(8,128)} %copy-done, f32[4,1024]{1,0:T(4,128)} %log_add_fusion, pred[1024,1024]{0,1:T(8,128)(4,1)S(1)} %broadcast_compare_fusion, bf16[1024,4,64]{0,2,1:T(8,128)(2,1)} %bitcast.611, bf16[1024,4,64]{0,2,1:T(8,128)(2,1)} %bitcast.604), kind=kOutput, calls=%fused_computation.1 | convolution fusion | flops 557838336 | bytes 35684352 | tf_op jit(solution)/shard_map/qhd,nhd->hqn/dot_general | solution.py:187
  1320.0 10.9 multiply_convert_fusion
  (801 shorter events, 720.6 us)
Async XLA Ops:
  7.2 208.6 %all-gather.20.cloned.1.call-start = ((), (), s32[]{:S(2)}) async-start(), calls=%async_computation.22 | async-start | bytes 3072000 | tf_op jit(solution)/shard_map/all_gather | solution.py:146
  39.2 176.6 %all-gather.18.cloned.1.call-start = ((), (), s32[]{:S(2)}) async-start(), calls=%async_computation.21 | async-start | bytes 3686400 | tf_op jit(solution)/shard_map/all_gather | solution.py:102
  39.3 96.9 %collective-permute-start.1 = (bf16[128,1600]{0,1:T(8,128)(2,1)S(1)}, bf16[128,1600]{0,1:T(8,128)(2,1)S(1)}, u32[]{:S(2)}, u32[]{:S(2)}) collective-permute-start(bf16[128,1600]{0,1:T(8,128)(2,1)S(1)} %get-tuple-element.125), channel_id=1, source_target_pairs={{0,0},{1,1},{8,2},{9,3},{2,8},{3,9},{10,10},{11,11},{20,16},{21,17... | collective-permute-start | bytes 1228808 | tf_op jit(solution)/shard_map/ppermute | solution.py:79
  40.6 95.6 %collective-permute-start = (bf16[128,1600]{0,1:T(8,128)(2,1)S(1)}, bf16[128,1600]{0,1:T(8,128)(2,1)S(1)}, u32[]{:S(2)}, u32[]{:S(2)}) collective-permute-start(bf16[128,1600]{0,1:T(8,128)(2,1)S(1)} %get-tuple-element.126), channel_id=1, source_target_pairs={{0,4},{1,5},{8,6},{9,7},{2,12},{3,13},{10,14},{11,15},{20,20},{21,... | collective-permute-start | bytes 1228808 | tf_op jit(solution)/shard_map/ppermute | solution.py:79
  140.9 42.6 %all-to-all-start.1 = ((bf16[8,100,200]{1,2,0:T(8,128)(2,1)}), bf16[8,100,200]{1,2,0:T(8,128)(2,1)S(1)}, u32[]{:S(2)}, u32[]{:S(2)}) async-start(bf16[8,100,200]{1,2,0:T(8,128)(2,1)} %bitcast.24), calls=%async_computation.1 | async-start | bytes 819200 | tf_op jit(solution)/shard_map/all_to_all | solution.py:137
  258.5 42.9 %all-to-all-start.3 = ((bf16[8,128,1600]{1,2,0:T(8,128)(2,1)}), bf16[8,128,1600]{1,2,0:T(8,128)(2,1)}, u32[]{:S(2)}, u32[]{:S(2)}) async-start(bf16[8,128,1600]{1,2,0:T(8,128)(2,1)} %bitcast.525), calls=%async_computation.3 | async-start | bytes 6553600 | tf_op jit(solution)/shard_map/all_to_all | solution.py:107
  263.6 88.1 %all-gather.24.cloned.1.call-start = ((), (), s32[]{:S(2)}) async-start(), calls=%async_computation.24 | async-start | bytes 3584000 | tf_op jit(solution)/shard_map/all_gather | solution.py:146
  267.3 96.3 %all-gather.22.cloned.1.call-start = ((), (), s32[]{:S(2)}) async-start(), calls=%async_computation.23 | async-start | bytes 3686400 | tf_op jit(solution)/shard_map/all_gather | solution.py:102
  306.9 113.7 %all-gather.42.cloned.1.call-start = ((), (), s32[]{:S(2)}) async-start(), calls=%async_computation.33 | async-start | bytes 3328000 | tf_op jit(solution)/shard_map/all_gather | solution.py:146
  430.0 43.2 %all-to-all-start.6 = ((bf16[8,128,1600]{1,2,0:T(8,128)(2,1)}), bf16[8,128,1600]{1,2,0:T(8,128)(2,1)}, u32[]{:S(2)}, u32[]{:S(2)}) async-start(bf16[8,128,1600]{1,2,0:T(8,128)(2,1)} %bitcast.526), calls=%async_computation.6 | async-start | bytes 6553600 | tf_op jit(solution)/shard_map/all_to_all | solution.py:107
  435.4 73.6 %all-gather.28.cloned.1.call-start = ((), (), s32[]{:S(2)}) async-start(), calls=%async_computation.26 | async-start | bytes 3072000 | tf_op jit(solution)/shard_map/all_gather | solution.py:146
  436.4 95.8 %all-gather.26.cloned.1.call-start = ((), (), s32[]{:S(2)}) async-start(), calls=%async_computation.25 | async-start | bytes 3686400 | tf_op jit(solution)/shard_map/all_gather | solution.py:102
  503.9 48.1 %all-to-all-start.7 = ((bf16[8,256,200]{1,2,0:T(8,128)(2,1)}), bf16[8,256,200]{1,2,0:T(8,128)(2,1)S(1)}, u32[]{:S(2)}, u32[]{:S(2)}) async-start(bf16[8,256,200]{1,2,0:T(8,128)(2,1)} %bitcast.493), calls=%async_computation.7 | async-start | bytes 1638400 | tf_op jit(solution)/shard_map/all_to_all | solution.py:152
  555.4 42.8 %all-to-all-start.8 = ((bf16[8,128,1600]{1,2,0:T(8,128)(2,1)}), bf16[8,128,1600]{1,2,0:T(8,128)(2,1)}, u32[]{:S(2)}, u32[]{:S(2)}) async-start(bf16[8,128,1600]{1,2,0:T(8,128)(2,1)} %bitcast.527), calls=%async_computation.8 | async-start | bytes 6553600 | tf_op jit(solution)/shard_map/all_to_all | solution.py:107
  560.4 76.3 %all-gather.32.cloned.1.call-start = ((), (), s32[]{:S(2)}) async-start(), calls=%async_computation.28 | async-start | bytes 3584000 | tf_op jit(solution)/shard_map/all_gather | solution.py:146
  561.6 110.5 %all-gather.30.cloned.1.call-start = ((), (), s32[]{:S(2)}) async-start(), calls=%async_computation.27 | async-start | bytes 3686400 | tf_op jit(solution)/shard_map/all_gather | solution.py:102
  604.1 125.0 %all-gather.44.cloned.1.call-start = ((), (), s32[]{:S(2)}) async-start(), calls=%async_computation.34 | async-start | bytes 3328000 | tf_op jit(solution)/shard_map/all_gather | solution.py:146
  604.7 159.0 %all-gather.34.cloned.1.call-start = ((), (), s32[]{:S(2)}) async-start(), calls=%async_computation.29 | async-start | bytes 3686400 | tf_op jit(solution)/shard_map/all_gather | solution.py:102
  778.6 43.0 %all-to-all-start.10 = ((bf16[8,128,1600]{1,2,0:T(8,128)(2,1)}), bf16[8,128,1600]{1,2,0:T(8,128)(2,1)}, u32[]{:S(2)}, u32[]{:S(2)}) async-start(bf16[8,128,1600]{1,2,0:T(8,128)(2,1)} %bitcast.529), calls=%async_computation.10 | async-start | bytes 6553600 | tf_op jit(solution)/shard_map/all_to_all | solution.py:107
  821.6 43.0 %all-to-all-start.9 = ((bf16[8,128,1600]{1,2,0:T(8,128)(2,1)}), bf16[8,128,1600]{1,2,0:T(8,128)(2,1)}, u32[]{:S(2)}, u32[]{:S(2)}) async-start(bf16[8,128,1600]{1,2,0:T(8,128)(2,1)} %bitcast.528), calls=%async_computation.9 | async-start | bytes 6553600 | tf_op jit(solution)/shard_map/all_to_all | solution.py:107
  826.9 77.4 %all-gather.36.cloned.1.call-start = ((), (), s32[]{:S(2)}) async-start(), calls=%async_computation.30 | async-start | bytes 3686400 | tf_op jit(solution)/shard_map/all_gather | solution.py:102
  951.7 42.7 %all-to-all-start.11 = ((bf16[8,128,1600]{1,2,0:T(8,128)(2,1)}), bf16[8,128,1600]{1,2,0:T(8,128)(2,1)}, u32[]{:S(2)}, u32[]{:S(2)}) async-start(bf16[8,128,1600]{1,2,0:T(8,128)(2,1)} %bitcast.530), calls=%async_computation.11 | async-start | bytes 6553600 | tf_op jit(solution)/shard_map/all_to_all | solution.py:107
  956.6 80.1 %all-gather.38.cloned.1.call-start = ((), (), s32[]{:S(2)}) async-start(), calls=%async_computation.31 | async-start | bytes 3686400 | tf_op jit(solution)/shard_map/all_gather | solution.py:102
  1051.6 78.2 %all-to-all-start.12 = ((bf16[8,128,1600]{1,2,0:T(8,128)(2,1)}), bf16[8,128,1600]{1,2,0:T(8,128)(2,1)}, u32[]{:S(2)}, u32[]{:S(2)}) async-start(bf16[8,128,1600]{1,2,0:T(8,128)(2,1)} %bitcast.524), calls=%async_computation.12 | async-start | bytes 6553600 | tf_op jit(solution)/shard_map/all_to_all | solution.py:107
  1056.2 204.9 %all-gather.40.cloned.1.call-start = ((), (), s32[]{:S(2)}) async-start(), calls=%async_computation.32 | async-start | bytes 3686400 | tf_op jit(solution)/shard_map/all_gather | solution.py:102
  1082.0 335.6 %collective-permute-start.3 = (bf16[128,1600]{0,1:T(8,128)(2,1)}, bf16[128,1600]{0,1:T(8,128)(2,1)}, u32[]{:S(2)}, u32[]{:S(2)}) collective-permute-start(bf16[128,1600]{0,1:T(8,128)(2,1)} %bitcast.62), channel_id=1, source_target_pairs={{0,0},{1,1},{2,8},{3,9},{8,2},{9,3},{10,10},{11,11},{16,4},{17,5},... | collective-permute-start | bytes 1228808 | tf_op jit(solution)/shard_map/ppermute | solution.py:93
  1109.5 308.1 %collective-permute-start.2 = (bf16[128,1600]{0,1:T(8,128)(2,1)}, bf16[128,1600]{0,1:T(8,128)(2,1)}, u32[]{:S(2)}, u32[]{:S(2)}) collective-permute-start(bf16[128,1600]{0,1:T(8,128)(2,1)} %bitcast.60), channel_id=1, source_target_pairs={{0,16},{1,17},{2,24},{3,25},{8,18},{9,19},{10,26},{11,27},{16,20},... | collective-permute-start | bytes 1228808 | tf_op jit(solution)/shard_map/ppermute | solution.py:93
  1181.3 232.3 %collective-permute-start.16 = (bf16[400,768]{1,0:T(8,128)(2,1)}, bf16[400,768]{1,0:T(8,128)(2,1)}, u32[]{:S(2)}, u32[]{:S(2)}) collective-permute-start(bf16[400,768]{1,0:T(8,128)(2,1)} %fusion.84), channel_id=1, source_target_pairs={{0,2},{2,4},{4,6},{6,0},{1,3},{3,5},{5,7},{7,1},{8,10},{10,12},{12... | collective-permute-start | bytes 1843208 | tf_op jit(solution)/shard_map/ppermute | solution.py:119
  1264.9 76.2 %all-to-all-start.15 = ((bf16[8,256,200]{1,2,0:T(8,128)(2,1)}), bf16[8,256,200]{1,2,0:T(8,128)(2,1)}, u32[]{:S(2)}, u32[]{:S(2)}) async-start(bf16[8,256,200]{1,2,0:T(8,128)(2,1)} %bitcast.120), calls=%async_computation.15 | async-start | bytes 1638400 | tf_op jit(solution)/shard_map/all_to_all | solution.py:313
  1408.9 97.8 %all-to-all-start.13 = ((bf16[8,128,1600]{1,2,0:T(8,128)(2,1)}), bf16[8,128,1600]{1,2,0:T(8,128)(2,1)}, u32[]{:S(2)}, u32[]{:S(2)}) async-start(bf16[8,128,1600]{1,2,0:T(8,128)(2,1)} %bitcast.523), calls=%async_computation.13 | async-start | bytes 6553600 | tf_op jit(solution)/shard_map/all_to_all | solution.py:107
  1465.0 92.9 %collective-permute-start.10 = (bf16[128,1600]{0,1:T(8,128)(2,1)}, bf16[128,1600]{0,1:T(8,128)(2,1)}, u32[]{:S(2)}, u32[]{:S(2)}) collective-permute-start(bf16[128,1600]{0,1:T(8,128)(2,1)} %bitcast.86), channel_id=1, source_target_pairs={{4,16},{5,17},{6,24},{7,25},{12,18},{13,19},{14,26},{15,27},{20,20... | collective-permute-start | bytes 1228808 | tf_op jit(solution)/shard_map/ppermute | solution.py:93
  1466.3 92.6 %collective-permute-start.8 = (bf16[128,1600]{0,1:T(8,128)(2,1)}, bf16[128,1600]{0,1:T(8,128)(2,1)}, u32[]{:S(2)}, u32[]{:S(2)}) collective-permute-start(bf16[128,1600]{0,1:T(8,128)(2,1)} %bitcast.86), channel_id=1, source_target_pairs={{0,16},{1,17},{2,24},{3,25},{8,18},{9,19},{10,26},{11,27},{16,20},... | collective-permute-start | bytes 1228808 | tf_op jit(solution)/shard_map/ppermute | solution.py:93
  (205 other events, 4101.3 us)
Sparse Core Ops, SparseCore 0:
  39.3 63.8 all-gather.19
  138.2 38.0 all-gather.17
  267.4 57.5 all-gather.23
  326.7 36.8 all-gather.21
  365.6 55.0 all-gather.41
  438.0 54.8 all-gather.27
  495.4 36.7 all-gather.25
  563.4 73.2 all-gather.31
  639.1 32.9 all-gather.29
  674.1 55.0 all-gather.43
  731.0 32.6 all-gather.33
  870.5 33.6 all-gather.35
  1002.7 33.7 all-gather.37
  1136.8 54.4 all-gather.39

commit v2 on v1

--- a/solution.py
+++ b/solution.py
@@ -1,6 +1,8 @@
 import jax
 import jax.numpy as jnp
 from jax import lax
+from jax.experimental import pallas as pl
+from jax.experimental.pallas import tpu as pltpu
 from jax.sharding import Mesh
 from jax.sharding import PartitionSpec as P
 
@@ -9,6 +11,7 @@
 
 SLAB = ("section", "dp", "r")
 ALL = ("section", "dp", "z", "r")
+MESH = pl.DeviceIdType.MESH
 
 
 def normalize(rows_in, gain_col, shift_col):
@@ -98,14 +101,138 @@
         return jnp.stack(result)[None, :, None]
 
 
-def slab_gather(a):
-    return lax.all_gather(a, SLAB, axis=0, tiled=True)
-
-
-def slab_sum(a, lay):
-    parts = a.astype(jnp.bfloat16).reshape(lay.slab, lay.rows, a.shape[1])
-    got = lax.all_to_all(parts, SLAB, 0, 0, tiled=True)
-    return jnp.sum(got.astype(jnp.float32), axis=0)
+class Peers:
+    def __init__(self):
+        self.sections, self.rest = lax.axis_size("section"), lax.axis_size("r")
+        self.chips = self.sections * self.rest
+        self.x, self.c, self.r = (lax.axis_index(a) for a in ("section", "dp", "r"))
+        self.chip = self.x * self.rest + self.r
+
+    def ahead(self, k):
+        return lax.rem(self.chip + k, self.chips)
+
+    def behind(self, k):
+        return lax.rem(self.chip + self.chips - k, self.chips)
+
+    def device(self, chip, core):
+        return {"section": chip // self.rest, "dp": core, "r": lax.rem(chip, self.rest)}
+
+    def slot(self, chip, core):
+        return (chip // self.rest * 2 + core) * self.rest + lax.rem(chip, self.rest)
+
+    def greet(self):
+        barrier = pltpu.get_barrier_semaphore()
+        for k in range(1, self.chips):
+            pl.semaphore_signal(barrier, inc=1, device_id=self.device(self.ahead(k), self.c), device_id_type=MESH)
+        pl.semaphore_signal(barrier, inc=1, device_id=self.device(self.chip, 1 - self.c), device_id_type=MESH)
+        pl.semaphore_wait(barrier, self.chips)
+
+
+def remote(src, dst, send, recv, device):
+    return pltpu.make_async_remote_copy(src_ref=src, dst_ref=dst, send_sem=send, recv_sem=recv, device_id=device, device_id_type=MESH)
+
+
+def gather_steps(peers, src, out, local, chip_send, chip_recv, core_send, core_recv):
+    me, c = peers.slot(peers.chip, peers.c), peers.c
+    sibling = peers.device(peers.chip, 1 - c)
+    sent = []
+    for k in range(1, peers.chips):
+        copy = remote(src, out.at[me], chip_send.at[k], chip_recv.at[k], peers.device(peers.ahead(k), c))
+        copy.start()
+        sent.append(copy)
+    copy = remote(src, out.at[me], core_send.at[0], core_recv.at[0], sibling)
+    copy.start()
+    sent.append(copy)
+    own = pltpu.make_async_copy(src, out.at[me], local)
+    own.start()
+    for k in range(1, peers.chips):
+        block = out.at[peers.slot(peers.behind(k), c)]
+        remote(block, block, chip_send.at[k], chip_recv.at[k], sibling).wait_recv()
+        copy = remote(block, block, core_send.at[k], core_recv.at[k], sibling)
+        copy.start()
+        sent.append(copy)
+    for k in range(peers.chips):
+        block = out.at[peers.slot(peers.behind(k), 1 - c)]
+        remote(block, block, core_send.at[k], core_recv.at[k], sibling).wait_recv()
+    for copy in sent:
+        copy.wait_send()
+    own.wait()
+
+
+def gather_kernel(src, out, local, chip_send, chip_recv, core_send, core_recv):
+    peers = Peers()
+    peers.greet()
+    gather_steps(peers, src, out, local, chip_send, chip_recv, core_send, core_recv)
+
+
+def slab_gather(a, name=1):
+    chips = lax.axis_size("section") * lax.axis_size("r")
+    sems = pltpu.SemaphoreType.DMA((chips,))
+    out = pl.pallas_call(
+        gather_kernel,
+        out_shape=jax.ShapeDtypeStruct((2 * chips, *a.shape), a.dtype),
+        in_specs=[pl.BlockSpec(memory_space=pl.ANY)],
+        out_specs=pl.BlockSpec(memory_space=pl.ANY),
+        scratch_shapes=[pltpu.SemaphoreType.DMA] + [sems] * 4,
+        compiler_params=pltpu.CompilerParams(collective_id=name, has_side_effects=True),
+    )(a)
+    return out.reshape(2 * chips * a.shape[0], a.shape[1])
+
+
+def sum_steps(peers, part, mine, other, out, going, coming, local, chip_send, chip_recv, core_send, core_recv):
+    c = peers.c
+    sibling = peers.device(peers.chip, 1 - c)
+    sent = []
+    order = [k for k in range(1, peers.chips)] + [0]
+    for k in order:
+        chip = peers.ahead(k)
+        copy = remote(part.at[peers.slot(chip, 1 - c)], other.at[k], core_send.at[k], core_recv.at[k], sibling)
+        copy.start()
+        sent.append(copy)
+        pltpu.make_async_copy(part.at[peers.slot(chip, c)], mine.at[k], local.at[k]).start()
+    for k in order:
+        chip = peers.ahead(k)
+        remote(mine.at[k], other.at[k], core_send.at[k], core_recv.at[k], sibling).wait_recv()
+        pltpu.make_async_copy(part.at[peers.slot(chip, c)], mine.at[k], local.at[k]).wait()
+        if k:
+            going[k - 1] = (mine[k].astype(jnp.float32) + other[k].astype(jnp.float32)).astype(going.dtype)
+            copy = remote(going.at[k - 1], coming.at[k - 1], chip_send.at[k], chip_recv.at[k], peers.device(chip, c))
+            copy.start()
+            sent.append(copy)
+    out[...] = mine[0].astype(jnp.float32) + other[0].astype(jnp.float32)
+    for k in range(1, peers.chips):
+        remote(going.at[k - 1], coming.at[k - 1], chip_send.at[k], chip_recv.at[k], sibling).wait_recv()
+        out[...] += coming[k - 1].astype(jnp.float32)
+    for copy in sent:
+        copy.wait_send()
+
+
+def sum_scratch(chips, rows, width):
+    return [
+        pltpu.VMEM((chips, rows, width), jnp.bfloat16),
+        pltpu.VMEM((chips, rows, width), jnp.bfloat16),
+        pltpu.VMEM((chips - 1, rows, width), jnp.bfloat16),
+        pltpu.VMEM((chips - 1, rows, width), jnp.bfloat16),
+    ] + [pltpu.SemaphoreType.DMA((chips,))] * 5
+
+
+def sum_kernel(part, out, mine, other, going, coming, local, chip_send, chip_recv, core_send, core_recv):
+    peers = Peers()
+    peers.greet()
+    sum_steps(peers, part, mine, other, out, going, coming, local, chip_send, chip_recv, core_send, core_recv)
+
+
+def slab_sum(a, name=2):
+    chips = lax.axis_size("section") * lax.axis_size("r")
+    rows, width = a.shape[0] // (2 * chips), a.shape[1]
+    return pl.pallas_call(
+        sum_kernel,
+        out_shape=jax.ShapeDtypeStruct((rows, width), jnp.float32),
+        in_specs=[pl.BlockSpec(memory_space=pl.ANY)],
+        out_specs=pl.BlockSpec(memory_space=pltpu.VMEM),
+        scratch_shapes=sum_scratch(chips, rows, width),
+        compiler_params=pltpu.CompilerParams(collective_id=name, has_side_effects=True, vmem_limit_bytes=40 * 2**20),
+    )(a.astype(jnp.bfloat16).reshape(2 * chips, rows, width))
 
 
 def ring_sum(part, lay):
@@ -205,11 +332,11 @@
     k = qkv[:, span : 2 * span].astype(jnp.bfloat16)
     v = (qkv[:, 2 * span :] + v_bias).astype(jnp.bfloat16)
     attended, logs = attend(q, k, v, places, lay)
-    mid = h + (slab_sum(dot(attended, w_out, 1, 0), lay) + shifts[3])
+    mid = h + (slab_sum(dot(attended, w_out, 1, 0)) + shifts[3])
     normed_two = slab_gather(normalize(mid, gains[1], shifts[4]).astype(jnp.bfloat16))
     hidden = dot(normed_two, w_fc, 1, 0) + unit_bias
     activated = smooth(hidden).astype(jnp.bfloat16)
-    result = mid + (slab_sum(dot(activated, w_proj, 1, 0), lay) + shifts[5])
+    result = mid + (slab_sum(dot(activated, w_proj, 1, 0)) + shifts[5])
     kept = (h, mid, normed, q, k, v, attended, logs, normed_two, hidden, activated)
     return result.astype(jnp.bfloat16), kept
 
@@ -224,7 +351,7 @@
     _, smooth_back = jax.vjp(smooth, hidden)
     g_hidden = smooth_back(g_activated)[0].astype(jnp.bfloat16)
     grad_proj = dot(activated, branch, 0, 0)
-    g_normed_two = slab_sum(dot(g_hidden, w_fc, 1, 1), lay)
+    g_normed_two = slab_sum(dot(g_hidden, w_fc, 1, 1))
     grad_fc = dot(normed_two, g_hidden, 0, 0)
     _, second_back = jax.vjp(normalize, mid, gains[1], shifts[4])
     mid_part, gain_two, shift_two = second_back(g_normed_two)
@@ -235,7 +362,7 @@
     grad_out = dot(attended, g_attn, 0, 0)
     gq, gk, gv = attend_back(q, k, v, g_attended, logs, places, lay)
     joint = jnp.concatenate([gq, gk, gv], axis=1)
-    g_normed = slab_sum(dot(joint, w_qkv, 1, 1), lay)
+    g_normed = slab_sum(dot(joint, w_qkv, 1, 1))
     grad_qkv = dot(normed, joint, 0, 0)
     _, first_back = jax.vjp(normalize, h, gains[0], shifts[0])
     in_part, gain_one, shift_one = first_back(g_normed)

time: 1580 us -> 1580 us (level)
  waiting for transfers between devices: 628 us -> 182 us
  Pallas kernels: 0 us -> 395 us
  blocking collectives: 189 us -> 239 us
  local copies, waits for them, and re-layouts: 192 us -> 238 us
  other arithmetic: 126 us -> 97.6 us
  starting transfers between devices: 206 us -> 189 us
    pallas_call x0 -> x16, Pallas kernels: none -> 395 us  [the longest x8 201 us: slab_sum(): pl.pallas_call(sum_kernel, out_shape=jax.ShapeDtypeStruct((rows, width),...]
    all_to_all x8 -> x0, waiting for transfers between devices: 203 us -> none  [slab_sum(): got = lax.all_to_all(parts, SLAB, 0, 0, tiled=True)]
    all_gather x8 -> x0, waiting for transfers between devices: 138 us -> none  [slab_gather(): return lax.all_gather(a, SLAB, axis=0, tiled=True)]
    all_gather x6, waiting for transfers between devices: 103 us -> 0.07 us  [spread_weights(): lax.all_gather(a, 'z', axis=0, tiled=True)]
    convert_element_type x0 -> x18, local copies, waits for them, and re-layouts: none -> 45.1 us  [the longest x8 34.8 us: slab_sum(): a.astype(jnp.bfloat16).reshape(2 * chips, rows, width)]
    all_to_all x8 -> x0, starting transfers between devices: 40.2 us -> none  [slab_sum(): got = lax.all_to_all(parts, SLAB, 0, 0, tiled=True)]
    ppermute x24, starting transfers between devices: 26.1 us -> 61.1 us  [ring_sum(): acc = lax.ppermute(acc, 'z', ring)]
    ppermute x24, waiting for transfers between devices: 143 us -> 177 us  [ring_sum(): acc = lax.ppermute(acc, 'z', ring)]
  transfers between devices with their start and end apart: 69 -> 52, of which waited for: 34 -> 18; matrix products, arithmetic and copies ran while one was open for 26% -> 32% of each run, Pallas kernels for 0% -> 25%
where the time goes in v2:
time: 1580 us; the launch traced here: 1570 us
  Pallas kernels  395 us (25%)
  blocking collectives  239 us (15%)
  local copies, waits for them, and re-layouts  238 us (15%)
  matrix products  213 us (13%)
  starting transfers between devices  189 us (12%)
  waiting for transfers between devices  182 us (12%)
  other arithmetic  97.6 us (6%)
  between operations  17.5 us (1%)
    pallas_call x8, Pallas kernels, slab_sum(): pl.pallas_call(sum_kernel, out_shape=jax.ShapeDtypeStruct((rows, width),...  201 us
    pallas_call x8, Pallas kernels, slab_gather(): pl.pallas_call(gather_kernel, out_shape=jax.ShapeDtypeStruct((2 * chips,...  193 us
    ppermute x24, waiting for transfers between devices, ring_sum(): acc = lax.ppermute(acc, 'z', ring)  177 us
    dot_general x24, matrix products, dot(): lax.dot_general(a, b, (((ca,), (cb,)), ((), ())), preferred_element_type=...  136 us
    all_gather x1, blocking collectives, on_device(): thin = lax.all_gather(thin, ALL, axis=0, tiled=True).astype(jnp.float32)  118 us
    ppermute x24, starting transfers between devices, ring_sum(): acc = lax.ppermute(acc, 'z', ring)  61.1 us
    all_gather x2, blocking collectives, spread_weights(): lax.all_gather(a, 'z', axis=0, tiled=True)  44.3 us
    all_to_all x2, blocking collectives, move(): got = lax.all_to_all(a, SLAB, 0, 0, tiled=True)  42.5 us
  transfers between devices with their start and end apart: 52, of which 18 were waited for; matrix products, arithmetic and copies ran while one was open for 32% of the time, Pallas kernels for 25%

profile of v2, /device:TPU:3, one launch (start us, length us, event | category | flops | bytes accessed | tf_op | source)
XLA Modules:
  0.0 1571.0 jit_solution(6136101922636957988)
XLA Ops:
  12.6 20.5 %all_to_all.69 = bf16[8,100,768]{2,1,0:T(8,128)(2,1)S(1)} all-to-all(bf16[8,100,768]{2,1,0:T(8,128)(2,1)S(1)} %reshape.714), channel_id=1, replica_groups=mesh['section'=2,'dp'=2,'z'=4,'r'=2] {'section','dp','r'}, dimensions={0} | all-to-all | bytes 2457600 | tf_op jit(solution)/shard_map/all_to_all | solution.py:264
  44.5 22.0 %all_to_all.70 = bf16[8,100,800]{2,1,0:T(8,128)(2,1)S(1)} all-to-all(bf16[8,100,800]{2,1,0:T(8,128)(2,1)S(1)} %copy.502), channel_id=1, replica_groups=mesh['section'=2,'dp'=2,'z'=4,'r'=2] {'section','dp','r'}, dimensions={0} | all-to-all | bytes 2560000 | tf_op jit(solution)/shard_map/all_to_all | solution.py:264
  79.0 18.9 %all_to_all.71 = bf16[2,200,1600]{2,1,0:T(8,128)(2,1)S(1)} all-to-all(bf16[2,200,1600]{2,1,0:T(8,128)(2,1)S(1)} %reshape_reshape.15), channel_id=1, replica_groups=mesh['section'=2,'dp'=2,'z'=4,'r'=2] {'section'}, dimensions={0} | all-to-all | bytes 2560000 | tf_op jit(solution)/shard_map/all_to_all | solution.py:269
  115.3 118.2 %all-gather.2 = bf16[32,100,12]{1,2,0:T(8,128)(2,1)S(1)} all-gather(bf16[1,100,12]{1,2,0:T(8,128)(2,1)S(1)} %maximum_bitcast_fusion.2), channel_id=1, replica_groups=mesh['section'=2,'dp'=2,'z'=4,'r'=2] {'section','dp','z','r'}, dimensions={0}, use_global_device_ids=true | all-gather | bytes 79200 | tf_op jit(solution)/shard_map/all_gather | solution.py:391
  247.0 15.3 all_gather.30
  264.8 27.4 %all_gather.37 = bf16[1600,200]{1,0:T(8,128)(2,1)S(1)} all-gather(bf16[400,200]{1,0:T(8,128)(2,1)S(1)} %squeeze.148), channel_id=1, replica_groups=mesh['section'=2,'dp'=2,'z'=4,'r'=2] {'z'}, dimensions={0}, use_global_device_ids=true | all-gather | bytes 800000 | tf_op jit(solution)/shard_map/all_gather | solution.py:273
  295.0 16.9 %all_gather.33 = bf16[1600,200]{1,0:T(8,128)(2,1)S(1)} all-gather(bf16[400,200]{1,0:T(8,128)(2,1)S(1)} %squeeze.142), channel_id=1, replica_groups=mesh['section'=2,'dp'=2,'z'=4,'r'=2] {'z'}, dimensions={0}, use_global_device_ids=true | all-gather | bytes 800000 | tf_op jit(solution)/shard_map/all_gather | solution.py:273
  314.6 15.4 all-to-all-start.2
  344.1 23.6 %shard_map.169 = bf16[8,128,1600]{2,1,0:T(8,128)(2,1)} custom-call(bf16[128,1600]{1,0:T(8,128)(2,1)} %add_convert_fusion.6.src), custom_call_target="tpu_custom_call" | custom-call | tf_op jit(solution)/shard_map/pallas_call | solution.py:171
  373.3 24.3 %shard_map.177 = bf16[8,128,1600]{2,1,0:T(8,128)(2,1)} custom-call(bf16[128,1600]{1,0:T(8,128)(2,1)} %copy.527.src), custom_call_target="tpu_custom_call" | custom-call | tf_op jit(solution)/shard_map/pallas_call | solution.py:171
  430.9 24.2 %shard_map.170 = f32[128,1600]{1,0:T(8,128)S(1)} custom-call(bf16[8,128,1600]{2,1,0:T(8,128)(2,1)S(1)} %bitcast.469), custom_call_target="tpu_custom_call" | custom-call | tf_op jit(solution)/shard_map/pallas_call | solution.py:228
  457.2 24.2 %shard_map.171 = bf16[8,128,1600]{2,1,0:T(8,128)(2,1)} custom-call(bf16[128,1600]{1,0:T(8,128)(2,1)} %add_convert_fusion.5.src), custom_call_target="tpu_custom_call" | custom-call | tf_op jit(solution)/shard_map/pallas_call | solution.py:171
  507.6 24.7 %shard_map.172 = f32[128,1600]{1,0:T(8,128)S(1)} custom-call(bf16[8,128,1600]{2,1,0:T(8,128)(2,1)S(1)} %bitcast.470), custom_call_target="tpu_custom_call" | custom-call | tf_op jit(solution)/shard_map/pallas_call | solution.py:228
  543.5 23.6 %shard_map.173 = bf16[8,128,1600]{2,1,0:T(8,128)(2,1)} custom-call(bf16[128,1600]{1,0:T(8,128)(2,1)} %fusion.125.src), custom_call_target="tpu_custom_call" | custom-call | tf_op jit(solution)/shard_map/pallas_call | solution.py:171
  597.6 25.1 %shard_map.174 = f32[128,1600]{1,0:T(8,128)S(1)} custom-call(bf16[8,128,1600]{2,1,0:T(8,128)(2,1)S(1)} %bitcast.471), custom_call_target="tpu_custom_call" | custom-call | tf_op jit(solution)/shard_map/pallas_call | solution.py:228
  624.8 24.2 %shard_map.175 = bf16[8,128,1600]{2,1,0:T(8,128)(2,1)} custom-call(bf16[128,1600]{1,0:T(8,128)(2,1)} %add_convert_fusion.3.src), custom_call_target="tpu_custom_call" | custom-call | tf_op jit(solution)/shard_map/pallas_call | solution.py:171
  671.4 24.4 %shard_map.176 = f32[128,1600]{1,0:T(8,128)S(1)} custom-call(bf16[8,128,1600]{2,1,0:T(8,128)(2,1)S(1)} %bitcast.472), custom_call_target="tpu_custom_call" | custom-call | tf_op jit(solution)/shard_map/pallas_call | solution.py:228
  715.0 24.7 %shard_map.178 = f32[128,1600]{1,0:T(8,128)S(1)} custom-call(bf16[8,128,1600]{2,1,0:T(8,128)(2,1)S(1)} %bitcast.473), custom_call_target="tpu_custom_call" | custom-call | tf_op jit(solution)/shard_map/pallas_call | solution.py:228
  743.4 14.8 collective-permute-start.2
  759.7 25.0 %shard_map.179 = bf16[8,128,1600]{2,1,0:T(8,128)(2,1)} custom-call(bf16[128,1600]{1,0:T(8,128)(2,1)} %get-tuple-element.88.src), custom_call_target="tpu_custom_call" | custom-call | tf_op jit(solution)/shard_map/pallas_call | solution.py:171
  800.2 15.4 multiply_reduce_fusion.1
  841.2 29.3 %shard_map.180 = f32[128,1600]{1,0:T(8,128)S(1)} custom-call(bf16[8,128,1600]{2,1,0:T(8,128)(2,1)S(1)} %bitcast.474), custom_call_target="tpu_custom_call" | custom-call | tf_op jit(solution)/shard_map/pallas_call | solution.py:228
  874.5 24.2 %shard_map.181 = bf16[8,128,1600]{2,1,0:T(8,128)(2,1)} custom-call(bf16[128,1600]{1,0:T(8,128)(2,1)} %copy-done.22), custom_call_target="tpu_custom_call" | custom-call | tf_op jit(solution)/shard_map/pallas_call | solution.py:171
  917.4 24.4 %shard_map.182 = f32[128,1600]{1,0:T(8,128)S(1)} custom-call(bf16[8,128,1600]{2,1,0:T(8,128)(2,1)S(1)} %bitcast.475), custom_call_target="tpu_custom_call" | custom-call | tf_op jit(solution)/shard_map/pallas_call | solution.py:228
  944.7 24.2 %shard_map.183 = bf16[8,128,1600]{2,1,0:T(8,128)(2,1)} custom-call(bf16[128,1600]{1,0:T(8,128)(2,1)} %get-tuple-element.86.src), custom_call_target="tpu_custom_call" | custom-call | tf_op jit(solution)/shard_map/pallas_call | solution.py:171
  982.5 15.4 multiply_reduce_fusion
  1099.6 24.4 %shard_map.184 = f32[128,1600]{1,0:T(8,128)S(1)} custom-call(bf16[8,128,1600]{2,1,0:T(8,128)(2,1)S(1)} %bitcast.476), custom_call_target="tpu_custom_call" | custom-call | tf_op jit(solution)/shard_map/pallas_call | solution.py:228
  1169.8 19.2 %collective-permute-done.15 = bf16[400,768]{1,0:T(8,128)(2,1)S(1)} collective-permute-done((bf16[400,768]{1,0:T(8,128)(2,1)}, bf16[400,768]{1,0:T(8,128)(2,1)S(1)}, u32[]{:S(2)}, u32[]{:S(2)}) %collective-permute-start.15) | collective-permute-done | bytes 614432 | tf_op jit(solution)/shard_map/ppermute | solution.py:246
  1200.2 16.3 %collective-permute-done.12 = bf16[400,768]{1,0:T(8,128)(2,1)S(1)} collective-permute-done((bf16[400,768]{1,0:T(8,128)(2,1)}, bf16[400,768]{1,0:T(8,128)(2,1)S(1)}, u32[]{:S(2)}, u32[]{:S(2)}) %collective-permute-start.12) | collective-permute-done | bytes 614432 | tf_op jit(solution)/shard_map/ppermute | solution.py:246
  1274.9 17.1 %collective-permute-done.21 = bf16[400,200]{1,0:T(8,128)(2,1)S(1)} collective-permute-done((bf16[400,200]{1,0:T(8,128)(2,1)S(1)}, bf16[400,200]{1,0:T(8,128)(2,1)S(1)}, u32[]{:S(2)}, u32[]{:S(2)}) %collective-permute-start.21) | collective-permute-done | bytes 160032 | tf_op jit(solution)/shard_map/ppermute | solution.py:246
  1382.0 15.2 collective-permute-done.25
  1492.8 15.7 %all-to-all-start.10 = ((bf16[8,100,800]{2,1,0:T(8,128)(2,1)}), bf16[8,100,800]{2,1,0:T(8,128)(2,1)}, u32[]{:S(2)}, u32[]{:S(2)}) async-start(bf16[8,100,800]{2,1,0:T(8,128)(2,1)} %reshape.665), calls=%async_computation.10 | async-start | bytes 2981888 | tf_op jit(solution)/shard_map/all_to_all | solution.py:447
  (768 shorter events, 774.8 us)
Async XLA Ops:
  7.2 390.5 %all-gather.10.cloned.1.call-start = ((), (), s32[]{:S(2)}) async-start(), calls=%async_computation.13 | async-start | bytes 3072000 | tf_op jit(solution)/shard_map/all_gather | solution.py:273
  35.0 452.2 %all-gather.12.cloned.1.call-start = ((), (), s32[]{:S(2)}) async-start(), calls=%async_computation.14 | async-start | bytes 3584000 | tf_op jit(solution)/shard_map/all_gather | solution.py:273
  68.7 425.8 %all-gather.18.cloned.1.call-start = ((), (), s32[]{:S(2)}) async-start(), calls=%async_computation.17 | async-start | bytes 3328000 | tf_op jit(solution)/shard_map/all_gather | solution.py:273
  99.1 468.0 %all-gather.14.cloned.1.call-start = ((), (), s32[]{:S(2)}) async-start(), calls=%async_computation.15 | async-start | bytes 3072000 | tf_op jit(solution)/shard_map/all_gather | solution.py:273
  102.2 162.1 %all-to-all-start.1 = ((bf16[8,100,200]{1,2,0:T(8,128)(2,1)}), bf16[8,100,200]{1,2,0:T(8,128)(2,1)S(1)}, u32[]{:S(2)}, u32[]{:S(2)}) async-start(bf16[8,100,200]{1,2,0:T(8,128)(2,1)} %bitcast.24), calls=%async_computation.1 | async-start | bytes 819200 | tf_op jit(solution)/shard_map/all_to_all | solution.py:264
  107.7 541.9 %all-gather.16.cloned.1.call-start = ((), (), s32[]{:S(2)}) async-start(), calls=%async_computation.16 | async-start | bytes 3584000 | tf_op jit(solution)/shard_map/all_gather | solution.py:273
  108.7 221.7 %collective-permute-start.1 = (bf16[128,1600]{0,1:T(8,128)(2,1)}, bf16[128,1600]{0,1:T(8,128)(2,1)}, u32[]{:S(2)}, u32[]{:S(2)}) collective-permute-start(bf16[128,1600]{0,1:T(8,128)(2,1)} %get-tuple-element.116), channel_id=1, source_target_pairs={{0,0},{1,1},{8,2},{9,3},{2,8},{3,9},{10,10},{11,11},{20,16},{21,17... | collective-permute-start | bytes 1228808 | tf_op jit(solution)/shard_map/ppermute | solution.py:82
  110.0 220.4 %collective-permute-start = (bf16[128,1600]{0,1:T(8,128)(2,1)}, bf16[128,1600]{0,1:T(8,128)(2,1)}, u32[]{:S(2)}, u32[]{:S(2)}) collective-permute-start(bf16[128,1600]{0,1:T(8,128)(2,1)} %get-tuple-element.117), channel_id=1, source_target_pairs={{0,4},{1,5},{8,6},{9,7},{2,12},{3,13},{10,14},{11,15},{20,20},{21,... | collective-permute-start | bytes 1228808 | tf_op jit(solution)/shard_map/ppermute | solution.py:82
  112.3 222.3 %collective-permute-start.7 = (bf16[128,1600]{0,1:T(8,128)(2,1)}, bf16[128,1600]{0,1:T(8,128)(2,1)}, u32[]{:S(2)}, u32[]{:S(2)}) collective-permute-start(bf16[128,1600]{0,1:T(8,128)(2,1)} %get-tuple-element.114), channel_id=1, source_target_pairs={{0,0},{1,1},{8,2},{9,3},{2,8},{3,9},{10,10},{11,11},{20,16},{21,17... | collective-permute-start | bytes 1228808 | tf_op jit(solution)/shard_map/ppermute | solution.py:82
  113.6 221.0 %collective-permute-start.6 = (bf16[128,1600]{0,1:T(8,128)(2,1)}, bf16[128,1600]{0,1:T(8,128)(2,1)}, u32[]{:S(2)}, u32[]{:S(2)}) collective-permute-start(bf16[128,1600]{0,1:T(8,128)(2,1)} %get-tuple-element.115), channel_id=1, source_target_pairs={{0,4},{1,5},{8,6},{9,7},{2,12},{3,13},{10,14},{11,15},{20,20},{21,... | collective-permute-start | bytes 1228808 | tf_op jit(solution)/shard_map/ppermute | solution.py:82
  314.6 103.7 %all-to-all-start.2 = ((bf16[8,256,200]{1,2,0:T(8,128)(2,1)}), bf16[8,256,200]{1,2,0:T(8,128)(2,1)S(1)}, u32[]{:S(2)}, u32[]{:S(2)}) async-start(bf16[8,256,200]{1,2,0:T(8,128)(2,1)} %bitcast.464), calls=%async_computation.2 | async-start | bytes 1638400 | tf_op jit(solution)/shard_map/all_to_all | solution.py:279
  330.0 327.7 %all-gather.20.cloned.1.call-start = ((), (), s32[]{:S(2)}) async-start(), calls=%async_computation.18 | async-start | bytes 3328000 | tf_op jit(solution)/shard_map/all_gather | solution.py:273
  418.3 170.2 %all-to-all-start.5 = ((bf16[8,256,200]{1,2,0:T(8,128)(2,1)}), bf16[8,256,200]{1,2,0:T(8,128)(2,1)}, u32[]{:S(2)}, u32[]{:S(2)}) async-start(bf16[8,256,200]{1,2,0:T(8,128)(2,1)} %bitcast.463), calls=%async_computation.5 | async-start | bytes 1638400 | tf_op jit(solution)/shard_map/all_to_all | solution.py:279
  533.5 629.6 %collective-permute-start.5 = (bf16[128,1600]{0,1:T(8,128)(2,1)}, bf16[128,1600]{0,1:T(8,128)(2,1)}, u32[]{:S(2)}, u32[]{:S(2)}) collective-permute-start(bf16[128,1600]{0,1:T(8,128)(2,1)} %bitcast.67), channel_id=1, source_target_pairs={{4,0},{5,1},{6,8},{7,9},{12,2},{13,3},{14,10},{15,11},{20,4},{21,5... | collective-permute-start | bytes 1228808 | tf_op jit(solution)/shard_map/ppermute | solution.py:96
  534.9 632.9 %collective-permute-start.3 = (bf16[128,1600]{0,1:T(8,128)(2,1)}, bf16[128,1600]{0,1:T(8,128)(2,1)}, u32[]{:S(2)}, u32[]{:S(2)}) collective-permute-start(bf16[128,1600]{0,1:T(8,128)(2,1)} %bitcast.67), channel_id=1, source_target_pairs={{0,0},{1,1},{2,8},{3,9},{8,2},{9,3},{10,10},{11,11},{16,4},{17,5},... | collective-permute-start | bytes 1228808 | tf_op jit(solution)/shard_map/ppermute | solution.py:96
  742.1 424.6 %collective-permute-start.4 = (bf16[128,1600]{0,1:T(8,128)(2,1)}, bf16[128,1600]{0,1:T(8,128)(2,1)}, u32[]{:S(2)}, u32[]{:S(2)}) collective-permute-start(bf16[128,1600]{0,1:T(8,128)(2,1)} %bitcast.64), channel_id=1, source_target_pairs={{4,16},{5,17},{6,24},{7,25},{12,18},{13,19},{14,26},{15,27},{20,20... | collective-permute-start | bytes 1228808 | tf_op jit(solution)/shard_map/ppermute | solution.py:96
  743.4 424.6 %collective-permute-start.2 = (bf16[128,1600]{0,1:T(8,128)(2,1)}, bf16[128,1600]{0,1:T(8,128)(2,1)}, u32[]{:S(2)}, u32[]{:S(2)}) collective-permute-start(bf16[128,1600]{0,1:T(8,128)(2,1)} %bitcast.64), channel_id=1, source_target_pairs={{0,16},{1,17},{2,24},{3,25},{8,18},{9,19},{10,26},{11,27},{16,20},... | collective-permute-start | bytes 1228808 | tf_op jit(solution)/shard_map/ppermute | solution.py:96
  1051.8 411.5 %collective-permute-start.10 = (bf16[128,1600]{0,1:T(8,128)(2,1)}, bf16[128,1600]{0,1:T(8,128)(2,1)}, u32[]{:S(2)}, u32[]{:S(2)}) collective-permute-start(bf16[128,1600]{0,1:T(8,128)(2,1)} %bitcast.91), channel_id=1, source_target_pairs={{4,16},{5,17},{6,24},{7,25},{12,18},{13,19},{14,26},{15,27},{20,20... | collective-permute-start | bytes 1228808 | tf_op jit(solution)/shard_map/ppermute | solution.py:96
  1155.8 76.1 %all-to-all-start.8 = ((bf16[8,256,200]{1,2,0:T(8,128)(2,1)}), bf16[8,256,200]{1,2,0:T(8,128)(2,1)S(1)}, u32[]{:S(2)}, u32[]{:S(2)}) async-start(bf16[8,256,200]{1,2,0:T(8,128)(2,1)} %bitcast.560), calls=%async_computation.8 | async-start | bytes 1638400 | tf_op jit(solution)/shard_map/all_to_all | solution.py:440
  1163.1 345.4 %collective-permute-start.8 = (bf16[128,1600]{0,1:T(8,128)(2,1)}, bf16[128,1600]{0,1:T(8,128)(2,1)}, u32[]{:S(2)}, u32[]{:S(2)}) collective-permute-start(bf16[128,1600]{0,1:T(8,128)(2,1)} %bitcast.91), channel_id=1, source_target_pairs={{0,16},{1,17},{2,24},{3,25},{8,18},{9,19},{10,26},{11,27},{16,20},... | collective-permute-start | bytes 1228808 | tf_op jit(solution)/shard_map/ppermute | solution.py:96
  1167.9 59.6 %collective-permute-start.33 = (bf16[200,1600]{1,0:T(8,128)(2,1)}, bf16[200,1600]{1,0:T(8,128)(2,1)S(1)}, u32[]{:S(2)}, u32[]{:S(2)}) collective-permute-start(bf16[200,1600]{1,0:T(8,128)(2,1)} %fusion.134), channel_id=1, source_target_pairs={{0,2},{2,4},{4,6},{6,0},{1,3},{3,5},{5,7},{7,1},{8,10},{10,12},{12... | collective-permute-start | bytes 1920008 | tf_op jit(solution)/shard_map/ppermute | solution.py:246
  1168.0 48.5 %collective-permute-start.12 = (bf16[400,768]{1,0:T(8,128)(2,1)}, bf16[400,768]{1,0:T(8,128)(2,1)S(1)}, u32[]{:S(2)}, u32[]{:S(2)}) collective-permute-start(bf16[400,768]{1,0:T(8,128)(2,1)} %fusion.137), channel_id=1, source_target_pairs={{0,2},{2,4},{4,6},{6,0},{1,3},{3,5},{5,7},{7,1},{8,10},{10,12},{12... | collective-permute-start | bytes 1843208 | tf_op jit(solution)/shard_map/ppermute | solution.py:246
  1189.0 68.3 %collective-permute-start.27 = (bf16[400,800]{1,0:T(8,128)(2,1)S(1)}, bf16[400,800]{1,0:T(8,128)(2,1)}, u32[]{:S(2)}, u32[]{:S(2)}) collective-permute-start(bf16[400,800]{1,0:T(8,128)(2,1)S(1)} %copy-done.61), channel_id=1, source_target_pairs={{0,2},{2,4},{4,6},{6,0},{1,3},{3,5},{5,7},{7,1},{8,10},{10,12},{12... | collective-permute-start | bytes 1920008 | tf_op jit(solution)/shard_map/ppermute | solution.py:246
  1227.5 36.7 %collective-permute-start.24 = (bf16[400,800]{1,0:T(8,128)(2,1)}, bf16[400,800]{1,0:T(8,128)(2,1)}, u32[]{:S(2)}, u32[]{:S(2)}) collective-permute-start(bf16[400,800]{1,0:T(8,128)(2,1)} %fusion.129), channel_id=1, source_target_pairs={{0,2},{2,4},{4,6},{6,0},{1,3},{3,5},{5,7},{7,1},{8,10},{10,12},{12... | collective-permute-start | bytes 1920008 | tf_op jit(solution)/shard_map/ppermute | solution.py:246
  1231.9 40.9 %all-to-all-start.7 = ((bf16[8,256,200]{1,2,0:T(8,128)(2,1)}), bf16[8,256,200]{1,2,0:T(8,128)(2,1)S(1)}, u32[]{:S(2)}, u32[]{:S(2)}) async-start(bf16[8,256,200]{1,2,0:T(8,128)(2,1)} %bitcast.130), calls=%async_computation.7 | async-start | bytes 1638400 | tf_op jit(solution)/shard_map/all_to_all | solution.py:440
  1246.1 96.6 %collective-permute-start.16 = (bf16[400,768]{1,0:T(8,128)(2,1)}, bf16[400,768]{1,0:T(8,128)(2,1)}, u32[]{:S(2)}, u32[]{:S(2)}) collective-permute-start(bf16[400,768]{1,0:T(8,128)(2,1)} %fusion.110), channel_id=1, source_target_pairs={{0,2},{2,4},{4,6},{6,0},{1,3},{3,5},{5,7},{7,1},{8,10},{10,12},{12... | collective-permute-start | bytes 1843208 | tf_op jit(solution)/shard_map/ppermute | solution.py:246
  1257.3 88.5 %collective-permute-start.13 = (bf16[400,768]{1,0:T(8,128)(2,1)}, bf16[400,768]{1,0:T(8,128)(2,1)}, u32[]{:S(2)}, u32[]{:S(2)}) collective-permute-start(bf16[400,768]{1,0:T(8,128)(2,1)} %fusion.113), channel_id=1, source_target_pairs={{0,2},{2,4},{4,6},{6,0},{1,3},{3,5},{5,7},{7,1},{8,10},{10,12},{12... | collective-permute-start | bytes 1843208 | tf_op jit(solution)/shard_map/ppermute | solution.py:246
  1332.9 115.4 %all-to-all-start.9 = ((bf16[8,100,200]{1,2,0:T(8,128)(2,1)}), bf16[8,100,200]{1,2,0:T(8,128)(2,1)S(1)}, u32[]{:S(2)}, u32[]{:S(2)}) async-start(bf16[8,100,200]{1,2,0:T(8,128)(2,1)} %copy.558), calls=%async_computation.9 | async-start | bytes 819200 | tf_op jit(solution)/shard_map/all_to_all | solution.py:447
  1342.7 131.7 %collective-permute-start.11 = (bf16[128,1600]{0,1:T(8,128)(2,1)}, bf16[128,1600]{0,1:T(8,128)(2,1)}, u32[]{:S(2)}, u32[]{:S(2)}) collective-permute-start(bf16[128,1600]{0,1:T(8,128)(2,1)} %bitcast.106), channel_id=1, source_target_pairs={{4,0},{5,1},{6,8},{7,9},{12,2},{13,3},{14,10},{15,11},{20,4},{21,5... | collective-permute-start | bytes 1228808 | tf_op jit(solution)/shard_map/ppermute | solution.py:96
  1349.7 32.2 %collective-permute-start.31 = (bf16[200,1600]{1,0:T(8,128)(2,1)}, bf16[200,1600]{1,0:T(8,128)(2,1)S(1)}, u32[]{:S(2)}, u32[]{:S(2)}) collective-permute-start(bf16[200,1600]{1,0:T(8,128)(2,1)} %fusion.93), channel_id=1, source_target_pairs={{0,2},{2,4},{4,6},{6,0},{1,3},{3,5},{5,7},{7,1},{8,10},{10,12},{12... | collective-permute-start | bytes 1920008 | tf_op jit(solution)/shard_map/ppermute | solution.py:246
  1439.8 68.8 %collective-permute-start.9 = (bf16[128,1600]{0,1:T(8,128)(2,1)}, bf16[128,1600]{0,1:T(8,128)(2,1)}, u32[]{:S(2)}, u32[]{:S(2)}) collective-permute-start(bf16[128,1600]{0,1:T(8,128)(2,1)} %bitcast.106), channel_id=1, source_target_pairs={{0,0},{1,1},{2,8},{3,9},{8,2},{9,3},{10,10},{11,11},{16,4},{17,5},... | collective-permute-start | bytes 1228808 | tf_op jit(solution)/shard_map/ppermute | solution.py:96
  1492.8 49.2 %all-to-all-start.10 = ((bf16[8,100,800]{2,1,0:T(8,128)(2,1)}), bf16[8,100,800]{2,1,0:T(8,128)(2,1)}, u32[]{:S(2)}, u32[]{:S(2)}) async-start(bf16[8,100,800]{2,1,0:T(8,128)(2,1)} %reshape.665), calls=%async_computation.10 | async-start | bytes 2981888 | tf_op jit(solution)/shard_map/all_to_all | solution.py:447
  (173 other events, 2929.4 us)
Sparse Core Ops, SparseCore 0:
  35.1 52.2 all-gather.9
  89.6 91.2 all-gather.11
  182.5 55.0 all-gather.17
  239.0 65.8 all-gather.13
  306.9 59.4 all-gather.15
  397.8 56.5 all-gather.19

commit v3 on v2

--- a/solution.py
+++ b/solution.py
@@ -1,3 +1,5 @@
+import functools
+
 import jax
 import jax.numpy as jnp
 from jax import lax
@@ -120,12 +122,15 @@
     def slot(self, chip, core):
         return (chip // self.rest * 2 + core) * self.rest + lax.rem(chip, self.rest)
 
-    def greet(self):
+    def greet(self, zs=1):
         barrier = pltpu.get_barrier_semaphore()
+        z = lax.axis_index("z")
+        for k in range(1, zs):
+            pl.semaphore_signal(barrier, inc=1, device_id={"z": lax.rem(z + k, zs)}, device_id_type=MESH)
         for k in range(1, self.chips):
             pl.semaphore_signal(barrier, inc=1, device_id=self.device(self.ahead(k), self.c), device_id_type=MESH)
         pl.semaphore_signal(barrier, inc=1, device_id=self.device(self.chip, 1 - self.c), device_id_type=MESH)
-        pl.semaphore_wait(barrier, self.chips)
+        pl.semaphore_wait(barrier, self.chips + zs - 1)
 
 
 def remote(src, dst, send, recv, device):
@@ -159,24 +164,61 @@
     own.wait()
 
 
-def gather_kernel(src, out, local, chip_send, chip_recv, core_send, core_recv):
+def gather_kernel(ties, src, *rest):
+    out, local, chip_send, chip_recv, core_send, core_recv = rest[ties:]
     peers = Peers()
     peers.greet()
     gather_steps(peers, src, out, local, chip_send, chip_recv, core_send, core_recv)
 
 
-def slab_gather(a, name=1):
+def slab_gather(a, ties, name):
     chips = lax.axis_size("section") * lax.axis_size("r")
     sems = pltpu.SemaphoreType.DMA((chips,))
     out = pl.pallas_call(
-        gather_kernel,
+        functools.partial(gather_kernel, len(ties)),
         out_shape=jax.ShapeDtypeStruct((2 * chips, *a.shape), a.dtype),
-        in_specs=[pl.BlockSpec(memory_space=pl.ANY)],
+        in_specs=[pl.BlockSpec(memory_space=pl.ANY)] * (1 + len(ties)),
         out_specs=pl.BlockSpec(memory_space=pl.ANY),
         scratch_shapes=[pltpu.SemaphoreType.DMA] + [sems] * 4,
         compiler_params=pltpu.CompilerParams(collective_id=name, has_side_effects=True),
+    )(a, *ties)
+    return out.reshape(2 * chips * a.shape[0], a.shape[1])
+
+
+def tiny_kernel(src, out, stage, local, z_send, z_recv, chip_send, chip_recv, core_send, core_recv):
+    peers = Peers()
+    zs, z = lax.axis_size("z"), lax.axis_index("z")
+    peers.greet(zs)
+    sent = []
+    for k in range(1, zs):
+        copy = remote(src, stage.at[z], z_send.at[k], z_recv.at[k], {"z": lax.rem(z + k, zs)})
+        copy.start()
+        sent.append(copy)
+    stage[z] = src[...]
+    for k in range(1, zs):
+        block = stage.at[lax.rem(z + zs - k, zs)]
+        remote(block, block, z_send.at[k], z_recv.at[k], {"z": lax.rem(z + k, zs)}).wait_recv()
+    gather_steps(peers, stage, out, local, chip_send, chip_recv, core_send, core_recv)
+    for copy in sent:
+        copy.wait_send()
+
+
+def tiny_gather(a, name=0):
+    sections, rest, zs = (lax.axis_size(i) for i in ("section", "r", "z"))
+    chips = sections * rest
+    sems = pltpu.SemaphoreType.DMA((chips,))
+    vmem = pl.BlockSpec(memory_space=pltpu.VMEM)
+    out = pl.pallas_call(
+        tiny_kernel,
+        out_shape=jax.ShapeDtypeStruct((2 * chips, zs, *a.shape), a.dtype),
+        in_specs=[vmem],
+        out_specs=vmem,
+        scratch_shapes=[pltpu.VMEM((zs, *a.shape), a.dtype), pltpu.SemaphoreType.DMA]
+        + [pltpu.SemaphoreType.DMA((zs,))] * 2
+        + [sems] * 4,
+        compiler_params=pltpu.CompilerParams(collective_id=name, has_side_effects=True),
     )(a)
-    return out.reshape(2 * chips * a.shape[0], a.shape[1])
+    return out.reshape(sections, 2, rest, zs, *a.shape)
 
 
 def sum_steps(peers, part, mine, other, out, going, coming, local, chip_send, chip_recv, core_send, core_recv):
@@ -216,36 +258,60 @@
     ] + [pltpu.SemaphoreType.DMA((chips,))] * 5
 
 
-def sum_kernel(part, out, mine, other, going, coming, local, chip_send, chip_recv, core_send, core_recv):
+def sum_kernel(ties, part, *rest):
+    out, mine, other, going, coming, local, chip_send, chip_recv, core_send, core_recv = rest[ties:]
     peers = Peers()
     peers.greet()
     sum_steps(peers, part, mine, other, out, going, coming, local, chip_send, chip_recv, core_send, core_recv)
 
 
-def slab_sum(a, name=2):
+def slab_sum(a, ties, name):
     chips = lax.axis_size("section") * lax.axis_size("r")
     rows, width = a.shape[0] // (2 * chips), a.shape[1]
     return pl.pallas_call(
-        sum_kernel,
+        functools.partial(sum_kernel, len(ties)),
         out_shape=jax.ShapeDtypeStruct((rows, width), jnp.float32),
-        in_specs=[pl.BlockSpec(memory_space=pl.ANY)],
+        in_specs=[pl.BlockSpec(memory_space=pl.ANY)] * (1 + len(ties)),
         out_specs=pl.BlockSpec(memory_space=pltpu.VMEM),
         scratch_shapes=sum_scratch(chips, rows, width),
         compiler_params=pltpu.CompilerParams(collective_id=name, has_side_effects=True, vmem_limit_bytes=40 * 2**20),
-    )(a.astype(jnp.bfloat16).reshape(2 * chips, rows, width))
-
-
-def ring_sum(part, lay):
-    ring = [(i, (i + 1) % lay.zs) for i in range(lay.zs)]
-
-    def own(step):
-        return lax.dynamic_index_in_dim(part, (lay.z - 1 - step) % lay.zs, 0, keepdims=False)
-
-    acc = own(0).astype(jnp.bfloat16)
-    for step in range(1, lay.zs):
-        acc = lax.ppermute(acc, "z", ring)
-        acc = (acc.astype(jnp.float32) + own(step).astype(jnp.float32)).astype(jnp.bfloat16)
-    return acc
+    )(a.astype(jnp.bfloat16).reshape(2 * chips, rows, width), *ties)
+
+
+class Rings:
+    def __init__(self, lay):
+        self.lay = lay
+        self.live = []
+
+    def own(self, part, step):
+        lay = self.lay
+        block = lax.dynamic_index_in_dim(part, (lay.z - 1 - step) % lay.zs, 0, keepdims=False)
+        return block.astype(jnp.float32)
+
+    def add(self, term):
+        zs = self.lay.zs
+        part = term.reshape(zs, term.shape[0] // zs, term.shape[1])
+        ring = [self.own(part, 0).astype(jnp.bfloat16), part, 0]
+        self.live.append(ring)
+        return ring
+
+    def step(self):
+        zs = self.lay.zs
+        self.live = [ring for ring in self.live if ring[2] < zs - 1]
+        route = [(i, (i + 1) % zs) for i in range(zs)]
+        for ring in self.live:
+            got = lax.ppermute(ring[0], "z", route).astype(jnp.float32)
+            ring[2] += 1
+            ring[0] = (got + self.own(ring[1], ring[2])).astype(jnp.bfloat16)
+
+    def ties(self):
+        now = [ring[0] for ring in self.live]
+        self.step()
+        return now
+
+    def finish(self):
+        while any(ring[2] < self.lay.zs - 1 for ring in self.live):
+            self.step()
 
 
 def spread_weights(lay, w_qkv, w_attn_out, w_fc, w_proj):
@@ -265,20 +331,21 @@
         got = got.reshape(lay.sections, lay.cores * lay.rest * block, a.shape[2])
         return [got[layer] for layer in range(lay.sections)]
 
-    qkv, out, fc = move(qkv), move(out), move(fc)
+    first = move(jnp.concatenate([qkv, out], axis=2))
+    fc = move(fc)
     proj = lax.all_to_all(proj, ("section",), 0, 0, tiled=True)
     params = []
     for layer in range(lay.sections):
         full = [
-            lax.all_gather(a, "z", axis=0, tiled=True)
-            for a in (qkv[layer], out[layer], fc[layer], proj[layer])
+            lax.all_gather(a, "z", axis=0, tiled=True) for a in (first[layer], fc[layer], proj[layer])
         ]
-        wo = full[1].reshape(lay.zs, lay.cores, lay.rest * block, lay.cols)
+        wo = full[0][:, 3 * slot_cols :]
+        wo = wo.reshape(lay.zs, lay.cores, lay.rest * block, lay.cols)
         wo = jnp.swapaxes(wo, 0, 1).reshape(width, lay.cols)
         wo = jnp.pad(wo, ((0, n * slot_cols - width), (0, 0))).reshape(n, slot_cols, lay.cols)
         wo = lax.all_to_all(wo, SLAB, 0, 0, tiled=True)
         wo = wo.transpose(1, 0, 2).reshape(slot_cols, width)
-        params.append((full[0], wo, full[2], full[3]))
+        params.append((full[0][:, : 3 * slot_cols], wo, full[1], full[2]))
     return params
 
 
@@ -322,48 +389,53 @@
     return [a.reshape(tokens, -1).astype(jnp.bfloat16) for a in (gq, gk, gv)]
 
 
-def forward(h, params, small, places, lay):
+def forward(h, params, small, places, lay, name):
     w_qkv, w_out, w_fc, w_proj = params
     gains, shifts, q_bias, v_bias, unit_bias = small
     span = lay.slots * lay.head
-    normed = slab_gather(normalize(h, gains[0], shifts[0]).astype(jnp.bfloat16))
+    normed = slab_gather(normalize(h, gains[0], shifts[0]).astype(jnp.bfloat16), (), name)
     qkv = dot(normed, w_qkv, 1, 0)
     q = (qkv[:, :span] + q_bias).astype(jnp.bfloat16)
     k = qkv[:, span : 2 * span].astype(jnp.bfloat16)
     v = (qkv[:, 2 * span :] + v_bias).astype(jnp.bfloat16)
     attended, logs = attend(q, k, v, places, lay)
-    mid = h + (slab_sum(dot(attended, w_out, 1, 0)) + shifts[3])
-    normed_two = slab_gather(normalize(mid, gains[1], shifts[4]).astype(jnp.bfloat16))
+    mid = h + (slab_sum(dot(attended, w_out, 1, 0), (), name + 1) + shifts[3])
+    normed_two = slab_gather(normalize(mid, gains[1], shifts[4]).astype(jnp.bfloat16), (), name + 2)
     hidden = dot(normed_two, w_fc, 1, 0) + unit_bias
     activated = smooth(hidden).astype(jnp.bfloat16)
-    result = mid + (slab_sum(dot(activated, w_proj, 1, 0)) + shifts[5])
+    result = mid + (slab_sum(dot(activated, w_proj, 1, 0), (), name + 3) + shifts[5])
     kept = (h, mid, normed, q, k, v, attended, logs, normed_two, hidden, activated)
     return result.astype(jnp.bfloat16), kept
 
 
-def backward(g_rows, kept, params, small, places, lay):
+def backward(g_rows, branch, kept, params, small, places, lay, rings, name):
     w_qkv, w_out, w_fc, w_proj = params
     gains, shifts, q_bias, v_bias, unit_bias = small
     h, mid, normed, q, k, v, attended, logs, normed_two, hidden, activated = kept
     branch_rows = g_rows.astype(jnp.bfloat16)
-    branch = slab_gather(branch_rows)
+    if branch is None:
+        branch = slab_gather(branch_rows, rings.ties(), name)
     g_activated = dot(branch, w_proj, 1, 1)
     _, smooth_back = jax.vjp(smooth, hidden)
     g_hidden = smooth_back(g_activated)[0].astype(jnp.bfloat16)
-    grad_proj = dot(activated, branch, 0, 0)
-    g_normed_two = slab_sum(dot(g_hidden, w_fc, 1, 1))
-    grad_fc = dot(normed_two, g_hidden, 0, 0)
+    grad_proj = rings.add(dot(activated, branch, 0, 0))
+    g_normed_two = slab_sum(dot(g_hidden, w_fc, 1, 1), rings.ties(), name + 1)
+    grad_fc = rings.add(dot(normed_two, g_hidden, 0, 0))
     _, second_back = jax.vjp(normalize, mid, gains[1], shifts[4])
     mid_part, gain_two, shift_two = second_back(g_normed_two)
     g_mid = g_rows + mid_part
     g_attn_rows = g_mid.astype(jnp.bfloat16)
-    g_attn = slab_gather(g_attn_rows)
+    g_attn = slab_gather(g_attn_rows, rings.ties(), name + 2)
     g_attended = dot(g_attn, w_out, 1, 1).astype(jnp.bfloat16)
-    grad_out = dot(attended, g_attn, 0, 0)
+    n, span, block, width = lay.slab, lay.slots * lay.head, lay.block, lay.width
+    wo = dot(attended, g_attn, 0, 0).astype(jnp.bfloat16).reshape(span, n, lay.cols)
+    wo = lax.all_to_all(wo.transpose(1, 0, 2), SLAB, 0, 0, tiled=True)
+    wo = wo.reshape(n * span, lay.cols)[:width].reshape(lay.cores, lay.zs, lay.rest * block, lay.cols)
+    wo = jnp.swapaxes(wo, 0, 1).reshape(width, lay.cols)
     gq, gk, gv = attend_back(q, k, v, g_attended, logs, places, lay)
     joint = jnp.concatenate([gq, gk, gv], axis=1)
-    g_normed = slab_sum(dot(joint, w_qkv, 1, 1))
-    grad_qkv = dot(normed, joint, 0, 0)
+    g_normed = slab_sum(dot(joint, w_qkv, 1, 1), rings.ties(), name + 3)
+    grad_qkv = rings.add(jnp.concatenate([dot(normed, joint, 0, 0), wo.astype(jnp.float32)], axis=1))
     _, first_back = jax.vjp(normalize, h, gains[0], shifts[0])
     in_part, gain_one, shift_one = first_back(g_normed)
     g_in = g_mid + in_part
@@ -373,7 +445,7 @@
 
     local = (gain_one, gain_two, shift_one, total(g_attn_rows), shift_two, total(branch_rows))
     shard = (total(gq), total(gv), total(g_hidden))
-    return g_in, (grad_qkv, grad_out, grad_fc, grad_proj), local, shard
+    return g_in, (grad_qkv, grad_fc, grad_proj), local, shard
 
 
 def on_device(
@@ -388,8 +460,15 @@
 
     per_row = lay.unit_block // block
     thin = jnp.concatenate([norm_gains[0], biases[0], fc_bias[0].reshape(block, per_row)], axis=1)
-    thin = lax.all_gather(thin, ALL, axis=0, tiled=True).astype(jnp.float32)
-    thin = thin.reshape(lay.sections, width, 8 + per_row)
+    thin = jnp.concatenate([thin.reshape(-1).astype(jnp.float32), positions.reshape(-1).astype(jnp.float32)])
+    used, spots = block * (8 + per_row), positions.size
+    thin = jnp.pad(thin, (0, -thin.size % 1024)).reshape(-1, 128)
+    thin = tiny_gather(thin).reshape(lay.sections, lay.cores, lay.rest, lay.zs, -1)
+    places = thin[0, 0, :, :, used : used + spots].astype(jnp.int32)
+    places = places.reshape(lay.rest, lay.zs, lay.micros, lay.rows).transpose(2, 1, 0, 3)
+    places = places.reshape(lay.micros, lay.tokens)
+    places = lax.dynamic_index_in_dim(places, micro, 0, keepdims=False)
+    thin = jnp.swapaxes(thin[..., :used], 2, 3).reshape(lay.sections, width, 8 + per_row)
     smalls = []
     for layer in range(lay.sections):
         gains = [lay.order(thin[layer, :, i]) for i in range(2)]
@@ -405,56 +484,52 @@
         unit = lax.dynamic_index_in_dim(unit, lay.t, 0, keepdims=False)
         smalls.append((gains, shifts, heads[0], heads[1], unit))
 
-    places = lax.all_gather(positions, ("z", "r"), axis=1, tiled=True)
-    places = lax.dynamic_index_in_dim(places, micro, 0, keepdims=False)
-
     h = lay.order(lay.tokens_in(inputs))
     g = lay.order(lay.tokens_in(cotangent))
 
     outs, keeps = [], []
     for layer in range(lay.sections):
-        h, kept = forward(h.astype(jnp.float32), params[layer], smalls[layer], places, lay)
+        h, kept = forward(h.astype(jnp.float32), params[layer], smalls[layer], places, lay, 1 + 4 * layer)
         outs.append(h)
         keeps.append(kept)
 
     grads = [None] * lay.sections
     grad_rows = [None] * lay.sections
     locals_, shards = [None] * lay.sections, [None] * lay.sections
+    rings = Rings(lay)
+    first_name = 1 + 4 * lay.sections
+    branch = slab_gather(g, (), first_name)
     for layer in reversed(range(lay.sections)):
         g, grads[layer], locals_[layer], shards[layer] = backward(
-            g.astype(jnp.float32), keeps[layer], params[layer], smalls[layer], places, lay
+            g.astype(jnp.float32),
+            branch,
+            keeps[layer],
+            params[layer],
+            smalls[layer],
+            places,
+            lay,
+            rings,
+            first_name + 1 + 4 * layer,
         )
-        g = g.astype(jnp.bfloat16)
+        g, branch = g.astype(jnp.bfloat16), None
         grad_rows[layer] = g
+    rings.finish()
 
     section_out = lay.tokens_out([lay.restore(a) for a in outs])
     section_grad = lay.tokens_out([lay.restore(a) for a in grad_rows])
 
-    def by_z(a):
-        return a.reshape(lay.zs, a.shape[0] // lay.zs, a.shape[1])
-
-    sums = []
-    for layer in range(lay.sections):
-        grad_qkv, grad_out, grad_fc, grad_proj = grads[layer]
-        wo = grad_out.astype(jnp.bfloat16).reshape(span, n, lay.cols).transpose(1, 0, 2)
-        wo = lax.all_to_all(wo, SLAB, 0, 0, tiled=True).reshape(n * span, lay.cols)[:width]
-        wo = wo.reshape(lay.cores, lay.zs, lay.rest * block, lay.cols)
-        wo = jnp.swapaxes(wo, 0, 1).reshape(width, lay.cols)
-        sums.append([ring_sum(by_z(a), lay) for a in (grad_qkv, wo, grad_fc, grad_proj)])
-
     def back(i):
-        both = jnp.stack([sums[layer][i] for layer in range(lay.sections)])
-        return lax.all_to_all(
-            both.reshape(n, block, both.shape[2]), SLAB, 0, 0, tiled=True
-        )
-
-    got = back(0).reshape(n, block, 3, span).transpose(1, 2, 0, 3).reshape(block, 3, n * span)
-    out_qkv = got[:, :, :width].reshape(block, 3 * width).astype(jnp.float32)
-    got = back(1).transpose(1, 0, 2).reshape(block, width)
+        both = jnp.stack([grads[layer][i][0] for layer in range(lay.sections)])
+        return lax.all_to_all(both.reshape(n, block, both.shape[2]), SLAB, 0, 0, tiled=True)
+
+    first = back(0)
+    got = first[:, :, : 3 * span].reshape(n, block, 3, span).transpose(1, 2, 0, 3)
+    out_qkv = got.reshape(block, 3, n * span)[:, :, :width].reshape(block, 3 * width).astype(jnp.float32)
+    got = first[:, :, 3 * span :].transpose(1, 0, 2).reshape(block, width)
     out_attn = lay.restore(got).astype(jnp.float32)
-    got = back(2).reshape(lay.sections, lay.cores, lay.rest, block, lay.zs, lay.half)
+    got = back(1).reshape(lay.sections, lay.cores, lay.rest, block, lay.zs, lay.half)
     out_fc = got.transpose(3, 1, 4, 2, 0, 5).reshape(block, lay.units).astype(jnp.float32)
-    both = jnp.stack([sums[layer][3] for layer in range(lay.sections)])
+    both = jnp.stack([grads[layer][2][0] for layer in range(lay.sections)])
     got = lax.all_to_all(both, ("section",), 0, 0, tiled=True)
     out_proj = lay.restore(got.reshape(lay.unit_block, width)).astype(jnp.float32)
 

time: 1580 us -> 1270 us (0.80)
  blocking collectives: 239 us -> 66.5 us
  waiting for transfers between devices: 182 us -> 13.2 us
  Pallas kernels: 395 us -> 504 us
  starting transfers between devices: 189 us -> 106 us
  local copies, waits for them, and re-layouts: 238 us -> 219 us
    all_gather x4 -> x0, blocking collectives: 178 us -> none  [the longest x1 118 us: on_device(): thin = lax.all_gather(thin, ALL, axis=0, tiled=True).astype(jnp.float32)]
    ppermute x24 -> x18, waiting for transfers between devices: 177 us -> 12.9 us  [step(): got = lax.ppermute(ring[0], 'z', route).astype(jnp.float32)]
    pallas_call x16 -> x17, Pallas kernels: 395 us -> 504 us  [the longest x8 225 us: slab_gather(): pl.pallas_call(functools.partial(gather_kernel, len(ties)), out_shape=jax...]
    ppermute x24 -> x18, starting transfers between devices: 61.1 us -> 19.3 us  [step(): got = lax.ppermute(ring[0], 'z', route).astype(jnp.float32)]
    all_to_all x3 -> x2, starting transfers between devices: 34.7 us -> 13.7 us  [back(): lax.all_to_all(both.reshape(n, block, both.shape[2]), SLAB, 0, 0, tiled=T...]
    convert_element_type x20 -> x23, other arithmetic: 30.2 us -> 43.4 us  [the longest x15 37.5 us: step(): ring[0] = (got + self.own(ring[1], ring[2])).astype(jnp.bfloat16)]
    unnamed x310 -> x305, local copies, waits for them, and re-layouts: 32.6 us -> 25.6 us
  transfers between devices with their start and end apart: 52 -> 44, of which waited for: 18 -> 3; matrix products, arithmetic and copies ran while one was open for 32% -> 40% of each run, Pallas kernels for 25% -> 40%
where the time goes in v3:
time: 1270 us; the launch traced here: 1250 us
  Pallas kernels  504 us (40%)
  local copies, waits for them, and re-layouts  219 us (17%)
  matrix products  214 us (17%)
  other arithmetic  109 us (9%)
  starting transfers between devices  106 us (8%)
  blocking collectives  66.5 us (5%)
  between operations  17.6 us (1%)
  waiting for transfers between devices  13.2 us (1%)
    pallas_call x8, Pallas kernels, slab_gather(): pl.pallas_call(functools.partial(gather_kernel, len(ties)), out_shape=jax...  225 us
    pallas_call x8, Pallas kernels, slab_sum(): pl.pallas_call(functools.partial(sum_kernel, len(ties)), out_shape=jax.Sh...  199 us
    dot_general x24, matrix products, dot(): lax.dot_general(a, b, (((ca,), (cb,)), ((), ())), preferred_element_type=...  140 us
    pallas_call x1, Pallas kernels, tiny_gather(): pl.pallas_call(tiny_kernel, out_shape=jax.ShapeDtypeStruct((2 * chips, zs...  81.1 us
    all_to_all x2, blocking collectives, move(): got = lax.all_to_all(a, SLAB, 0, 0, tiled=True)  47.3 us
    ppermute x8, starting transfers between devices, tokens_out(): got.append(lax.ppermute(part, ALL, route))  40.5 us
    convert_element_type x15, other arithmetic, step(): ring[0] = (got + self.own(ring[1], ring[2])).astype(jnp.bfloat16)  37.5 us
    convert_element_type x8, local copies, waits for them, and re-layouts, slab_sum(): a.astype(jnp.bfloat16).reshape(2 * chips, rows, width)  34.9 us
  transfers between devices with their start and end apart: 44, of which 3 were waited for; matrix products, arithmetic and copies ran while one was open for 40% of the time, Pallas kernels for 40%

profile of v3, /device:TPU:3, one launch (start us, length us, event | category | flops | bytes accessed | tf_op | source)
XLA Modules:
  0.0 1249.5 jit_solution(5615746217535253992)
XLA Ops:
  18.5 25.0 %all_to_all.59 = bf16[8,100,968]{2,1,0:T(8,128)(2,1)S(1)} all-to-all(bf16[8,100,968]{2,1,0:T(8,128)(2,1)S(1)} %copy.444), channel_id=1, replica_groups=mesh['section'=2,'dp'=2,'z'=4,'r'=2] {'section','dp','r'}, dimensions={0} | all-to-all | bytes 3097600 | tf_op jit(solution)/shard_map/all_to_all | solution.py:330
  55.6 22.3 %all_to_all.60 = bf16[8,100,800]{2,1,0:T(8,128)(2,1)S(1)} all-to-all(bf16[8,100,800]{2,1,0:T(8,128)(2,1)S(1)} %copy.454), channel_id=1, replica_groups=mesh['section'=2,'dp'=2,'z'=4,'r'=2] {'section','dp','r'}, dimensions={0} | all-to-all | bytes 2560000 | tf_op jit(solution)/shard_map/all_to_all | solution.py:330
  90.5 19.2 %all_to_all.61 = bf16[2,200,1600]{2,1,0:T(8,128)(2,1)S(1)} all-to-all(bf16[2,200,1600]{2,1,0:T(8,128)(2,1)S(1)} %reshape_reshape.13), channel_id=1, replica_groups=mesh['section'=2,'dp'=2,'z'=4,'r'=2] {'section'}, dimensions={0} | all-to-all | bytes 2560000 | tf_op jit(solution)/shard_map/all_to_all | solution.py:336
  120.7 81.1 %shard_map.169 = f32[8,4,16,128]{3,2,1,0:T(8,128)} custom-call(f32[16,128]{1,0:T(8,128)} %fusion.147.src), custom_call_target="tpu_custom_call" | custom-call | tf_op jit(solution)/shard_map/pallas_call | solution.py:211
  230.0 24.6 %shard_map.170 = bf16[8,128,1600]{2,1,0:T(8,128)(2,1)} custom-call(bf16[128,1600]{1,0:T(8,128)(2,1)} %add_convert_fusion.6.src), custom_call_target="tpu_custom_call" | custom-call | tf_op jit(solution)/shard_map/pallas_call | solution.py:177
  254.7 24.6 %shard_map.178 = bf16[8,128,1600]{2,1,0:T(8,128)(2,1)} custom-call(bf16[128,1600]{1,0:T(8,128)(2,1)} %copy.476.src), custom_call_target="tpu_custom_call" | custom-call | tf_op jit(solution)/shard_map/pallas_call | solution.py:177
  324.1 24.3 %shard_map.171 = f32[128,1600]{1,0:T(8,128)S(1)} custom-call(bf16[8,128,1600]{2,1,0:T(8,128)(2,1)S(1)} %bitcast.430), custom_call_target="tpu_custom_call" | custom-call | tf_op jit(solution)/shard_map/pallas_call | solution.py:271
  350.5 24.1 %shard_map.172 = bf16[8,128,1600]{2,1,0:T(8,128)(2,1)} custom-call(bf16[128,1600]{1,0:T(8,128)(2,1)} %add_convert_fusion.5.src), custom_call_target="tpu_custom_call" | custom-call | tf_op jit(solution)/shard_map/pallas_call | solution.py:177
  396.5 24.8 %shard_map.173 = f32[128,1600]{1,0:T(8,128)S(1)} custom-call(bf16[8,128,1600]{2,1,0:T(8,128)(2,1)S(1)} %bitcast.431), custom_call_target="tpu_custom_call" | custom-call | tf_op jit(solution)/shard_map/pallas_call | solution.py:271
  432.1 23.8 %shard_map.174 = bf16[8,128,1600]{2,1,0:T(8,128)(2,1)} custom-call(bf16[128,1600]{1,0:T(8,128)(2,1)} %fusion.127.src), custom_call_target="tpu_custom_call" | custom-call | tf_op jit(solution)/shard_map/pallas_call | solution.py:177
  486.8 25.1 %shard_map.175 = f32[128,1600]{1,0:T(8,128)S(1)} custom-call(bf16[8,128,1600]{2,1,0:T(8,128)(2,1)S(1)} %bitcast.432), custom_call_target="tpu_custom_call" | custom-call | tf_op jit(solution)/shard_map/pallas_call | solution.py:271
  514.1 24.2 %shard_map.176 = bf16[8,128,1600]{2,1,0:T(8,128)(2,1)} custom-call(bf16[128,1600]{1,0:T(8,128)(2,1)} %add_convert_fusion.3.src), custom_call_target="tpu_custom_call" | custom-call | tf_op jit(solution)/shard_map/pallas_call | solution.py:177
  560.1 24.4 %shard_map.177 = f32[128,1600]{1,0:T(8,128)S(1)} custom-call(bf16[8,128,1600]{2,1,0:T(8,128)(2,1)S(1)} %bitcast.433), custom_call_target="tpu_custom_call" | custom-call | tf_op jit(solution)/shard_map/pallas_call | solution.py:271
  608.9 24.7 %shard_map.179 = f32[128,1600]{1,0:T(8,128)S(1)} custom-call(bf16[8,128,1600]{2,1,0:T(8,128)(2,1)S(1)} %bitcast.429, bf16[200,1600]{1,0:T(8,128)(2,1)S(1)} %fusion.137.rest_0_), custom_call_target="tpu_custom_call" | custom-call | tf_op jit(solution)/shard_map/pallas_call | solution.py:271
  636.0 16.0 %collective-permute-start.2 = (bf16[128,1600]{0,1:T(8,128)(2,1)S(1)}, bf16[128,1600]{0,1:T(8,128)(2,1)S(1)}, u32[]{:S(2)}, u32[]{:S(2)}) collective-permute-start(bf16[128,1600]{0,1:T(8,128)(2,1)S(1)} %bitcast.536), channel_id=1, source_target_pairs={{0,16},{1,17},{2,24},{3,25},{8,18},{9,19},{10,26},{11,27},{16,20},... | collective-permute-start | bytes 1228808 | tf_op jit(solution)/shard_map/ppermute | solution.py:98
  657.8 8.5 fusion.72
  683.7 52.3 %shard_map.180 = bf16[8,128,1600]{2,1,0:T(8,128)(2,1)} custom-call(bf16[128,1600]{1,0:T(8,128)(2,1)} %get-tuple-element.88.src, bf16[200,1600]{1,0:T(8,128)(2,1)} %fusion.101.rest_0_, bf16[400,800]{1,0:T(8,128)(2,1)} %fusion.134.rest_1_), custom_call_target="tpu_custom_call" | custom-call | tf_op jit(solution)/shard_map/pallas_call | solution.py:177
  740.2 8.8 convert_reduce_fusion.4
  749.0 15.4 %multiply_reduce_fusion.1 = (f32[4,1024]{1,0:T(4,128)}, f32[4,1024,1024]{1,2,0:T(8,128)}) fusion(f32[4,1024,1024]{1,2,0:T(8,128)} %copy-done.11, f32[4,1024]{1,0:T(4,128)} %log_add_fusion.1, pred[1024,1024]{0,1:T(8,128)(4,1)S(1)} %copy-done.14, bf16[1024,4,64]{0,2,1:T(8,128)(2,1)} %bitcast.522, bf16[1024,4,64]{0,2,1:T(8,128)(2,1)} %bitcast.509), kind=kOutput, calls=%fused_computation.4 | convolution fusion | flops 557838336 | bytes 35684352 | tf_op jit(solution)/shard_map/qhd,nhd->hqn/dot_general | solution.py:381
  764.5 8.3 multiply_convert_fusion.1
  812.9 24.3 %shard_map.181 = f32[128,1600]{1,0:T(8,128)S(1)} custom-call(bf16[8,128,1600]{2,1,0:T(8,128)(2,1)S(1)} %bitcast.436, bf16[200,1600]{1,0:T(8,128)(2,1)} %fusion.100.rest_0_, bf16[400,800]{1,0:T(8,128)(2,1)} %fusion.89.rest_1_), custom_call_target="tpu_custom_call" | custom-call | tf_op jit(solution)/shard_map/pallas_call | solution.py:271
  869.1 23.5 %shard_map.182 = bf16[8,128,1600]{2,1,0:T(8,128)(2,1)} custom-call(bf16[128,1600]{1,0:T(8,128)(2,1)} %copy-done.30, bf16[200,1600]{1,0:T(8,128)(2,1)} %fusion.99.rest_0_, bf16[400,800]{1,0:T(8,128)(2,1)} %fusion.88.rest_1_, bf16[400,968]{1,0:T(8,128)(2,1)} %fusion.131.rest_2_), custom_call_target="tpu_custom_call" | custom-call | tf_op jit(solution)/shard_map/pallas_call | solution.py:177
  892.7 9.4 convert_reduce_fusion.1
  933.8 25.9 %shard_map.183 = f32[128,1600]{1,0:T(8,128)S(1)} custom-call(bf16[8,128,1600]{2,1,0:T(8,128)(2,1)S(1)} %bitcast.435, bf16[400,800]{1,0:T(8,128)(2,1)S(1)} %fusion.87.rest_0_, bf16[400,968]{1,0:T(8,128)(2,1)} %fusion.71.rest_1_, bf16[200,1600]{1,0:T(8,128)(2,1)} %fusion.138.rest_2_), custom_call_target="tpu_custom_call" | custom-call | tf_op jit(solution)/shard_map/pallas_call | solution.py:271
  975.1 27.5 %shard_map.184 = bf16[8,128,1600]{2,1,0:T(8,128)(2,1)} custom-call(bf16[128,1600]{1,0:T(8,128)(2,1)} %get-tuple-element.86.src, bf16[400,968]{1,0:T(8,128)(2,1)} %fusion.70.rest_0_, bf16[200,1600]{1,0:T(8,128)(2,1)} %fusion.98.rest_1_, bf16[400,800]{1,0:T(8,128)(2,1)} %fusion.135.rest_2_), custom_call_target="tpu_custom_call" | custom-call | tf_op jit(solution)/shard_map/pallas_call | solution.py:177
  1008.4 9.3 convert_reduce_fusion.6
  1017.7 15.5 %multiply_reduce_fusion = (f32[4,1024]{1,0:T(4,128)}, f32[4,1024,1024]{1,2,0:T(8,128)}) fusion(f32[4,1024,1024]{1,2,0:T(8,128)} %copy-done.10, f32[4,1024]{1,0:T(4,128)} %log_add_fusion, pred[1024,1024]{0,1:T(8,128)(4,1)S(1)} %copy-done.15, bf16[1024,4,64]{0,2,1:T(8,128)(2,1)} %bitcast.520, bf16[1024,4,64]{0,2,1:T(8,128)(2,1)} %bitcast.507), kind=kOutput, calls=%fused_computation.1 | convolution fusion | flops 557838336 | bytes 35684352 | tf_op jit(solution)/shard_map/qhd,nhd->hqn/dot_general | solution.py:381
  1033.2 8.3 multiply_convert_fusion
  1094.8 25.1 %shard_map.185 = f32[128,1600]{1,0:T(8,128)S(1)} custom-call(bf16[8,128,1600]{2,1,0:T(8,128)(2,1)S(1)} %bitcast.434, bf16[400,968]{1,0:T(8,128)(2,1)S(1)} %fusion.67.rest_0_, bf16[200,1600]{1,0:T(8,128)(2,1)} %fusion.97.rest_1_, bf16[400,800]{1,0:T(8,128)(2,1)} %fusion.86.rest_2_), custom_call_target="tpu_custom_call" | custom-call | tf_op jit(solution)/shard_map/pallas_call | solution.py:271
  1142.5 10.3 collective-permute-done.25
  1179.8 8.3 all-to-all-start.7
  1218.0 9.4 reshape.703
  (733 shorter events, 533.7 us)
Async XLA Ops:
  7.2 272.2 %all-gather.9.cloned.1.call-start = ((), (), s32[]{:S(2)}) async-start(), calls=%async_computation.11 | async-start | bytes 4096000 | tf_op jit(solution)/shard_map/all_gather | solution.py:340
  44.8 263.0 %all-gather.13.cloned.1.call-start = ((), (), s32[]{:S(2)}) async-start(), calls=%async_computation.13 | async-start | bytes 4096000 | tf_op jit(solution)/shard_map/all_gather | solution.py:340
  46.1 328.5 %all-gather.11.cloned.1.call-start = ((), (), s32[]{:S(2)}) async-start(), calls=%async_computation.12 | async-start | bytes 3584000 | tf_op jit(solution)/shard_map/all_gather | solution.py:340
  80.1 302.6 %all-gather.17.cloned.1.call-start = ((), (), s32[]{:S(2)}) async-start(), calls=%async_computation.15 | async-start | bytes 3328000 | tf_op jit(solution)/shard_map/all_gather | solution.py:340
  110.9 427.4 %all-gather.15.cloned.1.call-start = ((), (), s32[]{:S(2)}) async-start(), calls=%async_computation.14 | async-start | bytes 3584000 | tf_op jit(solution)/shard_map/all_gather | solution.py:340
  111.9 111.4 %collective-permute-start.1 = (bf16[128,1600]{0,1:T(8,128)(2,1)}, bf16[128,1600]{0,1:T(8,128)(2,1)}, u32[]{:S(2)}, u32[]{:S(2)}) collective-permute-start(bf16[128,1600]{0,1:T(8,128)(2,1)} %get-tuple-element.118), channel_id=1, source_target_pairs={{0,0},{1,1},{8,2},{9,3},{2,8},{3,9},{10,10},{11,11},{20,16},{21,17... | collective-permute-start | bytes 1228808 | tf_op jit(solution)/shard_map/ppermute | solution.py:84
  113.2 110.1 %collective-permute-start = (bf16[128,1600]{0,1:T(8,128)(2,1)}, bf16[128,1600]{0,1:T(8,128)(2,1)}, u32[]{:S(2)}, u32[]{:S(2)}) collective-permute-start(bf16[128,1600]{0,1:T(8,128)(2,1)} %get-tuple-element.119), channel_id=1, source_target_pairs={{0,4},{1,5},{8,6},{9,7},{2,12},{3,13},{10,14},{11,15},{20,20},{21,... | collective-permute-start | bytes 1228808 | tf_op jit(solution)/shard_map/ppermute | solution.py:84
  115.6 109.9 %collective-permute-start.7 = (bf16[128,1600]{0,1:T(8,128)(2,1)}, bf16[128,1600]{0,1:T(8,128)(2,1)}, u32[]{:S(2)}, u32[]{:S(2)}) collective-permute-start(bf16[128,1600]{0,1:T(8,128)(2,1)} %get-tuple-element.116), channel_id=1, source_target_pairs={{0,0},{1,1},{8,2},{9,3},{2,8},{3,9},{10,10},{11,11},{20,16},{21,17... | collective-permute-start | bytes 1228808 | tf_op jit(solution)/shard_map/ppermute | solution.py:84
  116.9 108.6 %collective-permute-start.6 = (bf16[128,1600]{0,1:T(8,128)(2,1)}, bf16[128,1600]{0,1:T(8,128)(2,1)}, u32[]{:S(2)}, u32[]{:S(2)}) collective-permute-start(bf16[128,1600]{0,1:T(8,128)(2,1)} %get-tuple-element.117), channel_id=1, source_target_pairs={{0,4},{1,5},{8,6},{9,7},{2,12},{3,13},{10,14},{11,15},{20,20},{21,... | collective-permute-start | bytes 1228808 | tf_op jit(solution)/shard_map/ppermute | solution.py:84
  119.7 426.7 %all-gather.19.cloned.1.call-start = ((), (), s32[]{:S(2)}) async-start(), calls=%async_computation.16 | async-start | bytes 3328000 | tf_op jit(solution)/shard_map/all_gather | solution.py:340
  312.5 165.1 %all-to-all-start.4 = ((bf16[8,256,200]{1,2,0:T(8,128)(2,1)}), bf16[8,256,200]{1,2,0:T(8,128)(2,1)}, u32[]{:S(2)}, u32[]{:S(2)}) async-start(bf16[8,256,200]{1,2,0:T(8,128)(2,1)} %bitcast.422), calls=%async_computation.4 | async-start | bytes 1638400 | tf_op jit(solution)/shard_map/all_to_all | solution.py:346
  422.6 256.2 %collective-permute-start.5 = (bf16[128,1600]{0,1:T(8,128)(2,1)}, bf16[128,1600]{0,1:T(8,128)(2,1)}, u32[]{:S(2)}, u32[]{:S(2)}) collective-permute-start(bf16[128,1600]{0,1:T(8,128)(2,1)} %bitcast.71), channel_id=1, source_target_pairs={{4,0},{5,1},{6,8},{7,9},{12,2},{13,3},{14,10},{15,11},{20,4},{21,5... | collective-permute-start | bytes 1228808 | tf_op jit(solution)/shard_map/ppermute | solution.py:98
  424.0 255.9 %collective-permute-start.3 = (bf16[128,1600]{0,1:T(8,128)(2,1)}, bf16[128,1600]{0,1:T(8,128)(2,1)}, u32[]{:S(2)}, u32[]{:S(2)}) collective-permute-start(bf16[128,1600]{0,1:T(8,128)(2,1)} %bitcast.71), channel_id=1, source_target_pairs={{0,0},{1,1},{2,8},{3,9},{8,2},{9,3},{10,10},{11,11},{16,4},{17,5},... | collective-permute-start | bytes 1228808 | tf_op jit(solution)/shard_map/ppermute | solution.py:98
  634.8 44.1 %collective-permute-start.4 = (bf16[128,1600]{0,1:T(8,128)(2,1)S(1)}, bf16[128,1600]{0,1:T(8,128)(2,1)}, u32[]{:S(2)}, u32[]{:S(2)}) collective-permute-start(bf16[128,1600]{0,1:T(8,128)(2,1)S(1)} %bitcast.535), channel_id=1, source_target_pairs={{4,16},{5,17},{6,24},{7,25},{12,18},{13,19},{14,26},{15,27},{20,20... | collective-permute-start | bytes 1228808 | tf_op jit(solution)/shard_map/ppermute | solution.py:98
  636.0 43.9 %collective-permute-start.2 = (bf16[128,1600]{0,1:T(8,128)(2,1)S(1)}, bf16[128,1600]{0,1:T(8,128)(2,1)S(1)}, u32[]{:S(2)}, u32[]{:S(2)}) collective-permute-start(bf16[128,1600]{0,1:T(8,128)(2,1)S(1)} %bitcast.536), channel_id=1, source_target_pairs={{0,16},{1,17},{2,24},{3,25},{8,18},{9,19},{10,26},{11,27},{16,20},... | collective-permute-start | bytes 1228808 | tf_op jit(solution)/shard_map/ppermute | solution.py:98
  678.8 100.7 %collective-permute-start.10 = (bf16[400,800]{1,0:T(8,128)(2,1)}, bf16[400,800]{1,0:T(8,128)(2,1)}, u32[]{:S(2)}, u32[]{:S(2)}) collective-permute-start(bf16[400,800]{1,0:T(8,128)(2,1)} %fusion.134.rest_1_), channel_id=1, source_target_pairs={{0,2},{2,4},{4,6},{6,0},{1,3},{3,5},{5,7},{7,1},{8,10},{10,12},{12... | collective-permute-start | bytes 1920008 | tf_op jit(solution)/shard_map/ppermute | solution.py:303
  683.3 127.2 %collective-permute-start.9 = (bf16[200,1600]{1,0:T(8,128)(2,1)}, bf16[200,1600]{1,0:T(8,128)(2,1)}, u32[]{:S(2)}, u32[]{:S(2)}) collective-permute-start(bf16[200,1600]{1,0:T(8,128)(2,1)} %fusion.101.rest_0_), channel_id=1, source_target_pairs={{0,2},{2,4},{4,6},{6,0},{1,3},{3,5},{5,7},{7,1},{8,10},{10,12},{12... | collective-permute-start | bytes 1920008 | tf_op jit(solution)/shard_map/ppermute | solution.py:303
  782.3 65.3 %collective-permute-start.13 = (bf16[400,800]{1,0:T(8,128)(2,1)}, bf16[400,800]{1,0:T(8,128)(2,1)}, u32[]{:S(2)}, u32[]{:S(2)}) collective-permute-start(bf16[400,800]{1,0:T(8,128)(2,1)} %fusion.89.rest_1_), channel_id=1, source_target_pairs={{0,2},{2,4},{4,6},{6,0},{1,3},{3,5},{5,7},{7,1},{8,10},{10,12},{12... | collective-permute-start | bytes 1920008 | tf_op jit(solution)/shard_map/ppermute | solution.py:303
  786.7 67.9 %all-to-all-start.5 = ((bf16[8,256,200]{1,2,0:T(8,128)(2,1)}), bf16[8,256,200]{1,2,0:T(8,128)(2,1)}, u32[]{:S(2)}, u32[]{:S(2)}) async-start(bf16[8,256,200]{1,2,0:T(8,128)(2,1)} %bitcast.110), calls=%async_computation.5 | async-start | bytes 1638400 | tf_op jit(solution)/shard_map/all_to_all | solution.py:432
  812.9 53.8 %collective-permute-start.12 = (bf16[200,1600]{1,0:T(8,128)(2,1)}, bf16[200,1600]{1,0:T(8,128)(2,1)}, u32[]{:S(2)}, u32[]{:S(2)}) collective-permute-start(bf16[200,1600]{1,0:T(8,128)(2,1)} %fusion.100.rest_0_), channel_id=1, source_target_pairs={{0,2},{2,4},{4,6},{6,0},{1,3},{3,5},{5,7},{7,1},{8,10},{10,12},{12... | collective-permute-start | bytes 1920008 | tf_op jit(solution)/shard_map/ppermute | solution.py:303
  839.7 348.5 %collective-permute-start.22 = (bf16[128,1600]{0,1:T(8,128)(2,1)}, bf16[128,1600]{0,1:T(8,128)(2,1)}, u32[]{:S(2)}, u32[]{:S(2)}) collective-permute-start(bf16[128,1600]{0,1:T(8,128)(2,1)} %bitcast.106), channel_id=1, source_target_pairs={{4,16},{5,17},{6,24},{7,25},{12,18},{13,19},{14,26},{15,27},{20,20... | collective-permute-start | bytes 1228808 | tf_op jit(solution)/shard_map/ppermute | solution.py:98
  841.0 348.2 %collective-permute-start.11 = (bf16[128,1600]{0,1:T(8,128)(2,1)}, bf16[128,1600]{0,1:T(8,128)(2,1)}, u32[]{:S(2)}, u32[]{:S(2)}) collective-permute-start(bf16[128,1600]{0,1:T(8,128)(2,1)} %bitcast.106), channel_id=1, source_target_pairs={{0,16},{1,17},{2,24},{3,25},{8,18},{9,19},{10,26},{11,27},{16,20},... | collective-permute-start | bytes 1228808 | tf_op jit(solution)/shard_map/ppermute | solution.py:98
  850.2 74.9 %collective-permute-start.14 = (bf16[400,800]{1,0:T(8,128)(2,1)}, bf16[400,800]{1,0:T(8,128)(2,1)}, u32[]{:S(2)}, u32[]{:S(2)}) collective-permute-start(bf16[400,800]{1,0:T(8,128)(2,1)} %fusion.88.rest_1_), channel_id=1, source_target_pairs={{0,2},{2,4},{4,6},{6,0},{1,3},{3,5},{5,7},{7,1},{8,10},{10,12},{12... | collective-permute-start | bytes 1920008 | tf_op jit(solution)/shard_map/ppermute | solution.py:303
  866.3 62.9 %collective-permute-start.15 = (bf16[400,968]{1,0:T(8,128)(2,1)}, bf16[400,968]{1,0:T(8,128)(2,1)}, u32[]{:S(2)}, u32[]{:S(2)}) collective-permute-start(bf16[400,968]{1,0:T(8,128)(2,1)} %fusion.131.rest_2_), channel_id=1, source_target_pairs={{0,2},{2,4},{4,6},{6,0},{1,3},{3,5},{5,7},{7,1},{8,10},{10,12},{12... | collective-permute-start | bytes 2323208 | tf_op jit(solution)/shard_map/ppermute | solution.py:303
  920.9 43.3 %collective-permute-start.20 = (bf16[400,800]{1,0:T(8,128)(2,1)}, bf16[400,800]{1,0:T(8,128)(2,1)}, u32[]{:S(2)}, u32[]{:S(2)}) collective-permute-start(bf16[400,800]{1,0:T(8,128)(2,1)} %fusion.135.rest_2_), channel_id=1, source_target_pairs={{0,2},{2,4},{4,6},{6,0},{1,3},{3,5},{5,7},{7,1},{8,10},{10,12},{12... | collective-permute-start | bytes 1920008 | tf_op jit(solution)/shard_map/ppermute | solution.py:303
  925.1 43.3 %collective-permute-start.17 = (bf16[200,1600]{1,0:T(8,128)(2,1)}, bf16[200,1600]{1,0:T(8,128)(2,1)}, u32[]{:S(2)}, u32[]{:S(2)}) collective-permute-start(bf16[200,1600]{1,0:T(8,128)(2,1)} %fusion.138.rest_2_), channel_id=1, source_target_pairs={{0,2},{2,4},{4,6},{6,0},{1,3},{3,5},{5,7},{7,1},{8,10},{10,12},{12... | collective-permute-start | bytes 1920008 | tf_op jit(solution)/shard_map/ppermute | solution.py:303
  966.6 102.6 %collective-permute-start.27 = (bf16[400,800]{1,0:T(8,128)(2,1)}, bf16[400,800]{1,0:T(8,128)(2,1)}, u32[]{:S(2)}, u32[]{:S(2)}) collective-permute-start(bf16[400,800]{1,0:T(8,128)(2,1)} %fusion.86.rest_2_), channel_id=1, source_target_pairs={{0,2},{2,4},{4,6},{6,0},{1,3},{3,5},{5,7},{7,1},{8,10},{10,12},{12... | collective-permute-start | bytes 1920008 | tf_op jit(solution)/shard_map/ppermute | solution.py:303
  970.9 101.1 %collective-permute-start.19 = (bf16[200,1600]{1,0:T(8,128)(2,1)}, bf16[200,1600]{1,0:T(8,128)(2,1)}, u32[]{:S(2)}, u32[]{:S(2)}) collective-permute-start(bf16[200,1600]{1,0:T(8,128)(2,1)} %fusion.98.rest_1_), channel_id=1, source_target_pairs={{0,2},{2,4},{4,6},{6,0},{1,3},{3,5},{5,7},{7,1},{8,10},{10,12},{12... | collective-permute-start | bytes 1920008 | tf_op jit(solution)/shard_map/ppermute | solution.py:303
  975.1 114.5 %collective-permute-start.18 = (bf16[400,968]{1,0:T(8,128)(2,1)}, bf16[400,968]{1,0:T(8,128)(2,1)}, u32[]{:S(2)}, u32[]{:S(2)}) collective-permute-start(bf16[400,968]{1,0:T(8,128)(2,1)} %fusion.70.rest_0_), channel_id=1, source_target_pairs={{0,2},{2,4},{4,6},{6,0},{1,3},{3,5},{5,7},{7,1},{8,10},{10,12},{12... | collective-permute-start | bytes 2323208 | tf_op jit(solution)/shard_map/ppermute | solution.py:303
  1071.8 67.6 %collective-permute-start.28 = (bf16[400,800]{1,0:T(8,128)(2,1)}, bf16[400,800]{1,0:T(8,128)(2,1)}, u32[]{:S(2)}, u32[]{:S(2)}) collective-permute-start(bf16[400,800]{1,0:T(8,128)(2,1)} %fusion.85), channel_id=1, source_target_pairs={{0,2},{2,4},{4,6},{6,0},{1,3},{3,5},{5,7},{7,1},{8,10},{10,12},{12... | collective-permute-start | bytes 1920008 | tf_op jit(solution)/shard_map/ppermute | solution.py:303
  1074.4 58.0 %collective-permute-start.29 = (bf16[200,1600]{1,0:T(8,128)(2,1)}, bf16[200,1600]{1,0:T(8,128)(2,1)}, u32[]{:S(2)}, u32[]{:S(2)}) collective-permute-start(bf16[200,1600]{1,0:T(8,128)(2,1)} %fusion.97.rest_1_), channel_id=1, source_target_pairs={{0,2},{2,4},{4,6},{6,0},{1,3},{3,5},{5,7},{7,1},{8,10},{10,12},{12... | collective-permute-start | bytes 1920008 | tf_op jit(solution)/shard_map/ppermute | solution.py:303
  1179.8 47.6 %all-to-all-start.7 = ((bf16[8,100,968]{2,1,0:T(8,128)(2,1)}), bf16[8,100,968]{2,1,0:T(8,128)(2,1)}, u32[]{:S(2)}, u32[]{:S(2)}) async-start(bf16[8,100,968]{2,1,0:T(8,128)(2,1)} %reshape.661), calls=%async_computation.7 | async-start | bytes 3407872 | tf_op jit(solution)/shard_map/all_to_all | solution.py:523
  (162 other events, 2939.3 us)
Sparse Core Ops, SparseCore 0:
  44.9 65.9 all-gather.8
  113.0 93.4 all-gather.12
  208.6 60.0 all-gather.10
  270.1 54.1 all-gather.16
  326.3 57.6 all-gather.14
  386.0 56.8 all-gather.18

commit v4 on v3

v4 whole, which is shorter than its diff:
```python
import functools

import jax
import jax.numpy as jnp
from jax import lax
from jax.experimental import pallas as pl
from jax.experimental.pallas import tpu as pltpu
from jax.sharding import Mesh
from jax.sharding import PartitionSpec as P

HEADS = 25
EPSILON = 1e-05

SLAB = ("section", "dp", "r")
ALL = ("section", "dp", "z", "r")
MESH = pl.DeviceIdType.MESH


class Layout:
    def __init__(self, inputs, w_fc):
        self.micros, _, self.rows, self.width = inputs.shape
        self.sections = lax.axis_size("section")
        self.cores = lax.axis_size("dp")
        self.zs = lax.axis_size("z")
        self.rest = lax.axis_size("r")
        self.slab = self.sections * self.cores * self.rest
        self.shards = self.cores * self.zs * self.rest
        self.units = w_fc.shape[2]
        self.tokens = self.rows * self.slab
        self.seqs = self.cores
        self.head = self.width // HEADS
        self.slots = -(-HEADS // self.slab)
        self.block = self.width // self.shards
        self.unit_block = self.units // self.shards
        self.half = self.unit_block // self.sections
        self.cols = self.width // self.slab
        self.x = lax.axis_index("section")
        self.c = lax.axis_index("dp")
        self.z = lax.axis_index("z")
        self.r = lax.axis_index("r")
        self.t = (self.x * self.cores + self.c) * self.rest + self.r

    def number(self, x, c, z, r):
        return ((x * self.cores + c) * self.zs + z) * self.rest + r

    def order(self, a):
        lead = a.shape[:-1]
        a = a.reshape(*lead, self.cores, self.zs, self.rest * self.block)
        return jnp.swapaxes(a, -3, -2).reshape(*lead, self.width)

    def restore(self, a):
        lead = a.shape[:-1]
        a = a.reshape(*lead, self.zs, self.cores, self.rest * self.block)
        return jnp.swapaxes(a, -3, -2).reshape(*lead, self.width)

    def routes(self, micro):
        pairs = []
        for x in range(self.sections):
            for c in range(self.cores):
                for s in range(self.seqs):
                    for r in range(self.rest):
                        place = x * self.cores + c
                        pairs.append(((x, s, place, r), (x, c, micro * self.seqs + s, r)))
        return pairs

    def tokens_in(self, a):
        got = []
        for micro in range(self.micros):
            route = [(self.number(*f), self.number(*g)) for f, g in self.routes(micro)]
            got.append(lax.ppermute(a[micro, 0], ALL, route))
        out = got[0]
        for micro in range(1, self.micros):
            out = jnp.where(self.z // self.seqs == micro, got[micro], out)
        return out

    def tokens_out(self, parts):
        result = []
        for micro in range(self.micros):
            got = []
            for layer, part in enumerate(parts):
                route = [
                    (self.number(*g), self.number(layer, *f[1:])) for f, g in self.routes(micro)
                ]
                got.append(lax.ppermute(part, ALL, route))
            out = got[0]
            for layer in range(1, len(parts)):
                out = jnp.where(self.x == layer, got[layer], out)
            result.append(out)
        return jnp.stack(result)[None, :, None]


LOW = -1e30
BF = jnp.bfloat16
F32 = jnp.float32


class Peers:
    def __init__(self):
        self.sections, self.rest = lax.axis_size("section"), lax.axis_size("r")
        self.chips = self.sections * self.rest
        self.x, self.c, self.r = (lax.axis_index(a) for a in ("section", "dp", "r"))
        self.chip = self.x * self.rest + self.r

    def away(self, k, sign):
        x = lax.rem(self.x + self.sections + sign * (k // self.rest), self.sections)
        r = lax.rem(self.r + self.rest + sign * (k % self.rest), self.rest)
        return x, r

    def ahead(self, k):
        x, r = self.away(k, 1)
        return {"section": x, "dp": self.c, "r": r}

    def behind(self, k):
        x, r = self.away(k, -1)
        return {"section": x, "dp": self.c, "r": r}

    def sibling(self):
        return {"section": self.x, "dp": 1 - self.c, "r": self.r}

    def behind_chip(self, k):
        x, r = self.away(k, -1)
        return x * self.rest + r

    def greet(self, zs=1):
        barrier = pltpu.get_barrier_semaphore()
        z = lax.axis_index("z")
        for k in range(1, zs):
            pl.semaphore_signal(barrier, inc=1, device_id={"z": lax.rem(z + k, zs)}, device_id_type=MESH)
        for k in range(1, self.chips):
            pl.semaphore_signal(barrier, inc=1, device_id=self.ahead(k), device_id_type=MESH)
        pl.semaphore_signal(barrier, inc=1, device_id=self.sibling(), device_id_type=MESH)
        pl.semaphore_wait(barrier, self.chips + zs - 1)


def remote(src, dst, send, recv, device):
    return pltpu.make_async_remote_copy(
        src_ref=src, dst_ref=dst, send_sem=send, recv_sem=recv, device_id=device, device_id_type=MESH
    )


class Gather:
    def __init__(self, peers, full, sems):
        self.peers, self.full = peers, full
        self.chip_send, self.chip_recv, self.core_send, self.core_recv = sems
        self.sent = []

    def start(self, src):
        p = self.peers
        mine = self.full.at[p.chip, p.c]
        mine[...] = src[...]
        for k in range(1, p.chips):
            self.send(remote(mine, mine, self.chip_send.at[k], self.chip_recv.at[k], p.ahead(k)))
        self.send(remote(mine, mine, self.core_send.at[0], self.core_recv.at[0], p.sibling()))

    def send(self, copy):
        copy.start()
        self.sent.append(copy)

    def forward(self, k):
        p = self.peers
        block = self.full.at[p.behind_chip(k), p.c]
        remote(block, block, self.chip_send.at[k], self.chip_recv.at[k], p.sibling()).wait_recv()
        self.send(remote(block, block, self.core_send.at[k], self.core_recv.at[k], p.sibling()))

    def chip(self, k):
        p = self.peers
        block = self.full.at[p.behind_chip(k), 1 - p.c]
        remote(block, block, self.core_send.at[k], self.core_recv.at[k], p.sibling()).wait_recv()
        return p.behind_chip(k)

    def arrivals(self):
        yield 0, self.chip(0)
        chips = self.peers.chips
        for k in range(1, chips):
            for later in (1, 2) if k == 1 else (k + 1,):
                if later < chips:
                    self.forward(later)
            yield k, self.chip(k)

    def finish(self):
        for copy in self.sent:
            copy.wait_send()


class Reduce:
    def __init__(self, peers, mine, stage, other, going, coming, sems):
        self.peers = peers
        self.mine, self.stage, self.other, self.going, self.coming = mine, stage, other, going, coming
        self.chip_send, self.chip_recv, self.core_send, self.core_recv = sems
        self.sent = []

    def send(self, copy):
        copy.start()
        self.sent.append(copy)

    def put(self, k, both):
        p = self.peers
        rows = both.shape[0] // 2
        low, high = both[:rows], both[rows:]
        first = p.c == 0
        self.mine[k] = jnp.where(first, low, high)
        self.stage[k] = jnp.where(first, high, low).astype(BF)
        self.send(remote(self.stage.at[k], self.other.at[k], self.core_send.at[k], self.core_recv.at[k], p.sibling()))

    def arrived(self, k):
        p = self.peers
        remote(self.stage.at[k], self.other.at[k], self.core_send.at[k], self.core_recv.at[k], p.sibling()).wait_recv()
        return self.mine[k] + self.other[k].astype(F32)

    def push(self, k):
        p = self.peers
        if k:
            self.going[k - 1] = self.arrived(k).astype(BF)
            self.send(remote(self.going.at[k - 1], self.coming.at[k - 1], self.chip_send.at[k], self.chip_recv.at[k], p.behind(k)))

    def total(self):
        p = self.peers
        out = self.arrived(0)
        for k in range(1, p.chips):
            remote(self.going.at[k - 1], self.coming.at[k - 1], self.chip_send.at[k], self.chip_recv.at[k], p.sibling()).wait_recv()
            out = out + self.coming[k - 1].astype(F32)
        return out

    def finish(self):
        for copy in self.sent:
            copy.wait_send()


def gather_scratch(chips, rows, width):
    return [pltpu.VMEM((chips, 2, rows, width), BF)] + [pltpu.SemaphoreType.DMA((chips,))] * 4


def reduce_scratch(chips, rows, width):
    return [
        pltpu.VMEM((chips, rows, width), F32),
        pltpu.VMEM((chips, rows, width), BF),
        pltpu.VMEM((chips, rows, width), BF),
        pltpu.VMEM((chips - 1, rows, width), BF),
        pltpu.VMEM((chips - 1, rows, width), BF),
    ] + [pltpu.SemaphoreType.DMA((chips,))] * 4


def norm_parts(v):
    centred = v - jnp.mean(v, axis=-1, keepdims=True)
    spread = jnp.mean(centred * centred, axis=-1, keepdims=True)
    scale = lax.rsqrt(spread + EPSILON)
    return centred * scale, scale


def norm_back(v, gain, grad):
    unit, scale = norm_parts(v)
    scaled = grad * gain
    part = scaled - jnp.mean(scaled, axis=-1, keepdims=True)
    part = part - unit * jnp.mean(scaled * unit, axis=-1, keepdims=True)
    return part * scale, jnp.sum(grad * unit, axis=0, keepdims=True), jnp.sum(grad, axis=0, keepdims=True)


def dot(a, b, ca=1, cb=0):
    return lax.dot_general(a, b, (((ca,), (cb,)), ((), ())), preferred_element_type=F32)


def chip_rows(chip, rows):
    return pl.ds(pl.multiple_of(chip * (2 * rows), 2 * rows), 2 * rows)


def groups(span, head):
    wide = 128 if span % 128 == 0 else span
    for g in range(span // wide):
        yield slice(g * wide, (g + 1) * wide), [(g * wide // head + i, i * head) for i in range(wide // head)]


def only(a, start, head):
    lane = lax.broadcasted_iota(jnp.int32, a.shape, 1)
    return jnp.where((lane >= start) & (lane < start + head), a, jnp.zeros_like(a))


def attention_forward(head, ties, *refs):
    (src, h, w_qkv, w_out, bias, col, row, vec) = refs[:8]
    refs = refs[8 + ties :]
    (normed, qkv, attended, logs, mid, normed_two), refs = refs[:6], refs[6:]
    gather_refs, reduce_refs = refs[:5], refs[5:]
    rows, width = src.shape
    span = w_out.shape[0]
    peers = Peers()
    gather = Gather(peers, gather_refs[0], gather_refs[1:])
    reduce = Reduce(peers, *reduce_refs[:5], reduce_refs[5:9])
    kept_sem = reduce_refs[9]
    full = gather.full
    peers.greet()
    gather.start(src)
    for k, chip in gather.arrivals():
        part = dot(full[chip].reshape(2 * rows, width), w_qkv[...]) + bias[...]
        qkv[chip_rows(chip, rows), :] = part.astype(BF)
    kept = pltpu.make_async_copy(full, normed, kept_sem)
    kept.start()
    scale = head ** (-0.5)
    order = list(range(1, peers.chips)) + [0]
    before = None
    for k in order:
        chip = peers.behind_chip(k)
        here = chip_rows(chip, rows)
        block = jnp.where(col[...] <= row[:, here], 0.0, LOW).astype(F32)
        for lanes, heads in groups(span, head):
            q = qkv[here, lanes]
            keys = qkv[:, slice(span + lanes.start, span + lanes.stop)]
            values = qkv[:, slice(2 * span + lanes.start, 2 * span + lanes.stop)]
            merged = None
            for slot, start in heads:
                scores = dot(keys, only(q, start, head) * scale, 1, 1) + block
                top = jnp.max(scores, axis=0, keepdims=True)
                weights = jnp.exp(scores - top)
                total = jnp.sum(weights, axis=0, keepdims=True)
                logs[slot : slot + 1, here] = top + jnp.log(total)
                mixed = dot(values, weights.astype(BF), 0, 0) / total
                lane = lax.broadcasted_iota(jnp.int32, mixed.shape, 0)
                merged = mixed if merged is None else jnp.where(lane >= start, mixed, merged)
            attended[here, lanes] = merged.T.astype(BF)
        reduce.put(k, dot(attended[here, :], w_out[...]))
        if before is not None:
            reduce.push(before)
        before = k
    reduce.push(before)
    out = h[...].astype(F32) + (reduce.total() + vec[4:5, :])
    mid[...] = out
    normed_two[...] = (norm_parts(out)[0] * vec[1:2, :] + vec[3:4, :]).astype(BF)
    gather.finish()
    reduce.finish()
    kept.wait()


ROOT = 0.7978845608028654


def feed_forward(ties, *refs):
    (src, mid, w_fc, w_proj, bias, vec, next_vec) = refs[:7]
    refs = refs[7 + ties :]
    (normed_two, slope, activated, result, normed), refs = refs[:5], refs[5:]
    gather_refs, reduce_refs = refs[:5], refs[5:]
    rows, width = src.shape
    peers = Peers()
    gather = Gather(peers, gather_refs[0], gather_refs[1:])
    reduce = Reduce(peers, *reduce_refs[:5], reduce_refs[5:9])
    kept_sem = reduce_refs[9]
    full = gather.full
    peers.greet()
    gather.start(src)
    before = None
    for k, chip in gather.arrivals():
        here = chip_rows(chip, rows)
        u = dot(full[chip].reshape(2 * rows, width), w_fc[...]) + bias[...]
        bend = jnp.tanh(ROOT * (u + 0.044715 * (u * u * u)))
        slope[here, :] = (0.5 * (1.0 + bend) + 0.5 * u * (1.0 - bend * bend) * (ROOT * (1.0 + 3 * 0.044715 * (u * u)))).astype(BF)
        act = (0.5 * u * (1.0 + bend)).astype(BF)
        activated[here, :] = act
        reduce.put(k, dot(act, w_proj[...]))
        if before is not None:
            reduce.push(before)
        before = k
    kept = pltpu.make_async_copy(full, normed_two, kept_sem)
    kept.start()
    reduce.push(before)
    out = (mid[...] + (reduce.total() + vec[5:6, :])).astype(BF)
    result[...] = out
    normed[...] = (norm_parts(out.astype(F32))[0] * next_vec[0:1, :] + next_vec[2:3, :]).astype(BF)
    gather.finish()
    reduce.finish()
    kept.wait()


def chunks(size, step):
    return [(a, min(a + step, size)) for a in range(0, size, step)]


def feed_backward(ties, *refs):
    (src, mid, w_fc, w_proj, slope, activated, normed_two, vec) = refs[:8]
    refs = refs[8 + ties :]
    (grad_mid, attn_rows, grad_proj, grad_fc, sums, unit_sums), refs = refs[:6], refs[6:]
    gather_refs, reduce_refs = refs[:5], refs[5:]
    hidden, = reduce_refs[9:10]
    rows, width = src.shape
    tokens = slope.shape[0]
    peers = Peers()
    gather = Gather(peers, gather_refs[0], gather_refs[1:])
    reduce = Reduce(peers, *reduce_refs[:5], reduce_refs[5:9])
    full = gather.full
    peers.greet()
    gather.start(src)
    before = None
    for k, chip in gather.arrivals():
        here = chip_rows(chip, rows)
        back = dot(full[chip].reshape(2 * rows, width), w_proj[...], 1, 1) * slope[here, :].astype(F32)
        back = back.astype(BF)
        hidden[here, :] = back
        reduce.put(k, dot(back, w_fc[...], 1, 1))
        if before is not None:
            reduce.push(before)
        before = k
    reduce.push(before)
    branch = full[...].reshape(tokens, width)
    for a, b in chunks(activated.shape[1], 256):
        grad_proj[a:b, :] = dot(activated[:, a:b], branch, 0, 0).astype(BF)
    back = hidden[...]
    for a, b in chunks(width, 512):
        grad_fc[a:b, :] = dot(normed_two[:, a:b], back, 0, 0).astype(BF)
    unit_sums[...] = jnp.sum(back.astype(F32), axis=0, keepdims=True)
    own = src[...].astype(F32)
    part, gain, shift = norm_back(mid[...], vec[1:2, :], reduce.total())
    out = own + part
    grad_mid[...] = out
    low = out.astype(BF)
    attn_rows[...] = low
    sums[0:1, :] = gain
    sums[1:2, :] = shift
    sums[2:3, :] = jnp.sum(own, axis=0, keepdims=True)
    sums[3:4, :] = jnp.sum(low.astype(F32), axis=0, keepdims=True)
    sums[4:8, :] = jnp.zeros((4, width), F32)
    gather.finish()
    reduce.finish()


def attention_backward(head, ties, *refs):
    (src, grad_mid, h, w_qkv, w_out, qkv, attended, logs, normed, col, row, vec) = refs[:12]
    refs = refs[12 + ties :]
    (grad_in, grad_qkv, grad_out, sums, head_sums), refs = refs[:5], refs[5:]
    gather_refs, reduce_refs = refs[:5], refs[5:]
    joint, key_sum, value_sum = reduce_refs[9:12]
    rows, width = src.shape
    tokens, span = attended.shape
    scale = head ** (-0.5)
    peers = Peers()
    gather = Gather(peers, gather_refs[0], gather_refs[1:])
    reduce = Reduce(peers, *reduce_refs[:5], reduce_refs[5:9])
    full = gather.full
    peers.greet()
    gather.start(src)
    for k, chip in gather.arrivals():
        here = chip_rows(chip, rows)
        g_all = dot(full[chip].reshape(2 * rows, width), w_out[...], 1, 1).astype(BF)
        block = jnp.where(col[...] <= row[:, here], 0.0, LOW).astype(F32)
        for lanes, heads in groups(span, head):
            q = qkv[here, lanes]
            g = g_all[:, lanes]
            keys = qkv[:, slice(span + lanes.start, span + lanes.stop)]
            values = qkv[:, slice(2 * span + lanes.start, 2 * span + lanes.stop)]
            merged = None
            key_term, value_term = 0.0, 0.0
            for slot, start in heads:
                q_one, g_one = only(q, start, head) * scale, only(g, start, head)
                probs = jnp.exp(dot(keys, q_one, 1, 1) + block - logs[slot : slot + 1, here])
                g_probs = dot(values, g_one, 1, 1)
                both = probs * g_probs
                centre = jnp.sum(both, axis=0, keepdims=True)
                g_scores = (both - probs * centre).astype(BF)
                value_term += dot(probs.astype(BF), g_one)
                key_term += dot(g_scores, q_one)
                g_query = dot(keys, g_scores, 0, 0)
                lane = lax.broadcasted_iota(jnp.int32, g_query.shape, 0)
                merged = g_query if merged is None else jnp.where(lane >= start, g_query, merged)
            joint[here, lanes] = (merged.T * scale).astype(BF)
            if k == 0:
                key_sum[:, lanes] = key_term
                value_sum[:, lanes] = value_term
            else:
                key_sum[:, lanes] += key_term
                value_sum[:, lanes] += value_term
    joint[:, span : 2 * span] = key_sum[...].astype(BF)
    joint[:, 2 * span :] = value_sum[...].astype(BF)
    order = list(range(1, peers.chips)) + [0]
    before = None
    for k in order:
        reduce.put(k, dot(joint[chip_rows(peers.behind_chip(k), rows), :], w_qkv[...], 1, 1))
        if before is not None:
            reduce.push(before)
        before = k
    grads = joint[...]
    for a, b in chunks(width, 512):
        grad_qkv[a:b, :] = dot(normed[:, a:b], grads, 0, 0).astype(BF)
    grad_out[...] = dot(attended[...], full[...].reshape(tokens, width), 0, 0).astype(BF)
    head_sums[...] = jnp.sum(grads.astype(F32), axis=0, keepdims=True)
    part, gain, shift = norm_back(h[...].astype(F32), vec[0:1, :], reduce.total())
    grad_in[...] = (grad_mid[...] + part).astype(BF)
    sums[0:1, :] = gain
    sums[1:2, :] = shift
    sums[2:8, :] = jnp.zeros((6, width), F32)
    gather.finish()
    reduce.finish()


def call(kernel, name, outs, operands, ties, kept, scratch):
    chips = lax.axis_size("section") * lax.axis_size("r")
    rows, width = operands[0].shape
    vmem, hbm = pl.BlockSpec(memory_space=pltpu.VMEM), pl.BlockSpec(memory_space=pl.ANY)
    return pl.pallas_call(
        kernel,
        out_shape=[jax.ShapeDtypeStruct(*o) for o in outs],
        in_specs=[vmem] * len(operands) + [hbm] * len(ties),
        out_specs=[hbm if i in kept else vmem for i in range(len(outs))],
        scratch_shapes=gather_scratch(chips, rows, width) + reduce_scratch(chips, rows, width) + scratch,
        compiler_params=pltpu.CompilerParams(collective_id=name, has_side_effects=True, vmem_limit_bytes=60 * 2**20),
    )(*operands, *ties)


def run_attention_forward(name, head, ties, *operands):
    src, h, w_qkv, w_out, bias, col, row, vec = operands
    rows, width = src.shape
    tokens, span = col.shape[0], w_out.shape[0]
    slots = -(-(span // head) // 8) * 8
    chips = tokens // (2 * rows)
    outs = [
        ((chips, 2, rows, width), BF),
        ((tokens, 3 * span), BF),
        ((tokens, span), BF),
        ((slots, tokens), F32),
        ((rows, width), F32),
        ((rows, width), BF),
    ]
    return call(functools.partial(attention_forward, head, len(ties)), name, outs, operands, ties, (0,), [pltpu.SemaphoreType.DMA])


def run_feed_forward(name, ties, *operands):
    src, mid, w_fc, w_proj, bias, vec, next_vec = operands
    rows, width = src.shape
    units = w_fc.shape[1]
    chips = lax.axis_size("section") * lax.axis_size("r")
    tokens = 2 * chips * rows
    outs = [
        ((chips, 2, rows, width), BF),
        ((tokens, units), BF),
        ((tokens, units), BF),
        ((rows, width), BF),
        ((rows, width), BF),
    ]
    return call(functools.partial(feed_forward, len(ties)), name, outs, operands, ties, (0,), [pltpu.SemaphoreType.DMA])


def run_feed_backward(name, ties, *operands):
    src, mid, w_fc, w_proj, slope, activated, normed_two, vec = operands
    rows, width = src.shape
    tokens, units = slope.shape
    outs = [
        ((rows, width), F32),
        ((rows, width), BF),
        ((units, width), BF),
        ((width, units), BF),
        ((8, width), F32),
        ((1, units), F32),
    ]
    return call(functools.partial(feed_backward, len(ties)), name, outs, operands, ties, (), [pltpu.VMEM((tokens, units), BF)])


def run_attention_backward(name, head, ties, *operands):
    src, grad_mid, h, w_qkv, w_out, qkv, attended, logs, normed, col, row, vec = operands
    rows, width = src.shape
    tokens, span = attended.shape
    outs = [
        ((rows, width), BF),
        ((width, 3 * span), BF),
        ((span, width), BF),
        ((8, width), F32),
        ((1, 3 * span), F32),
    ]
    scratch = [pltpu.VMEM((tokens, 3 * span), BF), pltpu.VMEM((tokens, span), F32), pltpu.VMEM((tokens, span), F32)]
    return call(functools.partial(attention_backward, head, len(ties)), name, outs, operands, ties, (), scratch)


def tiny_kernel(src, out, stage, z_send, z_recv, *sems):
    peers = Peers()
    zs, z = lax.axis_size("z"), lax.axis_index("z")
    peers.greet(zs)
    sent = []
    for k in range(1, zs):
        copy = remote(src, stage.at[z], z_send.at[k], z_recv.at[k], {"z": lax.rem(z + k, zs)})
        copy.start()
        sent.append(copy)
    stage[z] = src[...]
    for k in range(1, zs):
        block = stage.at[lax.rem(z + zs - k, zs)]
        remote(block, block, z_send.at[k], z_recv.at[k], {"z": lax.rem(z + k, zs)}).wait_recv()
    gather = Gather(peers, out, sems)
    gather.start(stage)
    for _ in gather.arrivals():
        pass
    gather.finish()
    for copy in sent:
        copy.wait_send()


def tiny_gather(a, name):
    sections, rest, zs = (lax.axis_size(i) for i in ("section", "r", "z"))
    chips = sections * rest
    vmem = pl.BlockSpec(memory_space=pltpu.VMEM)
    out = pl.pallas_call(
        tiny_kernel,
        out_shape=jax.ShapeDtypeStruct((chips, 2, zs, *a.shape), a.dtype),
        in_specs=[vmem],
        out_specs=vmem,
        scratch_shapes=[pltpu.VMEM((zs, *a.shape), a.dtype)]
        + [pltpu.SemaphoreType.DMA((zs,))] * 2
        + [pltpu.SemaphoreType.DMA((chips,))] * 4,
        compiler_params=pltpu.CompilerParams(collective_id=name, has_side_effects=True),
    )(a)
    return out.reshape(sections, rest, 2, zs, *a.shape)


class Rings:
    def __init__(self, lay):
        self.lay = lay
        self.live = []

    def own(self, part, step):
        lay = self.lay
        block = lax.dynamic_index_in_dim(part, (lay.z - 1 - step) % lay.zs, 0, keepdims=False)
        return block.astype(jnp.float32)

    def add(self, term):
        zs = self.lay.zs
        part = term.reshape(zs, term.shape[0] // zs, term.shape[1])
        ring = [self.own(part, 0).astype(jnp.bfloat16), part, 0]
        self.live.append(ring)
        return ring

    def step(self):
        zs = self.lay.zs
        self.live = [ring for ring in self.live if ring[2] < zs - 1]
        route = [(i, (i + 1) % zs) for i in range(zs)]
        for ring in self.live:
            got = lax.ppermute(ring[0], "z", route).astype(jnp.float32)
            ring[2] += 1
            ring[0] = (got + self.own(ring[1], ring[2])).astype(jnp.bfloat16)

    def ties(self):
        now = [ring[0] for ring in self.live]
        self.step()
        return now

    def finish(self):
        while any(ring[2] < self.lay.zs - 1 for ring in self.live):
            self.step()


def spread_weights(lay, w_qkv, w_attn_out, w_fc, w_proj):
    n = lay.slab
    width, block = lay.width, lay.block
    slot_cols = lay.slots * lay.head
    qkv = w_qkv[0].reshape(block, 3, width)
    qkv = jnp.pad(qkv, ((0, 0), (0, 0), (0, n * slot_cols - width)))
    qkv = qkv.reshape(block, 3, n, slot_cols).transpose(2, 0, 1, 3).reshape(n, block, 3 * slot_cols)
    out = lay.order(w_attn_out[0]).reshape(block, n, lay.cols).transpose(1, 0, 2)
    fc = w_fc[0].reshape(block, lay.cores, lay.zs, lay.rest, lay.sections, lay.half)
    fc = fc.transpose(4, 1, 3, 0, 2, 5).reshape(n, block, lay.zs * lay.half)
    proj = lay.order(w_proj[0]).reshape(lay.sections, lay.half, width)

    def move(a):
        got = lax.all_to_all(a, SLAB, 0, 0, tiled=True)
        got = got.reshape(lay.sections, lay.cores * lay.rest * block, a.shape[2])
        return [got[layer] for layer in range(lay.sections)]

    first = move(jnp.concatenate([qkv, out], axis=2))
    fc = move(fc)
    proj = lax.all_to_all(proj, ("section",), 0, 0, tiled=True)
    params = []
    for layer in range(lay.sections):
        full = [
            lax.all_gather(a, "z", axis=0, tiled=True) for a in (first[layer], fc[layer], proj[layer])
        ]
        wo = full[0][:, 3 * slot_cols :]
        wo = wo.reshape(lay.zs, lay.cores, lay.rest * block, lay.cols)
        wo = jnp.swapaxes(wo, 0, 1).reshape(width, lay.cols)
        wo = jnp.pad(wo, ((0, n * slot_cols - width), (0, 0))).reshape(n, slot_cols, lay.cols)
        wo = lax.all_to_all(wo, SLAB, 0, 0, tiled=True)
        wo = wo.transpose(1, 0, 2).reshape(slot_cols, width)
        params.append((full[0][:, : 3 * slot_cols], wo, full[1], full[2]))
    return params


def on_device(
    inputs, cotangent, positions, w_qkv, w_attn_out, w_fc, w_proj, norm_gains, biases, fc_bias
):
    lay = Layout(inputs, w_fc)
    n, block, width = lay.slab, lay.block, lay.width
    span = lay.slots * lay.head
    micro = lay.z // lay.seqs

    params = spread_weights(lay, w_qkv, w_attn_out, w_fc, w_proj)

    per_row = lay.unit_block // block
    thin = jnp.concatenate([norm_gains[0], biases[0], fc_bias[0].reshape(block, per_row)], axis=1)
    thin = jnp.concatenate([thin.reshape(-1).astype(jnp.float32), positions.reshape(-1).astype(jnp.float32)])
    used, spots = block * (8 + per_row), positions.size
    thin = jnp.pad(thin, (0, -thin.size % 1024)).reshape(-1, 128)
    thin = tiny_gather(thin, 0).reshape(lay.sections, lay.rest, lay.cores, lay.zs, -1)
    places = thin[0, :, 0, :, used : used + spots].astype(jnp.int32)
    places = places.reshape(lay.rest, lay.sections, lay.cores, lay.micros, lay.rows)
    places = places.transpose(3, 1, 0, 2, 4).reshape(lay.micros, lay.tokens)
    places = lax.dynamic_slice_in_dim(places, micro, 1, 0)
    col, row = places.reshape(lay.tokens, 1), places
    thin = thin[..., :used].transpose(0, 2, 3, 1, 4).reshape(lay.sections, width, 8 + per_row)
    smalls = []
    for layer in range(lay.sections):
        vec = jnp.stack([thin[layer, :, i] for i in (0, 1, 2, 6, 5, 7)] + [thin[layer, :, 0]] * 2)
        vec = lay.order(vec)
        heads = [
            lax.dynamic_slice_in_dim(
                jnp.pad(thin[layer, :, 2 + i], (0, n * span - width)), lay.t * span, span
            )
            for i in (1, 2)
        ]
        bias = jnp.concatenate([heads[0], jnp.zeros_like(heads[0]), heads[1]])[None]
        unit = thin[layer, :, 8:].reshape(lay.cores, lay.zs, lay.rest, lay.sections, lay.half)
        unit = unit.transpose(3, 0, 2, 1, 4).reshape(n, lay.zs * lay.half)
        unit = lax.dynamic_slice_in_dim(unit, lay.t, 1, 0)
        smalls.append((vec, bias, unit))

    h = lay.order(lay.tokens_in(inputs))
    g = lay.order(lay.tokens_in(cotangent))

    vec = smalls[0][0]
    normed = (norm_parts(h.astype(F32))[0] * vec[0:1] + vec[2:3]).astype(BF)
    outs, keeps = [], []
    for layer in range(lay.sections):
        w_qkv, w_out, w_fc, w_proj = params[layer]
        vec, bias, unit = smalls[layer]
        full, qkv, attended, logs, mid, normed_two = run_attention_forward(
            1, lay.head, (), normed, h, w_qkv, w_out, bias, col, row, vec
        )
        next_vec = smalls[min(layer + 1, lay.sections - 1)][0]
        full_two, slope, activated, result, normed = run_feed_forward(
            2, (), normed_two, mid, w_fc, w_proj, unit, vec, next_vec
        )
        keeps.append((h, full, qkv, attended, logs, mid, full_two, slope, activated))
        h = result
        outs.append(h)

    grads, grad_rows, sums = [None] * lay.sections, [None] * lay.sections, [None] * lay.sections
    rings = Rings(lay)
    for layer in reversed(range(lay.sections)):
        w_qkv, w_out, w_fc, w_proj = params[layer]
        vec = smalls[layer][0]
        h, full, qkv, attended, logs, mid, full_two, slope, activated = keeps[layer]
        full, full_two = (a.reshape(lay.tokens, width) for a in (full, full_two))
        grad_mid, attn_rows, grad_proj, grad_fc, feed_sums, unit_sums = run_feed_backward(
            3 + 2 * layer, rings.ties(), g, mid, w_fc, w_proj, slope, activated, full_two, vec
        )
        grad_proj, grad_fc = rings.add(grad_proj), rings.add(grad_fc)
        g, grad_qkv, grad_out, attn_sums, head_sums = run_attention_backward(
            4 + 2 * layer, lay.head, rings.ties(), attn_rows, grad_mid, h, w_qkv, w_out, qkv, attended, logs, full, col, row, vec
        )
        wo = grad_out.reshape(span, n, lay.cols).transpose(1, 0, 2)
        wo = lax.all_to_all(wo, SLAB, 0, 0, tiled=True)
        wo = wo.reshape(n * span, lay.cols)[:width].reshape(lay.cores, lay.zs, lay.rest * block, lay.cols)
        wo = jnp.swapaxes(wo, 0, 1).reshape(width, lay.cols)
        first = rings.add(jnp.concatenate([grad_qkv, wo], axis=1))
        grads[layer] = (first, grad_fc, grad_proj)
        grad_rows[layer] = g
        sums[layer] = (feed_sums, unit_sums, attn_sums, head_sums)
    rings.finish()

    section_out = lay.tokens_out([lay.restore(a) for a in outs])
    section_grad = lay.tokens_out([lay.restore(a) for a in grad_rows])

    def back(i):
        both = jnp.stack([grads[layer][i][0] for layer in range(lay.sections)])
        return lax.all_to_all(both.reshape(n, block, both.shape[2]), SLAB, 0, 0, tiled=True)

    first = back(0)
    got = first[:, :, : 3 * span].reshape(n, block, 3, span).transpose(1, 2, 0, 3)
    out_qkv = got.reshape(block, 3, n * span)[:, :, :width].reshape(block, 3 * width).astype(jnp.float32)
    got = first[:, :, 3 * span :].transpose(1, 0, 2).reshape(block, width)
    out_attn = lay.restore(got).astype(jnp.float32)
    got = back(1).reshape(lay.sections, lay.cores, lay.rest, block, lay.zs, lay.half)
    out_fc = got.transpose(3, 1, 4, 2, 0, 5).reshape(block, lay.units).astype(jnp.float32)
    both = jnp.stack([grads[layer][2][0] for layer in range(lay.sections)])
    got = lax.all_to_all(both, ("section",), 0, 0, tiled=True)
    out_proj = lay.restore(got.reshape(lay.unit_block, width)).astype(jnp.float32)

    rows = []
    for layer in range(lay.sections):
        feed_sums, unit_sums, attn_sums, head_sums = sums[layer]
        feed_sums, attn_sums = lay.restore(feed_sums), lay.restore(attn_sums)
        zero = jnp.zeros((n * span,), jnp.float32)
        s_q = lax.dynamic_update_slice_in_dim(zero, head_sums[0, :span], lay.t * span, 0)[:width]
        s_v = lax.dynamic_update_slice_in_dim(zero, head_sums[0, 2 * span :], lay.t * span, 0)[:width]
        cols = [attn_sums[0], feed_sums[0], attn_sums[1], s_q, s_v, feed_sums[3], feed_sums[1], feed_sums[2]]
        cols = jnp.stack(cols, axis=1).reshape(lay.shards, block * 8)
        spots = jnp.zeros((n, lay.zs, lay.half), jnp.float32)
        spots = lax.dynamic_update_index_in_dim(
            spots, unit_sums.reshape(lay.zs, lay.half), lay.t, 0
        )
        spots = spots.reshape(lay.sections, lay.cores, lay.rest, lay.zs, lay.half)
        spots = spots.transpose(1, 3, 2, 0, 4).reshape(lay.shards, lay.unit_block)
        rows.append(jnp.concatenate([cols, spots], axis=1))
    rows = jnp.concatenate(rows, axis=0)
    rows = jnp.sum(lax.all_to_all(rows, ALL, 0, 0, tiled=True), axis=0)
    cols = rows[: block * 8].reshape(block, 8)
    return (
        section_out,
        section_grad,
        out_qkv[None],
        out_attn[None],
        out_fc[None],
        out_proj[None],
        cols[None, :, :2],
        cols[None, :, 2:],
        rows[None, block * 8 :],
    )


def solution(mesh):
    sections, cores, contexts = (mesh.shape[a] for a in ("section", "dp", "ctx"))
    zs = sections * cores
    shape = (sections, cores, zs, contexts // zs)
    inner = Mesh(mesh.devices.reshape(shape), ALL)
    tokens = P(None, "dp", ("z", "r"), None)
    rows = P("section", ("dp", "z", "r"), None)
    units = P("section", ("dp", "z", "r"))
    out_tokens = P("section", None, "dp", ("z", "r"), None)
    return jax.shard_map(
        on_device,
        mesh=inner,
        in_specs=(tokens, tokens, P(None, ("z", "r"))) + (rows,) * 6 + (units,),
        out_specs=(out_tokens, out_tokens) + (rows,) * 6 + (units,),
        check_vma=False,
    )
```

time: 1270 us -> 1120 us (0.88)
  matrix products: 214 us -> 0 us
  waiting for transfers between devices: 13.2 us -> 87.6 us
  Pallas kernels: 504 us -> 569 us
  other arithmetic: 109 us -> 57.4 us
  local copies, waits for them, and re-layouts: 219 us -> 177 us
  starting transfers between devices: 106 us -> 128 us
    dot_general x36 -> x0, matrix products: 214 us -> none  [the longest x24 140 us: dot(): lax.dot_general(a, b, (((ca,), (cb,)), ((), ())), preferred_element_type=...]
    pallas_call x17 -> x9, Pallas kernels: 504 us -> 569 us  [the longest x8 484 us: call(): pl.pallas_call(kernel, out_shape=[jax.ShapeDtypeStruct(*o) for o in outs]...]
    ppermute x18, waiting for transfers between devices: 12.9 us -> 69.5 us  [step(): got = lax.ppermute(ring[0], 'z', route).astype(jnp.float32)]
    convert_element_type x24 -> x2, local copies, waits for them, and re-layouts: 54.5 us -> 1.46 us  [the longest x1 1.44 us: on_device(): normed = (norm_parts(h.astype(F32))[0] * vec[0:1] + vec[2:3]).astype(BF)]
    ppermute x18, starting transfers between devices: 19.3 us -> 60.2 us  [step(): got = lax.ppermute(ring[0], 'z', route).astype(jnp.float32)]
    ppermute x8, starting transfers between devices: 40.5 us -> 18.9 us  [tokens_out(): got.append(lax.ppermute(part, ALL, route))]
    convert_element_type x11 -> x3, other arithmetic: 23.2 us -> 2.02 us  [the longest x2 1.95 us: on_device(): normed = (norm_parts(h.astype(F32))[0] * vec[0:1] + vec[2:3]).astype(BF)]
    reshape x4 -> x10, local copies, waits for them, and re-layouts: 3.06 us -> 20.8 us  [the longest x2 11.2 us: spread_weights(): wo = wo.transpose(1, 0, 2).reshape(slot_cols, width)]
  transfers between devices with their start and end apart: 44 -> 44, of which waited for: 3 -> 11; matrix products, arithmetic and copies ran while one was open for 40% -> 19% of each run, Pallas kernels for 40% -> 47%
where the time goes in v4:
time: 1120 us; the launch traced here: 1100 us
  Pallas kernels  569 us (51%)
  local copies, waits for them, and re-layouts  177 us (16%)
  starting transfers between devices  128 us (11%)
  waiting for transfers between devices  87.6 us (8%)
  blocking collectives  67 us (6%)
  other arithmetic  57.4 us (5%)
  between operations  15.8 us (1%)
    pallas_call x8, Pallas kernels, call(): pl.pallas_call(kernel, out_shape=[jax.ShapeDtypeStruct(*o) for o in outs]...  484 us
    pallas_call x1, Pallas kernels, tiny_gather(): pl.pallas_call(tiny_kernel, out_shape=jax.ShapeDtypeStruct((chips, 2, zs,...  84.6 us
    ppermute x18, waiting for transfers between devices, step(): got = lax.ppermute(ring[0], 'z', route).astype(jnp.float32)  69.5 us
    ppermute x18, starting transfers between devices, step(): got = lax.ppermute(ring[0], 'z', route).astype(jnp.float32)  60.2 us
    all_to_all x2, blocking collectives, move(): got = lax.all_to_all(a, SLAB, 0, 0, tiled=True)  48.1 us
    convert_element_type x12, other arithmetic, step(): ring[0] = (got + self.own(ring[1], ring[2])).astype(jnp.bfloat16)  25.8 us
  transfers between devices with their start and end apart: 44, of which 11 were waited for; matrix products, arithmetic and copies ran while one was open for 19% of the time, Pallas kernels for 47%

profile of v4, /device:TPU:3, one launch (start us, length us, event | category | flops | bytes accessed | tf_op | source)
XLA Modules:
  0.0 1101.6 jit_solution(1866478118614929602)
XLA Ops:
  15.6 25.0 %all_to_all.59 = bf16[8,100,968]{2,1,0:T(8,128)(2,1)S(1)} all-to-all(bf16[8,100,968]{2,1,0:T(8,128)(2,1)S(1)} %copy.325), channel_id=1, replica_groups=mesh['section'=2,'dp'=2,'z'=4,'r'=2] {'section','dp','r'}, dimensions={0} | all-to-all | bytes 3097600 | tf_op jit(solution)/shard_map/all_to_all | solution.py:654
  43.3 6.6 reshape_squeeze.25
  53.5 18.9 %all_to_all.60 = bf16[2,200,1600]{2,1,0:T(8,128)(2,1)S(1)} all-to-all(bf16[2,200,1600]{2,1,0:T(8,128)(2,1)S(1)} %reshape_reshape.13), channel_id=1, replica_groups=mesh['section'=2,'dp'=2,'z'=4,'r'=2] {'section'}, dimensions={0} | all-to-all | bytes 2560000 | tf_op jit(solution)/shard_map/all_to_all | solution.py:660
  81.6 23.2 %all_to_all.61 = bf16[8,100,800]{2,1,0:T(8,128)(2,1)S(1)} all-to-all(bf16[8,100,800]{2,1,0:T(8,128)(2,1)S(1)} %copy.335), channel_id=1, replica_groups=mesh['section'=2,'dp'=2,'z'=4,'r'=2] {'section','dp','r'}, dimensions={0} | all-to-all | bytes 2560000 | tf_op jit(solution)/shard_map/all_to_all | solution.py:654
  115.3 84.6 %shard_map.169 = f32[4,2,4,16,128]{4,3,2,1,0:T(8,128)} custom-call(f32[16,128]{1,0:T(8,128)} %fusion.45.src), custom_call_target="tpu_custom_call" | custom-call | tf_op jit(solution)/shard_map/pallas_call | solution.py:592
  201.7 6.5 slice_reduce_fusion.1
  233.5 6.3 all-to-all-done.1
  256.0 9.8 copy.341.refs_3_.refs_4_
  265.8 60.3 %shard_map.170 = (bf16[4,2,128,1600]{3,2,1,0:T(8,128)(2,1)}, bf16[1024,768]{1,0:T(8,128)(2,1)}, bf16[1024,256]{1,0:T(8,128)(2,1)}, f32[8,1024]{1,0:T(8,128)}, f3...) custom-call(bf16[128,1600]{1,0:T(8,128)(2,1)} %add_convert_fusion.refs_0_, bf16[128,1600]{1,0:T(8,128)(2,1)} %copy.331.refs_1_.refs_2_, ...), custom_call_target="tpu_custom_call" | custom-call | tf_op jit(solution)/shard_map/pallas_call | solution.py:493
  326.2 52.0 %shard_map.171 = (bf16[4,2,128,1600]{3,2,1,0:T(8,128)(2,1)}, bf16[1024,800]{1,0:T(8,128)(2,1)}, bf16[1024,800]{1,0:T(8,128)(2,1)}, bf16[128,1600]{1,0:T(8,128)(2,1)}, bf16[128,1600]{1,0:T(8,128)(2,1)}) custom-call(bf16[128,1600]{1,0:T(8,128)(2,1)} %get-tuple-element.52.refs_0_, f32[128,1600]{1,0:T(8,128)} %get-tuple-element.53.refs_1_, ...), custom_call_target="tpu_custom_call" | custom-call | tf_op jit(solution)/shard_map/pallas_call | solution.py:493
  379.5 61.1 %shard_map.172 = (bf16[4,2,128,1600]{3,2,1,0:T(8,128)(2,1)}, bf16[1024,768]{1,0:T(8,128)(2,1)}, bf16[1024,256]{1,0:T(8,128)(2,1)}, f32[8,1024]{1,0:T(8,128)}, f3...) custom-call(bf16[128,1600]{1,0:T(8,128)(2,1)} %get-tuple-element.54.refs_0_, ...), custom_call_target="tpu_custom_call" | custom-call | tf_op jit(solution)/shard_map/pallas_call | solution.py:493
  440.6 51.7 %shard_map.173 = (bf16[4,2,128,1600]{3,2,1,0:T(8,128)(2,1)}, bf16[1024,800]{1,0:T(8,128)(2,1)}, bf16[1024,800]{1,0:T(8,128)(2,1)}, bf16[128,1600]{1,0:T(8,128)(2,1)}, bf16[128,1600]{1,0:T(8,128)(2,1)}) custom-call(bf16[128,1600]{1,0:T(8,128)(2,1)} %get-tuple-element.56.refs_0_, f32[128,1600]{1,0:T(8,128)} %get-tuple-element.57.refs_1_, ...), custom_call_target="tpu_custom_call" | custom-call | tf_op jit(solution)/shard_map/pallas_call | solution.py:493
  498.7 63.6 %shard_map.174 = (f32[128,1600]{1,0:T(8,128)}, bf16[128,1600]{1,0:T(8,128)(2,1)}, bf16[800,1600]{1,0:T(8,128)(2,1)}, bf16[1600,800]{1,0:T(8,128)(2,1)}, f32[8,1600]{1,0:T(8,128)}, /*index=5*/f32[1,800]{1,0:T(1,128)}) custom-call(bf16[128,1600]{1,0:T(8,128)(2,1)} %copy.349.refs_0_, f32[128,1600]{1,0:T(8,128)} %get-tuple-element.57.refs_1_, ...), custom_call_target="tpu_custom_call" | custom-call | tf_op jit(solution)/shard_map/pallas_call | solution.py:493
  565.7 71.3 %shard_map.175 = (bf16[128,1600]{1,0:T(8,128)(2,1)}, bf16[1600,768]{1,0:T(8,128)(2,1)}, bf16[256,1600]{1,0:T(8,128)(2,1)}, f32[8,1600]{1,0:T(8,128)}, f32[1,768]{1,0:T(1,128)}) custom-call(bf16[128,1600]{1,0:T(8,128)(2,1)} %get-tuple-element.62.refs_0_, f32[128,1600]{1,0:T(8,128)} %get-tuple-element.63.refs_1_, ...), custom_call_target="tpu_custom_call" | custom-call | tf_op jit(solution)/shard_map/pallas_call | solution.py:493
  665.7 18.9 %collective-permute-start.12 = (bf16[400,800]{1,0:T(8,128)(2,1)}, bf16[400,800]{1,0:T(8,128)(2,1)}, u32[]{:S(2)}, u32[]{:S(2)}) collective-permute-start(bf16[400,800]{1,0:T(8,128)(2,1)} %fusion.11.refs_9_), channel_id=1, source_target_pairs={{0,2},{2,4},{4,6},{6,0},{1,3},{3,5},{5,7},{7,1},{8,10},{10,12},{12... | collective-permute-start | bytes 1920008 | tf_op jit(solution)/shard_map/ppermute | solution.py:627
  692.1 62.0 %shard_map.176 = (f32[128,1600]{1,0:T(8,128)}, bf16[128,1600]{1,0:T(8,128)(2,1)}, bf16[800,1600]{1,0:T(8,128)(2,1)}, bf16[1600,800]{1,0:T(8,128)(2,1)}, f32[8,1600]{1,0:T(8,128)}, /*index=5*/f32[1,800]{1,0:T(1,128)}) custom-call(bf16[128,1600]{1,0:T(8,128)(2,1)} %get-tuple-element.70.refs_0_, f32[128,1600]{1,0:T(8,128)} %get-tuple-element.53.refs_1_, ...), custom_call_target="tpu_custom_call" | custom-call | tf_op jit(solution)/shard_map/pallas_call | solution.py:493
  761.0 6.1 collective-permute-start.26
  774.0 62.1 %shard_map.177 = (bf16[128,1600]{1,0:T(8,128)(2,1)}, bf16[1600,768]{1,0:T(8,128)(2,1)}, bf16[256,1600]{1,0:T(8,128)(2,1)}, f32[8,1600]{1,0:T(8,128)}, f32[1,768]{1,0:T(1,128)}) custom-call(bf16[128,1600]{1,0:T(8,128)(2,1)} %get-tuple-element.76.refs_0_, f32[128,1600]{1,0:T(8,128)} %get-tuple-element.77.refs_1_, bf16[128,1600]{1,0:T(8,128)(2,1)} %copy.331.refs_1_.refs_2_, ...), custom_call_target="tpu_custom_call" | custom-call | tf_op jit(solution)/shard_map/pallas_call | solution.py:493
  843.0 11.1 %all-to-all-start.10 = ((f32[32,1,1200]{2,1,0:T(1,128)}), f32[32,1,1200]{2,1,0:T(1,128)S(1)}, u32[]{:S(2)}, u32[]{:S(2)}) async-start(f32[32,1,1200]{2,1,0:T(1,128)} %copy.380), calls=%async_computation.10 | async-start | bytes 327680 | tf_op jit(solution)/shard_map/all_to_all | solution.py:793
  867.1 5.2 all-to-all-start.6
  896.7 9.1 collective-permute-done.23
  908.2 15.2 %collective-permute-done.20 = bf16[400,968]{1,0:T(8,128)(2,1)} collective-permute-done((bf16[400,968]{1,0:T(8,128)(2,1)}, bf16[400,968]{1,0:T(8,128)(2,1)}, u32[]{:S(2)}, u32[]{:S(2)}) %collective-permute-start.20) | collective-permute-done | bytes 774432 | tf_op jit(solution)/shard_map/ppermute | solution.py:627
  929.7 11.0 %collective-permute-done.17 = bf16[400,968]{1,0:T(8,128)(2,1)S(1)} collective-permute-done((bf16[400,968]{1,0:T(8,128)(2,1)S(1)}, bf16[400,968]{1,0:T(8,128)(2,1)S(1)}, u32[]{:S(2)}, u32[]{:S(2)}) %collective-permute-start.17) | collective-permute-done | bytes 774432 | tf_op jit(solution)/shard_map/ppermute | solution.py:627
  942.0 13.1 %collective-permute-done.28 = bf16[200,1600]{1,0:T(8,128)(2,1)S(1)} collective-permute-done((bf16[200,1600]{1,0:T(8,128)(2,1)S(1)}, bf16[200,1600]{1,0:T(8,128)(2,1)S(1)}, u32[]{:S(2)}, u32[]{:S(2)}) %collective-permute-start.28) | collective-permute-done | bytes 640032 | tf_op jit(solution)/shard_map/ppermute | solution.py:627
  955.0 7.1 collective-permute-start.18
  968.1 7.5 collective-permute-done.24
  975.5 11.1 %collective-permute-start.21 = (bf16[400,968]{1,0:T(8,128)(2,1)}, bf16[400,968]{1,0:T(8,128)(2,1)}, u32[]{:S(2)}, u32[]{:S(2)}) collective-permute-start(bf16[400,968]{1,0:T(8,128)(2,1)} %fusion.1), channel_id=1, source_target_pairs={{0,2},{2,4},{4,6},{6,0},{1,3},{3,5},{5,7},{7,1},{8,10},{10,12},{12... | collective-permute-start | bytes 2323208 | tf_op jit(solution)/shard_map/ppermute | solution.py:627
  995.6 11.1 %collective-permute-start.19 = (bf16[400,968]{1,0:T(8,128)(2,1)}, bf16[400,968]{1,0:T(8,128)(2,1)}, u32[]{:S(2)}, u32[]{:S(2)}) collective-permute-start(bf16[400,968]{1,0:T(8,128)(2,1)} %fusion.3), channel_id=1, source_target_pairs={{0,2},{2,4},{4,6},{6,0},{1,3},{3,5},{5,7},{7,1},{8,10},{10,12},{12... | collective-permute-start | bytes 2323208 | tf_op jit(solution)/shard_map/ppermute | solution.py:627
  1019.6 8.7 collective-permute-done.19
  1033.8 5.4 all-to-all-start.7
  1042.4 8.1 reshape.503
  1070.1 9.4 reshape.506
  (388 shorter events, 262.8 us)
Async XLA Ops:
  7.2 213.0 %all-gather.9.cloned.1.call-start = ((), (), s32[]{:S(2)}) async-start(), calls=%async_computation.11 | async-start | bytes 4096000 | tf_op jit(solution)/shard_map/all_gather | solution.py:664
  42.0 187.6 %all-gather.13.cloned.1.call-start = ((), (), s32[]{:S(2)}) async-start(), calls=%async_computation.13 | async-start | bytes 4096000 | tf_op jit(solution)/shard_map/all_gather | solution.py:664
  43.3 282.9 %all-gather.17.cloned.1.call-start = ((), (), s32[]{:S(2)}) async-start(), calls=%async_computation.15 | async-start | bytes 3328000 | tf_op jit(solution)/shard_map/all_gather | solution.py:664
  73.6 252.6 %all-gather.11.cloned.1.call-start = ((), (), s32[]{:S(2)}) async-start(), calls=%async_computation.12 | async-start | bytes 3584000 | tf_op jit(solution)/shard_map/all_gather | solution.py:664
  106.0 334.6 %all-gather.19.cloned.1.call-start = ((), (), s32[]{:S(2)}) async-start(), calls=%async_computation.16 | async-start | bytes 3328000 | tf_op jit(solution)/shard_map/all_gather | solution.py:664
  106.7 333.9 %all-gather.15.cloned.1.call-start = ((), (), s32[]{:S(2)}) async-start(), calls=%async_computation.14 | async-start | bytes 3584000 | tf_op jit(solution)/shard_map/all_gather | solution.py:664
  107.7 110.5 %collective-permute-start = (bf16[128,1600]{0,1:T(8,128)(2,1)}, bf16[128,1600]{0,1:T(8,128)(2,1)}, u32[]{:S(2)}, u32[]{:S(2)}) collective-permute-start(bf16[128,1600]{0,1:T(8,128)(2,1)} %get-tuple-element.167), channel_id=1, source_target_pairs={{0,4},{1,5},{8,6},{9,7},{2,12},{3,13},{10,14},{11,15},{20,20},{21,... | collective-permute-start | bytes 1228808 | tf_op jit(solution)/shard_map/ppermute | solution.py:70
  109.1 109.1 %collective-permute-start.1 = (bf16[128,1600]{0,1:T(8,128)(2,1)}, bf16[128,1600]{0,1:T(8,128)(2,1)}, u32[]{:S(2)}, u32[]{:S(2)}) collective-permute-start(bf16[128,1600]{0,1:T(8,128)(2,1)} %get-tuple-element.166), channel_id=1, source_target_pairs={{0,0},{1,1},{8,2},{9,3},{2,8},{3,9},{10,10},{11,11},{20,16},{21,17... | collective-permute-start | bytes 1228808 | tf_op jit(solution)/shard_map/ppermute | solution.py:70
  111.3 106.9 %collective-permute-start.6 = (bf16[128,1600]{0,1:T(8,128)(2,1)}, bf16[128,1600]{0,1:T(8,128)(2,1)}, u32[]{:S(2)}, u32[]{:S(2)}) collective-permute-start(bf16[128,1600]{0,1:T(8,128)(2,1)} %get-tuple-element.165), channel_id=1, source_target_pairs={{0,4},{1,5},{8,6},{9,7},{2,12},{3,13},{10,14},{11,15},{20,20},{21,... | collective-permute-start | bytes 1228808 | tf_op jit(solution)/shard_map/ppermute | solution.py:70
  112.7 105.5 %collective-permute-start.7 = (bf16[128,1600]{0,1:T(8,128)(2,1)}, bf16[128,1600]{0,1:T(8,128)(2,1)}, u32[]{:S(2)}, u32[]{:S(2)}) collective-permute-start(bf16[128,1600]{0,1:T(8,128)(2,1)} %get-tuple-element.164), channel_id=1, source_target_pairs={{0,0},{1,1},{8,2},{9,3},{2,8},{3,9},{10,10},{11,11},{20,16},{21,17... | collective-permute-start | bytes 1228808 | tf_op jit(solution)/shard_map/ppermute | solution.py:70
  494.4 158.2 %collective-permute-start.2 = (bf16[128,1600]{0,1:T(8,128)(2,1)}, bf16[128,1600]{0,1:T(8,128)(2,1)}, u32[]{:S(2)}, u32[]{:S(2)}) collective-permute-start(bf16[128,1600]{0,1:T(8,128)(2,1)} %bitcast.37), channel_id=1, source_target_pairs={{0,16},{1,17},{2,24},{3,25},{8,18},{9,19},{10,26},{11,27},{16,20},... | collective-permute-start | bytes 1228808 | tf_op jit(solution)/shard_map/ppermute | solution.py:84
  497.4 162.7 %collective-permute-start.4 = (bf16[128,1600]{0,1:T(8,128)(2,1)}, bf16[128,1600]{0,1:T(8,128)(2,1)}, u32[]{:S(2)}, u32[]{:S(2)}) collective-permute-start(bf16[128,1600]{0,1:T(8,128)(2,1)} %bitcast.37), channel_id=1, source_target_pairs={{4,16},{5,17},{6,24},{7,25},{12,18},{13,19},{14,26},{15,27},{20,20... | collective-permute-start | bytes 1228808 | tf_op jit(solution)/shard_map/ppermute | solution.py:84
  564.9 98.5 %collective-permute-start.10 = (bf16[400,800]{1,0:T(8,128)(2,1)S(1)}, bf16[400,800]{1,0:T(8,128)(2,1)}, u32[]{:S(2)}, u32[]{:S(2)}) collective-permute-start(bf16[400,800]{1,0:T(8,128)(2,1)S(1)} %dynamic-slice_bitcast_fusion.1.refs_13_), channel_id=1, source_target_pairs={{0,2},{2,4},{4,6},{6,0},{1,3},{3,5},{5,7},{7,1},{8,10},{10,12},{12... | collective-permute-start | bytes 1920008 | tf_op jit(solution)/shard_map/ppermute | solution.py:627
  565.5 119.2 %collective-permute-start.9 = (bf16[200,1600]{1,0:T(8,128)(2,1)S(1)}, bf16[200,1600]{1,0:T(8,128)(2,1)}, u32[]{:S(2)}, u32[]{:S(2)}) collective-permute-start(bf16[200,1600]{1,0:T(8,128)(2,1)S(1)} %dynamic-slice_bitcast_fusion.3.refs_12_), channel_id=1, source_target_pairs={{0,2},{2,4},{4,6},{6,0},{1,3},{3,5},{5,7},{7,1},{8,10},{10,12},{12... | collective-permute-start | bytes 1920008 | tf_op jit(solution)/shard_map/ppermute | solution.py:627
  639.2 47.8 %all-to-all-start.5 = ((bf16[8,256,200]{1,2,0:T(8,128)(2,1)}), bf16[8,256,200]{1,2,0:T(8,128)(2,1)S(1)}, u32[]{:S(2)}, u32[]{:S(2)}) async-start(bf16[8,256,200]{1,2,0:T(8,128)(2,1)} %bitcast.64), calls=%async_computation.5 | async-start | bytes 1638400 | tf_op jit(solution)/shard_map/all_to_all | solution.py:749
  657.1 382.2 %collective-permute-start.8 = (bf16[128,1600]{0,1:T(8,128)(2,1)}, bf16[128,1600]{0,1:T(8,128)(2,1)}, u32[]{:S(2)}, u32[]{:S(2)}) collective-permute-start(bf16[128,1600]{0,1:T(8,128)(2,1)} %bitcast.58), channel_id=1, source_target_pairs={{0,16},{1,17},{2,24},{3,25},{8,18},{9,19},{10,26},{11,27},{16,20},... | collective-permute-start | bytes 1228808 | tf_op jit(solution)/shard_map/ppermute | solution.py:84
  660.0 380.3 %collective-permute-start.15 = (bf16[128,1600]{0,1:T(8,128)(2,1)}, bf16[128,1600]{0,1:T(8,128)(2,1)}, u32[]{:S(2)}, u32[]{:S(2)}) collective-permute-start(bf16[128,1600]{0,1:T(8,128)(2,1)} %bitcast.58), channel_id=1, source_target_pairs={{4,16},{5,17},{6,24},{7,25},{12,18},{13,19},{14,26},{15,27},{20,20... | collective-permute-start | bytes 1228808 | tf_op jit(solution)/shard_map/ppermute | solution.py:84
  665.7 95.3 %collective-permute-start.12 = (bf16[400,800]{1,0:T(8,128)(2,1)}, bf16[400,800]{1,0:T(8,128)(2,1)}, u32[]{:S(2)}, u32[]{:S(2)}) collective-permute-start(bf16[400,800]{1,0:T(8,128)(2,1)} %fusion.11.refs_9_), channel_id=1, source_target_pairs={{0,2},{2,4},{4,6},{6,0},{1,3},{3,5},{5,7},{7,1},{8,10},{10,12},{12... | collective-permute-start | bytes 1920008 | tf_op jit(solution)/shard_map/ppermute | solution.py:627
  687.0 82.5 %collective-permute-start.11 = (bf16[200,1600]{1,0:T(8,128)(2,1)}, bf16[200,1600]{1,0:T(8,128)(2,1)}, u32[]{:S(2)}, u32[]{:S(2)}) collective-permute-start(bf16[200,1600]{1,0:T(8,128)(2,1)} %fusion.17.refs_8_), channel_id=1, source_target_pairs={{0,2},{2,4},{4,6},{6,0},{1,3},{3,5},{5,7},{7,1},{8,10},{10,12},{12... | collective-permute-start | bytes 1920008 | tf_op jit(solution)/shard_map/ppermute | solution.py:627
  691.9 79.8 %collective-permute-start.13 = (bf16[400,968]{1,0:T(8,128)(2,1)}, bf16[400,968]{1,0:T(8,128)(2,1)}, u32[]{:S(2)}, u32[]{:S(2)}) collective-permute-start(bf16[400,968]{1,0:T(8,128)(2,1)} %fusion.33.refs_10_), channel_id=1, source_target_pairs={{0,2},{2,4},{4,6},{6,0},{1,3},{3,5},{5,7},{7,1},{8,10},{10,12},{12... | collective-permute-start | bytes 2323208 | tf_op jit(solution)/shard_map/ppermute | solution.py:627
  761.0 93.2 %collective-permute-start.26 = (bf16[200,1600]{1,0:T(8,128)(2,1)}, bf16[200,1600]{1,0:T(8,128)(2,1)}, u32[]{:S(2)}, u32[]{:S(2)}) collective-permute-start(bf16[200,1600]{1,0:T(8,128)(2,1)} %dynamic-slice_bitcast_fusion.2.refs_15_), channel_id=1, source_target_pairs={{0,2},{2,4},{4,6},{6,0},{1,3},{3,5},{5,7},{7,1},{8,10},{10,12},{12... | collective-permute-start | bytes 1920008 | tf_op jit(solution)/shard_map/ppermute | solution.py:627
  769.4 88.3 %collective-permute-start.22 = (bf16[400,800]{1,0:T(8,128)(2,1)}, bf16[400,800]{1,0:T(8,128)(2,1)}, u32[]{:S(2)}, u32[]{:S(2)}) collective-permute-start(bf16[400,800]{1,0:T(8,128)(2,1)} %dynamic-slice_bitcast_fusion.refs_16_), channel_id=1, source_target_pairs={{0,2},{2,4},{4,6},{6,0},{1,3},{3,5},{5,7},{7,1},{8,10},{10,12},{12... | collective-permute-start | bytes 1920008 | tf_op jit(solution)/shard_map/ppermute | solution.py:627
  771.7 101.5 %collective-permute-start.29 = (bf16[200,1600]{1,0:T(8,128)(2,1)}, bf16[200,1600]{1,0:T(8,128)(2,1)}, u32[]{:S(2)}, u32[]{:S(2)}) collective-permute-start(bf16[200,1600]{1,0:T(8,128)(2,1)} %fusion.16.refs_12_), channel_id=1, source_target_pairs={{0,2},{2,4},{4,6},{6,0},{1,3},{3,5},{5,7},{7,1},{8,10},{10,12},{12... | collective-permute-start | bytes 1920008 | tf_op jit(solution)/shard_map/ppermute | solution.py:627
  857.7 36.5 %collective-permute-start.27 = (bf16[200,1600]{1,0:T(8,128)(2,1)}, bf16[200,1600]{1,0:T(8,128)(2,1)}, u32[]{:S(2)}, u32[]{:S(2)}) collective-permute-start(bf16[200,1600]{1,0:T(8,128)(2,1)} %fusion.15), channel_id=1, source_target_pairs={{0,2},{2,4},{4,6},{6,0},{1,3},{3,5},{5,7},{7,1},{8,10},{10,12},{12... | collective-permute-start | bytes 1920008 | tf_op jit(solution)/shard_map/ppermute | solution.py:627
  876.8 46.5 %collective-permute-start.20 = (bf16[400,968]{1,0:T(8,128)(2,1)}, bf16[400,968]{1,0:T(8,128)(2,1)}, u32[]{:S(2)}, u32[]{:S(2)}) collective-permute-start(bf16[400,968]{1,0:T(8,128)(2,1)} %fusion.5.refs_14_), channel_id=1, source_target_pairs={{0,2},{2,4},{4,6},{6,0},{1,3},{3,5},{5,7},{7,1},{8,10},{10,12},{12... | collective-permute-start | bytes 2323208 | tf_op jit(solution)/shard_map/ppermute | solution.py:627
  894.2 46.6 %collective-permute-start.17 = (bf16[400,968]{1,0:T(8,128)(2,1)S(1)}, bf16[400,968]{1,0:T(8,128)(2,1)S(1)}, u32[]{:S(2)}, u32[]{:S(2)}) collective-permute-start(bf16[400,968]{1,0:T(8,128)(2,1)S(1)} %fusion.25), channel_id=1, source_target_pairs={{0,2},{2,4},{4,6},{6,0},{1,3},{3,5},{5,7},{7,1},{8,10},{10,12},{12... | collective-permute-start | bytes 2323208 | tf_op jit(solution)/shard_map/ppermute | solution.py:627
  905.8 49.3 %collective-permute-start.28 = (bf16[200,1600]{1,0:T(8,128)(2,1)S(1)}, bf16[200,1600]{1,0:T(8,128)(2,1)S(1)}, u32[]{:S(2)}, u32[]{:S(2)}) collective-permute-start(bf16[200,1600]{1,0:T(8,128)(2,1)S(1)} %fusion.14), channel_id=1, source_target_pairs={{0,2},{2,4},{4,6},{6,0},{1,3},{3,5},{5,7},{7,1},{8,10},{10,12},{12... | collective-permute-start | bytes 1920008 | tf_op jit(solution)/shard_map/ppermute | solution.py:627
  923.3 115.9 %collective-permute-start.14 = (bf16[128,1600]{0,1:T(8,128)(2,1)}, bf16[128,1600]{0,1:T(8,128)(2,1)}, u32[]{:S(2)}, u32[]{:S(2)}) collective-permute-start(bf16[128,1600]{0,1:T(8,128)(2,1)} %bitcast.78), channel_id=1, source_target_pairs={{0,0},{1,1},{2,8},{3,9},{8,2},{9,3},{10,10},{11,11},{16,4},{17,5},... | collective-permute-start | bytes 1228808 | tf_op jit(solution)/shard_map/ppermute | solution.py:84
  955.0 38.1 %collective-permute-start.18 = (bf16[400,968]{1,0:T(8,128)(2,1)}, bf16[400,968]{1,0:T(8,128)(2,1)}, u32[]{:S(2)}, u32[]{:S(2)}) collective-permute-start(bf16[400,968]{1,0:T(8,128)(2,1)} %fusion.4), channel_id=1, source_target_pairs={{0,2},{2,4},{4,6},{6,0},{1,3},{3,5},{5,7},{7,1},{8,10},{10,12},{12... | collective-permute-start | bytes 2323208 | tf_op jit(solution)/shard_map/ppermute | solution.py:627
  963.5 46.9 %all-to-all-start.9 = ((bf16[2,200,1600]{2,1,0:T(8,128)(2,1)}), bf16[2,200,1600]{2,1,0:T(8,128)(2,1)}, u32[]{:S(2)}, u32[]{:S(2)}) async-start(bf16[2,200,1600]{2,1,0:T(8,128)(2,1)} %pad_maximum_fusion.3), calls=%async_computation.9 | async-start | bytes 2662400 | tf_op jit(solution)/shard_map/all_to_all | solution.py:773
  975.5 41.0 %collective-permute-start.21 = (bf16[400,968]{1,0:T(8,128)(2,1)}, bf16[400,968]{1,0:T(8,128)(2,1)}, u32[]{:S(2)}, u32[]{:S(2)}) collective-permute-start(bf16[400,968]{1,0:T(8,128)(2,1)} %fusion.1), channel_id=1, source_target_pairs={{0,2},{2,4},{4,6},{6,0},{1,3},{3,5},{5,7},{7,1},{8,10},{10,12},{12... | collective-permute-start | bytes 2323208 | tf_op jit(solution)/shard_map/ppermute | solution.py:627
  1033.8 45.7 %all-to-all-start.7 = ((bf16[8,100,968]{2,1,0:T(8,128)(2,1)}), bf16[8,100,968]{2,1,0:T(8,128)(2,1)}, u32[]{:S(2)}, u32[]{:S(2)}) async-start(bf16[8,100,968]{2,1,0:T(8,128)(2,1)} %reshape.463), calls=%async_computation.7 | async-start | bytes 3407872 | tf_op jit(solution)/shard_map/all_to_all | solution.py:763
  (40 other events, 488.3 us)
Sparse Core Ops, SparseCore 0:
  42.1 65.9 all-gather.8
  110.2 94.4 all-gather.12
  206.2 52.6 all-gather.16
  260.3 57.6 all-gather.10
  320.0 54.1 all-gather.18
  375.7 57.6 all-gather.14

commit v5 on v4

--- a/solution.py
+++ b/solution.py
@@ -121,15 +121,26 @@
         x, r = self.away(k, -1)
         return x * self.rest + r
 
+    def other(self, dx, dc, dr):
+        x = lax.rem(self.x + self.sections + dx, self.sections)
+        c = lax.rem(self.c + 2 + dc, 2)
+        r = lax.rem(self.r + self.rest + dr, self.rest)
+        return {"section": x, "dp": c, "r": r}, (x * 2 + c) * self.rest + r
+
+    def offsets(self):
+        every = [(x, c, r) for x in range(self.sections) for c in range(2) for r in range(self.rest)]
+        return list(enumerate(every))[1:]
+
     def greet(self, zs=1):
         barrier = pltpu.get_barrier_semaphore()
         z = lax.axis_index("z")
+        size = lax.axis_size("z")
         for k in range(1, zs):
-            pl.semaphore_signal(barrier, inc=1, device_id={"z": lax.rem(z + k, zs)}, device_id_type=MESH)
-        for k in range(1, self.chips):
-            pl.semaphore_signal(barrier, inc=1, device_id=self.ahead(k), device_id_type=MESH)
-        pl.semaphore_signal(barrier, inc=1, device_id=self.sibling(), device_id_type=MESH)
-        pl.semaphore_wait(barrier, self.chips + zs - 1)
+            pl.semaphore_signal(barrier, inc=1, device_id={"z": lax.rem(z + size - k, size)}, device_id_type=MESH)
+        others = self.offsets()
+        for _, place in others:
+            pl.semaphore_signal(barrier, inc=1, device_id=self.other(*place)[0], device_id_type=MESH)
+        pl.semaphore_wait(barrier, len(others) + zs - 1)
 
 
 def remote(src, dst, send, recv, device):
@@ -226,6 +237,205 @@
             copy.wait_send()
 
 
+class RingGather:
+    def __init__(self, pairs, local, send, recv):
+        self.pairs, self.local, self.send_sem, self.recv_sem = pairs, local, send, recv
+        self.zs, self.z = lax.axis_size("z"), lax.axis_index("z")
+        self.steps = [(p, s) for s in range(self.zs - 1) for p in range(len(pairs))]
+        self.sent = []
+
+    def block(self, step):
+        return lax.rem(self.z + self.zs - step, self.zs)
+
+    def send(self, p, step, src):
+        dst = self.pairs[p][1].at[self.block(step)]
+        copy = remote(src, dst, self.send_sem.at[p, step], self.recv_sem.at[p, step], {"z": lax.rem(self.z + 1, self.zs)})
+        copy.start()
+        self.sent.append(copy)
+
+    def start(self):
+        for p, (shard, full) in enumerate(self.pairs):
+            self.send(p, 0, shard)
+            pltpu.make_async_copy(shard, full.at[self.z], self.local.at[p]).start()
+
+    def tick(self):
+        if not self.steps:
+            return None
+        p, step = self.steps.pop(0)
+        block = self.pairs[p][1].at[self.block(step + 1)]
+        remote(block, block, self.send_sem.at[p, step], self.recv_sem.at[p, step], {"z": lax.rem(self.z + 1, self.zs)}).wait_recv()
+        if step < self.zs - 2:
+            self.send(p, step + 1, block)
+            return None
+        shard, full = self.pairs[p]
+        pltpu.make_async_copy(shard, full.at[self.z], self.local.at[p]).wait()
+        return p
+
+    def finish(self):
+        while self.steps:
+            self.tick()
+        for copy in self.sent:
+            copy.wait_send()
+
+
+class RingSum:
+    def __init__(self, triples, send, recv):
+        self.triples, self.send_sem, self.recv_sem = triples, send, recv
+        self.zs, self.z = lax.axis_size("z"), lax.axis_index("z")
+        self.steps = [(p, s) for s in range(self.zs - 1) for p in range(len(triples))]
+        self.sent = []
+
+    def copy(self, p, step, src):
+        dst = self.triples[p][1].at[step]
+        return remote(src, dst, self.send_sem.at[p, step], self.recv_sem.at[p, step], {"z": lax.rem(self.z + 1, self.zs)})
+
+    def send(self, p, step, src):
+        copy = self.copy(p, step, src)
+        copy.start()
+        self.sent.append(copy)
+
+    def start(self):
+        for p, (part, came, out) in enumerate(self.triples):
+            self.send(p, 0, part.at[lax.rem(self.z + self.zs - 1, self.zs)])
+
+    def tick(self):
+        if not self.steps:
+            return
+        p, step = self.steps.pop(0)
+        part, came, out = self.triples[p]
+        self.copy(p, step, came.at[step]).wait_recv()
+        own = part[lax.rem(self.z + 2 * self.zs - 2 - step, self.zs)]
+        total = (came[step].astype(F32) + own.astype(F32)).astype(BF)
+        if step < self.zs - 2:
+            came[step] = total
+            self.send(p, step + 1, came.at[step])
+        else:
+            out[...] = total
+
+    def finish(self):
+        while self.steps:
+            self.tick()
+        for copy in self.sent:
+            copy.wait_send()
+
+
+class Turn:
+    def __init__(self, peers, full, nat, land, w_out, send, recv):
+        self.peers, self.full, self.nat, self.land, self.w_out = peers, full, nat, land, w_out
+        self.send_sem, self.recv_sem = send, recv
+        self.sent = []
+
+    def start(self):
+        zs, rows, cols = self.full.shape
+        part, span = rows // 2, self.w_out.shape[0]
+        for c in range(2):
+            for z in range(zs):
+                at = (c * zs + z) * part
+                self.nat[at : at + part, :] = self.full[z, c * part : (c + 1) * part, :]
+        used = zs * rows
+        if used < self.nat.shape[0]:
+            self.nat[used:, :] = jnp.zeros((self.nat.shape[0] - used, cols), BF)
+        _, me = self.peers.other(0, 0, 0)
+        for i, place in self.peers.offsets():
+            device, t = self.peers.other(*place)
+            src = self.nat.at[pl.ds(pl.multiple_of(t * span, span), span)]
+            copy = remote(src, self.land.at[me], self.send_sem.at[i], self.recv_sem.at[i], device)
+            copy.start()
+            self.sent.append(copy)
+        self.land[me] = self.nat[pl.ds(pl.multiple_of(me * span, span), span), :]
+
+    def finish(self):
+        for i, place in self.peers.offsets():
+            device, t = self.peers.other(*(-d for d in place))
+            block = self.land.at[t]
+            remote(block, block, self.send_sem.at[i], self.recv_sem.at[i], device).wait_recv()
+        slab, _, cols = self.land.shape
+        for t in range(slab):
+            self.w_out[:, t * cols : (t + 1) * cols] = self.land[t]
+        for copy in self.sent:
+            copy.wait_send()
+
+
+class NoSide:
+    def start(self):
+        pass
+
+    def tick(self):
+        pass
+
+    def finish(self):
+        pass
+
+
+class Both:
+    def __init__(self, ring, turn):
+        self.ring, self.turn, self.turned = ring, turn, False
+
+    def start(self):
+        self.ring.start()
+
+    def tick(self):
+        if self.ring.tick() == 0:
+            self.turn.start()
+
+    def finish(self):
+        while self.ring.steps:
+            self.tick()
+        self.ring.finish()
+        self.turn.finish()
+
+
+class SideWork:
+    def __init__(self, operands=(), in_hbm=(), outs=(), out_hbm=(), scratch=(), build=None):
+        self.operands, self.in_hbm, self.outs, self.out_hbm = operands, in_hbm, outs, out_hbm
+        self.scratch, self.build = scratch, build
+        self.zs = 1 if build is None else 2
+
+    def make(self, peers, ins, outs, scratch):
+        return NoSide() if self.build is None else self.build(peers, ins, outs, scratch)
+
+
+def gather_side(shards, turn=None):
+    zs = lax.axis_size("z")
+    n = len(shards)
+    outs = [((zs, *a.shape), BF) for a in shards]
+    sems = [pltpu.SemaphoreType.DMA((n,))] + [pltpu.SemaphoreType.DMA((n, zs - 1))] * 2
+    if turn is None:
+
+        def build(peers, ins, outs, scratch):
+            return RingGather(list(zip(ins, outs)), *scratch)
+
+        return SideWork(shards, (True,) * n, outs, (True,) * n, sems, build)
+    slab = 2 * lax.axis_size("section") * lax.axis_size("r")
+    cols = shards[0].shape[1]
+    outs[0] = ((turn, slab * cols), BF)
+    more = [
+        pltpu.VMEM((zs, *shards[0].shape), BF),
+        pltpu.VMEM((slab * turn, cols), BF),
+        pltpu.VMEM((slab, turn, cols), BF),
+    ] + [pltpu.SemaphoreType.DMA((slab,))] * 2
+
+    def build_turn(peers, ins, outs, scratch):
+        pairs = [(ins[0], scratch[3])] + list(zip(ins[1:], outs[1:]))
+        return Both(RingGather(pairs, *scratch[:3]), Turn(peers, scratch[3], scratch[4], scratch[5], outs[0], *scratch[6:8]))
+
+    return SideWork(shards, (True,) * n, outs, (False,) + (True,) * (n - 1), sems + more, build_turn)
+
+
+def sum_side(parts):
+    zs = lax.axis_size("z")
+    parts = [a.reshape(zs, a.shape[0] // zs, a.shape[1]) for a in parts]
+    n = len(parts)
+    outs = [(a.shape[1:], BF) for a in parts]
+    scratch = [pltpu.VMEM((zs - 1, *a.shape[1:]), BF) for a in parts]
+    scratch += [pltpu.SemaphoreType.DMA((n, zs - 1))] * 2
+
+    def build(peers, ins, outs, scratch):
+        return RingSum(list(zip(ins, scratch[:n], outs)), *scratch[n:])
+
+    return SideWork(parts, (False,) * n, outs, (False,) * n, scratch, build)
+
+
 def gather_scratch(chips, rows, width):
     return [pltpu.VMEM((chips, 2, rows, width), BF)] + [pltpu.SemaphoreType.DMA((chips,))] * 4
 
@@ -274,11 +484,12 @@
     return jnp.where((lane >= start) & (lane < start + head), a, jnp.zeros_like(a))
 
 
-def attention_forward(head, ties, *refs):
+def attention_forward(head, side, *refs):
     (src, h, w_qkv, w_out, bias, col, row, vec) = refs[:8]
-    refs = refs[8 + ties :]
+    ins, refs = refs[8 : 8 + len(side.operands)], refs[8 + len(side.operands) :]
     (normed, qkv, attended, logs, mid, normed_two), refs = refs[:6], refs[6:]
-    gather_refs, reduce_refs = refs[:5], refs[5:]
+    side_outs, refs = refs[: len(side.outs)], refs[len(side.outs) :]
+    gather_refs, reduce_refs, side_refs = refs[:5], refs[5 : 14 + 1], refs[14 + 1 :]
     rows, width = src.shape
     span = w_out.shape[0]
     peers = Peers()
@@ -286,11 +497,14 @@
     reduce = Reduce(peers, *reduce_refs[:5], reduce_refs[5:9])
     kept_sem = reduce_refs[9]
     full = gather.full
-    peers.greet()
+    work = side.make(peers, ins, side_outs, side_refs)
+    peers.greet(side.zs)
     gather.start(src)
+    work.start()
     for k, chip in gather.arrivals():
         part = dot(full[chip].reshape(2 * rows, width), w_qkv[...]) + bias[...]
         qkv[chip_rows(chip, rows), :] = part.astype(BF)
+    work.tick()
     kept = pltpu.make_async_copy(full, normed, kept_sem)
     kept.start()
     scale = head ** (-0.5)
@@ -318,11 +532,13 @@
         reduce.put(k, dot(attended[here, :], w_out[...]))
         if before is not None:
             reduce.push(before)
+        work.tick()
         before = k
     reduce.push(before)
     out = h[...].astype(F32) + (reduce.total() + vec[4:5, :])
     mid[...] = out
     normed_two[...] = (norm_parts(out)[0] * vec[1:2, :] + vec[3:4, :]).astype(BF)
+    work.finish()
     gather.finish()
     reduce.finish()
     kept.wait()
@@ -331,19 +547,22 @@
 ROOT = 0.7978845608028654
 
 
-def feed_forward(ties, *refs):
+def feed_forward(side, *refs):
     (src, mid, w_fc, w_proj, bias, vec, next_vec) = refs[:7]
-    refs = refs[7 + ties :]
+    ins, refs = refs[7 : 7 + len(side.operands)], refs[7 + len(side.operands) :]
     (normed_two, slope, activated, result, normed), refs = refs[:5], refs[5:]
-    gather_refs, reduce_refs = refs[:5], refs[5:]
+    side_outs, refs = refs[: len(side.outs)], refs[len(side.outs) :]
+    gather_refs, reduce_refs, side_refs = refs[:5], refs[5 : 14 + 1], refs[14 + 1 :]
     rows, width = src.shape
     peers = Peers()
     gather = Gather(peers, gather_refs[0], gather_refs[1:])
     reduce = Reduce(peers, *reduce_refs[:5], reduce_refs[5:9])
     kept_sem = reduce_refs[9]
     full = gather.full
-    peers.greet()
+    work = side.make(peers, ins, side_outs, side_refs)
+    peers.greet(side.zs)
     gather.start(src)
+    work.start()
     before = None
     for k, chip in gather.arrivals():
         here = chip_rows(chip, rows)
@@ -355,6 +574,8 @@
         reduce.put(k, dot(act, w_proj[...]))
         if before is not None:
             reduce.push(before)
+        if k:
+            work.tick()
         before = k
     kept = pltpu.make_async_copy(full, normed_two, kept_sem)
     kept.start()
@@ -362,6 +583,7 @@
     out = (mid[...] + (reduce.total() + vec[5:6, :])).astype(BF)
     result[...] = out
     normed[...] = (norm_parts(out.astype(F32))[0] * next_vec[0:1, :] + next_vec[2:3, :]).astype(BF)
+    work.finish()
     gather.finish()
     reduce.finish()
     kept.wait()
@@ -371,11 +593,12 @@
     return [(a, min(a + step, size)) for a in range(0, size, step)]
 
 
-def feed_backward(ties, *refs):
+def feed_backward(side, *refs):
     (src, mid, w_fc, w_proj, slope, activated, normed_two, vec) = refs[:8]
-    refs = refs[8 + ties :]
+    ins, refs = refs[8 : 8 + len(side.operands)], refs[8 + len(side.operands) :]
     (grad_mid, attn_rows, grad_proj, grad_fc, sums, unit_sums), refs = refs[:6], refs[6:]
-    gather_refs, reduce_refs = refs[:5], refs[5:]
+    side_outs, refs = refs[: len(side.outs)], refs[len(side.outs) :]
+    gather_refs, reduce_refs, side_refs = refs[:5], refs[5 : 14 + 1], refs[14 + 1 :]
     hidden, = reduce_refs[9:10]
     rows, width = src.shape
     tokens = slope.shape[0]
@@ -383,8 +606,10 @@
     gather = Gather(peers, gather_refs[0], gather_refs[1:])
     reduce = Reduce(peers, *reduce_refs[:5], reduce_refs[5:9])
     full = gather.full
-    peers.greet()
+    work = side.make(peers, ins, side_outs, side_refs)
+    peers.greet(side.zs)
     gather.start(src)
+    work.start()
     before = None
     for k, chip in gather.arrivals():
         here = chip_rows(chip, rows)
@@ -394,11 +619,14 @@
         reduce.put(k, dot(back, w_fc[...], 1, 1))
         if before is not None:
             reduce.push(before)
+        if k > 1:
+            work.tick()
         before = k
     reduce.push(before)
     branch = full[...].reshape(tokens, width)
     for a, b in chunks(activated.shape[1], 256):
         grad_proj[a:b, :] = dot(activated[:, a:b], branch, 0, 0).astype(BF)
+    work.tick()
     back = hidden[...]
     for a, b in chunks(width, 512):
         grad_fc[a:b, :] = dot(normed_two[:, a:b], back, 0, 0).astype(BF)
@@ -414,15 +642,17 @@
     sums[2:3, :] = jnp.sum(own, axis=0, keepdims=True)
     sums[3:4, :] = jnp.sum(low.astype(F32), axis=0, keepdims=True)
     sums[4:8, :] = jnp.zeros((4, width), F32)
+    work.finish()
     gather.finish()
     reduce.finish()
 
 
-def attention_backward(head, ties, *refs):
+def attention_backward(head, side, *refs):
     (src, grad_mid, h, w_qkv, w_out, qkv, attended, logs, normed, col, row, vec) = refs[:12]
-    refs = refs[12 + ties :]
+    ins, refs = refs[12 : 12 + len(side.operands)], refs[12 + len(side.operands) :]
     (grad_in, grad_qkv, grad_out, sums, head_sums), refs = refs[:5], refs[5:]
-    gather_refs, reduce_refs = refs[:5], refs[5:]
+    side_outs, refs = refs[: len(side.outs)], refs[len(side.outs) :]
+    gather_refs, reduce_refs, side_refs = refs[:5], refs[5 : 14 + 3], refs[14 + 3 :]
     joint, key_sum, value_sum = reduce_refs[9:12]
     rows, width = src.shape
     tokens, span = attended.shape
@@ -431,8 +661,10 @@
     gather = Gather(peers, gather_refs[0], gather_refs[1:])
     reduce = Reduce(peers, *reduce_refs[:5], reduce_refs[5:9])
     full = gather.full
-    peers.greet()
+    work = side.make(peers, ins, side_outs, side_refs)
+    peers.greet(side.zs)
     gather.start(src)
+    work.start()
     for k, chip in gather.arrivals():
         here = chip_rows(chip, rows)
         g_all = dot(full[chip].reshape(2 * rows, width), w_out[...], 1, 1).astype(BF)
@@ -463,6 +695,8 @@
             else:
                 key_sum[:, lanes] += key_term
                 value_sum[:, lanes] += value_term
+        if k:
+            work.tick()
     joint[:, span : 2 * span] = key_sum[...].astype(BF)
     joint[:, 2 * span :] = value_sum[...].astype(BF)
     order = list(range(1, peers.chips)) + [0]
@@ -472,6 +706,7 @@
         if before is not None:
             reduce.push(before)
         before = k
+    work.tick()
     grads = joint[...]
     for a, b in chunks(width, 512):
         grad_qkv[a:b, :] = dot(normed[:, a:b], grads, 0, 0).astype(BF)
@@ -482,25 +717,27 @@
     sums[0:1, :] = gain
     sums[1:2, :] = shift
     sums[2:8, :] = jnp.zeros((6, width), F32)
+    work.finish()
     gather.finish()
     reduce.finish()
 
 
-def call(kernel, name, outs, operands, ties, kept, scratch):
+def call(kernel, name, outs, operands, side, kept, scratch):
     chips = lax.axis_size("section") * lax.axis_size("r")
     rows, width = operands[0].shape
     vmem, hbm = pl.BlockSpec(memory_space=pltpu.VMEM), pl.BlockSpec(memory_space=pl.ANY)
-    return pl.pallas_call(
+    out = pl.pallas_call(
         kernel,
-        out_shape=[jax.ShapeDtypeStruct(*o) for o in outs],
-        in_specs=[vmem] * len(operands) + [hbm] * len(ties),
-        out_specs=[hbm if i in kept else vmem for i in range(len(outs))],
-        scratch_shapes=gather_scratch(chips, rows, width) + reduce_scratch(chips, rows, width) + scratch,
+        out_shape=[jax.ShapeDtypeStruct(*o) for o in (*outs, *side.outs)],
+        in_specs=[vmem] * len(operands) + [hbm if i else vmem for i in side.in_hbm],
+        out_specs=[hbm if i in kept else vmem for i in range(len(outs))] + [hbm if i else vmem for i in side.out_hbm],
+        scratch_shapes=gather_scratch(chips, rows, width) + reduce_scratch(chips, rows, width) + scratch + list(side.scratch),
         compiler_params=pltpu.CompilerParams(collective_id=name, has_side_effects=True, vmem_limit_bytes=60 * 2**20),
-    )(*operands, *ties)
-
-
-def run_attention_forward(name, head, ties, *operands):
+    )(*operands, *side.operands)
+    return out[: len(outs)], out[len(outs) :]
+
+
+def run_attention_forward(name, head, side, *operands):
     src, h, w_qkv, w_out, bias, col, row, vec = operands
     rows, width = src.shape
     tokens, span = col.shape[0], w_out.shape[0]
@@ -514,10 +751,10 @@
         ((rows, width), F32),
         ((rows, width), BF),
     ]
-    return call(functools.partial(attention_forward, head, len(ties)), name, outs, operands, ties, (0,), [pltpu.SemaphoreType.DMA])
-
-
-def run_feed_forward(name, ties, *operands):
+    return call(functools.partial(attention_forward, head, side), name, outs, operands, side, (0,), [pltpu.SemaphoreType.DMA])
+
+
+def run_feed_forward(name, side, *operands):
     src, mid, w_fc, w_proj, bias, vec, next_vec = operands
     rows, width = src.shape
     units = w_fc.shape[1]
@@ -530,10 +767,10 @@
         ((rows, width), BF),
         ((rows, width), BF),
     ]
-    return call(functools.partial(feed_forward, len(ties)), name, outs, operands, ties, (0,), [pltpu.SemaphoreType.DMA])
-
-
-def run_feed_backward(name, ties, *operands):
+    return call(functools.partial(feed_forward, side), name, outs, operands, side, (0,), [pltpu.SemaphoreType.DMA])
+
+
+def run_feed_backward(name, side, *operands):
     src, mid, w_fc, w_proj, slope, activated, normed_two, vec = operands
     rows, width = src.shape
     tokens, units = slope.shape
@@ -545,10 +782,10 @@
         ((8, width), F32),
         ((1, units), F32),
     ]
-    return call(functools.partial(feed_backward, len(ties)), name, outs, operands, ties, (), [pltpu.VMEM((tokens, units), BF)])
-
-
-def run_attention_backward(name, head, ties, *operands):
+    return call(functools.partial(feed_backward, side), name, outs, operands, side, (), [pltpu.VMEM((tokens, units), BF)])
+
+
+def run_attention_backward(name, head, side, *operands):
     src, grad_mid, h, w_qkv, w_out, qkv, attended, logs, normed, col, row, vec = operands
     rows, width = src.shape
     tokens, span = attended.shape
@@ -560,85 +797,285 @@
         ((1, 3 * span), F32),
     ]
     scratch = [pltpu.VMEM((tokens, 3 * span), BF), pltpu.VMEM((tokens, span), F32), pltpu.VMEM((tokens, span), F32)]
-    return call(functools.partial(attention_backward, head, len(ties)), name, outs, operands, ties, (), scratch)
-
-
-def tiny_kernel(src, out, stage, z_send, z_recv, *sems):
+    return call(functools.partial(attention_backward, head, side), name, outs, operands, side, (), scratch)
+
+
+def start_kernel(ties, block, *refs):
+    (tiny, qkv_src, wo_src, fc_src, proj_src), refs = refs[:5], refs[5 + ties :]
+    (tiny_out, qkv, wo, fc, proj, qkv_full, w_out), refs = refs[:7], refs[7:]
+    stage, qkv_land, wo_land, fc_land, wo_full, nat, land = refs[:7]
+    z_send, z_recv, *sems = refs[7:13]
+    all_send, all_recv, far_send, far_recv, turn_send, turn_recv, ring_local, ring_send, ring_recv = refs[13:]
     peers = Peers()
     zs, z = lax.axis_size("z"), lax.axis_index("z")
+    x, rest = peers.x, peers.rest
+    spot = peers.c * rest + peers.r
     peers.greet(zs)
     sent = []
-    for k in range(1, zs):
-        copy = remote(src, stage.at[z], z_send.at[k], z_recv.at[k], {"z": lax.rem(z + k, zs)})
+
+    def send(copy):
         copy.start()
         sent.append(copy)
-    stage[z] = src[...]
+
     for k in range(1, zs):
-        block = stage.at[lax.rem(z + zs - k, zs)]
-        remote(block, block, z_send.at[k], z_recv.at[k], {"z": lax.rem(z + k, zs)}).wait_recv()
-    gather = Gather(peers, out, sems)
-    gather.start(stage)
+        send(remote(tiny, stage.at[z], z_send.at[k], z_recv.at[k], {"z": lax.rem(z + k, zs)}))
+    stage[z] = tiny[...]
+    moves = [(wo_src, wo_land), (qkv_src, qkv_land), (fc_src, fc_land)]
+    for a, (src, dst) in enumerate(moves):
+        for i, place in peers.offsets():
+            device, t = peers.other(*place)
+            send(remote(src.at[t], dst.at[x, spot], all_send.at[a, i], all_recv.at[a, i], device))
+        if a == 1:
+            for k in range(1, zs):
+                came = stage.at[lax.rem(z + zs - k, zs)]
+                remote(came, came, z_send.at[k], z_recv.at[k], {"z": lax.rem(z + k, zs)}).wait_recv()
+            gather = Gather(peers, tiny_out, sems)
+            gather.start(stage)
+    for d in range(1, peers.sections):
+        device, _ = peers.other(d, 0, 0)
+        there = lax.rem(x + d, peers.sections)
+        send(remote(proj_src.at[there], proj.at[x], far_send.at[d], far_recv.at[d], device))
+    _, me = peers.other(0, 0, 0)
+    own = []
+    for a, (src, dst) in enumerate(moves):
+        own.append(pltpu.make_async_copy(src.at[me], dst.at[x, spot], all_recv.at[a, 0]))
+    own.append(pltpu.make_async_copy(proj_src.at[x], proj.at[x], far_recv.at[0]))
+    for copy in own:
+        copy.start()
+
+    def settle(a, shard):
+        dst = moves[a][1]
+        for i, place in peers.offsets():
+            device, _ = peers.other(*(-d for d in place))
+            came = dst.at[device["section"], device["dp"] * rest + device["r"]]
+            remote(came, came, all_send.at[a, i], all_recv.at[a, i], device).wait_recv()
+        own[a].wait()
+        for layer in range(peers.sections):
+            for i in range(2 * rest):
+                shard[layer, i * block : (i + 1) * block, :] = dst[layer, i, :block, :]
+
+    settle(0, wo)
+    settle(1, qkv)
+    turn = Turn(peers, wo_full, nat, land, w_out, turn_send, turn_recv)
+    ring = RingGather([(wo.at[0], wo_full), (qkv.at[0], qkv_full)], ring_local, ring_send, ring_recv)
+    work = Both(ring, turn)
+    work.start()
     for _ in gather.arrivals():
         pass
+    settle(2, fc)
+    for d in range(1, peers.sections):
+        device, _ = peers.other(-d, 0, 0)
+        came = proj.at[device["section"]]
+        remote(came, came, far_send.at[d], far_recv.at[d], device).wait_recv()
+    own[3].wait()
+    work.finish()
     gather.finish()
     for copy in sent:
         copy.wait_send()
 
 
-def tiny_gather(a, name):
-    sections, rest, zs = (lax.axis_size(i) for i in ("section", "r", "z"))
-    chips = sections * rest
+def run_start(name, lay, ties, tiny, qkv, wo, fc, proj):
+    zs, n, chips = lay.zs, lay.slab, lay.slab // 2
+    span = lay.slots * lay.head
+    spots = lay.cores * lay.rest
+    rows = spots * lay.block
+    vmem, hbm = pl.BlockSpec(memory_space=pltpu.VMEM), pl.BlockSpec(memory_space=pl.ANY)
+    widths = [a.shape[2] for a in (qkv, wo, fc)]
+    outs = [((chips, 2, zs, *tiny.shape), F32)]
+    outs += [((lay.sections, rows, m), BF) for m in widths]
+    outs += [(proj.shape, BF), ((zs, rows, widths[0]), BF), ((span, lay.width), BF)]
+    dma = pltpu.SemaphoreType.DMA
+    return pl.pallas_call(
+        functools.partial(start_kernel, len(ties), lay.block),
+        out_shape=[jax.ShapeDtypeStruct(*o) for o in outs],
+        in_specs=[vmem] + [hbm] * (4 + len(ties)),
+        out_specs=[vmem] * 5 + [hbm, vmem],
+        scratch_shapes=[pltpu.VMEM((zs, *tiny.shape), F32)]
+        + [pltpu.VMEM((lay.sections, spots, qkv.shape[1], m), BF) for m in widths]
+        + [pltpu.VMEM((zs, rows, widths[1]), BF), pltpu.VMEM((n * span, widths[1]), BF), pltpu.VMEM((n, span, widths[1]), BF)]
+        + [dma((zs,))] * 2
+        + [dma((chips,))] * 4
+        + [dma((3, n))] * 2
+        + [dma((lay.sections,))] * 2
+        + [dma((n,))] * 2
+        + [dma((2,))]
+        + [dma((2, zs - 1))] * 2,
+        compiler_params=pltpu.CompilerParams(collective_id=name, has_side_effects=True, vmem_limit_bytes=60 * 2**20),
+    )(tiny, qkv, wo, fc, proj, *ties)
+
+
+def end_kernel(sizes, *refs):
+    block, width, units, heads = sizes
+    (part, turned, qkv_one, wo_one, fc_zero, fc_one, proj_zero, proj_one, small), refs = refs[:9], refs[9:]
+    (out_qkv, out_wo, out_fc, out_proj, out_small), refs = refs[:5], refs[5:]
+    (qkv_total, wo_part, wo_total, wo_cut, wo_back, proj_both, proj_land), refs = refs[:7], refs[7:]
+    stages, lands, refs = refs[:3], refs[3:6], refs[6:]
+    (small_land, small_sum, z_land, came_qkv, came_wo), refs = refs[:5], refs[5:]
+    all_send, all_recv, far_send, far_recv, z_send, z_recv, turn_send, turn_recv, ring_send, ring_recv, late_send, late_recv = refs
+    peers = Peers()
+    zs, z = lax.axis_size("z"), lax.axis_index("z")
+    x, rest, slab = peers.x, peers.rest, 2 * peers.chips
+    spot = peers.c * rest + peers.r
+    span, cols = turned.shape[0], wo_total.shape[1]
+    half, wide = proj_zero.shape[0], rest * block
+    _, me = peers.other(0, 0, 0)
+    offsets = peers.offsets()
+    peers.greet(zs)
+    sent = []
+
+    def send(copy):
+        copy.start()
+        sent.append(copy)
+
+    ring = RingSum([(part, came_qkv, qkv_total)], ring_send, ring_recv)
+    ring.start()
+    for t in range(slab):
+        wo_cut[t] = turned[:, t * cols : (t + 1) * cols]
+    for i, place in offsets:
+        device, t = peers.other(*place)
+        send(remote(wo_cut.at[t], wo_back.at[me], turn_send.at[i], turn_recv.at[i], device))
+    wo_back[me] = wo_cut[me]
+    for i, place in offsets:
+        device, t = peers.other(*place)
+        send(remote(small.at[t], small_land.at[me], all_send.at[3, i], all_recv.at[3, i], device))
+    small_land[me] = small[me]
+
+    def cut(a, totals):
+        for layer, total in enumerate(totals):
+            for i in range(2 * rest):
+                stages[a][layer, i, :block, :] = total[i * block : (i + 1) * block, :]
+        for i, place in offsets:
+            device, t = peers.other(*place)
+            src = stages[a].at[device["section"], device["dp"] * rest + device["r"]]
+            send(remote(src, lands[a].at[me], all_send.at[a, i], all_recv.at[a, i], device))
+        lands[a][me] = stages[a][x, spot]
+
+    def settle(a, land):
+        for i, place in offsets:
+            device, t = peers.other(*(-d for d in place))
+            came = land.at[t]
+            remote(came, came, all_send.at[a, i], all_recv.at[a, i], device).wait_recv()
+
+    cut(0, (fc_zero, fc_one))
+    proj_both[0] = proj_zero[...]
+    proj_both[1] = proj_one[...]
+    device, _ = peers.other(1, 0, 0)
+    send(remote(proj_both.at[1 - x], proj_land.at[x], far_send, far_recv, device))
+    proj_land[x] = proj_both[x]
+
+    for i, place in offsets:
+        device, t = peers.other(*(-d for d in place))
+        came = wo_back.at[t]
+        remote(came, came, turn_send.at[i], turn_recv.at[i], device).wait_recv()
+    for c in range(2):
+        for k in range(zs):
+            at, done = (c * zs + k) * wide, 0
+            while done < wide:
+                t, row = divmod(at + done, span)
+                count = min(wide - done, span - row)
+                wo_part[k, c * wide + done : c * wide + done + count, :] = wo_back[t, row : row + count, :]
+                done += count
+    wo_ring = RingSum([(wo_part, came_wo, wo_total)], late_send, late_recv)
+    wo_ring.start()
+    settle(3, small_land)
+    total = small_land[0]
+    for t in range(1, slab):
+        total = total + small_land[t]
+    small_sum[...] = total
+    for k in range(1, zs):
+        there = lax.rem(z + k, zs)
+        send(remote(small_sum.at[there], z_land.at[z], z_send.at[k], z_recv.at[k], {"z": there}))
+    z_land[z] = small_sum[z]
+    ring.tick()
+    wo_ring.tick()
+    settle(0, lands[0])
+    for t in range(slab):
+        h, c, r = t // (2 * rest), t // rest % 2, t % rest
+        for k in range(zs):
+            at = ((c * zs + k) * rest + r) * (units // (2 * zs * rest)) + h * half
+            out_fc[:, at : at + half] = lands[0][t, :block, k * half : (k + 1) * half].astype(F32)
+    ring.tick()
+    wo_ring.tick()
+    came = proj_land.at[1 - x]
+    remote(came, came, far_send, far_recv, device).wait_recv()
+    for h in range(2):
+        for c in range(2):
+            for k in range(zs):
+                at, of = (c * zs + k) * wide, (k * 2 + c) * wide
+                out_proj[h * half : (h + 1) * half, at : at + wide] = proj_land[h, :, of : of + wide].astype(F32)
+    for k in range(1, zs):
+        came = z_land.at[lax.rem(z + zs - k, zs)]
+        remote(came, came, z_send.at[k], z_recv.at[k], {"z": lax.rem(z + k, zs)}).wait_recv()
+    total = z_land[0]
+    for k in range(1, zs):
+        total = total + z_land[k]
+    out_small[...] = total
+    wo_ring.finish()
+    cut(2, (wo_total, wo_one))
+    ring.finish()
+    cut(1, (qkv_total, qkv_one))
+    settle(2, lands[2])
+    for t in range(slab):
+        big, off = divmod(t * cols, wide)
+        at = (big % 2 * zs + big // 2) * wide + off
+        out_wo[:, at : at + cols] = lands[2][t, :block, :].astype(F32)
+    settle(1, lands[1])
+    for t in range(slab):
+        count = min(span, width - t * span)
+        for p in range(3):
+            if count > 0:
+                at = p * width + t * span
+                out_qkv[:, at : at + count] = lands[1][t, :block, p * span : p * span + count].astype(F32)
+    for copy in sent:
+        copy.wait_send()
+
+
+def run_end(name, lay, part, turned, qkv_one, wo_one, fcs, projs, small):
+    zs, n = lay.zs, lay.slab
+    span, width, block = lay.slots * lay.head, lay.width, lay.block
+    part = part.reshape(zs, part.shape[0] // zs, part.shape[1])
+    rows = part.shape[1]
+    spots = lay.cores * lay.rest
+    tall = -(-block // 16) * 16
     vmem = pl.BlockSpec(memory_space=pltpu.VMEM)
-    out = pl.pallas_call(
-        tiny_kernel,
-        out_shape=jax.ShapeDtypeStruct((chips, 2, zs, *a.shape), a.dtype),
-        in_specs=[vmem],
-        out_specs=vmem,
-        scratch_shapes=[pltpu.VMEM((zs, *a.shape), a.dtype)]
-        + [pltpu.SemaphoreType.DMA((zs,))] * 2
-        + [pltpu.SemaphoreType.DMA((chips,))] * 4,
-        compiler_params=pltpu.CompilerParams(collective_id=name, has_side_effects=True),
-    )(a)
-    return out.reshape(sections, rest, 2, zs, *a.shape)
-
-
-class Rings:
-    def __init__(self, lay):
-        self.lay = lay
-        self.live = []
-
-    def own(self, part, step):
-        lay = self.lay
-        block = lax.dynamic_index_in_dim(part, (lay.z - 1 - step) % lay.zs, 0, keepdims=False)
-        return block.astype(jnp.float32)
-
-    def add(self, term):
-        zs = self.lay.zs
-        part = term.reshape(zs, term.shape[0] // zs, term.shape[1])
-        ring = [self.own(part, 0).astype(jnp.bfloat16), part, 0]
-        self.live.append(ring)
-        return ring
-
-    def step(self):
-        zs = self.lay.zs
-        self.live = [ring for ring in self.live if ring[2] < zs - 1]
-        route = [(i, (i + 1) % zs) for i in range(zs)]
-        for ring in self.live:
-            got = lax.ppermute(ring[0], "z", route).astype(jnp.float32)
-            ring[2] += 1
-            ring[0] = (got + self.own(ring[1], ring[2])).astype(jnp.bfloat16)
-
-    def ties(self):
-        now = [ring[0] for ring in self.live]
-        self.step()
-        return now
-
-    def finish(self):
-        while any(ring[2] < self.lay.zs - 1 for ring in self.live):
-            self.step()
-
-
-def spread_weights(lay, w_qkv, w_attn_out, w_fc, w_proj):
+    dma = pltpu.SemaphoreType.DMA
+    widths = [fcs[0].shape[1], part.shape[2], lay.cols]
+    half = projs[0].shape[0]
+    tile = small.shape[2:]
+    outs = [(block, 3 * width), (block, width), (block, lay.units), (lay.unit_block, width), tile]
+    return pl.pallas_call(
+        functools.partial(end_kernel, (block, width, lay.units, lay.slots)),
+        out_shape=[jax.ShapeDtypeStruct(o, F32) for o in outs],
+        in_specs=[vmem] * 9,
+        out_specs=[vmem] * 5,
+        scratch_shapes=[
+            pltpu.VMEM((rows, part.shape[2]), BF),
+            pltpu.VMEM((zs, rows, lay.cols), BF),
+            pltpu.VMEM((rows, lay.cols), BF),
+            pltpu.VMEM((n, span, lay.cols), BF),
+            pltpu.VMEM((n, span, lay.cols), BF),
+            pltpu.VMEM((2, half, width), BF),
+            pltpu.VMEM((2, half, width), BF),
+        ]
+        + [pltpu.VMEM((lay.sections, spots, tall, m), BF) for m in widths]
+        + [pltpu.VMEM((n, tall, m), BF) for m in widths]
+        + [
+            pltpu.VMEM((n, zs, *tile), F32),
+            pltpu.VMEM((zs, *tile), F32),
+            pltpu.VMEM((zs, *tile), F32),
+            pltpu.VMEM((zs - 1, rows, part.shape[2]), BF),
+            pltpu.VMEM((zs - 1, rows, lay.cols), BF),
+        ]
+        + [dma((4, n))] * 2
+        + [dma] * 2
+        + [dma((zs,))] * 2
+        + [dma((n,))] * 2
+        + [dma((1, zs - 1))] * 4,
+        compiler_params=pltpu.CompilerParams(collective_id=name, has_side_effects=True, vmem_limit_bytes=60 * 2**20),
+    )(part, turned, qkv_one, wo_one, *fcs, *projs, small)
+
+
+def weight_parts(lay, w_qkv, w_attn_out, w_fc, w_proj):
     n = lay.slab
     width, block = lay.width, lay.block
     slot_cols = lay.slots * lay.head
@@ -650,27 +1087,8 @@
     fc = fc.transpose(4, 1, 3, 0, 2, 5).reshape(n, block, lay.zs * lay.half)
     proj = lay.order(w_proj[0]).reshape(lay.sections, lay.half, width)
 
-    def move(a):
-        got = lax.all_to_all(a, SLAB, 0, 0, tiled=True)
-        got = got.reshape(lay.sections, lay.cores * lay.rest * block, a.shape[2])
-        return [got[layer] for layer in range(lay.sections)]
-
-    first = move(jnp.concatenate([qkv, out], axis=2))
-    fc = move(fc)
-    proj = lax.all_to_all(proj, ("section",), 0, 0, tiled=True)
-    params = []
-    for layer in range(lay.sections):
-        full = [
-            lax.all_gather(a, "z", axis=0, tiled=True) for a in (first[layer], fc[layer], proj[layer])
-        ]
-        wo = full[0][:, 3 * slot_cols :]
-        wo = wo.reshape(lay.zs, lay.cores, lay.rest * block, lay.cols)
-        wo = jnp.swapaxes(wo, 0, 1).reshape(width, lay.cols)
-        wo = jnp.pad(wo, ((0, n * slot_cols - width), (0, 0))).reshape(n, slot_cols, lay.cols)
-        wo = lax.all_to_all(wo, SLAB, 0, 0, tiled=True)
-        wo = wo.transpose(1, 0, 2).reshape(slot_cols, width)
-        params.append((full[0][:, : 3 * slot_cols], wo, full[1], full[2]))
-    return params
+    spare = ((0, 0), (0, -block % 16), (0, 0))
+    return jnp.pad(qkv, spare), jnp.pad(out, spare), jnp.pad(fc, spare), proj
 
 
 def on_device(
@@ -681,14 +1099,17 @@
     span = lay.slots * lay.head
     micro = lay.z // lay.seqs
 
-    params = spread_weights(lay, w_qkv, w_attn_out, w_fc, w_proj)
+    sources = weight_parts(lay, w_qkv, w_attn_out, w_fc, w_proj)
+    h = lay.order(lay.tokens_in(inputs))
+    g = lay.order(lay.tokens_in(cotangent))
 
     per_row = lay.unit_block // block
     thin = jnp.concatenate([norm_gains[0], biases[0], fc_bias[0].reshape(block, per_row)], axis=1)
     thin = jnp.concatenate([thin.reshape(-1).astype(jnp.float32), positions.reshape(-1).astype(jnp.float32)])
     used, spots = block * (8 + per_row), positions.size
     thin = jnp.pad(thin, (0, -thin.size % 1024)).reshape(-1, 128)
-    thin = tiny_gather(thin, 0).reshape(lay.sections, lay.rest, lay.cores, lay.zs, -1)
+    thin, qkv_cut, wo_cut, fc_cut, proj_cut, w_qkv, w_out = run_start(0, lay, (h, g), thin, *sources)
+    thin = thin.reshape(lay.sections, lay.rest, lay.cores, lay.zs, -1)
     places = thin[0, :, 0, :, used : used + spots].astype(jnp.int32)
     places = places.reshape(lay.rest, lay.sections, lay.cores, lay.micros, lay.rows)
     places = places.transpose(3, 1, 0, 2, 4).reshape(lay.micros, lay.tokens)
@@ -711,67 +1132,77 @@
         unit = lax.dynamic_slice_in_dim(unit, lay.t, 1, 0)
         smalls.append((vec, bias, unit))
 
-    h = lay.order(lay.tokens_in(inputs))
-    g = lay.order(lay.tokens_in(cotangent))
-
     vec = smalls[0][0]
     normed = (norm_parts(h.astype(F32))[0] * vec[0:1] + vec[2:3]).astype(BF)
-    outs, keeps = [], []
+    outs, keeps, params = [], [], []
     for layer in range(lay.sections):
-        w_qkv, w_out, w_fc, w_proj = params[layer]
+        last = layer == lay.sections - 1
         vec, bias, unit = smalls[layer]
-        full, qkv, attended, logs, mid, normed_two = run_attention_forward(
-            1, lay.head, (), normed, h, w_qkv, w_out, bias, col, row, vec
+        w_qkv = w_qkv.reshape(width, 3 * span)
+        (full, qkv, attended, logs, mid, normed_two), (w_fc, w_proj) = run_attention_forward(
+            1 + 2 * layer,
+            lay.head,
+            gather_side([fc_cut[layer], proj_cut[layer]]),
+            normed,
+            h,
+            w_qkv,
+            w_out,
+            bias,
+            col,
+            row,
+            vec,
         )
+        w_fc, w_proj = w_fc.reshape(width, -1), w_proj.reshape(-1, width)
         next_vec = smalls[min(layer + 1, lay.sections - 1)][0]
-        full_two, slope, activated, result, normed = run_feed_forward(
-            2, (), normed_two, mid, w_fc, w_proj, unit, vec, next_vec
+        side = SideWork() if last else gather_side([wo_cut[layer + 1], qkv_cut[layer + 1]], span)
+        (full_two, slope, activated, result, normed), later = run_feed_forward(
+            2 + 2 * layer, side, normed_two, mid, w_fc, w_proj, unit, vec, next_vec
         )
+        params.append((w_qkv, w_out, w_fc, w_proj))
+        if not last:
+            w_out, w_qkv = later
         keeps.append((h, full, qkv, attended, logs, mid, full_two, slope, activated))
         h = result
         outs.append(h)
 
-    grads, grad_rows, sums = [None] * lay.sections, [None] * lay.sections, [None] * lay.sections
-    rings = Rings(lay)
+    def turned(grad_out):
+        wo = grad_out.reshape(span, n, lay.cols).transpose(1, 0, 2)
+        wo = lax.all_to_all(wo, SLAB, 0, 0, tiled=True)
+        wo = wo.reshape(n * span, lay.cols)[:width].reshape(lay.cores, lay.zs, lay.rest * block, lay.cols)
+        return jnp.swapaxes(wo, 0, 1).reshape(width, lay.cols)
+
+    totals = {}
+    waiting = []
+
+    def carry(count):
+        now = waiting[:count]
+        del waiting[:count]
+        return [key for key, _ in now], sum_side([part for _, part in now]) if now else SideWork()
+
+    grad_rows, sums = [None] * lay.sections, [None] * lay.sections
     for layer in reversed(range(lay.sections)):
         w_qkv, w_out, w_fc, w_proj = params[layer]
         vec = smalls[layer][0]
         h, full, qkv, attended, logs, mid, full_two, slope, activated = keeps[layer]
         full, full_two = (a.reshape(lay.tokens, width) for a in (full, full_two))
-        grad_mid, attn_rows, grad_proj, grad_fc, feed_sums, unit_sums = run_feed_backward(
-            3 + 2 * layer, rings.ties(), g, mid, w_fc, w_proj, slope, activated, full_two, vec
+        name = 1 + 4 * lay.sections - 2 * layer
+        keys, side = carry(1)
+        (grad_mid, attn_rows, grad_proj, grad_fc, feed_sums, unit_sums), done = run_feed_backward(
+            name, side, g, mid, w_fc, w_proj, slope, activated, full_two, vec
         )
-        grad_proj, grad_fc = rings.add(grad_proj), rings.add(grad_fc)
-        g, grad_qkv, grad_out, attn_sums, head_sums = run_attention_backward(
-            4 + 2 * layer, lay.head, rings.ties(), attn_rows, grad_mid, h, w_qkv, w_out, qkv, attended, logs, full, col, row, vec
+        totals.update(zip(keys, done))
+        waiting = [(("proj", layer), grad_proj), (("fc", layer), grad_fc)] + waiting
+        keys, side = carry(3)
+        (g, grad_qkv, grad_out, attn_sums, head_sums), done = run_attention_backward(
+            name + 1, lay.head, side, attn_rows, grad_mid, h, w_qkv, w_out, qkv, attended, logs, full, col, row, vec
         )
-        wo = grad_out.reshape(span, n, lay.cols).transpose(1, 0, 2)
-        wo = lax.all_to_all(wo, SLAB, 0, 0, tiled=True)
-        wo = wo.reshape(n * span, lay.cols)[:width].reshape(lay.cores, lay.zs, lay.rest * block, lay.cols)
-        wo = jnp.swapaxes(wo, 0, 1).reshape(width, lay.cols)
-        first = rings.add(jnp.concatenate([grad_qkv, wo], axis=1))
-        grads[layer] = (first, grad_fc, grad_proj)
+        totals.update(zip(keys, done))
+        if layer:
+            waiting = waiting + [(("qkv", layer), grad_qkv), (("out", layer), turned(grad_out))]
         grad_rows[layer] = g
         sums[layer] = (feed_sums, unit_sums, attn_sums, head_sums)
-    rings.finish()
-
     section_out = lay.tokens_out([lay.restore(a) for a in outs])
     section_grad = lay.tokens_out([lay.restore(a) for a in grad_rows])
-
-    def back(i):
-        both = jnp.stack([grads[layer][i][0] for layer in range(lay.sections)])
-        return lax.all_to_all(both.reshape(n, block, both.shape[2]), SLAB, 0, 0, tiled=True)
-
-    first = back(0)
-    got = first[:, :, : 3 * span].reshape(n, block, 3, span).transpose(1, 2, 0, 3)
-    out_qkv = got.reshape(block, 3, n * span)[:, :, :width].reshape(block, 3 * width).astype(jnp.float32)
-    got = first[:, :, 3 * span :].transpose(1, 0, 2).reshape(block, width)
-    out_attn = lay.restore(got).astype(jnp.float32)
-    got = back(1).reshape(lay.sections, lay.cores, lay.rest, block, lay.zs, lay.half)
-    out_fc = got.transpose(3, 1, 4, 2, 0, 5).reshape(block, lay.units).astype(jnp.float32)
-    both = jnp.stack([grads[layer][2][0] for layer in range(lay.sections)])
-    got = lax.all_to_all(both, ("section",), 0, 0, tiled=True)
-    out_proj = lay.restore(got.reshape(lay.unit_block, width)).astype(jnp.float32)
 
     rows = []
     for layer in range(lay.sections):
@@ -789,8 +1220,22 @@
         spots = spots.reshape(lay.sections, lay.cores, lay.rest, lay.zs, lay.half)
         spots = spots.transpose(1, 3, 2, 0, 4).reshape(lay.shards, lay.unit_block)
         rows.append(jnp.concatenate([cols, spots], axis=1))
-    rows = jnp.concatenate(rows, axis=0)
-    rows = jnp.sum(lax.all_to_all(rows, ALL, 0, 0, tiled=True), axis=0)
+    rows = jnp.stack(rows).reshape(lay.sections, lay.cores, lay.zs, lay.rest, -1)
+    used = rows.shape[-1]
+    rows = jnp.pad(jnp.swapaxes(rows, 2, 3), ((0, 0),) * 4 + ((0, -used % 1024),))
+    rows = rows.reshape(n, lay.zs, -1, 128)
+    out_qkv, out_attn, out_fc, out_proj, rows = run_end(
+        3 + 4 * lay.sections,
+        lay,
+        grad_qkv,
+        grad_out,
+        totals["qkv", 1],
+        totals["out", 1],
+        [totals["fc", layer] for layer in range(2)],
+        [totals["proj", layer] for layer in range(2)],
+        rows,
+    )
+    rows = rows.reshape(-1)[:used]
     cols = rows[: block * 8].reshape(block, 8)
     return (
         section_out,

time: 1120 us -> 1030 us (0.920)
  Pallas kernels: 569 us -> 890 us
  starting transfers between devices: 128 us -> 28.4 us
  local copies, waits for them, and re-layouts: 177 us -> 89 us
  waiting for transfers between devices: 87.6 us -> 3.57 us
  blocking collectives: 67 us -> 0 us
  other arithmetic: 57.4 us -> 8.98 us
  between operations: 15.8 us -> 2.05 us
    pallas_call x9 -> x10, Pallas kernels: 569 us -> 890 us  [the longest x8 685 us: call(): pl.pallas_call(kernel, out_shape=[jax.ShapeDtypeStruct(*o) for o in (*out...]
    ppermute x18 -> x0, waiting for transfers between devices: 69.5 us -> none  [step(): got = lax.ppermute(ring[0], 'z', route).astype(jnp.float32)]
    all_to_all x3 -> x0, blocking collectives: 67 us -> none  [the longest x2 48.1 us: move(): got = lax.all_to_all(a, SLAB, 0, 0, tiled=True)]
    ppermute x18 -> x0, starting transfers between devices: 60.2 us -> none  [step(): got = lax.ppermute(ring[0], 'z', route).astype(jnp.float32)]
    convert_element_type x9 -> x0, local copies, waits for them, and re-layouts: 39.2 us -> none  [the longest x3 18.4 us: on_device(): got.transpose(3, 1, 4, 2, 0, 5).reshape(block, lay.units)]
    all_to_all x8 -> x1, starting transfers between devices: 43.4 us -> 5.66 us  [turned(): wo = lax.all_to_all(wo, SLAB, 0, 0, tiled=True)]
    convert_element_type x15 -> x0, other arithmetic: 31.5 us -> none  [the longest x12 25.8 us: step(): ring[0] = (got + self.own(ring[1], ring[2])).astype(jnp.bfloat16)]
    reshape x24 -> x8, local copies, waits for them, and re-layouts: 34.2 us -> 7.66 us  [the longest x2 2.79 us: weight_parts(): qkv.reshape(block, 3, n, slot_cols).transpose(2, 0, 1, 3)]
  transfers between devices with their start and end apart: 44 -> 13, of which waited for: 11 -> 1; matrix products, arithmetic and copies ran while one was open for 19% -> 6% of each run, Pallas kernels for 47% -> 30%
where the time goes in v5:
time: 1030 us; the launch traced here: 1020 us
  Pallas kernels  890 us (86%)
  local copies, waits for them, and re-layouts  89 us (9%)
  starting transfers between devices  28.4 us (3%)
    pallas_call x8, Pallas kernels, call(): pl.pallas_call(kernel, out_shape=[jax.ShapeDtypeStruct(*o) for o in (*out...  685 us
    pallas_call x1, Pallas kernels, run_start(): pl.pallas_call(functools.partial(start_kernel, len(ties), lay.block), out...  107 us
    pallas_call x1, Pallas kernels, run_end(): pl.pallas_call(functools.partial(end_kernel, (block, width, lay.units, la...  97.4 us
  transfers between devices with their start and end apart: 13, of which 1 were waited for; matrix products, arithmetic and copies ran while one was open for 6% of the time, Pallas kernels for 30%

profile of v5, /device:TPU:3, one launch (start us, length us, event | category | flops | bytes accessed | tf_op | source)
XLA Modules:
  0.0 1022.0 jit_solution(7545444801409955693)
XLA Ops:
  0.7 2.2 slice_bitcast_fusion.7
  9.3 5.0 reshape_squeeze.24
  16.8 2.4 copy.144
  22.7 1.5 reshape.338
  25.3 6.6 reshape_squeeze.25
  31.9 1.7 copy.213
  33.6 2.8 reshape_reshape.10.refs_4_
  42.8 107.3 %shard_map.169 = (f32[4,2,4,16,128]{4,3,2,1,0:T(8,128)}, bf16[2,400,768]{2,1,0:T(8,128)(2,1)}, bf16[2,400,200]{2,1,0:T(8,128)(2,1)}, bf16[2,400,800]{2,1,0:T(8,1...) custom-call(f32[16,128]{1,0:T(8,128)} %fusion.5.refs_0_, ...), custom_call_target="tpu_custom_call" | custom-call | tf_op jit(solution)/shard_map/pallas_call | solution.py:888
  151.9 6.5 slice_reduce_fusion.1
  160.5 1.6 fusion.8
  165.2 1.6 reshape.299.refs_7_.refs_5_.refs_11_
  171.3 1.9 slice_bitcast_fusion.4.refs_8_
  177.2 96.9 %shard_map.170 = (bf16[4,2,128,1600]{3,2,1,0:T(8,128)(2,1)}, bf16[1024,768]{1,0:T(8,128)(2,1)}, bf16[1024,256]{1,0:T(8,128)(2,1)}, f32[8,1024]{1,0:T(8,128)}, f3...) custom-call(bf16[128,1600]{1,0:T(8,128)(2,1)} %add_convert_fusion.re, ...), custom_call_target="tpu_custom_call" | custom-call | tf_op jit(solution)/shard_map/pallas_call | solution.py:729
  274.0 69.2 %shard_map.171 = (bf16[4,2,128,1600]{3,2,1,0:T(8,128)(2,1)}, bf16[1024,800]{1,0:T(8,128)(2,1)}, bf16[1024,800]{1,0:T(8,128)(2,1)}, bf16[128,1600]{1,0:T(8,128)(2...) custom-call(bf16[128,1600]{1,0:T(8,128)(2,1)} %get-tuple-element.81.refs_0_, ...), custom_call_target="tpu_custom_call" | custom-call | tf_op jit(solution)/shard_map/pallas_call | solution.py:729
  343.2 99.4 %shard_map.172 = (bf16[4,2,128,1600]{3,2,1,0:T(8,128)(2,1)}, bf16[1024,768]{1,0:T(8,128)(2,1)}, bf16[1024,256]{1,0:T(8,128)(2,1)}, f32[8,1024]{1,0:T(8,128)}, f3...) custom-call(bf16[128,1600]{1,0:T(8,128)(2,1)} %get-tuple-element.87., ...), custom_call_target="tpu_custom_call" | custom-call | tf_op jit(solution)/shard_map/pallas_call | solution.py:729
  442.7 52.8 %shard_map.173 = (bf16[4,2,128,1600]{3,2,1,0:T(8,128)(2,1)}, bf16[1024,800]{1,0:T(8,128)(2,1)}, bf16[1024,800]{1,0:T(8,128)(2,1)}, bf16[128,1600]{1,0:T(8,128)(2,1)}, bf16[128,1600]{1,0:T(8,128)(2,1)}) custom-call(bf16[128,1600]{1,0:T(8,128)(2,1)} %get-tuple-element.91.refs_0_, f32[128,1600]{1,0:T(8,128)} %get-tuple-element.92.refs_1_, ...), custom_call_target="tpu_custom_call" | custom-call | tf_op jit(solution)/shard_map/pallas_call | solution.py:729
  495.5 56.1 %shard_map.174 = (f32[128,1600]{1,0:T(8,128)}, bf16[128,1600]{1,0:T(8,128)(2,1)}, bf16[800,1600]{1,0:T(8,128)(2,1)}, bf16[1600,800]{1,0:T(8,128)(2,1)}, f32[8,1600]{1,0:T(8,128)}, /*index=5*/f32[1,800]{1,0:T(1,128)}) custom-call(bf16[128,1600]{1,0:T(8,128)(2,1)} %copy.154.refs_6_.refs_0_, f32[128,1600]{1,0:T(8,128)} %get-tuple-element.92.refs_1_, ...), custom_call_target="tpu_custom_call" | custom-call | tf_op jit(solution)/shard_map/pallas_call | solution.py:729
  551.7 100.2 %shard_map.175 = (bf16[128,1600]{1,0:T(8,128)(2,1)}, bf16[1600,768]{1,0:T(8,128)(2,1)}, bf16[256,1600]{1,0:T(8,128)(2,1)}, f32[8,1600]{1,0:T(8,128)}, f32[1,768]...) custom-call(bf16[128,1600]{1,0:T(8,128)(2,1)} %get-tuple-element.99.refs_0_, ...), custom_call_target="tpu_custom_call" | custom-call | tf_op jit(solution)/shard_map/pallas_call | solution.py:729
  653.3 4.7 collective-permute-start.8
  659.8 2.5 collective-permute-start.4
  664.8 5.7 all-to-all-start
  670.5 80.2 %shard_map.176 = (f32[128,1600]{1,0:T(8,128)}, bf16[128,1600]{1,0:T(8,128)(2,1)}, bf16[800,1600]{1,0:T(8,128)(2,1)}, bf16[1600,800]{1,0:T(8,128)(2,1)}, f32[8,16...) custom-call(bf16[128,1600]{1,0:T(8,128)(2,1)} %get-tuple-element.107.refs_0_, ...), custom_call_target="tpu_custom_call" | custom-call | tf_op jit(solution)/shard_map/pallas_call | solution.py:729
  753.3 2.1 collective-permute-start.5
  757.8 3.5 collective-permute-done.5
  765.9 1.4 copy.177
  767.4 130.6 %shard_map.177 = (bf16[128,1600]{1,0:T(8,128)(2,1)}, bf16[1600,768]{1,0:T(8,128)(2,1)}, bf16[256,1600]{1,0:T(8,128)(2,1)}, f32[8,1600]{1,0:T(8,128)}, f32[1,768]...) custom-call(bf16[128,1600]{1,0:T(8,128)(2,1)} %get-tuple-element.112.refs_0_, ...), custom_call_target="tpu_custom_call" | custom-call | tf_op jit(solution)/shard_map/pallas_call | solution.py:729
  899.3 4.1 collective-permute-start.9
  907.7 97.4 %shard_map.178 = (f32[100,4800]{1,0:T(8,128)}, f32[100,1600]{1,0:T(8,128)}, f32[100,6400]{1,0:T(8,128)}, f32[400,1600]{1,0:T(8,128)}, f32[16,128]{1,0:T(8,128)}) custom-call(bf16[4,400,768]{2,1,0:T(8,128)(2,1)} %bitcast.200, bf16[256,1600]{1,0:T(8,128)(2,1)} %get-tuple-element.123.refs_1_, bf16[400,768]{1,0:T(8,128)(2,1)} %get-tuple-element.124.refs_2_, ...), custom_call_target="tpu_custom_call" | custom-call | tf_op jit(solution)/shard_map/pallas_call | solution.py:1046
  1005.1 6.0 copy.195
  1011.1 3.3 copy.193
  1014.4 1.5 copy.194
  1020.3 1.5 copy.242
  (253 shorter events, 59.8 us)
Async XLA Ops:
  0.6 5.0 copy-start.10
  0.7 8.6 copy-start.7
  2.9 36.3 %collective-permute-start = (bf16[128,1600]{0,1:T(8,128)(2,1)}, bf16[128,1600]{0,1:T(8,128)(2,1)}, u32[]{:S(2)}, u32[]{:S(2)}) collective-permute-start(bf16[128,1600]{0,1:T(8,128)(2,1)} %get-tuple-element.204), channel_id=1, source_target_pairs={{0,4},{1,5},{8,6},{9,7},{2,12},{3,13},{10,14},{11,15},{20,20},{21,... | collective-permute-start | bytes 1228808 | tf_op jit(solution)/shard_map/ppermute | solution.py:70
  4.3 34.9 %collective-permute-start.1 = (bf16[128,1600]{0,1:T(8,128)(2,1)}, bf16[128,1600]{0,1:T(8,128)(2,1)}, u32[]{:S(2)}, u32[]{:S(2)}) collective-permute-start(bf16[128,1600]{0,1:T(8,128)(2,1)} %get-tuple-element.203), channel_id=1, source_target_pairs={{0,0},{1,1},{8,2},{9,3},{2,8},{3,9},{10,10},{11,11},{20,16},{21,17... | collective-permute-start | bytes 1228808 | tf_op jit(solution)/shard_map/ppermute | solution.py:70
  6.6 32.6 %collective-permute-start.2 = (bf16[128,1600]{0,1:T(8,128)(2,1)}, bf16[128,1600]{0,1:T(8,128)(2,1)}, u32[]{:S(2)}, u32[]{:S(2)}) collective-permute-start(bf16[128,1600]{0,1:T(8,128)(2,1)} %get-tuple-element.202), channel_id=1, source_target_pairs={{0,4},{1,5},{8,6},{9,7},{2,12},{3,13},{10,14},{11,15},{20,20},{21,... | collective-permute-start | bytes 1228808 | tf_op jit(solution)/shard_map/ppermute | solution.py:70
  8.0 31.2 %collective-permute-start.3 = (bf16[128,1600]{0,1:T(8,128)(2,1)}, bf16[128,1600]{0,1:T(8,128)(2,1)}, u32[]{:S(2)}, u32[]{:S(2)}) collective-permute-start(bf16[128,1600]{0,1:T(8,128)(2,1)} %get-tuple-element.201), channel_id=1, source_target_pairs={{0,0},{1,1},{8,2},{9,3},{2,8},{3,9},{10,10},{11,11},{20,16},{21,17... | collective-permute-start | bytes 1228808 | tf_op jit(solution)/shard_map/ppermute | solution.py:70
  33.6 2.8 copy-start.13
  162.1 5.7 copy-start.6
  169.7 3.6 copy-start.14
  170.9 3.7 copy-start.2
  651.9 7.4 copy-start.1
  651.9 7.6 copy-start.12
  653.2 10.4 %copy-start.9 = (bf16[256,1600]{1,0:T(8,128)(2,1)S(1)}, bf16[256,1600]{1,0:T(8,128)(2,1)}, u32[]{:S(2)}) copy-start(bf16[256,1600]{1,0:T(8,128)(2,1)} %get-tuple-element.120) | copy-start | bytes 2457604
  653.3 364.8 %collective-permute-start.8 = (bf16[128,1600]{0,1:T(8,128)(2,1)S(1)}, bf16[128,1600]{0,1:T(8,128)(2,1)}, u32[]{:S(2)}, u32[]{:S(2)}) collective-permute-start(bf16[128,1600]{0,1:T(8,128)(2,1)S(1)} %bitcast.212), channel_id=1, source_target_pairs={{0,16},{1,17},{2,24},{3,25},{8,18},{9,19},{10,26},{11,27},{16,20},... | collective-permute-start | bytes 1228808 | tf_op jit(solution)/shard_map/ppermute | solution.py:84
  658.0 361.3 %collective-permute-start.10 = (bf16[128,1600]{0,1:T(8,128)(2,1)S(1)}, bf16[128,1600]{0,1:T(8,128)(2,1)S(1)}, u32[]{:S(2)}, u32[]{:S(2)}) collective-permute-start(bf16[128,1600]{0,1:T(8,128)(2,1)S(1)} %bitcast.213), channel_id=1, source_target_pairs={{4,16},{5,17},{6,24},{7,25},{12,18},{13,19},{14,26},{15,27},{20,20... | collective-permute-start | bytes 1228808 | tf_op jit(solution)/shard_map/ppermute | solution.py:84
  659.8 97.3 %collective-permute-start.4 = (bf16[128,1600]{0,1:T(8,128)(2,1)S(1)}, bf16[128,1600]{0,1:T(8,128)(2,1)}, u32[]{:S(2)}, u32[]{:S(2)}) collective-permute-start(bf16[128,1600]{0,1:T(8,128)(2,1)S(1)} %bitcast.214), channel_id=1, source_target_pairs={{0,16},{1,17},{2,24},{3,25},{8,18},{9,19},{10,26},{11,27},{16,20},... | collective-permute-start | bytes 1228808 | tf_op jit(solution)/shard_map/ppermute | solution.py:84
  662.3 100.1 %collective-permute-start.6 = (bf16[128,1600]{0,1:T(8,128)(2,1)S(1)}, bf16[128,1600]{0,1:T(8,128)(2,1)}, u32[]{:S(2)}, u32[]{:S(2)}) collective-permute-start(bf16[128,1600]{0,1:T(8,128)(2,1)S(1)} %bitcast.215), channel_id=1, source_target_pairs={{4,16},{5,17},{6,24},{7,25},{12,18},{13,19},{14,26},{15,27},{20,20... | collective-permute-start | bytes 1228808 | tf_op jit(solution)/shard_map/ppermute | solution.py:84
  664.8 99.6 %all-to-all-start = ((bf16[8,256,200]{1,2,0:T(8,128)(2,1)}), bf16[8,256,200]{1,2,0:T(8,128)(2,1)S(1)}, u32[]{:S(2)}, u32[]{:S(2)}) async-start(bf16[8,256,200]{1,2,0:T(8,128)(2,1)} %bitcast.66), calls=%async_computation | async-start | bytes 1638400 | tf_op jit(solution)/shard_map/all_to_all | solution.py:1170
  670.5 81.6 %copy-start.16 = (f32[8,1600]{1,0:T(8,128)S(1)}, f32[8,1600]{1,0:T(8,128)}, u32[]{:S(2)}) copy-start(f32[8,1600]{1,0:T(8,128)} %get-tuple-element.134) | copy-start | bytes 153604
  670.5 82.0 %copy-start.22 = (f32[1,768]{1,0:T(1,128)S(1)}, f32[1,768]{1,0:T(1,128)}, u32[]{:S(2)}) copy-start(f32[1,768]{1,0:T(1,128)} %get-tuple-element.136) | copy-start | bytes 9220
  670.5 82.6 %copy-start.15 = (f32[8,1600]{1,0:T(8,128)S(1)}, f32[8,1600]{1,0:T(8,128)}, u32[]{:S(2)}) copy-start(f32[8,1600]{1,0:T(8,128)} %get-tuple-element.135) | copy-start | bytes 153604
  751.6 4.9 copy-start.19
  752.0 4.9 copy-start.18
  753.3 8.1 collective-permute-start.5
  757.1 5.3 collective-permute-start.7
  898.0 7.3 copy-start.23
  899.3 118.8 %collective-permute-start.9 = (bf16[128,1600]{0,1:T(8,128)(2,1)S(1)}, bf16[128,1600]{0,1:T(8,128)(2,1)S(1)}, u32[]{:S(2)}, u32[]{:S(2)}) collective-permute-start(bf16[128,1600]{0,1:T(8,128)(2,1)S(1)} %bitcast.216), channel_id=1, source_target_pairs={{0,0},{1,1},{2,8},{3,9},{8,2},{9,3},{10,10},{11,11},{16,4},{17,5},... | collective-permute-start | bytes 1228808 | tf_op jit(solution)/shard_map/ppermute | solution.py:84
  903.4 115.9 %collective-permute-start.11 = (bf16[128,1600]{0,1:T(8,128)(2,1)S(1)}, bf16[128,1600]{0,1:T(8,128)(2,1)S(1)}, u32[]{:S(2)}, u32[]{:S(2)}) collective-permute-start(bf16[128,1600]{0,1:T(8,128)(2,1)S(1)} %bitcast.217), channel_id=1, source_target_pairs={{4,0},{5,1},{6,8},{7,9},{12,2},{13,3},{14,10},{15,11},{20,4},{21,5... | collective-permute-start | bytes 1228808 | tf_op jit(solution)/shard_map/ppermute | solution.py:84
  1005.1 6.0 copy-start.5
  1011.1 3.3 copy-start.11
  1011.1 4.8 copy-start.17
  1018.0 2.3 copy-start.4
  (7 other events, 12.9 us)

commit v6 on v5

--- a/solution.py
+++ b/solution.py
@@ -131,7 +131,7 @@
         every = [(x, c, r) for x in range(self.sections) for c in range(2) for r in range(self.rest)]
         return list(enumerate(every))[1:]
 
-    def greet(self, zs=1):
+    def greet(self, zs=1, work=None):
         barrier = pltpu.get_barrier_semaphore()
         z = lax.axis_index("z")
         size = lax.axis_size("z")
@@ -140,7 +140,8 @@
         others = self.offsets()
         for _, place in others:
             pl.semaphore_signal(barrier, inc=1, device_id=self.other(*place)[0], device_id_type=MESH)
-        pl.semaphore_wait(barrier, len(others) + zs - 1)
+        more = 0 if work is None else work.greet()
+        pl.semaphore_wait(barrier, len(others) + zs - 1 + more)
 
 
 def remote(src, dst, send, recv, device):
@@ -158,7 +159,7 @@
     def start(self, src):
         p = self.peers
         mine = self.full.at[p.chip, p.c]
-        mine[...] = src[...]
+        mine[...] = src if isinstance(src, jax.Array) else src[...]
         for k in range(1, p.chips):
             self.send(remote(mine, mine, self.chip_send.at[k], self.chip_recv.at[k], p.ahead(k)))
         self.send(remote(mine, mine, self.core_send.at[0], self.core_recv.at[0], p.sibling()))
@@ -238,23 +239,26 @@
 
 
 class RingGather:
-    def __init__(self, pairs, local, send, recv):
-        self.pairs, self.local, self.send_sem, self.recv_sem = pairs, local, send, recv
+    def greet(self):
+        return 0
+
+    def __init__(self, pieces, local, send, recv):
+        self.pieces, self.local, self.send_sem, self.recv_sem = pieces, local, send, recv
         self.zs, self.z = lax.axis_size("z"), lax.axis_index("z")
-        self.steps = [(p, s) for s in range(self.zs - 1) for p in range(len(pairs))]
+        self.steps = [(p, s) for s in range(self.zs - 1) for p in range(len(pieces)) if s < pieces[p][2]]
         self.sent = []
 
     def block(self, step):
         return lax.rem(self.z + self.zs - step, self.zs)
 
     def send(self, p, step, src):
-        dst = self.pairs[p][1].at[self.block(step)]
+        dst = self.pieces[p][1].at[self.block(step)]
         copy = remote(src, dst, self.send_sem.at[p, step], self.recv_sem.at[p, step], {"z": lax.rem(self.z + 1, self.zs)})
         copy.start()
         self.sent.append(copy)
 
     def start(self):
-        for p, (shard, full) in enumerate(self.pairs):
+        for p, (shard, full, _) in enumerate(self.pieces):
             self.send(p, 0, shard)
             pltpu.make_async_copy(shard, full.at[self.z], self.local.at[p]).start()
 
@@ -262,12 +266,12 @@
         if not self.steps:
             return None
         p, step = self.steps.pop(0)
-        block = self.pairs[p][1].at[self.block(step + 1)]
+        shard, full, count = self.pieces[p]
+        block = full.at[self.block(step + 1)]
         remote(block, block, self.send_sem.at[p, step], self.recv_sem.at[p, step], {"z": lax.rem(self.z + 1, self.zs)}).wait_recv()
-        if step < self.zs - 2:
+        if step < count - 1:
             self.send(p, step + 1, block)
             return None
-        shard, full = self.pairs[p]
         pltpu.make_async_copy(shard, full.at[self.z], self.local.at[p]).wait()
         return p
 
@@ -279,44 +283,119 @@
 
 
 class RingSum:
-    def __init__(self, triples, send, recv):
-        self.triples, self.send_sem, self.recv_sem = triples, send, recv
+    def greet(self):
+        return 0
+
+    def __init__(self, pieces, send, recv):
+        self.pieces, self.send_sem, self.recv_sem = pieces, send, recv
         self.zs, self.z = lax.axis_size("z"), lax.axis_index("z")
-        self.steps = [(p, s) for s in range(self.zs - 1) for p in range(len(triples))]
-        self.sent = []
-
-    def copy(self, p, step, src):
-        dst = self.triples[p][1].at[step]
-        return remote(src, dst, self.send_sem.at[p, step], self.recv_sem.at[p, step], {"z": lax.rem(self.z + 1, self.zs)})
-
-    def send(self, p, step, src):
-        copy = self.copy(p, step, src)
+        self.steps, self.sent = [], []
+        self.late = [p for p, piece in enumerate(pieces) if piece[0] is None]
+        ready = [p for p in range(len(pieces)) if p not in self.late]
+        self.steps = [(p, i) for i in range(self.zs - 1) for p in ready if i < pieces[p][5] - 1]
+        self.steps += [(p, pieces[p][5] - 1) for p in ready]
+        self.parts = [piece[0] for piece in pieces]
+
+    def copy(self, p, i, src):
+        dst = self.pieces[p][2].at[i]
+        return remote(src, dst, self.send_sem.at[p, i], self.recv_sem.at[p, i], {"z": lax.rem(self.z + 1, self.zs)})
+
+    def send(self, p, i, src):
+        copy = self.copy(p, i, src)
         copy.start()
         self.sent.append(copy)
 
+    def launch(self, p):
+        acc, first = self.pieces[p][1], self.pieces[p][4]
+        self.send(p, 0, acc if first else self.parts[p].at[lax.rem(self.z + self.zs - 1, self.zs)])
+
     def start(self):
-        for p, (part, came, out) in enumerate(self.triples):
-            self.send(p, 0, part.at[lax.rem(self.z + self.zs - 1, self.zs)])
+        for p in range(len(self.pieces)):
+            if p not in self.late:
+                self.launch(p)
+
+    def made(self, part):
+        if self.late:
+            p = self.late.pop(0)
+            self.parts[p] = part
+            self.launch(p)
+            self.steps += [(p, i) for i in range(self.pieces[p][5])]
 
     def tick(self):
         if not self.steps:
             return
-        p, step = self.steps.pop(0)
-        part, came, out = self.triples[p]
-        self.copy(p, step, came.at[step]).wait_recv()
-        own = part[lax.rem(self.z + 2 * self.zs - 2 - step, self.zs)]
-        total = (came[step].astype(F32) + own.astype(F32)).astype(BF)
-        if step < self.zs - 2:
-            came[step] = total
-            self.send(p, step + 1, came.at[step])
+        p, i = self.steps.pop(0)
+        part, acc, came, out, first, count = self.pieces[p]
+        self.copy(p, i, came.at[i]).wait_recv()
+        own = self.parts[p][lax.rem(self.z + 2 * self.zs - 2 - first - i, self.zs)]
+        total = (came[i].astype(F32) + own.astype(F32)).astype(BF)
+        if i < count - 1:
+            came[i] = total
+            self.send(p, i + 1, came.at[i])
         else:
             out[...] = total
+
+    def middle(self):
+        pass
 
     def finish(self):
         while self.steps:
             self.tick()
         for copy in self.sent:
             copy.wait_send()
+
+
+class TurnBack:
+    def __init__(self, peers, turned, part, pieces, came, send, recv):
+        self.peers, self.turned, self.part, self.pieces, self.came = peers, turned, part, pieces, came
+        self.send_sem, self.recv_sem = send, recv
+        self.sent = []
+
+    def start(self):
+        slab, _, cols = self.pieces.shape
+        for t in range(slab):
+            self.pieces[t] = self.turned[:, t * cols : (t + 1) * cols]
+        _, me = self.peers.other(0, 0, 0)
+        for i, place in self.peers.offsets():
+            device, t = self.peers.other(*place)
+            copy = remote(self.pieces.at[t], self.came.at[me], self.send_sem.at[i], self.recv_sem.at[i], device)
+            copy.start()
+            self.sent.append(copy)
+        self.came[me] = self.pieces[me]
+
+    def finish(self):
+        for i, place in self.peers.offsets():
+            device, t = self.peers.other(*(-d for d in place))
+            block = self.came.at[t]
+            remote(block, block, self.send_sem.at[i], self.recv_sem.at[i], device).wait_recv()
+        zs, rows, _ = self.part.shape
+        wide, span = rows // 2, self.came.shape[1]
+        for c in range(2):
+            for k in range(zs):
+                at, done = (c * zs + k) * wide, 0
+                while done < wide:
+                    t, row = divmod(at + done, span)
+                    count = min(wide - done, span - row)
+                    self.part[k, c * wide + done : c * wide + done + count, :] = self.came[t, row : row + count, :]
+                    done += count
+        for copy in self.sent:
+            copy.wait_send()
+
+
+class SumAndTurn:
+    def greet(self):
+        return 0
+
+    def __init__(self, ring, turn):
+        self.ring, self.turn = ring, turn
+        self.start, self.tick, self.made = ring.start, ring.tick, ring.made
+
+    def middle(self):
+        self.turn.start()
+
+    def finish(self):
+        self.turn.finish()
+        self.ring.finish()
 
 
 class Turn:
@@ -356,18 +435,125 @@
             copy.wait_send()
 
 
+class Route:
+    def __init__(self, layer, seqs, src, out, local, send, recv):
+        self.layer, self.seqs, self.src, self.out = layer, seqs, src, out
+        self.local, self.send_sem, self.recv_sem = local, send, recv
+        x, c, z = (lax.axis_index(a) for a in ("section", "dp", "z"))
+        self.here = x == layer
+        place = x * 2 + c
+        self.to = {"section": layer, "dp": lax.rem(z, seqs), "z": place}
+        self.micro = z // seqs
+        self.same = (x == layer) & (lax.rem(z, seqs) == c) & (place == z)
+        self.sources = []
+        for micro in range(out.shape[0]):
+            src_x, src_c, src_z = z // 2, lax.rem(z, 2), micro * seqs + c
+            same = (src_x == x) & (src_c == c) & (src_z == z)
+            self.sources.append(({"section": src_x, "dp": src_c, "z": src_z}, same))
+
+    def greet(self):
+        barrier = pltpu.get_barrier_semaphore()
+        for device, same in self.sources:
+
+            @pl.when(self.here & jnp.logical_not(same))
+            def _(device=device):
+                pl.semaphore_signal(barrier, inc=1, device_id=device, device_id_type=MESH)
+
+        return jnp.where(self.same, 0, 1)
+
+    def copy(self):
+        return remote(self.src, self.out.at[self.micro], self.send_sem, self.recv_sem.at[self.micro], self.to)
+
+    def own(self):
+        return pltpu.make_async_copy(self.src, self.out.at[self.micro], self.local)
+
+    def start(self):
+        @pl.when(jnp.logical_not(self.same))
+        def _():
+            self.copy().start()
+
+        @pl.when(self.same)
+        def _():
+            self.own().start()
+
+    def tick(self):
+        pass
+
+    def made(self, part):
+        pass
+
+    def middle(self):
+        pass
+
+    def finish(self):
+        for micro, (device, same) in enumerate(self.sources):
+
+            @pl.when(self.here & jnp.logical_not(same))
+            def _(micro=micro, device=device):
+                block = self.out.at[micro]
+                remote(block, block, self.send_sem, self.recv_sem.at[micro], device).wait_recv()
+
+        @pl.when(jnp.logical_not(self.same))
+        def _():
+            self.copy().wait_send()
+
+        @pl.when(self.same)
+        def _():
+            self.own().wait()
+
+
+class Several:
+    def __init__(self, works):
+        self.works = works
+
+    def greet(self):
+        return sum(work.greet() for work in self.works)
+
+    def start(self):
+        for work in self.works:
+            work.start()
+
+    def tick(self):
+        for work in self.works:
+            work.tick()
+
+    def made(self, part):
+        for work in self.works:
+            work.made(part)
+
+    def middle(self):
+        for work in self.works:
+            work.middle()
+
+    def finish(self):
+        for work in self.works:
+            work.finish()
+
+
 class NoSide:
+    def greet(self):
+        return 0
+
     def start(self):
         pass
 
     def tick(self):
         pass
 
+    def made(self, part):
+        pass
+
+    def middle(self):
+        pass
+
     def finish(self):
         pass
 
 
 class Both:
+    def greet(self):
+        return 0
+
     def __init__(self, ring, turn):
         self.ring, self.turn, self.turned = ring, turn, False
 
@@ -395,15 +581,44 @@
         return NoSide() if self.build is None else self.build(peers, ins, outs, scratch)
 
 
-def gather_side(shards, turn=None):
+def route_side(layer, lay, src):
+    dma = pltpu.SemaphoreType.DMA
+    outs = [((lay.micros, *src.shape), BF)]
+
+    def build(peers, ins, outs, scratch):
+        return Route(layer, lay.seqs, ins[0], outs[0], *scratch)
+
+    return SideWork([src], (True,), outs, (True,), [dma, dma, dma((lay.micros,))], build)
+
+
+def both_sides(*sides):
+    sides = [side for side in sides if side.build is not None]
+    joined = [[], [], [], [], []]
+    for side in sides:
+        for into, more in zip(joined, (side.operands, side.in_hbm, side.outs, side.out_hbm, side.scratch)):
+            into += list(more)
+
+    def build(peers, ins, outs, scratch):
+        works = []
+        for side in sides:
+            a, b, c = len(side.operands), len(side.outs), len(side.scratch)
+            works.append(side.build(peers, ins[:a], outs[:b], scratch[:c]))
+            ins, outs, scratch = ins[a:], outs[b:], scratch[c:]
+        return Several(works)
+
+    return SideWork(*joined, build)
+
+
+def gather_side(shards, counts=None, turn=None):
     zs = lax.axis_size("z")
     n = len(shards)
+    counts = counts or (zs - 1,) * n
     outs = [((zs, *a.shape), BF) for a in shards]
     sems = [pltpu.SemaphoreType.DMA((n,))] + [pltpu.SemaphoreType.DMA((n, zs - 1))] * 2
     if turn is None:
 
         def build(peers, ins, outs, scratch):
-            return RingGather(list(zip(ins, outs)), *scratch)
+            return RingGather(list(zip(ins, outs, counts)), *scratch)
 
         return SideWork(shards, (True,) * n, outs, (True,) * n, sems, build)
     slab = 2 * lax.axis_size("section") * lax.axis_size("r")
@@ -416,24 +631,40 @@
     ] + [pltpu.SemaphoreType.DMA((slab,))] * 2
 
     def build_turn(peers, ins, outs, scratch):
-        pairs = [(ins[0], scratch[3])] + list(zip(ins[1:], outs[1:]))
-        return Both(RingGather(pairs, *scratch[:3]), Turn(peers, scratch[3], scratch[4], scratch[5], outs[0], *scratch[6:8]))
+        pieces = list(zip(ins, [scratch[3], *outs[1:]], counts))
+        return Both(RingGather(pieces, *scratch[:3]), Turn(peers, scratch[3], scratch[4], scratch[5], outs[0], *scratch[6:8]))
 
     return SideWork(shards, (True,) * n, outs, (False,) + (True,) * (n - 1), sems + more, build_turn)
 
 
-def sum_side(parts):
+def sum_side(pieces, turned=None, cols=0):
     zs = lax.axis_size("z")
-    parts = [a.reshape(zs, a.shape[0] // zs, a.shape[1]) for a in parts]
-    n = len(parts)
-    outs = [(a.shape[1:], BF) for a in parts]
-    scratch = [pltpu.VMEM((zs - 1, *a.shape[1:]), BF) for a in parts]
+    n = len(pieces)
+    operands, outs, scratch = [], [], []
+    for part, shape, acc, first, count in pieces:
+        operands += [a for a in (part, acc) if a is not None]
+        outs.append((shape, BF))
+        scratch.append(pltpu.VMEM((count, *shape), BF))
     scratch += [pltpu.SemaphoreType.DMA((n, zs - 1))] * 2
+    if turned is not None:
+        operands.append(turned)
+        slab = turned.shape[1] // cols
+        rows = turned.shape[1] // zs
+        outs.append(((zs, rows, cols), BF))
+        scratch += [pltpu.VMEM((slab, turned.shape[0], cols), BF)] * 2 + [pltpu.SemaphoreType.DMA((slab,))] * 2
 
     def build(peers, ins, outs, scratch):
-        return RingSum(list(zip(ins, scratch[:n], outs)), *scratch[n:])
-
-    return SideWork(parts, (False,) * n, outs, (False,) * n, scratch, build)
+        ins, made = list(ins), []
+        for i, (part, shape, acc, first, count) in enumerate(pieces):
+            part_ref = None if part is None else ins.pop(0)
+            acc_ref = None if acc is None else ins.pop(0)
+            made.append((part_ref, acc_ref, scratch[i], outs[i], first, count))
+        ring = RingSum(made, *scratch[n : n + 2])
+        if turned is None:
+            return ring
+        return SumAndTurn(ring, TurnBack(peers, ins.pop(0), outs[n], *scratch[n + 2 :]))
+
+    return SideWork(operands, (False,) * len(operands), outs, (False,) * len(outs), scratch, build)
 
 
 def gather_scratch(chips, rows, width):
@@ -485,12 +716,12 @@
 
 
 def attention_forward(head, side, *refs):
-    (src, h, w_qkv, w_out, bias, col, row, vec) = refs[:8]
-    ins, refs = refs[8 : 8 + len(side.operands)], refs[8 + len(side.operands) :]
+    (h, w_qkv, w_out, bias, col, row, vec) = refs[:7]
+    ins, refs = refs[7 : 7 + len(side.operands)], refs[7 + len(side.operands) :]
     (normed, qkv, attended, logs, mid, normed_two), refs = refs[:6], refs[6:]
     side_outs, refs = refs[: len(side.outs)], refs[len(side.outs) :]
     gather_refs, reduce_refs, side_refs = refs[:5], refs[5 : 14 + 1], refs[14 + 1 :]
-    rows, width = src.shape
+    rows, width = h.shape
     span = w_out.shape[0]
     peers = Peers()
     gather = Gather(peers, gather_refs[0], gather_refs[1:])
@@ -498,8 +729,8 @@
     kept_sem = reduce_refs[9]
     full = gather.full
     work = side.make(peers, ins, side_outs, side_refs)
-    peers.greet(side.zs)
-    gather.start(src)
+    peers.greet(side.zs, work)
+    gather.start((norm_parts(h[...].astype(F32))[0] * vec[0:1, :] + vec[2:3, :]).astype(BF))
     work.start()
     for k, chip in gather.arrivals():
         part = dot(full[chip].reshape(2 * rows, width), w_qkv[...]) + bias[...]
@@ -548,41 +779,61 @@
 
 
 def feed_forward(side, *refs):
-    (src, mid, w_fc, w_proj, bias, vec, next_vec) = refs[:7]
-    ins, refs = refs[7 : 7 + len(side.operands)], refs[7 + len(side.operands) :]
-    (normed_two, slope, activated, result, normed), refs = refs[:5], refs[5:]
+    (src, mid, w_fc, w_proj, bias, vec) = refs[:6]
+    ins, refs = refs[6 : 6 + len(side.operands)], refs[6 + len(side.operands) :]
+    (normed_two, slope, activated, result, proj_out), refs = refs[:5], refs[5:]
     side_outs, refs = refs[: len(side.outs)], refs[len(side.outs) :]
-    gather_refs, reduce_refs, side_refs = refs[:5], refs[5 : 14 + 1], refs[14 + 1 :]
+    gather_refs, reduce_refs, side_refs = refs[:5], refs[5 : 14 + 6], refs[14 + 6 :]
     rows, width = src.shape
     peers = Peers()
     gather = Gather(peers, gather_refs[0], gather_refs[1:])
     reduce = Reduce(peers, *reduce_refs[:5], reduce_refs[5:9])
-    kept_sem = reduce_refs[9]
+    kept_sem, proj, proj_local, proj_send, proj_recv, proj_sem = reduce_refs[9:15]
     full = gather.full
     work = side.make(peers, ins, side_outs, side_refs)
-    peers.greet(side.zs)
+    zs, z = lax.axis_size("z"), lax.axis_index("z")
+    half = proj.shape[1]
+    peers.greet(2, work)
     gather.start(src)
-    work.start()
+    there = lax.rem(z + 2, zs)
+    last = remote(w_proj.at[there], proj.at[there], proj_send, proj_recv, {"z": lax.rem(z + 1, zs)})
+    last.start()
+    here = [lax.rem(z + zs - i, zs) for i in range(zs - 1)]
+    placed = [pltpu.make_async_copy(w_proj.at[b], proj.at[b], proj_local.at[i]) for i, b in enumerate(here)]
+    for copy in placed:
+        copy.start()
     before = None
     for k, chip in gather.arrivals():
+        if k == 0:
+            last.wait_recv()
+            work.start()
+            for copy in placed:
+                copy.wait()
+            proj_kept = pltpu.make_async_copy(proj, proj_out, proj_sem)
+            proj_kept.start()
         here = chip_rows(chip, rows)
         u = dot(full[chip].reshape(2 * rows, width), w_fc[...]) + bias[...]
         bend = jnp.tanh(ROOT * (u + 0.044715 * (u * u * u)))
         slope[here, :] = (0.5 * (1.0 + bend) + 0.5 * u * (1.0 - bend * bend) * (ROOT * (1.0 + 3 * 0.044715 * (u * u)))).astype(BF)
         act = (0.5 * u * (1.0 + bend)).astype(BF)
         activated[here, :] = act
-        reduce.put(k, dot(act, w_proj[...]))
+        back = dot(act[:, :half], proj[0])
+        for b in range(1, zs):
+            back = back + dot(act[:, b * half : (b + 1) * half], proj[b])
+        reduce.put(k, back)
         if before is not None:
             reduce.push(before)
-        if k:
+        if k == peers.chips - 1:
             work.tick()
         before = k
     kept = pltpu.make_async_copy(full, normed_two, kept_sem)
     kept.start()
     reduce.push(before)
+    work.tick()
     out = (mid[...] + (reduce.total() + vec[5:6, :])).astype(BF)
     result[...] = out
-    normed[...] = (norm_parts(out.astype(F32))[0] * next_vec[0:1, :] + next_vec[2:3, :]).astype(BF)
+    last.wait_send()
+    proj_kept.wait()
     work.finish()
     gather.finish()
     reduce.finish()
@@ -607,7 +858,7 @@
     reduce = Reduce(peers, *reduce_refs[:5], reduce_refs[5:9])
     full = gather.full
     work = side.make(peers, ins, side_outs, side_refs)
-    peers.greet(side.zs)
+    peers.greet(side.zs, work)
     gather.start(src)
     work.start()
     before = None
@@ -619,17 +870,21 @@
         reduce.put(k, dot(back, w_fc[...], 1, 1))
         if before is not None:
             reduce.push(before)
-        if k > 1:
+        if k == peers.chips - 1:
             work.tick()
         before = k
     reduce.push(before)
+    work.middle()
     branch = full[...].reshape(tokens, width)
-    for a, b in chunks(activated.shape[1], 256):
-        grad_proj[a:b, :] = dot(activated[:, a:b], branch, 0, 0).astype(BF)
+    half = grad_proj.shape[1]
+    for b in range(grad_proj.shape[0]):
+        grad_proj[b] = dot(activated[:, b * half : (b + 1) * half], branch, 0, 0).astype(BF)
+    work.made(grad_proj)
     work.tick()
     back = hidden[...]
     for a, b in chunks(width, 512):
         grad_fc[a:b, :] = dot(normed_two[:, a:b], back, 0, 0).astype(BF)
+    work.tick()
     unit_sums[...] = jnp.sum(back.astype(F32), axis=0, keepdims=True)
     own = src[...].astype(F32)
     part, gain, shift = norm_back(mid[...], vec[1:2, :], reduce.total())
@@ -662,7 +917,7 @@
     reduce = Reduce(peers, *reduce_refs[:5], reduce_refs[5:9])
     full = gather.full
     work = side.make(peers, ins, side_outs, side_refs)
-    peers.greet(side.zs)
+    peers.greet(side.zs, work)
     gather.start(src)
     work.start()
     for k, chip in gather.arrivals():
@@ -695,7 +950,7 @@
             else:
                 key_sum[:, lanes] += key_term
                 value_sum[:, lanes] += value_term
-        if k:
+        if k == peers.chips - 1:
             work.tick()
     joint[:, span : 2 * span] = key_sum[...].astype(BF)
     joint[:, 2 * span :] = value_sum[...].astype(BF)
@@ -710,6 +965,7 @@
     grads = joint[...]
     for a, b in chunks(width, 512):
         grad_qkv[a:b, :] = dot(normed[:, a:b], grads, 0, 0).astype(BF)
+    work.tick()
     grad_out[...] = dot(attended[...], full[...].reshape(tokens, width), 0, 0).astype(BF)
     head_sums[...] = jnp.sum(grads.astype(F32), axis=0, keepdims=True)
     part, gain, shift = norm_back(h[...].astype(F32), vec[0:1, :], reduce.total())
@@ -722,14 +978,14 @@
     reduce.finish()
 
 
-def call(kernel, name, outs, operands, side, kept, scratch):
+def call(kernel, name, outs, operands, side, kept, scratch, far=()):
     chips = lax.axis_size("section") * lax.axis_size("r")
     rows, width = operands[0].shape
     vmem, hbm = pl.BlockSpec(memory_space=pltpu.VMEM), pl.BlockSpec(memory_space=pl.ANY)
     out = pl.pallas_call(
         kernel,
         out_shape=[jax.ShapeDtypeStruct(*o) for o in (*outs, *side.outs)],
-        in_specs=[vmem] * len(operands) + [hbm if i else vmem for i in side.in_hbm],
+        in_specs=[hbm if i in far else vmem for i in range(len(operands))] + [hbm if i else vmem for i in side.in_hbm],
         out_specs=[hbm if i in kept else vmem for i in range(len(outs))] + [hbm if i else vmem for i in side.out_hbm],
         scratch_shapes=gather_scratch(chips, rows, width) + reduce_scratch(chips, rows, width) + scratch + list(side.scratch),
         compiler_params=pltpu.CompilerParams(collective_id=name, has_side_effects=True, vmem_limit_bytes=60 * 2**20),
@@ -738,8 +994,8 @@
 
 
 def run_attention_forward(name, head, side, *operands):
-    src, h, w_qkv, w_out, bias, col, row, vec = operands
-    rows, width = src.shape
+    h, w_qkv, w_out, bias, col, row, vec = operands
+    rows, width = h.shape
     tokens, span = col.shape[0], w_out.shape[0]
     slots = -(-(span // head) // 8) * 8
     chips = tokens // (2 * rows)
@@ -755,7 +1011,7 @@
 
 
 def run_feed_forward(name, side, *operands):
-    src, mid, w_fc, w_proj, bias, vec, next_vec = operands
+    src, mid, w_fc, w_proj, bias, vec = operands
     rows, width = src.shape
     units = w_fc.shape[1]
     chips = lax.axis_size("section") * lax.axis_size("r")
@@ -765,19 +1021,22 @@
         ((tokens, units), BF),
         ((tokens, units), BF),
         ((rows, width), BF),
-        ((rows, width), BF),
+        (w_proj.shape, BF),
     ]
-    return call(functools.partial(feed_forward, side), name, outs, operands, side, (0,), [pltpu.SemaphoreType.DMA])
+    dma = pltpu.SemaphoreType.DMA
+    scratch = [dma, pltpu.VMEM(w_proj.shape, BF), dma((w_proj.shape[0],)), dma, dma, dma]
+    return call(functools.partial(feed_forward, side), name, outs, operands, side, (0, 4), scratch, (3,))
 
 
 def run_feed_backward(name, side, *operands):
     src, mid, w_fc, w_proj, slope, activated, normed_two, vec = operands
     rows, width = src.shape
     tokens, units = slope.shape
+    zs = lax.axis_size("z")
     outs = [
         ((rows, width), F32),
         ((rows, width), BF),
-        ((units, width), BF),
+        ((zs, units // zs, width), BF),
         ((width, units), BF),
         ((8, width), F32),
         ((1, units), F32),
@@ -800,17 +1059,87 @@
     return call(functools.partial(attention_backward, head, side), name, outs, operands, side, (), scratch)
 
 
-def start_kernel(ties, block, *refs):
-    (tiny, qkv_src, wo_src, fc_src, proj_src), refs = refs[:5], refs[5 + ties :]
-    (tiny_out, qkv, wo, fc, proj, qkv_full, w_out), refs = refs[:7], refs[7:]
-    stage, qkv_land, wo_land, fc_land, wo_full, nat, land = refs[:7]
-    z_send, z_recv, *sems = refs[7:13]
-    all_send, all_recv, far_send, far_recv, turn_send, turn_recv, ring_local, ring_send, ring_recv = refs[13:]
+class RouteIn:
+    def __init__(self, seqs, pairs, local, send, recv):
+        self.pairs, self.local, self.send_sem, self.recv_sem = pairs, local, send, recv
+        x, c, z = (lax.axis_index(a) for a in ("section", "dp", "z"))
+        self.sends = z // 2 == x
+        self.targets = []
+        for micro in range(pairs[0][0].shape[0]):
+            to_c, to_z = lax.rem(z, 2), micro * seqs + c
+            self.targets.append(({"dp": to_c, "z": to_z}, (to_c == c) & (to_z == z)))
+        self.micro = z // seqs
+        self.source = {"dp": lax.rem(z, seqs), "z": x * 2 + c}
+        self.same = (lax.rem(z, seqs) == c) & (x * 2 + c == z)
+
+    def greet(self):
+        barrier = pltpu.get_barrier_semaphore()
+
+        @pl.when(jnp.logical_not(self.same))
+        def _():
+            pl.semaphore_signal(barrier, inc=1, device_id=self.source, device_id_type=MESH)
+
+        return sum(jnp.where(self.sends & jnp.logical_not(same), 1, 0) for _, same in self.targets)
+
+    def far(self, i, micro):
+        src, dst = self.pairs[i]
+        return remote(src.at[micro], dst, self.send_sem.at[i, micro], self.recv_sem.at[i], self.targets[micro][0])
+
+    def near(self, i, micro):
+        src, dst = self.pairs[i]
+        return pltpu.make_async_copy(src.at[micro], dst, self.local.at[i])
+
+    def start(self, i):
+        for micro, (_, same) in enumerate(self.targets):
+
+            @pl.when(self.sends & jnp.logical_not(same))
+            def _(micro=micro):
+                self.far(i, micro).start()
+
+            @pl.when(self.sends & same)
+            def _(micro=micro):
+                self.near(i, micro).start()
+
+    def arrived(self, i):
+        dst = self.pairs[i][1]
+
+        @pl.when(jnp.logical_not(self.same))
+        def _():
+            remote(dst, dst, self.send_sem.at[i, 0], self.recv_sem.at[i], self.source).wait_recv()
+
+        for micro, (_, same) in enumerate(self.targets):
+
+            @pl.when(self.sends & same)
+            def _(micro=micro):
+                self.near(i, micro).wait()
+
+    def finish(self):
+        for i in range(len(self.pairs)):
+            for micro, (_, same) in enumerate(self.targets):
+
+                @pl.when(self.sends & jnp.logical_not(same))
+                def _(i=i, micro=micro):
+                    self.far(i, micro).wait_send()
+
+
+def start_kernel(sizes, *refs):
+    block, span, half, seqs, micros = sizes
+    (tiny, w_qkv, w_attn, w_fc, w_proj, inputs, cotangent), refs = refs[:7], refs[7:]
+    (qkv, wo, fc, proj, qkv_full, w_out, h, g, row, *smalls), refs = refs[:15], refs[15:]
+    tiny_out, stage, h_raw, g_raw, natural, proj_cut = refs[:6]
+    cuts, lands, (wo_full, nat, land), refs = refs[6:9], refs[9:12], refs[12:15], refs[15:]
+    z_send, z_recv, *sems = refs[:6]
+    all_send, all_recv, far_send, far_recv, turn_send, turn_recv = refs[6:12]
+    ring_local, ring_send, ring_recv, *route_sems = refs[12:]
     peers = Peers()
     zs, z = lax.axis_size("z"), lax.axis_index("z")
-    x, rest = peers.x, peers.rest
+    x, rest, slab = peers.x, peers.rest, 2 * peers.chips
+    sections = peers.sections
     spot = peers.c * rest + peers.r
-    peers.greet(zs)
+    width, wide = w_attn.shape[1], rest * block
+    _, me = peers.other(0, 0, 0)
+    route = RouteIn(seqs, [(inputs, h_raw), (cotangent, g_raw)], *route_sems)
+    peers.greet(zs, route)
     sent = []
 
     def send(copy):
@@ -820,98 +1149,167 @@
     for k in range(1, zs):
         send(remote(tiny, stage.at[z], z_send.at[k], z_recv.at[k], {"z": lax.rem(z + k, zs)}))
     stage[z] = tiny[...]
-    moves = [(wo_src, wo_land), (qkv_src, qkv_land), (fc_src, fc_land)]
-    for a, (src, dst) in enumerate(moves):
+    route.start(0)
+
+    def share(a):
         for i, place in peers.offsets():
             device, t = peers.other(*place)
-            send(remote(src.at[t], dst.at[x, spot], all_send.at[a, i], all_recv.at[a, i], device))
-        if a == 1:
-            for k in range(1, zs):
-                came = stage.at[lax.rem(z + zs - k, zs)]
-                remote(came, came, z_send.at[k], z_recv.at[k], {"z": lax.rem(z + k, zs)}).wait_recv()
-            gather = Gather(peers, tiny_out, sems)
-            gather.start(stage)
-    for d in range(1, peers.sections):
-        device, _ = peers.other(d, 0, 0)
-        there = lax.rem(x + d, peers.sections)
-        send(remote(proj_src.at[there], proj.at[x], far_send.at[d], far_recv.at[d], device))
-    _, me = peers.other(0, 0, 0)
-    own = []
-    for a, (src, dst) in enumerate(moves):
-        own.append(pltpu.make_async_copy(src.at[me], dst.at[x, spot], all_recv.at[a, 0]))
-    own.append(pltpu.make_async_copy(proj_src.at[x], proj.at[x], far_recv.at[0]))
-    for copy in own:
-        copy.start()
+            send(remote(cuts[a].at[t], lands[a].at[x, spot], all_send.at[a, i], all_recv.at[a, i], device))
+        lands[a][x, spot] = cuts[a][me]
 
     def settle(a, shard):
-        dst = moves[a][1]
         for i, place in peers.offsets():
             device, _ = peers.other(*(-d for d in place))
-            came = dst.at[device["section"], device["dp"] * rest + device["r"]]
+            came = lands[a].at[device["section"], device["dp"] * rest + device["r"]]
             remote(came, came, all_send.at[a, i], all_recv.at[a, i], device).wait_recv()
-        own[a].wait()
-        for layer in range(peers.sections):
+        for layer in range(sections):
             for i in range(2 * rest):
-                shard[layer, i * block : (i + 1) * block, :] = dst[layer, i, :block, :]
-
+                shard[layer, i * block : (i + 1) * block, :] = lands[a][layer, i, :block, :]
+
+    cols = width // slab
+    for t in range(slab):
+        big, off = divmod(t * cols, wide)
+        at = (big % 2 * zs + big // 2) * wide + off
+        cuts[0][t, :block, :] = w_attn[:, at : at + cols]
+    share(0)
+    for t in range(slab):
+        count = max(0, min(span, width - t * span))
+        for p in range(3):
+            if count:
+                at = p * width + t * span
+                cuts[1][t, :block, p * span : p * span + count] = w_qkv[:, at : at + count]
+            if count < span:
+                cuts[1][t, :block, p * span + count : (p + 1) * span] = jnp.zeros((block, span - count), BF)
+    share(1)
+    for t in range(slab):
+        a, c, r = t // (2 * rest), t // rest % 2, t % rest
+        for k in range(zs):
+            at = ((c * zs + k) * rest + r) * (sections * half) + a * half
+            cuts[2][t, :block, k * half : (k + 1) * half] = w_fc[:, at : at + half]
+    for a in range(sections):
+        for c in range(2):
+            for k in range(zs):
+                at, to = (c * zs + k) * wide, (k * 2 + c) * wide
+                proj_cut[a, :, to : to + wide] = w_proj[a * half : (a + 1) * half, at : at + wide]
+    for k in range(1, zs):
+        came = stage.at[lax.rem(z + zs - k, zs)]
+        remote(came, came, z_send.at[k], z_recv.at[k], {"z": lax.rem(z + k, zs)}).wait_recv()
+    gather = Gather(peers, tiny_out, sems)
+    gather.start(stage)
     settle(0, wo)
     settle(1, qkv)
     turn = Turn(peers, wo_full, nat, land, w_out, turn_send, turn_recv)
-    ring = RingGather([(wo.at[0], wo_full), (qkv.at[0], qkv_full)], ring_local, ring_send, ring_recv)
+    ring = RingGather([(wo.at[0], wo_full, zs - 1), (qkv.at[0], qkv_full, zs - 1)], ring_local, ring_send, ring_recv)
     work = Both(ring, turn)
     work.start()
+    share(2)
+    for d in range(1, sections):
+        device, _ = peers.other(d, 0, 0)
+        there = lax.rem(x + d, sections)
+        send(remote(proj_cut.at[there], proj.at[x], far_send.at[d], far_recv.at[d], device))
+    proj[x] = proj_cut[x]
+    route.start(1)
     for _ in gather.arrivals():
         pass
+
+    per_row, halves = sections * half // block, half // block
+    for layer in range(sections):
+        vec, bias, unit = smalls[3 * layer : 3 * layer + 3]
+        natural[...] = jnp.zeros_like(natural)
+        for c in range(2):
+            for k in range(zs):
+                for r in range(rest):
+                    at = ((k * 2 + c) * rest + r) * block
+                    vec[:, at : at + block] = tiny_out[layer * rest + r, c, k, 0:8, :block]
+                    at = ((c * zs + k) * rest + r) * block
+                    natural[:, at : at + block] = tiny_out[layer * rest + r, c, k, 0:8, :block]
+        own = jnp.zeros((8, span), F32)
+        for t in range(slab):
+            own = jnp.where(me == t, natural[:, t * span : (t + 1) * span], own)
+        bias[:, :span] = own[6:7]
+        bias[:, span : 2 * span] = jnp.zeros((1, span), F32)
+        bias[:, 2 * span :] = own[7:8]
+        for k in range(zs):
+            for j in range(halves):
+                line = tiny_out[layer * rest + peers.r, peers.c, k, pl.ds(8 + x * halves + j, 1), :block]
+                unit[:, k * half + j * block : k * half + (j + 1) * block] = line
+    rows = h.shape[0]
+    for a in range(sections):
+        for r in range(rest):
+            for c in range(2):
+                at = ((a * rest + r) * 2 + c) * rows
+                line = tiny_out[r, 0, a * 2 + c, pl.ds(8 + per_row + z // seqs, 1), :rows]
+                row[:, at : at + rows] = line.astype(jnp.int32)
+    work.tick()
     settle(2, fc)
-    for d in range(1, peers.sections):
+    work.tick()
+    for i, (raw, ordered) in enumerate([(h_raw, h), (g_raw, g)]):
+        route.arrived(i)
+        for c in range(2):
+            for k in range(zs):
+                at, to = (c * zs + k) * wide, (k * 2 + c) * wide
+                ordered[:, to : to + wide] = raw[:, at : at + wide]
+    for d in range(1, sections):
         device, _ = peers.other(-d, 0, 0)
         came = proj.at[device["section"]]
         remote(came, came, far_send.at[d], far_recv.at[d], device).wait_recv()
-    own[3].wait()
     work.finish()
+    route.finish()
     gather.finish()
     for copy in sent:
         copy.wait_send()
 
 
-def run_start(name, lay, ties, tiny, qkv, wo, fc, proj):
-    zs, n, chips = lay.zs, lay.slab, lay.slab // 2
-    span = lay.slots * lay.head
+def run_start(name, lay, tiny, w_qkv, w_attn, w_fc, w_proj, inputs, cotangent):
+    zs, n, chips, sections = lay.zs, lay.slab, lay.slab // 2, lay.sections
+    span, block = lay.slots * lay.head, lay.block
     spots = lay.cores * lay.rest
-    rows = spots * lay.block
+    rows, tall = spots * block, -(-block // 16) * 16
     vmem, hbm = pl.BlockSpec(memory_space=pltpu.VMEM), pl.BlockSpec(memory_space=pl.ANY)
-    widths = [a.shape[2] for a in (qkv, wo, fc)]
-    outs = [((chips, 2, zs, *tiny.shape), F32)]
-    outs += [((lay.sections, rows, m), BF) for m in widths]
-    outs += [(proj.shape, BF), ((zs, rows, widths[0]), BF), ((span, lay.width), BF)]
+    units = lay.units // n
+    widths = [lay.cols, 3 * span, units]
+    flat = inputs.shape[1:]
+    outs = [((sections, rows, m), BF) for m in (3 * span, lay.cols, units)]
+    outs += [((sections, lay.half, lay.width), BF), ((zs, rows, 3 * span), BF), ((span, lay.width), BF)]
+    outs += [(flat, BF), (flat, BF), ((1, lay.tokens), jnp.int32)]
+    outs += [((8, lay.width), F32), ((1, 3 * span), F32), ((1, units), F32)] * sections
     dma = pltpu.SemaphoreType.DMA
     return pl.pallas_call(
-        functools.partial(start_kernel, len(ties), lay.block),
+        functools.partial(start_kernel, (block, span, lay.half, lay.seqs, lay.micros)),
         out_shape=[jax.ShapeDtypeStruct(*o) for o in outs],
-        in_specs=[vmem] + [hbm] * (4 + len(ties)),
-        out_specs=[vmem] * 5 + [hbm, vmem],
-        scratch_shapes=[pltpu.VMEM((zs, *tiny.shape), F32)]
-        + [pltpu.VMEM((lay.sections, spots, qkv.shape[1], m), BF) for m in widths]
-        + [pltpu.VMEM((zs, rows, widths[1]), BF), pltpu.VMEM((n * span, widths[1]), BF), pltpu.VMEM((n, span, widths[1]), BF)]
+        in_specs=[vmem] * 5 + [hbm] * 2,
+        out_specs=[vmem] * 4 + [hbm] + [vmem] * (4 + 3 * sections),
+        scratch_shapes=[
+            pltpu.VMEM((chips, 2, zs, *tiny.shape), F32),
+            pltpu.VMEM((zs, *tiny.shape), F32),
+            pltpu.VMEM(flat, BF),
+            pltpu.VMEM(flat, BF),
+            pltpu.VMEM((8, n * span), F32),
+            pltpu.VMEM((sections, lay.half, lay.width), BF),
+        ]
+        + [pltpu.VMEM((n, tall, m), BF) for m in widths]
+        + [pltpu.VMEM((sections, spots, tall, m), BF) for m in widths]
+        + [pltpu.VMEM((zs, rows, lay.cols), BF), pltpu.VMEM((n * span, lay.cols), BF), pltpu.VMEM((n, span, lay.cols), BF)]
         + [dma((zs,))] * 2
         + [dma((chips,))] * 4
         + [dma((3, n))] * 2
-        + [dma((lay.sections,))] * 2
+        + [dma((sections,))] * 2
         + [dma((n,))] * 2
         + [dma((2,))]
-        + [dma((2, zs - 1))] * 2,
+        + [dma((2, zs - 1))] * 2
+        + [dma((2,)), dma((2, lay.micros)), dma((2,))],
         compiler_params=pltpu.CompilerParams(collective_id=name, has_side_effects=True, vmem_limit_bytes=60 * 2**20),
-    )(tiny, qkv, wo, fc, proj, *ties)
+    )(tiny, w_qkv, w_attn, w_fc, w_proj, inputs, cotangent)
 
 
 def end_kernel(sizes, *refs):
-    block, width, units, heads = sizes
-    (part, turned, qkv_one, wo_one, fc_zero, fc_one, proj_zero, proj_one, small), refs = refs[:9], refs[9:]
-    (out_qkv, out_wo, out_fc, out_proj, out_small), refs = refs[:5], refs[5:]
+    block, width, units, seqs = sizes
+    (part, turned, qkv_one, wo_one, fc_zero, fc_one, proj_zero, proj_one, small, last_rows), refs = refs[:10], refs[10:]
+    (out_qkv, out_wo, out_fc, out_proj, out_small, out_rows), refs = refs[:6], refs[6:]
     (qkv_total, wo_part, wo_total, wo_cut, wo_back, proj_both, proj_land), refs = refs[:7], refs[7:]
     stages, lands, refs = refs[:3], refs[3:6], refs[6:]
     (small_land, small_sum, z_land, came_qkv, came_wo), refs = refs[:5], refs[5:]
-    all_send, all_recv, far_send, far_recv, z_send, z_recv, turn_send, turn_recv, ring_send, ring_recv, late_send, late_recv = refs
+    all_send, all_recv, far_send, far_recv, z_send, z_recv, turn_send, turn_recv, ring_send, ring_recv, late_send, late_recv, *route_sems = refs
     peers = Peers()
     zs, z = lax.axis_size("z"), lax.axis_index("z")
     x, rest, slab = peers.x, peers.rest, 2 * peers.chips
@@ -920,21 +1318,18 @@
     half, wide = proj_zero.shape[0], rest * block
     _, me = peers.other(0, 0, 0)
     offsets = peers.offsets()
-    peers.greet(zs)
+    route = Route(0, seqs, last_rows, out_rows, *route_sems)
+    peers.greet(zs, route)
     sent = []
 
     def send(copy):
         copy.start()
         sent.append(copy)
 
-    ring = RingSum([(part, came_qkv, qkv_total)], ring_send, ring_recv)
+    ring = RingSum([(part, None, came_qkv, qkv_total, 0, zs - 1)], ring_send, ring_recv)
     ring.start()
-    for t in range(slab):
-        wo_cut[t] = turned[:, t * cols : (t + 1) * cols]
-    for i, place in offsets:
-        device, t = peers.other(*place)
-        send(remote(wo_cut.at[t], wo_back.at[me], turn_send.at[i], turn_recv.at[i], device))
-    wo_back[me] = wo_cut[me]
+    turn = TurnBack(peers, turned, wo_part, wo_cut, wo_back, turn_send, turn_recv)
+    turn.start()
     for i, place in offsets:
         device, t = peers.other(*place)
         send(remote(small.at[t], small_land.at[me], all_send.at[3, i], all_recv.at[3, i], device))
@@ -956,6 +1351,7 @@
             came = land.at[t]
             remote(came, came, all_send.at[a, i], all_recv.at[a, i], device).wait_recv()
 
+    route.start()
     cut(0, (fc_zero, fc_one))
     proj_both[0] = proj_zero[...]
     proj_both[1] = proj_one[...]
@@ -963,19 +1359,8 @@
     send(remote(proj_both.at[1 - x], proj_land.at[x], far_send, far_recv, device))
     proj_land[x] = proj_both[x]
 
-    for i, place in offsets:
-        device, t = peers.other(*(-d for d in place))
-        came = wo_back.at[t]
-        remote(came, came, turn_send.at[i], turn_recv.at[i], device).wait_recv()
-    for c in range(2):
-        for k in range(zs):
-            at, done = (c * zs + k) * wide, 0
-            while done < wide:
-                t, row = divmod(at + done, span)
-                count = min(wide - done, span - row)
-                wo_part[k, c * wide + done : c * wide + done + count, :] = wo_back[t, row : row + count, :]
-                done += count
-    wo_ring = RingSum([(wo_part, came_wo, wo_total)], late_send, late_recv)
+    turn.finish()
+    wo_ring = RingSum([(wo_part, None, came_wo, wo_total, 0, zs - 1)], late_send, late_recv)
     wo_ring.start()
     settle(3, small_land)
     total = small_land[0]
@@ -1026,14 +1411,14 @@
             if count > 0:
                 at = p * width + t * span
                 out_qkv[:, at : at + count] = lands[1][t, :block, p * span : p * span + count].astype(F32)
+    route.finish()
     for copy in sent:
         copy.wait_send()
 
 
-def run_end(name, lay, part, turned, qkv_one, wo_one, fcs, projs, small):
+def run_end(name, lay, part, turned, qkv_one, wo_one, fcs, projs, small, last_rows):
     zs, n = lay.zs, lay.slab
     span, width, block = lay.slots * lay.head, lay.width, lay.block
-    part = part.reshape(zs, part.shape[0] // zs, part.shape[1])
     rows = part.shape[1]
     spots = lay.cores * lay.rest
     tall = -(-block // 16) * 16
@@ -1044,10 +1429,11 @@
     tile = small.shape[2:]
     outs = [(block, 3 * width), (block, width), (block, lay.units), (lay.unit_block, width), tile]
     return pl.pallas_call(
-        functools.partial(end_kernel, (block, width, lay.units, lay.slots)),
-        out_shape=[jax.ShapeDtypeStruct(o, F32) for o in outs],
-        in_specs=[vmem] * 9,
-        out_specs=[vmem] * 5,
+        functools.partial(end_kernel, (block, width, lay.units, lay.seqs)),
+        out_shape=[jax.ShapeDtypeStruct(o, F32) for o in outs]
+        + [jax.ShapeDtypeStruct((lay.micros, *last_rows.shape), BF)],
+        in_specs=[vmem] * 9 + [pl.BlockSpec(memory_space=pl.ANY)],
+        out_specs=[vmem] * 5 + [pl.BlockSpec(memory_space=pl.ANY)],
         scratch_shapes=[
             pltpu.VMEM((rows, part.shape[2]), BF),
             pltpu.VMEM((zs, rows, lay.cols), BF),
@@ -1070,25 +1456,35 @@
         + [dma] * 2
         + [dma((zs,))] * 2
         + [dma((n,))] * 2
-        + [dma((1, zs - 1))] * 4,
+        + [dma((2, zs - 1))] * 4
+        + [dma, dma, dma((lay.micros,))],
         compiler_params=pltpu.CompilerParams(collective_id=name, has_side_effects=True, vmem_limit_bytes=60 * 2**20),
-    )(part, turned, qkv_one, wo_one, *fcs, *projs, small)
-
-
-def weight_parts(lay, w_qkv, w_attn_out, w_fc, w_proj):
-    n = lay.slab
-    width, block = lay.width, lay.block
-    slot_cols = lay.slots * lay.head
-    qkv = w_qkv[0].reshape(block, 3, width)
-    qkv = jnp.pad(qkv, ((0, 0), (0, 0), (0, n * slot_cols - width)))
-    qkv = qkv.reshape(block, 3, n, slot_cols).transpose(2, 0, 1, 3).reshape(n, block, 3 * slot_cols)
-    out = lay.order(w_attn_out[0]).reshape(block, n, lay.cols).transpose(1, 0, 2)
-    fc = w_fc[0].reshape(block, lay.cores, lay.zs, lay.rest, lay.sections, lay.half)
-    fc = fc.transpose(4, 1, 3, 0, 2, 5).reshape(n, block, lay.zs * lay.half)
-    proj = lay.order(w_proj[0]).reshape(lay.sections, lay.half, width)
-
-    spare = ((0, 0), (0, -block % 16), (0, 0))
-    return jnp.pad(qkv, spare), jnp.pad(out, spare), jnp.pad(fc, spare), proj
+    )(part, turned, qkv_one, wo_one, *fcs, *projs, small, last_rows)
+
+
+class Rings:
+    def __init__(self, lay):
+        self.zs = lay.zs
+        self.state = {}
+
+    def put(self, kind, layer, part):
+        if part.ndim == 2:
+            part = part.reshape(self.zs, part.shape[0] // self.zs, part.shape[1])
+        _, acc, steps = self.state.get((kind, layer), (None, None, 0))
+        self.state[kind, layer] = (part, acc, steps)
+
+    def side(self, plan, makes={}, turned=None, cols=0):
+        pieces = []
+        for kind, layer, count in plan:
+            part, acc, steps = self.state.get((kind, layer), (None, None, 0))
+            shape = makes[kind] if part is None else part.shape[1:]
+            pieces.append((part, shape, acc, steps, count))
+        return sum_side(pieces, turned, cols)
+
+    def done(self, plan, outs):
+        for (kind, layer, count), acc in zip(plan, outs):
+            part, _, steps = self.state[kind, layer]
+            self.state[kind, layer] = (part, acc, steps + count)
 
 
 def on_device(
@@ -1097,43 +1493,19 @@
     lay = Layout(inputs, w_fc)
     n, block, width = lay.slab, lay.block, lay.width
     span = lay.slots * lay.head
-    micro = lay.z // lay.seqs
-
-    sources = weight_parts(lay, w_qkv, w_attn_out, w_fc, w_proj)
-    h = lay.order(lay.tokens_in(inputs))
-    g = lay.order(lay.tokens_in(cotangent))
-
-    per_row = lay.unit_block // block
-    thin = jnp.concatenate([norm_gains[0], biases[0], fc_bias[0].reshape(block, per_row)], axis=1)
-    thin = jnp.concatenate([thin.reshape(-1).astype(jnp.float32), positions.reshape(-1).astype(jnp.float32)])
-    used, spots = block * (8 + per_row), positions.size
-    thin = jnp.pad(thin, (0, -thin.size % 1024)).reshape(-1, 128)
-    thin, qkv_cut, wo_cut, fc_cut, proj_cut, w_qkv, w_out = run_start(0, lay, (h, g), thin, *sources)
-    thin = thin.reshape(lay.sections, lay.rest, lay.cores, lay.zs, -1)
-    places = thin[0, :, 0, :, used : used + spots].astype(jnp.int32)
-    places = places.reshape(lay.rest, lay.sections, lay.cores, lay.micros, lay.rows)
-    places = places.transpose(3, 1, 0, 2, 4).reshape(lay.micros, lay.tokens)
-    places = lax.dynamic_slice_in_dim(places, micro, 1, 0)
-    col, row = places.reshape(lay.tokens, 1), places
-    thin = thin[..., :used].transpose(0, 2, 3, 1, 4).reshape(lay.sections, width, 8 + per_row)
-    smalls = []
-    for layer in range(lay.sections):
-        vec = jnp.stack([thin[layer, :, i] for i in (0, 1, 2, 6, 5, 7)] + [thin[layer, :, 0]] * 2)
-        vec = lay.order(vec)
-        heads = [
-            lax.dynamic_slice_in_dim(
-                jnp.pad(thin[layer, :, 2 + i], (0, n * span - width)), lay.t * span, span
-            )
-            for i in (1, 2)
-        ]
-        bias = jnp.concatenate([heads[0], jnp.zeros_like(heads[0]), heads[1]])[None]
-        unit = thin[layer, :, 8:].reshape(lay.cores, lay.zs, lay.rest, lay.sections, lay.half)
-        unit = unit.transpose(3, 0, 2, 1, 4).reshape(n, lay.zs * lay.half)
-        unit = lax.dynamic_slice_in_dim(unit, lay.t, 1, 0)
-        smalls.append((vec, bias, unit))
-
-    vec = smalls[0][0]
-    normed = (norm_parts(h.astype(F32))[0] * vec[0:1] + vec[2:3]).astype(BF)
+
+    small = jnp.concatenate([norm_gains[0], biases[0]], axis=1).astype(F32).T
+    small = jnp.stack([small[i] for i in (0, 1, 2, 6, 5, 7, 3, 4)])
+    small = jnp.concatenate([small, fc_bias[0].reshape(-1, block).astype(F32)])
+    small = jnp.pad(small, ((0, 0), (0, 128 - block)))
+    places = jnp.pad(positions.astype(F32), ((0, 0), (0, 128 - lay.rows)))
+    small = jnp.concatenate([small, places])
+    small = jnp.pad(small, ((0, -small.shape[0] % 8), (0, 0)))
+    qkv_cut, wo_cut, fc_cut, proj_cut, w_qkv, w_out, h, g, row, *smalls = run_start(
+        0, lay, small, w_qkv[0], w_attn_out[0], w_fc[0], w_proj[0], inputs[:, 0], cotangent[:, 0]
+    )
+    smalls = [smalls[3 * layer : 3 * layer + 3] for layer in range(lay.sections)]
+    col = row.reshape(lay.tokens, 1)
     outs, keeps, params = [], [], []
     for layer in range(lay.sections):
         last = layer == lay.sections - 1
@@ -1142,8 +1514,7 @@
         (full, qkv, attended, logs, mid, normed_two), (w_fc, w_proj) = run_attention_forward(
             1 + 2 * layer,
             lay.head,
-            gather_side([fc_cut[layer], proj_cut[layer]]),
-            normed,
+            gather_side([fc_cut[layer], proj_cut[layer]], (lay.zs - 1, lay.zs - 2)),
             h,
             w_qkv,
             w_out,
@@ -1152,58 +1523,57 @@
             row,
             vec,
         )
-        w_fc, w_proj = w_fc.reshape(width, -1), w_proj.reshape(-1, width)
-        next_vec = smalls[min(layer + 1, lay.sections - 1)][0]
-        side = SideWork() if last else gather_side([wo_cut[layer + 1], qkv_cut[layer + 1]], span)
-        (full_two, slope, activated, result, normed), later = run_feed_forward(
-            2 + 2 * layer, side, normed_two, mid, w_fc, w_proj, unit, vec, next_vec
+        w_fc = w_fc.reshape(width, -1)
+        if last:
+            side = route_side(0, lay, outs[0])
+        else:
+            side = gather_side([wo_cut[layer + 1], qkv_cut[layer + 1]], turn=span)
+        (full_two, slope, activated, result, w_proj), later = run_feed_forward(
+            2 + 2 * layer, side, normed_two, mid, w_fc, w_proj, unit, vec
         )
-        params.append((w_qkv, w_out, w_fc, w_proj))
-        if not last:
+        params.append((w_qkv, w_out, w_fc, w_proj.reshape(-1, width)))
+        if last:
+            routed = [later[0]]
+        else:
             w_out, w_qkv = later
         keeps.append((h, full, qkv, attended, logs, mid, full_two, slope, activated))
         h = result
         outs.append(h)
 
-    def turned(grad_out):
-        wo = grad_out.reshape(span, n, lay.cols).transpose(1, 0, 2)
-        wo = lax.all_to_all(wo, SLAB, 0, 0, tiled=True)
-        wo = wo.reshape(n * span, lay.cols)[:width].reshape(lay.cores, lay.zs, lay.rest * block, lay.cols)
-        return jnp.swapaxes(wo, 0, 1).reshape(width, lay.cols)
-
-    totals = {}
-    waiting = []
-
-    def carry(count):
-        now = waiting[:count]
-        del waiting[:count]
-        return [key for key, _ in now], sum_side([part for _, part in now]) if now else SideWork()
-
+    rings = Rings(lay)
+    plans = {
+        ("feed", 1): [("proj", 1, 1)],
+        ("attention", 1): [("proj", 1, 2), ("fc", 1, 2)],
+        ("feed", 0): [("qkv", 1, 3), ("fc", 1, 1), ("proj", 0, 1)],
+        ("attention", 0): [("fc", 0, 3), ("proj", 0, 2), ("out", 1, 3)],
+    }
     grad_rows, sums = [None] * lay.sections, [None] * lay.sections
+    grad_out = None
     for layer in reversed(range(lay.sections)):
         w_qkv, w_out, w_fc, w_proj = params[layer]
         vec = smalls[layer][0]
         h, full, qkv, attended, logs, mid, full_two, slope, activated = keeps[layer]
         full, full_two = (a.reshape(lay.tokens, width) for a in (full, full_two))
         name = 1 + 4 * lay.sections - 2 * layer
-        keys, side = carry(1)
+        side = rings.side(plans["feed", layer], {"proj": (lay.half, width)}, grad_out, lay.cols)
+        side = both_sides(side, route_side(1, lay, outs[1] if grad_out is None else g))
         (grad_mid, attn_rows, grad_proj, grad_fc, feed_sums, unit_sums), done = run_feed_backward(
             name, side, g, mid, w_fc, w_proj, slope, activated, full_two, vec
         )
-        totals.update(zip(keys, done))
-        waiting = [(("proj", layer), grad_proj), (("fc", layer), grad_fc)] + waiting
-        keys, side = carry(3)
+        rings.put("proj", layer, grad_proj)
+        rings.put("fc", layer, grad_fc)
+        rings.done(plans["feed", layer], done)
+        routed.append(done[-1])
+        if grad_out is not None:
+            rings.put("out", layer + 1, done[-2])
+        side = rings.side(plans["attention", layer])
         (g, grad_qkv, grad_out, attn_sums, head_sums), done = run_attention_backward(
             name + 1, lay.head, side, attn_rows, grad_mid, h, w_qkv, w_out, qkv, attended, logs, full, col, row, vec
         )
-        totals.update(zip(keys, done))
-        if layer:
-            waiting = waiting + [(("qkv", layer), grad_qkv), (("out", layer), turned(grad_out))]
+        rings.done(plans["attention", layer], done)
+        rings.put("qkv", layer, grad_qkv)
         grad_rows[layer] = g
         sums[layer] = (feed_sums, unit_sums, attn_sums, head_sums)
-    section_out = lay.tokens_out([lay.restore(a) for a in outs])
-    section_grad = lay.tokens_out([lay.restore(a) for a in grad_rows])
-
     rows = []
     for layer in range(lay.sections):
         feed_sums, unit_sums, attn_sums, head_sums = sums[layer]
@@ -1224,17 +1594,21 @@
     used = rows.shape[-1]
     rows = jnp.pad(jnp.swapaxes(rows, 2, 3), ((0, 0),) * 4 + ((0, -used % 1024),))
     rows = rows.reshape(n, lay.zs, -1, 128)
-    out_qkv, out_attn, out_fc, out_proj, rows = run_end(
+    out_qkv, out_attn, out_fc, out_proj, rows, routed_grad = run_end(
         3 + 4 * lay.sections,
         lay,
-        grad_qkv,
+        rings.state["qkv", 0][0],
         grad_out,
-        totals["qkv", 1],
-        totals["out", 1],
-        [totals["fc", layer] for layer in range(2)],
-        [totals["proj", layer] for layer in range(2)],
+        rings.state["qkv", 1][1],
+        rings.state["out", 1][1],
+        [rings.state["fc", layer][1] for layer in range(2)],
+        [rings.state["proj", layer][1] for layer in range(2)],
         rows,
+        g,
     )
+    first = lay.x == 0
+    section_out = lay.restore(jnp.where(first, routed[0], routed[1]))[None, :, None]
+    section_grad = lay.restore(jnp.where(first, routed_grad, routed[2]))[None, :, None]
     rows = rows.reshape(-1)[:used]
     cols = rows[: block * 8].reshape(block, 8)
     return (

time: 1030 us -> 928 us (0.901)
  local copies, waits for them, and re-layouts: 89 us -> 37 us
  starting transfers between devices: 28.4 us -> 0 us
    ppermute x12 -> x0, starting transfers between devices: 22.7 us -> none  [the longest x8 17.3 us: tokens_out(): got.append(lax.ppermute(part, ALL, route))]
    pallas_call x8, Pallas kernels: 685 us -> 664 us  [call(): pl.pallas_call(kernel, out_shape=[jax.ShapeDtypeStruct(*o) for o in (*out...]
    another operation x28 -> x6, local copies, waits for them, and re-layouts: 19.6 us -> 0.02 us  [the longest x4 8.97 us: order(): a = a.reshape(*lead, self.cores, self.zs, self.rest * self.block)]
    reshape x17 -> x1, local copies, waits for them, and re-layouts: 13 us -> 1.79 us  [on_device(): col = row.reshape(lay.tokens, 1)]
  transfers between devices with their start and end apart: 13 -> 0, of which waited for: 1 -> 0; matrix products, arithmetic and copies ran while one was open for 6% -> 0% of each run, Pallas kernels for 30% -> 0%
where the time goes in v6:
time: 928 us; the launch traced here: 925 us
  Pallas kernels  883 us (95%)
  local copies, waits for them, and re-layouts  37 us (4%)
    pallas_call x8, Pallas kernels, call(): pl.pallas_call(kernel, out_shape=[jax.ShapeDtypeStruct(*o) for o in (*out...  664 us
    pallas_call x1, Pallas kernels, run_start(): pl.pallas_call(functools.partial(start_kernel, (block, span, lay.half, la...  112 us
    pallas_call x1, Pallas kernels, run_end(): pl.pallas_call(functools.partial(end_kernel, (block, width, lay.units, la...  108 us

profile of v6, /device:TPU:3, one launch (start us, length us, event | category | flops | bytes accessed | tf_op | source)
XLA Modules:
  0.0 925.2 jit_solution(17545424214781310092)
XLA Ops:
  0.6 0.7 convert_bitcast_fusion
  1.4 0.7 convert_reduce_fusion
  2.2 0.7 convert_element_type.18
  3.5 2.2 copy.50
  5.7 2.2 copy.51
  7.8 111.7 %shard_map.169 = (bf16[2,400,768]{2,1,0:T(8,128)(2,1)}, bf16[2,400,200]{2,1,0:T(8,128)(2,1)}, bf16[2,400,800]{2,1,0:T(8,128)(2,1)}, bf16[2,200,1600]{2,1,0:T(8,1...) custom-call(f32[16,128]{1,0:T(8,128)} %pad.13.refs_0_, ...), custom_call_target="tpu_custom_call" | custom-call | tf_op jit(solution)/shard_map/pallas_call | solution.py:1277
  119.5 1.8 copy.52.refs_4_.refs_9_
  121.3 2.5 slice_bitcast_fusion
  123.9 1.2 slice_bitcast_fusion.2
  125.0 84.8 %shard_map.170 = (bf16[4,2,128,1600]{3,2,1,0:T(8,128)(2,1)}, bf16[1024,768]{1,0:T(8,128)(2,1)}, bf16[1024,256]{1,0:T(8,128)(2,1)}, f32[8,1024]{1,0:T(8,128)}, f3...) custom-call(bf16[128,1600]{1,0:T(8,128)(2,1)} %get-tuple-element.93., ...), custom_call_target="tpu_custom_call" | custom-call | tf_op jit(solution)/shard_map/pallas_call | solution.py:985
  209.8 0.9 slice_bitcast_fusion.4.refs_7_
  210.7 0.7 slice_bitcast_fusion.5.refs_6_
  211.4 85.1 %shard_map.171 = (bf16[4,2,128,1600]{3,2,1,0:T(8,128)(2,1)}, bf16[1024,800]{1,0:T(8,128)(2,1)}, bf16[1024,800]{1,0:T(8,128)(2,1)}, bf16[128,1600]{1,0:T(8,128)(2...) custom-call(bf16[128,1600]{1,0:T(8,128)(2,1)} %get-tuple-element.101.refs_0_, ...), custom_call_target="tpu_custom_call" | custom-call | tf_op jit(solution)/shard_map/pallas_call | solution.py:985
  296.4 83.7 %shard_map.172 = (bf16[4,2,128,1600]{3,2,1,0:T(8,128)(2,1)}, bf16[1024,768]{1,0:T(8,128)(2,1)}, bf16[1024,256]{1,0:T(8,128)(2,1)}, f32[8,1024]{1,0:T(8,128)}, f3...) custom-call(bf16[128,1600]{1,0:T(8,128)(2,1)} %get-tuple-element.108, ...), custom_call_target="tpu_custom_call" | custom-call | tf_op jit(solution)/shard_map/pallas_call | solution.py:985
  380.2 57.0 %shard_map.173 = (bf16[4,2,128,1600]{3,2,1,0:T(8,128)(2,1)}, bf16[1024,800]{1,0:T(8,128)(2,1)}, bf16[1024,800]{1,0:T(8,128)(2,1)}, bf16[128,1600]{1,0:T(8,128)(2...) custom-call(bf16[128,1600]{1,0:T(8,128)(2,1)} %get-tuple-element.113.refs_0_, ...), custom_call_target="tpu_custom_call" | custom-call | tf_op jit(solution)/shard_map/pallas_call | solution.py:985
  437.2 71.0 %shard_map.174 = (f32[128,1600]{1,0:T(8,128)}, bf16[128,1600]{1,0:T(8,128)(2,1)}, bf16[4,200,1600]{2,1,0:T(8,128)(2,1)}, bf16[1600,800]{1,0:T(8,128)(2,1)}, f32[...) custom-call(bf16[128,1600]{1,0:T(8,128)(2,1)} %get-tuple-element.119.refs_0_, ...), custom_call_target="tpu_custom_call" | custom-call | tf_op jit(solution)/shard_map/pallas_call | solution.py:985
  508.2 79.7 %shard_map.175 = (bf16[128,1600]{1,0:T(8,128)(2,1)}, bf16[1600,768]{1,0:T(8,128)(2,1)}, bf16[256,1600]{1,0:T(8,128)(2,1)}, f32[8,1600]{1,0:T(8,128)}, f32[1,768]...) custom-call(bf16[128,1600]{1,0:T(8,128)(2,1)} %get-tuple-element.126.refs_0_, ...), custom_call_target="tpu_custom_call" | custom-call | tf_op jit(solution)/shard_map/pallas_call | solution.py:985
  587.9 92.0 %shard_map.176 = (f32[128,1600]{1,0:T(8,128)}, bf16[128,1600]{1,0:T(8,128)(2,1)}, bf16[4,200,1600]{2,1,0:T(8,128)(2,1)}, bf16[1600,800]{1,0:T(8,128)(2,1)}, f32[...) custom-call(bf16[128,1600]{1,0:T(8,128)(2,1)} %get-tuple-element.135, ...), custom_call_target="tpu_custom_call" | custom-call | tf_op jit(solution)/shard_map/pallas_call | solution.py:985
  679.9 110.7 %shard_map.177 = (bf16[128,1600]{1,0:T(8,128)(2,1)}, bf16[1600,768]{1,0:T(8,128)(2,1)}, bf16[256,1600]{1,0:T(8,128)(2,1)}, f32[8,1600]{1,0:T(8,128)}, f32[1,768]...) custom-call(bf16[128,1600]{1,0:T(8,128)(2,1)} %get-tuple-element.143.refs_0_, ...), custom_call_target="tpu_custom_call" | custom-call | tf_op jit(solution)/shard_map/pallas_call | solution.py:985
  790.7 1.0 reshape.163
  791.9 0.7 fusion.7
  797.6 0.8 reshape.169.refs_8_
  798.5 107.5 %shard_map.178 = (f32[100,4800]{1,0:T(8,128)}, f32[100,1600]{1,0:T(8,128)}, f32[100,6400]{1,0:T(8,128)}, f32[400,1600]{1,0:T(8,128)}, f32[16,128]{1,0:T(8,128)}, /*index=5*/bf16[2,128,1600]{2,1,0:T(8,128)(2,1)}) custom-call(bf16[4,400,768]{2,1,0:T(8,128)(2,1)} %bitcast.106, bf16[256,1600]{1,0:T(8,128)(2,1)} %get-tuple-element.154.refs_1_, ...), custom_call_target="tpu_custom_call" | custom-call | tf_op jit(solution)/shard_map/pallas_call | solution.py:1431
  906.0 1.4 broadcast_select_fusion
  908.0 1.0 copy.55
  909.5 1.0 copy.68
  910.5 6.0 copy.71
  916.5 3.3 copy.69
  919.8 1.5 copy.70
  921.5 0.7 copy.73
  922.8 0.6 slice.181
  923.4 1.5 copy.92
  (100 shorter events, 7.8 us)
Async XLA Ops:
  119.5 4.3 copy-start.2
  125.0 84.8 %copy-start.6 = (bf16[2,400,768]{2,1,0:T(8,128)(2,1)S(1)}, bf16[2,400,768]{2,1,0:T(8,128)(2,1)}, u32[]{:S(2)}) copy-start(bf16[2,400,768]{2,1,0:T(8,128)(2,1)} %get-tuple-element.107) | copy-start | bytes 3686404
  125.0 85.7 %copy-start.7 = (bf16[2,400,200]{2,1,0:T(8,128)(2,1)S(1)}, bf16[2,400,200]{2,1,0:T(8,128)(2,1)}, u32[]{:S(2)}) copy-start(bf16[2,400,200]{2,1,0:T(8,128)(2,1)} %get-tuple-element.106) | copy-start | bytes 960004
  679.9 113.1 %copy-start.10 = (f32[8,1600]{1,0:T(8,128)S(1)}, f32[8,1600]{1,0:T(8,128)}, u32[]{:S(2)}) copy-start(f32[8,1600]{1,0:T(8,128)} %get-tuple-element.162) | copy-start | bytes 153604
  790.6 3.8 copy-start.9
  790.6 4.2 copy-start.14
  790.7 4.8 copy-start.8
  792.8 4.1 copy-start.13
  793.2 3.9 copy-start.12
  798.5 107.5 %copy-start.3 = (bf16[2,128,1600]{2,1,0:T(8,128)(2,1)S(1)}, bf16[2,128,1600]{2,1,0:T(8,128)(2,1)}, u32[]{:S(2)}) copy-start(bf16[2,128,1600]{2,1,0:T(8,128)(2,1)} %get-tuple-element.118) | copy-start | bytes 2457604
  798.5 107.5 %copy-start.4 = (bf16[2,128,1600]{2,1,0:T(8,128)(2,1)S(1)}, bf16[2,128,1600]{2,1,0:T(8,128)(2,1)}, u32[]{:S(2)}) copy-start(bf16[2,128,1600]{2,1,0:T(8,128)(2,1)} %get-tuple-element.125) | copy-start | bytes 2457604
  910.5 6.0 copy-start.1
  916.5 3.3 copy-start.5
  916.5 4.8 copy-start.11
  916.5 6.9 copy-start

commit v7 on v6

--- a/solution.py
+++ b/solution.py
@@ -245,7 +245,9 @@
     def __init__(self, pieces, local, send, recv):
         self.pieces, self.local, self.send_sem, self.recv_sem = pieces, local, send, recv
         self.zs, self.z = lax.axis_size("z"), lax.axis_index("z")
-        self.steps = [(p, s) for s in range(self.zs - 1) for p in range(len(pieces)) if s < pieces[p][2]]
+        every = [(p, s) for s in range(self.zs - 1) for p in range(len(pieces)) if s < pieces[p][2]]
+        self.steps = [(p, s) for p, s in every if s < pieces[p][2] - 1] + [(p, s) for p, s in every if s == pieces[p][2] - 1]
+        self.forwards = len(every) - len(pieces)
         self.sent = []
 
     def block(self, step):
@@ -262,9 +264,12 @@
             self.send(p, 0, shard)
             pltpu.make_async_copy(shard, full.at[self.z], self.local.at[p]).start()
 
-    def tick(self):
-        if not self.steps:
-            return None
+    def tick(self, count=1):
+        for _ in range(min(count, self.forwards)):
+            self.forwards -= 1
+            self.take()
+
+    def take(self):
         p, step = self.steps.pop(0)
         shard, full, count = self.pieces[p]
         block = full.at[self.block(step + 1)]
@@ -277,7 +282,7 @@
 
     def finish(self):
         while self.steps:
-            self.tick()
+            self.take()
         for copy in self.sent:
             copy.wait_send()
 
@@ -293,6 +298,7 @@
         self.late = [p for p, piece in enumerate(pieces) if piece[0] is None]
         ready = [p for p in range(len(pieces)) if p not in self.late]
         self.steps = [(p, i) for i in range(self.zs - 1) for p in ready if i < pieces[p][5] - 1]
+        self.forwards = len(self.steps)
         self.steps += [(p, pieces[p][5] - 1) for p in ready]
         self.parts = [piece[0] for piece in pieces]
 
@@ -307,7 +313,7 @@
 
     def launch(self, p):
         acc, first = self.pieces[p][1], self.pieces[p][4]
-        self.send(p, 0, acc if first else self.parts[p].at[lax.rem(self.z + self.zs - 1, self.zs)])
+        self.send(p, 0, far(acc) if first else far(self.parts[p]).at[lax.rem(self.z + self.zs - 1, self.zs)])
 
     def start(self):
         for p in range(len(self.pieces)):
@@ -319,11 +325,17 @@
             p = self.late.pop(0)
             self.parts[p] = part
             self.launch(p)
-            self.steps += [(p, i) for i in range(self.pieces[p][5])]
-
-    def tick(self):
-        if not self.steps:
-            return
+            count = self.pieces[p][5]
+            self.steps[self.forwards : self.forwards] = [(p, i) for i in range(count - 1)]
+            self.forwards += count - 1
+            self.steps.append((p, count - 1))
+
+    def tick(self, count=1):
+        for _ in range(min(count, self.forwards)):
+            self.forwards -= 1
+            self.take()
+
+    def take(self):
         p, i = self.steps.pop(0)
         part, acc, came, out, first, count = self.pieces[p]
         self.copy(p, i, came.at[i]).wait_recv()
@@ -340,7 +352,7 @@
 
     def finish(self):
         while self.steps:
-            self.tick()
+            self.take()
         for copy in self.sent:
             copy.wait_send()
 
@@ -436,20 +448,20 @@
 
 
 class Route:
-    def __init__(self, layer, seqs, src, out, local, send, recv):
-        self.layer, self.seqs, self.src, self.out = layer, seqs, src, out
+    def __init__(self, seqs, src, out, local, send, recv, when="start"):
+        self.when = when
+        self.seqs, self.src, self.out = seqs, src, out
         self.local, self.send_sem, self.recv_sem = local, send, recv
         x, c, z = (lax.axis_index(a) for a in ("section", "dp", "z"))
-        self.here = x == layer
-        place = x * 2 + c
-        self.to = {"section": layer, "dp": lax.rem(z, seqs), "z": place}
+        self.here = lax.rem(z, 2) == x
+        place = c * 2 + x
+        self.to = {"dp": lax.rem(z, seqs), "z": place}
         self.micro = z // seqs
-        self.same = (x == layer) & (lax.rem(z, seqs) == c) & (place == z)
+        self.same = (lax.rem(z, seqs) == c) & (place == z)
         self.sources = []
         for micro in range(out.shape[0]):
-            src_x, src_c, src_z = z // 2, lax.rem(z, 2), micro * seqs + c
-            same = (src_x == x) & (src_c == c) & (src_z == z)
-            self.sources.append(({"section": src_x, "dp": src_c, "z": src_z}, same))
+            src_c, src_z = z // 2, micro * seqs + c
+            self.sources.append(({"dp": src_c, "z": src_z}, (src_c == c) & (src_z == z)))
 
     def greet(self):
         barrier = pltpu.get_barrier_semaphore()
@@ -468,6 +480,13 @@
         return pltpu.make_async_copy(self.src, self.out.at[self.micro], self.local)
 
     def start(self):
+        if self.when == "start":
+            self.go()
+
+    def middle(self):
+        pass
+
+    def go(self):
         @pl.when(jnp.logical_not(self.same))
         def _():
             self.copy().start()
@@ -476,16 +495,14 @@
         def _():
             self.own().start()
 
-    def tick(self):
-        pass
+    def tick(self, point):
+        if self.when == point:
+            self.go()
 
     def made(self, part):
         pass
 
-    def middle(self):
-        pass
-
-    def finish(self):
+    def arrived(self):
         for micro, (device, same) in enumerate(self.sources):
 
             @pl.when(self.here & jnp.logical_not(same))
@@ -493,13 +510,179 @@
                 block = self.out.at[micro]
                 remote(block, block, self.send_sem, self.recv_sem.at[micro], device).wait_recv()
 
+        @pl.when(self.same)
+        def _():
+            self.own().wait()
+
+    def sent(self):
         @pl.when(jnp.logical_not(self.same))
         def _():
             self.copy().wait_send()
 
-        @pl.when(self.same)
+    def finish(self):
+        self.arrived()
+        self.sent()
+
+
+class Across:
+    def __init__(self, layer, src, out, send, recv):
+        self.src, self.out, self.send_sem, self.recv_sem = src, out, send, recv
+        x, z = lax.axis_index("section"), lax.axis_index("z")
+        self.layer = layer
+        self.sends = (x != layer) & (lax.rem(z, 2) == x)
+        self.takes = (x == layer) & (lax.rem(z, 2) != x)
+        self.going = False
+
+    def greet(self):
+        barrier = pltpu.get_barrier_semaphore()
+
+        @pl.when(self.takes)
         def _():
-            self.own().wait()
+            pl.semaphore_signal(barrier, inc=1, device_id={"section": 1 - self.layer}, device_id_type=MESH)
+
+        return jnp.where(self.sends, 1, 0)
+
+    def copy(self):
+        return remote(self.src, self.out, self.send_sem, self.recv_sem, {"section": jnp.int32(self.layer)})
+
+    def back(self):
+        return remote(self.out, self.out, self.send_sem, self.recv_sem, {"section": jnp.int32(1 - self.layer)})
+
+    def start(self):
+        pass
+
+    def tick(self, point):
+        if not self.going:
+            self.going = True
+
+            @pl.when(self.sends)
+            def _():
+                self.copy().start()
+
+    def made(self, part):
+        pass
+
+    def middle(self):
+        pass
+
+    def finish(self):
+        self.tick("end")
+
+        @pl.when(self.takes)
+        def _():
+            self.back().wait_recv()
+
+        @pl.when(self.sends)
+        def _():
+            self.copy().wait_send()
+
+
+class RouteIn:
+    def __init__(self, seqs, pairs, local, send, recv):
+        self.pairs, self.local, self.send_sem, self.recv_sem = pairs, local, send, recv
+        x, c, z = (lax.axis_index(a) for a in ("section", "dp", "z"))
+        self.sends = lax.rem(z, 2) == x
+        self.targets = []
+        for micro in range(pairs[0][0].shape[0]):
+            to_c, to_z = z // 2, micro * seqs + c
+            self.targets.append(({"dp": to_c, "z": to_z}, (to_c == c) & (to_z == z)))
+        self.micro = z // seqs
+        self.source = {"dp": lax.rem(z, seqs), "z": c * 2 + x}
+        self.same = (lax.rem(z, seqs) == c) & (c * 2 + x == z)
+
+    def greet(self):
+        barrier = pltpu.get_barrier_semaphore()
+
+        @pl.when(jnp.logical_not(self.same))
+        def _():
+            pl.semaphore_signal(barrier, inc=1, device_id=self.source, device_id_type=MESH)
+
+        return sum(jnp.where(self.sends & jnp.logical_not(same), 1, 0) for _, same in self.targets)
+
+    def far(self, i, micro):
+        src, dst = self.pairs[i]
+        return remote(src.at[micro, 0], dst, self.send_sem.at[i, micro], self.recv_sem.at[i], self.targets[micro][0])
+
+    def near(self, i, micro):
+        src, dst = self.pairs[i]
+        return pltpu.make_async_copy(src.at[micro, 0], dst, self.local.at[i])
+
+    def start(self, i=0):
+        for micro, (_, same) in enumerate(self.targets):
+
+            @pl.when(self.sends & jnp.logical_not(same))
+            def _(micro=micro):
+                self.far(i, micro).start()
+
+            @pl.when(self.sends & same)
+            def _(micro=micro):
+                self.near(i, micro).start()
+
+    def tick(self, point):
+        pass
+
+    def made(self, part):
+        pass
+
+    def middle(self):
+        pass
+
+    def arrived(self, i):
+        dst = self.pairs[i][1]
+
+        @pl.when(jnp.logical_not(self.same))
+        def _():
+            remote(dst, dst, self.send_sem.at[i, 0], self.recv_sem.at[i], self.source).wait_recv()
+
+        for micro, (_, same) in enumerate(self.targets):
+
+            @pl.when(self.sends & same)
+            def _(micro=micro):
+                self.near(i, micro).wait()
+
+    def finish(self):
+        for i in range(len(self.pairs)):
+            for micro, (_, same) in enumerate(self.targets):
+
+                @pl.when(self.sends & jnp.logical_not(same))
+                def _(i=i, micro=micro):
+                    self.far(i, micro).wait_send()
+
+
+def reorder(raw, ordered, zs, wide):
+    for c in range(2):
+        for k in range(zs):
+            at, to = (c * zs + k) * wide, (k * 2 + c) * wide
+            ordered[:, to : to + wide] = raw[:, at : at + wide]
+
+
+class Shared:
+    def __init__(self, src, gather, points):
+        self.src, self.gather, self.points = src, gather, points
+
+    def greet(self):
+        return 0
+
+    def start(self):
+        pass
+
+    def made(self, part):
+        pass
+
+    def middle(self):
+        pass
+
+    def tick(self, point):
+        if point == self.points[0]:
+            self.gather.start(self.src)
+        if point == self.points[1]:
+            for k in range(1, self.gather.peers.chips):
+                self.gather.forward(k)
+
+    def finish(self):
+        for k in range(self.gather.peers.chips):
+            self.gather.chip(k)
+        self.gather.finish()
 
 
 class Several:
@@ -513,9 +696,9 @@
         for work in self.works:
             work.start()
 
-    def tick(self):
+    def tick(self, point):
         for work in self.works:
-            work.tick()
+            work.tick(point)
 
     def made(self, part):
         for work in self.works:
@@ -537,7 +720,7 @@
     def start(self):
         pass
 
-    def tick(self):
+    def tick(self, point):
         pass
 
     def made(self, part):
@@ -560,15 +743,56 @@
     def start(self):
         self.ring.start()
 
-    def tick(self):
-        if self.ring.tick() == 0:
-            self.turn.start()
+    def tick(self, count=1):
+        self.ring.tick(count)
 
     def finish(self):
         while self.ring.steps:
-            self.tick()
+            if self.ring.take() == 0:
+                self.turn.start()
         self.ring.finish()
         self.turn.finish()
+
+
+class Fetch:
+    def __init__(self, far, near, sem):
+        self.far, self.near = far, near
+        self.copy = pltpu.make_async_copy(far, near, sem)
+        self.copy.start()
+        self.here = False
+        self.shape = near.shape
+
+    def __getitem__(self, index):
+        if not self.here:
+            self.copy.wait()
+            self.here = True
+        return self.near[index]
+
+    def finish(self):
+        if not self.here:
+            self.copy.wait()
+
+
+def far(ref):
+    return ref.far if isinstance(ref, Fetch) else ref
+
+
+class Paced:
+    def __init__(self, work, pace):
+        self.work, self.pace = work, pace
+        self.greet, self.start, self.finish = work.greet, work.start, work.finish
+        self.middle = getattr(work, "middle", lambda: None)
+        self.part = None
+
+    def made(self, part):
+        self.part = part
+        if "launch" not in self.pace:
+            self.work.made(part)
+
+    def tick(self, point):
+        self.work.tick(self.pace.get(point, 0))
+        if self.part is not None and self.pace.get("launch") == point:
+            self.work.made(self.part)
 
 
 class SideWork:
@@ -581,14 +805,32 @@
         return NoSide() if self.build is None else self.build(peers, ins, outs, scratch)
 
 
-def route_side(layer, lay, src):
+def route_side(lay, src, when):
     dma = pltpu.SemaphoreType.DMA
     outs = [((lay.micros, *src.shape), BF)]
 
     def build(peers, ins, outs, scratch):
-        return Route(layer, lay.seqs, ins[0], outs[0], *scratch)
+        return Route(lay.seqs, ins[0], outs[0], *scratch, when)
 
     return SideWork([src], (True,), outs, (True,), [dma, dma, dma((lay.micros,))], build)
+
+
+def share_side(lay, a, points):
+    chips = lay.slab // 2
+
+    def build(peers, ins, outs, scratch):
+        return Shared(ins[0], Gather(peers, outs[0], scratch), points)
+
+    return SideWork([a], (False,), [((chips, 2, *a.shape), BF)], (False,), [pltpu.SemaphoreType.DMA((chips,))] * 4, build)
+
+
+def across_side(layer, a):
+    dma = pltpu.SemaphoreType.DMA
+
+    def build(peers, ins, outs, scratch):
+        return Across(layer, ins[0], outs[0], *scratch)
+
+    return SideWork([a], (True,), [(a.shape, a.dtype)], (True,), [dma, dma], build)
 
 
 def both_sides(*sides):
@@ -609,16 +851,19 @@
     return SideWork(*joined, build)
 
 
-def gather_side(shards, counts=None, turn=None):
+def gather_side(shards, pace, counts=None, turn=None):
     zs = lax.axis_size("z")
     n = len(shards)
     counts = counts or (zs - 1,) * n
-    outs = [((zs, *a.shape), BF) for a in shards]
+    places = [a[1] if isinstance(a, tuple) else None for a in shards]
+    shards = [a[0] if isinstance(a, tuple) else a for a in shards]
+    outs = [((zs, *a.shape[-2:]), BF) for a in shards]
     sems = [pltpu.SemaphoreType.DMA((n,))] + [pltpu.SemaphoreType.DMA((n, zs - 1))] * 2
     if turn is None:
 
         def build(peers, ins, outs, scratch):
-            return RingGather(list(zip(ins, outs, counts)), *scratch)
+            ins = [a if place is None else a.at[place] for a, place in zip(ins, places)]
+            return Paced(RingGather(list(zip(ins, outs, counts)), *scratch), pace)
 
         return SideWork(shards, (True,) * n, outs, (True,) * n, sems, build)
     slab = 2 * lax.axis_size("section") * lax.axis_size("r")
@@ -632,12 +877,13 @@
 
     def build_turn(peers, ins, outs, scratch):
         pieces = list(zip(ins, [scratch[3], *outs[1:]], counts))
-        return Both(RingGather(pieces, *scratch[:3]), Turn(peers, scratch[3], scratch[4], scratch[5], outs[0], *scratch[6:8]))
+        turning = Turn(peers, scratch[3], scratch[4], scratch[5], outs[0], *scratch[6:8])
+        return Paced(Both(RingGather(pieces, *scratch[:3]), turning), pace)
 
     return SideWork(shards, (True,) * n, outs, (False,) + (True,) * (n - 1), sems + more, build_turn)
 
 
-def sum_side(pieces, turned=None, cols=0):
+def sum_side(pieces, pace, turned=None, cols=0):
     zs = lax.axis_size("z")
     n = len(pieces)
     operands, outs, scratch = [], [], []
@@ -661,8 +907,8 @@
             made.append((part_ref, acc_ref, scratch[i], outs[i], first, count))
         ring = RingSum(made, *scratch[n : n + 2])
         if turned is None:
-            return ring
-        return SumAndTurn(ring, TurnBack(peers, ins.pop(0), outs[n], *scratch[n + 2 :]))
+            return Paced(ring, pace)
+        return Paced(SumAndTurn(ring, TurnBack(peers, ins.pop(0), outs[n], *scratch[n + 2 :])), pace)
 
     return SideWork(operands, (False,) * len(operands), outs, (False,) * len(outs), scratch, build)
 
@@ -735,7 +981,7 @@
     for k, chip in gather.arrivals():
         part = dot(full[chip].reshape(2 * rows, width), w_qkv[...]) + bias[...]
         qkv[chip_rows(chip, rows), :] = part.astype(BF)
-    work.tick()
+    work.tick("qkv")
     kept = pltpu.make_async_copy(full, normed, kept_sem)
     kept.start()
     scale = head ** (-0.5)
@@ -763,7 +1009,7 @@
         reduce.put(k, dot(attended[here, :], w_out[...]))
         if before is not None:
             reduce.push(before)
-        work.tick()
+        work.tick("q%d" % order.index(k))
         before = k
     reduce.push(before)
     out = h[...].astype(F32) + (reduce.total() + vec[4:5, :])
@@ -823,13 +1069,12 @@
         reduce.put(k, back)
         if before is not None:
             reduce.push(before)
-        if k == peers.chips - 1:
-            work.tick()
+        work.tick("k%d" % k)
         before = k
     kept = pltpu.make_async_copy(full, normed_two, kept_sem)
     kept.start()
     reduce.push(before)
-    work.tick()
+    work.tick("sent")
     out = (mid[...] + (reduce.total() + vec[5:6, :])).astype(BF)
     result[...] = out
     last.wait_send()
@@ -844,9 +1089,10 @@
     return [(a, min(a + step, size)) for a in range(0, size, step)]
 
 
-def feed_backward(side, *refs):
-    (src, mid, w_fc, w_proj, slope, activated, normed_two, vec) = refs[:8]
-    ins, refs = refs[8 : 8 + len(side.operands)], refs[8 + len(side.operands) :]
+def feed_backward(side, ready, *refs):
+    (src, mid, w_fc, w_proj, slope, activated, normed_two, vec, *given) = refs[: 8 + ready]
+    refs = refs[8 + ready :]
+    ins, refs = refs[: len(side.operands)], refs[len(side.operands) :]
     (grad_mid, attn_rows, grad_proj, grad_fc, sums, unit_sums), refs = refs[:6], refs[6:]
     side_outs, refs = refs[: len(side.outs)], refs[len(side.outs) :]
     gather_refs, reduce_refs, side_refs = refs[:5], refs[5 : 14 + 1], refs[14 + 1 :]
@@ -856,13 +1102,27 @@
     peers = Peers()
     gather = Gather(peers, gather_refs[0], gather_refs[1:])
     reduce = Reduce(peers, *reduce_refs[:5], reduce_refs[5:9])
-    full = gather.full
+    full = given[0] if ready else gather.full
     work = side.make(peers, ins, side_outs, side_refs)
     peers.greet(side.zs, work)
-    gather.start(src)
+    half = grad_proj.shape[1]
+
+    def proj_terms():
+        branch = full[...].reshape(tokens, width)
+        for b in range(grad_proj.shape[0]):
+            grad_proj[b] = dot(activated[:, b * half : (b + 1) * half], branch, 0, 0).astype(BF)
+        work.made(grad_proj)
+
+    if ready:
+        order = [(k, peers.behind_chip(k)) for k in (*range(1, peers.chips), 0)]
+    else:
+        gather.start(src)
+        order = gather.arrivals()
     work.start()
+    if ready:
+        proj_terms()
     before = None
-    for k, chip in gather.arrivals():
+    for k, chip in order:
         here = chip_rows(chip, rows)
         back = dot(full[chip].reshape(2 * rows, width), w_proj[...], 1, 1) * slope[here, :].astype(F32)
         back = back.astype(BF)
@@ -870,21 +1130,17 @@
         reduce.put(k, dot(back, w_fc[...], 1, 1))
         if before is not None:
             reduce.push(before)
-        if k == peers.chips - 1:
-            work.tick()
+        work.tick("k%d" % k)
         before = k
     reduce.push(before)
     work.middle()
-    branch = full[...].reshape(tokens, width)
-    half = grad_proj.shape[1]
-    for b in range(grad_proj.shape[0]):
-        grad_proj[b] = dot(activated[:, b * half : (b + 1) * half], branch, 0, 0).astype(BF)
-    work.made(grad_proj)
-    work.tick()
+    if not ready:
+        proj_terms()
+    work.tick("proj")
     back = hidden[...]
     for a, b in chunks(width, 512):
         grad_fc[a:b, :] = dot(normed_two[:, a:b], back, 0, 0).astype(BF)
-    work.tick()
+    work.tick("fc")
     unit_sums[...] = jnp.sum(back.astype(F32), axis=0, keepdims=True)
     own = src[...].astype(F32)
     part, gain, shift = norm_back(mid[...], vec[1:2, :], reduce.total())
@@ -898,7 +1154,8 @@
     sums[3:4, :] = jnp.sum(low.astype(F32), axis=0, keepdims=True)
     sums[4:8, :] = jnp.zeros((4, width), F32)
     work.finish()
-    gather.finish()
+    if not ready:
+        gather.finish()
     reduce.finish()
 
 
@@ -950,8 +1207,7 @@
             else:
                 key_sum[:, lanes] += key_term
                 value_sum[:, lanes] += value_term
-        if k == peers.chips - 1:
-            work.tick()
+        work.tick("k%d" % k)
     joint[:, span : 2 * span] = key_sum[...].astype(BF)
     joint[:, 2 * span :] = value_sum[...].astype(BF)
     order = list(range(1, peers.chips)) + [0]
@@ -961,11 +1217,11 @@
         if before is not None:
             reduce.push(before)
         before = k
-    work.tick()
+    work.tick("sent")
     grads = joint[...]
     for a, b in chunks(width, 512):
         grad_qkv[a:b, :] = dot(normed[:, a:b], grads, 0, 0).astype(BF)
-    work.tick()
+    work.tick("grad")
     grad_out[...] = dot(attended[...], full[...].reshape(tokens, width), 0, 0).astype(BF)
     head_sums[...] = jnp.sum(grads.astype(F32), axis=0, keepdims=True)
     part, gain, shift = norm_back(h[...].astype(F32), vec[0:1, :], reduce.total())
@@ -978,18 +1234,33 @@
     reduce.finish()
 
 
-def call(kernel, name, outs, operands, side, kept, scratch, far=()):
+def call(kernel, name, outs, operands, side, kept, scratch, keep=()):
     chips = lax.axis_size("section") * lax.axis_size("r")
     rows, width = operands[0].shape
     vmem, hbm = pl.BlockSpec(memory_space=pltpu.VMEM), pl.BlockSpec(memory_space=pl.ANY)
+    every = [*operands, *side.operands]
+    fetched = [i for i in range(len(every)) if i not in keep and not (i >= len(operands) and side.in_hbm[i - len(operands)])]
+    work = gather_scratch(chips, rows, width) + reduce_scratch(chips, rows, width) + scratch + list(side.scratch)
+
+    def body(*refs):
+        refs = list(refs)
+        near, sems = refs[-1 - len(fetched) : -1], refs[-1]
+        for k, i in enumerate(fetched):
+            refs[i] = Fetch(refs[i], near[k], sems.at[k])
+        kernel(*refs[: -1 - len(fetched)])
+        for i in fetched:
+            refs[i].finish()
+
     out = pl.pallas_call(
-        kernel,
+        body,
         out_shape=[jax.ShapeDtypeStruct(*o) for o in (*outs, *side.outs)],
-        in_specs=[hbm if i in far else vmem for i in range(len(operands))] + [hbm if i else vmem for i in side.in_hbm],
+        in_specs=[hbm] * len(every),
         out_specs=[hbm if i in kept else vmem for i in range(len(outs))] + [hbm if i else vmem for i in side.out_hbm],
-        scratch_shapes=gather_scratch(chips, rows, width) + reduce_scratch(chips, rows, width) + scratch + list(side.scratch),
+        scratch_shapes=work
+        + [pltpu.VMEM(every[i].shape, every[i].dtype) for i in fetched]
+        + [pltpu.SemaphoreType.DMA((len(fetched),))],
         compiler_params=pltpu.CompilerParams(collective_id=name, has_side_effects=True, vmem_limit_bytes=60 * 2**20),
-    )(*operands, *side.operands)
+    )(*every)
     return out[: len(outs)], out[len(outs) :]
 
 
@@ -1029,7 +1300,7 @@
 
 
 def run_feed_backward(name, side, *operands):
-    src, mid, w_fc, w_proj, slope, activated, normed_two, vec = operands
+    src, mid, w_fc, w_proj, slope, activated, normed_two, vec, *given = operands
     rows, width = src.shape
     tokens, units = slope.shape
     zs = lax.axis_size("z")
@@ -1041,7 +1312,7 @@
         ((8, width), F32),
         ((1, units), F32),
     ]
-    return call(functools.partial(feed_backward, side), name, outs, operands, side, (), [pltpu.VMEM((tokens, units), BF)])
+    return call(functools.partial(feed_backward, side, len(given)), name, outs, operands, side, (), [pltpu.VMEM((tokens, units), BF)])
 
 
 def run_attention_backward(name, head, side, *operands):
@@ -1059,73 +1330,10 @@
     return call(functools.partial(attention_backward, head, side), name, outs, operands, side, (), scratch)
 
 
-class RouteIn:
-    def __init__(self, seqs, pairs, local, send, recv):
-        self.pairs, self.local, self.send_sem, self.recv_sem = pairs, local, send, recv
-        x, c, z = (lax.axis_index(a) for a in ("section", "dp", "z"))
-        self.sends = z // 2 == x
-        self.targets = []
-        for micro in range(pairs[0][0].shape[0]):
-            to_c, to_z = lax.rem(z, 2), micro * seqs + c
-            self.targets.append(({"dp": to_c, "z": to_z}, (to_c == c) & (to_z == z)))
-        self.micro = z // seqs
-        self.source = {"dp": lax.rem(z, seqs), "z": x * 2 + c}
-        self.same = (lax.rem(z, seqs) == c) & (x * 2 + c == z)
-
-    def greet(self):
-        barrier = pltpu.get_barrier_semaphore()
-
-        @pl.when(jnp.logical_not(self.same))
-        def _():
-            pl.semaphore_signal(barrier, inc=1, device_id=self.source, device_id_type=MESH)
-
-        return sum(jnp.where(self.sends & jnp.logical_not(same), 1, 0) for _, same in self.targets)
-
-    def far(self, i, micro):
-        src, dst = self.pairs[i]
-        return remote(src.at[micro], dst, self.send_sem.at[i, micro], self.recv_sem.at[i], self.targets[micro][0])
-
-    def near(self, i, micro):
-        src, dst = self.pairs[i]
-        return pltpu.make_async_copy(src.at[micro], dst, self.local.at[i])
-
-    def start(self, i):
-        for micro, (_, same) in enumerate(self.targets):
-
-            @pl.when(self.sends & jnp.logical_not(same))
-            def _(micro=micro):
-                self.far(i, micro).start()
-
-            @pl.when(self.sends & same)
-            def _(micro=micro):
-                self.near(i, micro).start()
-
-    def arrived(self, i):
-        dst = self.pairs[i][1]
-
-        @pl.when(jnp.logical_not(self.same))
-        def _():
-            remote(dst, dst, self.send_sem.at[i, 0], self.recv_sem.at[i], self.source).wait_recv()
-
-        for micro, (_, same) in enumerate(self.targets):
-
-            @pl.when(self.sends & same)
-            def _(micro=micro):
-                self.near(i, micro).wait()
-
-    def finish(self):
-        for i in range(len(self.pairs)):
-            for micro, (_, same) in enumerate(self.targets):
-
-                @pl.when(self.sends & jnp.logical_not(same))
-                def _(i=i, micro=micro):
-                    self.far(i, micro).wait_send()
-
-
 def start_kernel(sizes, *refs):
     block, span, half, seqs, micros = sizes
     (tiny, w_qkv, w_attn, w_fc, w_proj, inputs, cotangent), refs = refs[:7], refs[7:]
-    (qkv, wo, fc, proj, qkv_full, w_out, h, g, row, *smalls), refs = refs[:15], refs[15:]
+    (qkv, wo, fc, (proj, qkv_full, w_out, h, g, row, *smalls)), refs = (refs[0:2], refs[2:4], refs[4:6], refs[6:18]), refs[18:]
     tiny_out, stage, h_raw, g_raw, natural, proj_cut = refs[:6]
     cuts, lands, (wo_full, nat, land), refs = refs[6:9], refs[9:12], refs[12:15], refs[15:]
     z_send, z_recv, *sems = refs[:6]
@@ -1150,6 +1358,7 @@
         send(remote(tiny, stage.at[z], z_send.at[k], z_recv.at[k], {"z": lax.rem(z + k, zs)}))
     stage[z] = tiny[...]
     route.start(0)
+    route.start(1)
 
     def share(a):
         for i, place in peers.offsets():
@@ -1164,7 +1373,7 @@
             remote(came, came, all_send.at[a, i], all_recv.at[a, i], device).wait_recv()
         for layer in range(sections):
             for i in range(2 * rest):
-                shard[layer, i * block : (i + 1) * block, :] = lands[a][layer, i, :block, :]
+                shard[layer][i * block : (i + 1) * block, :] = lands[a][layer, i, :block, :]
 
     cols = width // slab
     for t in range(slab):
@@ -1199,7 +1408,7 @@
     settle(0, wo)
     settle(1, qkv)
     turn = Turn(peers, wo_full, nat, land, w_out, turn_send, turn_recv)
-    ring = RingGather([(wo.at[0], wo_full, zs - 1), (qkv.at[0], qkv_full, zs - 1)], ring_local, ring_send, ring_recv)
+    ring = RingGather([(wo[0], wo_full, zs - 1), (qkv[0], qkv_full, zs - 1)], ring_local, ring_send, ring_recv)
     work = Both(ring, turn)
     work.start()
     share(2)
@@ -1208,7 +1417,6 @@
         there = lax.rem(x + d, sections)
         send(remote(proj_cut.at[there], proj.at[x], far_send.at[d], far_recv.at[d], device))
     proj[x] = proj_cut[x]
-    route.start(1)
     for _ in gather.arrivals():
         pass
 
@@ -1238,17 +1446,14 @@
         for r in range(rest):
             for c in range(2):
                 at = ((a * rest + r) * 2 + c) * rows
-                line = tiny_out[r, 0, a * 2 + c, pl.ds(8 + per_row + z // seqs, 1), :rows]
+                line = tiny_out[r, 0, c * 2 + a, pl.ds(8 + per_row + z // seqs, 1), :rows]
                 row[:, at : at + rows] = line.astype(jnp.int32)
     work.tick()
     settle(2, fc)
     work.tick()
     for i, (raw, ordered) in enumerate([(h_raw, h), (g_raw, g)]):
         route.arrived(i)
-        for c in range(2):
-            for k in range(zs):
-                at, to = (c * zs + k) * wide, (k * 2 + c) * wide
-                ordered[:, to : to + wide] = raw[:, at : at + wide]
+        reorder(raw, ordered, zs, wide)
     for d in range(1, sections):
         device, _ = peers.other(-d, 0, 0)
         came = proj.at[device["section"]]
@@ -1268,8 +1473,8 @@
     vmem, hbm = pl.BlockSpec(memory_space=pltpu.VMEM), pl.BlockSpec(memory_space=pl.ANY)
     units = lay.units // n
     widths = [lay.cols, 3 * span, units]
-    flat = inputs.shape[1:]
-    outs = [((sections, rows, m), BF) for m in (3 * span, lay.cols, units)]
+    flat = inputs.shape[2:]
+    outs = [((rows, m), BF) for m in (3 * span, lay.cols, units) for _ in range(sections)]
     outs += [((sections, lay.half, lay.width), BF), ((zs, rows, 3 * span), BF), ((span, lay.width), BF)]
     outs += [(flat, BF), (flat, BF), ((1, lay.tokens), jnp.int32)]
     outs += [((8, lay.width), F32), ((1, 3 * span), F32), ((1, units), F32)] * sections
@@ -1277,8 +1482,8 @@
     return pl.pallas_call(
         functools.partial(start_kernel, (block, span, lay.half, lay.seqs, lay.micros)),
         out_shape=[jax.ShapeDtypeStruct(*o) for o in outs],
-        in_specs=[vmem] * 5 + [hbm] * 2,
-        out_specs=[vmem] * 4 + [hbm] + [vmem] * (4 + 3 * sections),
+        in_specs=[vmem] * 7,
+        out_specs=[vmem] * (1 + 3 * sections) + [hbm] + [vmem] * (4 + 3 * sections),
         scratch_shapes=[
             pltpu.VMEM((chips, 2, zs, *tiny.shape), F32),
             pltpu.VMEM((zs, *tiny.shape), F32),
@@ -1304,12 +1509,13 @@
 
 def end_kernel(sizes, *refs):
     block, width, units, seqs = sizes
-    (part, turned, qkv_one, wo_one, fc_zero, fc_one, proj_zero, proj_one, small, last_rows), refs = refs[:10], refs[10:]
-    (out_qkv, out_wo, out_fc, out_proj, out_small, out_rows), refs = refs[:6], refs[6:]
+    (part, turned, qkv_one, wo_one, fc_zero, fc_one, proj_zero, proj_one), refs = refs[:8], refs[8:]
+    sums, (last_rows, *ready), refs = refs[:8], refs[8:15], refs[15:]
+    (out_qkv, out_wo, out_fc, out_proj, out_small, section_out, section_grad, home, out_rows), refs = refs[:9], refs[9:]
     (qkv_total, wo_part, wo_total, wo_cut, wo_back, proj_both, proj_land), refs = refs[:7], refs[7:]
     stages, lands, refs = refs[:3], refs[3:6], refs[6:]
-    (small_land, small_sum, z_land, came_qkv, came_wo), refs = refs[:5], refs[5:]
-    all_send, all_recv, far_send, far_recv, z_send, z_recv, turn_send, turn_recv, ring_send, ring_recv, late_send, late_recv, *route_sems = refs
+    (small_land, small_sum, z_land, came_qkv, came_wo, small, natural, rows_buf), refs = refs[:8], refs[8:]
+    all_send, all_recv, far_send, far_recv, z_send, z_recv, turn_send, turn_recv, ring_send, ring_recv, late_send, late_recv, *route_sems, rows_sem = refs
     peers = Peers()
     zs, z = lax.axis_size("z"), lax.axis_index("z")
     x, rest, slab = peers.x, peers.rest, 2 * peers.chips
@@ -1318,8 +1524,9 @@
     half, wide = proj_zero.shape[0], rest * block
     _, me = peers.other(0, 0, 0)
     offsets = peers.offsets()
-    route = Route(0, seqs, last_rows, out_rows, *route_sems)
-    peers.greet(zs, route)
+    route = Route(seqs, last_rows, home, *route_sems[:3])
+    across = Across(0, home, out_rows, *route_sems[3:5])
+    peers.greet(zs, Several([route, across]))
     sent = []
 
     def send(copy):
@@ -1328,8 +1535,50 @@
 
     ring = RingSum([(part, None, came_qkv, qkv_total, 0, zs - 1)], ring_send, ring_recv)
     ring.start()
+
+    def restore(first_crossed, second, first_home, out):
+        whole = lax.rem(z, 2) == x
+        for layer, choice in enumerate([(first_home, first_crossed), second]):
+            for kind, src in enumerate(choice):
+
+                @pl.when((x == layer) & (whole if kind == 0 else jnp.logical_not(whole)))
+                def _(src=src):
+                    pltpu.make_async_copy(src, rows_buf, rows_sem).start()
+
+        pltpu.make_async_copy(first_home, rows_buf, rows_sem).wait()
+        for micro in range(out.shape[0]):
+            for c in range(2):
+                for k in range(zs):
+                    at, of = (c * zs + k) * wide, (k * 2 + c) * wide
+                    out[micro, :, at : at + wide] = rows_buf[micro, :, of : of + wide]
+
     turn = TurnBack(peers, turned, wo_part, wo_cut, wo_back, turn_send, turn_recv)
     turn.start()
+    small[...] = jnp.zeros_like(small)
+    halves = half // block
+    for layer in range(2):
+        feed, attn, heads, unit = sums[4 * layer : 4 * layer + 4]
+        for t in range(slab):
+            natural[0:1, t * span : (t + 1) * span] = jnp.where(me == t, heads[:, :span], 0.0)
+            natural[1:2, t * span : (t + 1) * span] = jnp.where(me == t, heads[:, 2 * span :], 0.0)
+        for c in range(2):
+            for k in range(zs):
+                for r in range(rest):
+                    to = small.at[(layer * 2 + c) * rest + r, k]
+                    at = slice(((k * 2 + c) * rest + r) * block, ((k * 2 + c) * rest + r + 1) * block)
+                    to[0:1, :block] = attn[0:1, at]
+                    to[1:2, :block] = feed[0:1, at]
+                    to[2:3, :block] = attn[1:2, at]
+                    to[5:6, :block] = feed[3:4, at]
+                    to[6:8, :block] = feed[1:3, at]
+                    at = ((c * zs + k) * rest + r) * block
+                    to[3:5, :block] = natural[0:2, at : at + block]
+                    own = (peers.c == c) & (peers.r == r)
+                    for h in range(2):
+                        for j in range(halves):
+                            line = unit[0:1, k * half + j * block : k * half + (j + 1) * block]
+                            spot_row = 8 + h * halves + j
+                            to[spot_row : spot_row + 1, :block] = jnp.where(own & (x == h), line, 0.0)
     for i, place in offsets:
         device, t = peers.other(*place)
         send(remote(small.at[t], small_land.at[me], all_send.at[3, i], all_recv.at[3, i], device))
@@ -1373,21 +1622,24 @@
     z_land[z] = small_sum[z]
     ring.tick()
     wo_ring.tick()
+    route.arrived()
+    across.tick("middle")
     settle(0, lands[0])
     for t in range(slab):
         h, c, r = t // (2 * rest), t // rest % 2, t % rest
         for k in range(zs):
             at = ((c * zs + k) * rest + r) * (units // (2 * zs * rest)) + h * half
-            out_fc[:, at : at + half] = lands[0][t, :block, k * half : (k + 1) * half].astype(F32)
+            out_fc[:, at : at + half] = lands[0][t, :block, k * half : (k + 1) * half]
     ring.tick()
     wo_ring.tick()
+    restore(ready[1], ready[2:4], ready[0], section_out)
     came = proj_land.at[1 - x]
     remote(came, came, far_send, far_recv, device).wait_recv()
     for h in range(2):
         for c in range(2):
             for k in range(zs):
                 at, of = (c * zs + k) * wide, (k * 2 + c) * wide
-                out_proj[h * half : (h + 1) * half, at : at + wide] = proj_land[h, :, of : of + wide].astype(F32)
+                out_proj[h * half : (h + 1) * half, at : at + wide] = proj_land[h, :, of : of + wide]
     for k in range(1, zs):
         came = z_land.at[lax.rem(z + zs - k, zs)]
         remote(came, came, z_send.at[k], z_recv.at[k], {"z": lax.rem(z + k, zs)}).wait_recv()
@@ -1403,20 +1655,22 @@
     for t in range(slab):
         big, off = divmod(t * cols, wide)
         at = (big % 2 * zs + big // 2) * wide + off
-        out_wo[:, at : at + cols] = lands[2][t, :block, :].astype(F32)
+        out_wo[:, at : at + cols] = lands[2][t, :block, :]
     settle(1, lands[1])
     for t in range(slab):
         count = min(span, width - t * span)
         for p in range(3):
             if count > 0:
                 at = p * width + t * span
-                out_qkv[:, at : at + count] = lands[1][t, :block, p * span : p * span + count].astype(F32)
-    route.finish()
+                out_qkv[:, at : at + count] = lands[1][t, :block, p * span : p * span + count]
+    route.sent()
+    across.finish()
+    restore(out_rows, ready[4:], home, section_grad)
     for copy in sent:
         copy.wait_send()
 
 
-def run_end(name, lay, part, turned, qkv_one, wo_one, fcs, projs, small, last_rows):
+def run_end(name, lay, part, turned, qkv_one, wo_one, fcs, projs, sums, last_rows, ready):
     zs, n = lay.zs, lay.slab
     span, width, block = lay.slots * lay.head, lay.width, lay.block
     rows = part.shape[1]
@@ -1426,14 +1680,14 @@
     dma = pltpu.SemaphoreType.DMA
     widths = [fcs[0].shape[1], part.shape[2], lay.cols]
     half = projs[0].shape[0]
-    tile = small.shape[2:]
+    tile = (-(-(8 + lay.unit_block // block) // 8) * 8, 128)
     outs = [(block, 3 * width), (block, width), (block, lay.units), (lay.unit_block, width), tile]
     return pl.pallas_call(
         functools.partial(end_kernel, (block, width, lay.units, lay.seqs)),
-        out_shape=[jax.ShapeDtypeStruct(o, F32) for o in outs]
-        + [jax.ShapeDtypeStruct((lay.micros, *last_rows.shape), BF)],
-        in_specs=[vmem] * 9 + [pl.BlockSpec(memory_space=pl.ANY)],
-        out_specs=[vmem] * 5 + [pl.BlockSpec(memory_space=pl.ANY)],
+        out_shape=[jax.ShapeDtypeStruct(o, BF) for o in outs[:4]] + [jax.ShapeDtypeStruct(outs[4], F32)]
+        + [jax.ShapeDtypeStruct((lay.micros, *last_rows.shape), BF)] * 4,
+        in_specs=[vmem] * 16 + [pl.BlockSpec(memory_space=pl.ANY)] * 7,
+        out_specs=[vmem] * 7 + [pl.BlockSpec(memory_space=pl.ANY)] * 2,
         scratch_shapes=[
             pltpu.VMEM((rows, part.shape[2]), BF),
             pltpu.VMEM((zs, rows, lay.cols), BF),
@@ -1451,15 +1705,18 @@
             pltpu.VMEM((zs, *tile), F32),
             pltpu.VMEM((zs - 1, rows, part.shape[2]), BF),
             pltpu.VMEM((zs - 1, rows, lay.cols), BF),
+            pltpu.VMEM((n, zs, *tile), F32),
+            pltpu.VMEM((8, n * span), F32),
+            pltpu.VMEM((lay.micros, *last_rows.shape), BF),
         ]
         + [dma((4, n))] * 2
         + [dma] * 2
         + [dma((zs,))] * 2
         + [dma((n,))] * 2
         + [dma((2, zs - 1))] * 4
-        + [dma, dma, dma((lay.micros,))],
+        + [dma, dma, dma((lay.micros,)), dma, dma, dma],
         compiler_params=pltpu.CompilerParams(collective_id=name, has_side_effects=True, vmem_limit_bytes=60 * 2**20),
-    )(part, turned, qkv_one, wo_one, *fcs, *projs, small, last_rows)
+    )(part, turned, qkv_one, wo_one, *fcs, *projs, *sums, last_rows, *ready)
 
 
 class Rings:
@@ -1473,13 +1730,13 @@
         _, acc, steps = self.state.get((kind, layer), (None, None, 0))
         self.state[kind, layer] = (part, acc, steps)
 
-    def side(self, plan, makes={}, turned=None, cols=0):
+    def side(self, plan, pace, makes={}, turned=None, cols=0):
         pieces = []
         for kind, layer, count in plan:
             part, acc, steps = self.state.get((kind, layer), (None, None, 0))
             shape = makes[kind] if part is None else part.shape[1:]
             pieces.append((part, shape, acc, steps, count))
-        return sum_side(pieces, turned, cols)
+        return sum_side(pieces, pace, turned, cols)
 
     def done(self, plan, outs):
         for (kind, layer, count), acc in zip(plan, outs):
@@ -1501,20 +1758,24 @@
     places = jnp.pad(positions.astype(F32), ((0, 0), (0, 128 - lay.rows)))
     small = jnp.concatenate([small, places])
     small = jnp.pad(small, ((0, -small.shape[0] % 8), (0, 0)))
-    qkv_cut, wo_cut, fc_cut, proj_cut, w_qkv, w_out, h, g, row, *smalls = run_start(
-        0, lay, small, w_qkv[0], w_attn_out[0], w_fc[0], w_proj[0], inputs[:, 0], cotangent[:, 0]
+    *cut, proj_cut, w_qkv, w_out, h, g, row, vec_0, bias_0, unit_0, vec_1, bias_1, unit_1 = run_start(
+        0, lay, small, w_qkv[0], w_attn_out[0], w_fc[0], w_proj[0], inputs, cotangent
     )
-    smalls = [smalls[3 * layer : 3 * layer + 3] for layer in range(lay.sections)]
+    qkv_cut, wo_cut, fc_cut = cut[0:2], cut[2:4], cut[4:6]
+    smalls = [(vec_0, bias_0, unit_0), (vec_1, bias_1, unit_1)]
     col = row.reshape(lay.tokens, 1)
     outs, keeps, params = [], [], []
     for layer in range(lay.sections):
         last = layer == lay.sections - 1
         vec, bias, unit = smalls[layer]
         w_qkv = w_qkv.reshape(width, 3 * span)
-        (full, qkv, attended, logs, mid, normed_two), (w_fc, w_proj) = run_attention_forward(
+        side = gather_side([fc_cut[layer], (proj_cut, layer)], {"qkv": 1, "q0": 1, "q3": 1}, (lay.zs - 1, lay.zs - 2))
+        if last:
+            side = both_sides(side, share_side(lay, g, ("qkv", "q3")))
+        (full, qkv, attended, logs, mid, normed_two), (w_fc, w_proj, *shared) = run_attention_forward(
             1 + 2 * layer,
             lay.head,
-            gather_side([fc_cut[layer], proj_cut[layer]], (lay.zs - 1, lay.zs - 2)),
+            side,
             h,
             w_qkv,
             w_out,
@@ -1525,15 +1786,15 @@
         )
         w_fc = w_fc.reshape(width, -1)
         if last:
-            side = route_side(0, lay, outs[0])
+            side = route_side(lay, outs[0], "start")
         else:
-            side = gather_side([wo_cut[layer + 1], qkv_cut[layer + 1]], turn=span)
+            side = gather_side([wo_cut[layer + 1], qkv_cut[layer + 1]], {"k3": 2}, turn=span)
         (full_two, slope, activated, result, w_proj), later = run_feed_forward(
             2 + 2 * layer, side, normed_two, mid, w_fc, w_proj, unit, vec
         )
         params.append((w_qkv, w_out, w_fc, w_proj.reshape(-1, width)))
         if last:
-            routed = [later[0]]
+            (home,), (branch,) = later, shared
         else:
             w_out, w_qkv = later
         keeps.append((h, full, qkv, attended, logs, mid, full_two, slope, activated))
@@ -1542,12 +1803,19 @@
 
     rings = Rings(lay)
     plans = {
-        ("feed", 1): [("proj", 1, 1)],
-        ("attention", 1): [("proj", 1, 2), ("fc", 1, 2)],
-        ("feed", 0): [("qkv", 1, 3), ("fc", 1, 1), ("proj", 0, 1)],
+        ("feed", 1): [("proj", 1, 3)],
+        ("attention", 1): [("fc", 1, 3)],
+        ("feed", 0): [("qkv", 1, 3), ("proj", 0, 1)],
         ("attention", 0): [("fc", 0, 3), ("proj", 0, 2), ("out", 1, 3)],
     }
-    grad_rows, sums = [None] * lay.sections, [None] * lay.sections
+    paces = {
+        ("feed", 1): {"proj": 1, "fc": 1},
+        ("attention", 1): {"k2": 1, "grad": 1},
+        ("feed", 0): {"k2": 1, "fc": 1, "launch": "fc"},
+        ("attention", 0): {"k3": 3},
+    }
+    crossed = {}
+    sums = [None] * lay.sections
     grad_out = None
     for layer in reversed(range(lay.sections)):
         w_qkv, w_out, w_fc, w_proj = params[layer]
@@ -1555,46 +1823,33 @@
         h, full, qkv, attended, logs, mid, full_two, slope, activated = keeps[layer]
         full, full_two = (a.reshape(lay.tokens, width) for a in (full, full_two))
         name = 1 + 4 * lay.sections - 2 * layer
-        side = rings.side(plans["feed", layer], {"proj": (lay.half, width)}, grad_out, lay.cols)
-        side = both_sides(side, route_side(1, lay, outs[1] if grad_out is None else g))
+        side = rings.side(plans["feed", layer], paces["feed", layer], {"proj": (lay.half, width)}, grad_out, lay.cols)
+        late = grad_out is None
+        if late:
+            side = both_sides(side, route_side(lay, outs[1], "start"), across_side(0, home))
+        else:
+            side = both_sides(side, route_side(lay, g, "fc"))
         (grad_mid, attn_rows, grad_proj, grad_fc, feed_sums, unit_sums), done = run_feed_backward(
-            name, side, g, mid, w_fc, w_proj, slope, activated, full_two, vec
+            name, side, g, mid, w_fc, w_proj, slope, activated, full_two, vec, *([branch] if late else [])
         )
         rings.put("proj", layer, grad_proj)
         rings.put("fc", layer, grad_fc)
         rings.done(plans["feed", layer], done)
-        routed.append(done[-1])
-        if grad_out is not None:
+        if late:
+            crossed["out", 0] = (home, done[-1])
+            home = done[-2]
+        else:
+            home = done[-1]
             rings.put("out", layer + 1, done[-2])
-        side = rings.side(plans["attention", layer])
+        side = both_sides(rings.side(plans["attention", layer], paces["attention", layer]), across_side(1, home))
         (g, grad_qkv, grad_out, attn_sums, head_sums), done = run_attention_backward(
             name + 1, lay.head, side, attn_rows, grad_mid, h, w_qkv, w_out, qkv, attended, logs, full, col, row, vec
         )
         rings.done(plans["attention", layer], done)
+        crossed["out" if late else "grad", 1] = (home, done[-1])
         rings.put("qkv", layer, grad_qkv)
-        grad_rows[layer] = g
-        sums[layer] = (feed_sums, unit_sums, attn_sums, head_sums)
-    rows = []
-    for layer in range(lay.sections):
-        feed_sums, unit_sums, attn_sums, head_sums = sums[layer]
-        feed_sums, attn_sums = lay.restore(feed_sums), lay.restore(attn_sums)
-        zero = jnp.zeros((n * span,), jnp.float32)
-        s_q = lax.dynamic_update_slice_in_dim(zero, head_sums[0, :span], lay.t * span, 0)[:width]
-        s_v = lax.dynamic_update_slice_in_dim(zero, head_sums[0, 2 * span :], lay.t * span, 0)[:width]
-        cols = [attn_sums[0], feed_sums[0], attn_sums[1], s_q, s_v, feed_sums[3], feed_sums[1], feed_sums[2]]
-        cols = jnp.stack(cols, axis=1).reshape(lay.shards, block * 8)
-        spots = jnp.zeros((n, lay.zs, lay.half), jnp.float32)
-        spots = lax.dynamic_update_index_in_dim(
-            spots, unit_sums.reshape(lay.zs, lay.half), lay.t, 0
-        )
-        spots = spots.reshape(lay.sections, lay.cores, lay.rest, lay.zs, lay.half)
-        spots = spots.transpose(1, 3, 2, 0, 4).reshape(lay.shards, lay.unit_block)
-        rows.append(jnp.concatenate([cols, spots], axis=1))
-    rows = jnp.stack(rows).reshape(lay.sections, lay.cores, lay.zs, lay.rest, -1)
-    used = rows.shape[-1]
-    rows = jnp.pad(jnp.swapaxes(rows, 2, 3), ((0, 0),) * 4 + ((0, -used % 1024),))
-    rows = rows.reshape(n, lay.zs, -1, 128)
-    out_qkv, out_attn, out_fc, out_proj, rows, routed_grad = run_end(
+        sums[layer] = (feed_sums, attn_sums, head_sums, unit_sums)
+    out_qkv, out_attn, out_fc, out_proj, rows, section_out, section_grad, *_ = run_end(
         3 + 4 * lay.sections,
         lay,
         rings.state["qkv", 0][0],
@@ -1603,24 +1858,21 @@
         rings.state["out", 1][1],
         [rings.state["fc", layer][1] for layer in range(2)],
         [rings.state["proj", layer][1] for layer in range(2)],
-        rows,
+        [a for layer in range(2) for a in sums[layer]],
         g,
+        [*crossed["out", 0], *crossed["out", 1], *crossed["grad", 1]],
     )
-    first = lay.x == 0
-    section_out = lay.restore(jnp.where(first, routed[0], routed[1]))[None, :, None]
-    section_grad = lay.restore(jnp.where(first, routed_grad, routed[2]))[None, :, None]
-    rows = rows.reshape(-1)[:used]
-    cols = rows[: block * 8].reshape(block, 8)
+    cols = rows[:8, :block].T
     return (
-        section_out,
-        section_grad,
-        out_qkv[None],
-        out_attn[None],
-        out_fc[None],
-        out_proj[None],
+        section_out[None, :, None],
+        section_grad[None, :, None],
+        out_qkv.astype(F32)[None],
+        out_attn.astype(F32)[None],
+        out_fc.astype(F32)[None],
+        out_proj.astype(F32)[None],
         cols[None, :, :2],
         cols[None, :, 2:],
-        rows[None, block * 8 :],
+        rows[8 : 8 + lay.unit_block // block, :block].reshape(1, lay.unit_block),
     )
 
 

time: 928 us -> 842 us (0.907)
  Pallas kernels: 883 us -> 805 us
  local copies, waits for them, and re-layouts: 37 us -> 21.9 us
    pallas_call x8, Pallas kernels: 664 us -> 614 us  [call(): pl.pallas_call(body, out_shape=[jax.ShapeDtypeStruct(*o) for o in (*outs,...]
    pallas_call x1, Pallas kernels: 112 us -> 92.5 us  [run_start(): pl.pallas_call(functools.partial(start_kernel, (block, span, lay.half, la...]
where the time goes in v7:
time: 842 us; the launch traced here: 832 us
  Pallas kernels  805 us (96%)
  local copies, waits for them, and re-layouts  21.9 us (3%)
    pallas_call x8, Pallas kernels, call(): pl.pallas_call(body, out_shape=[jax.ShapeDtypeStruct(*o) for o in (*outs,...  614 us
    pallas_call x1, Pallas kernels, run_end(): pl.pallas_call(functools.partial(end_kernel, (block, width, lay.units, la...  98.9 us
    pallas_call x1, Pallas kernels, run_start(): pl.pallas_call(functools.partial(start_kernel, (block, span, lay.half, la...  92.5 us
    unnamed x18, local copies, waits for them, and re-layouts  18.3 us

profile of v7, /device:TPU:3, one launch (start us, length us, event | category | flops | bytes accessed | tf_op | source)
XLA Modules:
  0.0 832.5 jit_solution(4242791927706902009)
XLA Ops:
  0.6 0.7 convert_element_type.20
  1.3 0.7 convert_reduce_fusion
  2.0 0.1 reshape.84
  2.1 0.7 convert_bitcast_fusion
  2.9 0.6 pad.9.refs_0_
  3.5 2.2 copy.27.refs_5_
  5.7 2.2 copy.28.refs_6_
  7.8 92.5 %shard_map.169 = (bf16[400,768]{1,0:T(8,128)(2,1)}, bf16[400,768]{1,0:T(8,128)(2,1)}, bf16[400,200]{1,0:T(8,128)(2,1)}, bf16[400,200]{1,0:T(8,128)(2,1)}, bf16[4...) custom-call(f32[16,128]{1,0:T(8,128)} %pad.9.refs_0_, ...), custom_call_target="tpu_custom_call" | custom-call | tf_op jit(solution)/shard_map/pallas_call | solution.py:1482
  100.4 1.7 copy.29.refs_4_.refs_9_
  102.1 80.0 %shard_map.170 = (bf16[4,2,128,1600]{3,2,1,0:T(8,128)(2,1)}, bf16[1024,768]{1,0:T(8,128)(2,1)}, bf16[1024,256]{1,0:T(8,128)(2,1)}, f32[8,1024]{1,0:T(8,128)}, f3...) custom-call(bf16[128,1600]{1,0:T(8,128)(2,1)} %get-tuple-element.97., ...), custom_call_target="tpu_custom_call" | custom-call | tf_op jit(solution)/shard_map/pallas_call | solution.py:1254
  182.1 78.2 %shard_map.171 = (bf16[4,2,128,1600]{3,2,1,0:T(8,128)(2,1)}, bf16[1024,800]{1,0:T(8,128)(2,1)}, bf16[1024,800]{1,0:T(8,128)(2,1)}, bf16[128,1600]{1,0:T(8,128)(2...) custom-call(bf16[128,1600]{1,0:T(8,128)(2,1)} %get-tuple-element.105.refs_0_, ...), custom_call_target="tpu_custom_call" | custom-call | tf_op jit(solution)/shard_map/pallas_call | solution.py:1254
  260.3 82.2 %shard_map.172 = (bf16[4,2,128,1600]{3,2,1,0:T(8,128)(2,1)}, bf16[1024,768]{1,0:T(8,128)(2,1)}, bf16[1024,256]{1,0:T(8,128)(2,1)}, f32[8,1024]{1,0:T(8,128)}, f3...) custom-call(bf16[128,1600]{1,0:T(8,128)(2,1)} %get-tuple-element.112, ...), custom_call_target="tpu_custom_call" | custom-call | tf_op jit(solution)/shard_map/pallas_call | solution.py:1254
  342.5 56.7 %shard_map.173 = (bf16[4,2,128,1600]{3,2,1,0:T(8,128)(2,1)}, bf16[1024,800]{1,0:T(8,128)(2,1)}, bf16[1024,800]{1,0:T(8,128)(2,1)}, bf16[128,1600]{1,0:T(8,128)(2...) custom-call(bf16[128,1600]{1,0:T(8,128)(2,1)} %get-tuple-element.120.refs_0_, ...), custom_call_target="tpu_custom_call" | custom-call | tf_op jit(solution)/shard_map/pallas_call | solution.py:1254
  399.2 64.6 %shard_map.174 = (f32[128,1600]{1,0:T(8,128)}, bf16[128,1600]{1,0:T(8,128)(2,1)}, bf16[4,200,1600]{2,1,0:T(8,128)(2,1)}, bf16[1600,800]{1,0:T(8,128)(2,1)}, f32[...) custom-call(bf16[128,1600]{1,0:T(8,128)(2,1)} %get-tuple-element.96., ...), custom_call_target="tpu_custom_call" | custom-call | tf_op jit(solution)/shard_map/pallas_call | solution.py:1254
  463.8 69.4 %shard_map.175 = (bf16[128,1600]{1,0:T(8,128)(2,1)}, bf16[1600,768]{1,0:T(8,128)(2,1)}, bf16[256,1600]{1,0:T(8,128)(2,1)}, f32[8,1600]{1,0:T(8,128)}, f32[1,768]...) custom-call(bf16[128,1600]{1,0:T(8,128)(2,1)} %get-tuple-element.130.refs_0_, ...), custom_call_target="tpu_custom_call" | custom-call | tf_op jit(solution)/shard_map/pallas_call | solution.py:1254
  533.2 85.4 %shard_map.176 = (f32[128,1600]{1,0:T(8,128)}, bf16[128,1600]{1,0:T(8,128)(2,1)}, bf16[4,200,1600]{2,1,0:T(8,128)(2,1)}, bf16[1600,800]{1,0:T(8,128)(2,1)}, f32[...) custom-call(bf16[128,1600]{1,0:T(8,128)(2,1)} %get-tuple-element.138, ...), custom_call_target="tpu_custom_call" | custom-call | tf_op jit(solution)/shard_map/pallas_call | solution.py:1254
  618.7 97.4 %shard_map.177 = (bf16[128,1600]{1,0:T(8,128)(2,1)}, bf16[1600,768]{1,0:T(8,128)(2,1)}, bf16[256,1600]{1,0:T(8,128)(2,1)}, f32[8,1600]{1,0:T(8,128)}, f32[1,768]...) custom-call(bf16[128,1600]{1,0:T(8,128)(2,1)} %get-tuple-element.145, ...), custom_call_target="tpu_custom_call" | custom-call | tf_op jit(solution)/shard_map/pallas_call | solution.py:1254
  716.1 98.9 %shard_map.178 = (bf16[100,4800]{1,0:T(8,128)(2,1)}, bf16[100,1600]{1,0:T(8,128)(2,1)}, bf16[100,6400]{1,0:T(8,128)(2,1)}, bf16[400,1600]{1,0:T(8,128)(2,1)}, f3...) custom-call(bf16[4,400,768]{2,1,0:T(8,128)(2,1)} %bitcast.59, ...), custom_call_target="tpu_custom_call" | custom-call | tf_op jit(solution)/shard_map/pallas_call | solution.py:1685
  815.0 0.0 copy-start.4
  815.0 2.3 copy.33
  817.3 2.1 copy.34
  819.4 0.7 reshape.83
  820.1 0.6 slice_bitcast_fusion.2
  820.7 0.6 copy.38
  821.3 1.5 copy.36
  822.8 0.1 bitcast_convert_fusion.2
  823.0 0.0 copy-start.1
  823.0 3.3 copy.35
  826.3 0.0 copy-done.1
  826.3 0.2 bitcast_convert_fusion.1
  826.4 4.1 copy.37
  830.6 1.7 bitcast_convert_fusion
  (16 shorter events, 0.1 us)
Async XLA Ops:
  815.0 4.4 copy-start.4
  815.0 6.2 copy-start.3
  815.0 7.8 copy-start.2
  823.0 3.3 copy-start.1
  826.4 4.1 copy-start

commit v8 on v7

--- a/solution.py
+++ b/solution.py
@@ -260,9 +260,13 @@
         self.sent.append(copy)
 
     def start(self):
-        for p, (shard, full, _) in enumerate(self.pieces):
-            self.send(p, 0, shard)
-            pltpu.make_async_copy(shard, full.at[self.z], self.local.at[p]).start()
+        for p in range(len(self.pieces)):
+            self.launch(p)
+
+    def launch(self, p):
+        shard, full, _ = self.pieces[p]
+        self.send(p, 0, shard)
+        pltpu.make_async_copy(shard, full.at[self.z], self.local.at[p]).start()
 
     def tick(self, count=1):
         for _ in range(min(count, self.forwards)):
@@ -358,15 +362,33 @@
 
 
 class TurnBack:
-    def __init__(self, peers, turned, part, pieces, came, send, recv):
-        self.peers, self.turned, self.part, self.pieces, self.came = peers, turned, part, pieces, came
+    def __init__(self, peers, part, pieces, came, send, recv, given=None):
+        self.given = given
+        self.peers, self.part, self.pieces, self.came = peers, part, pieces, came
         self.send_sem, self.recv_sem = send, recv
         self.sent = []
 
+    def greet(self):
+        return 0
+
     def start(self):
+        pass
+
+    def tick(self, point):
+        pass
+
+    def middle(self):
+        if self.given is not None:
+            self.share(self.given)
+
+    def made(self, turned):
+        if self.given is None:
+            self.share(turned)
+
+    def share(self, turned):
         slab, _, cols = self.pieces.shape
         for t in range(slab):
-            self.pieces[t] = self.turned[:, t * cols : (t + 1) * cols]
+            self.pieces[t] = turned[:, t * cols : (t + 1) * cols]
         _, me = self.peers.other(0, 0, 0)
         for i, place in self.peers.offsets():
             device, t = self.peers.other(*place)
@@ -392,22 +414,6 @@
                     done += count
         for copy in self.sent:
             copy.wait_send()
-
-
-class SumAndTurn:
-    def greet(self):
-        return 0
-
-    def __init__(self, ring, turn):
-        self.ring, self.turn = ring, turn
-        self.start, self.tick, self.made = ring.start, ring.tick, ring.made
-
-    def middle(self):
-        self.turn.start()
-
-    def finish(self):
-        self.turn.finish()
-        self.ring.finish()
 
 
 class Turn:
@@ -653,7 +659,7 @@
     for c in range(2):
         for k in range(zs):
             at, to = (c * zs + k) * wide, (k * 2 + c) * wide
-            ordered[:, to : to + wide] = raw[:, at : at + wide]
+            ordered[:, to : to + wide] = raw[at : at + wide, :].astype(F32).T.astype(BF)
 
 
 class Shared:
@@ -737,19 +743,25 @@
     def greet(self):
         return 0
 
-    def __init__(self, ring, turn):
-        self.ring, self.turn, self.turned = ring, turn, False
+    def __init__(self, ring, turn, ahead):
+        self.ring, self.turn = ring, turn
+        if ahead:
+            ring.steps.sort(key=lambda step: step[1] if step[0] else step[1] * 0.5 - 0.6)
 
     def start(self):
         self.ring.start()
 
     def tick(self, count=1):
-        self.ring.tick(count)
+        for _ in range(count):
+            self.take()
+
+    def take(self):
+        if self.ring.take() == 0:
+            self.turn.start()
 
     def finish(self):
         while self.ring.steps:
-            if self.ring.take() == 0:
-                self.turn.start()
+            self.take()
         self.ring.finish()
         self.turn.finish()
 
@@ -813,6 +825,18 @@
         return Route(lay.seqs, ins[0], outs[0], *scratch, when)
 
     return SideWork([src], (True,), outs, (True,), [dma, dma, dma((lay.micros,))], build)
+
+
+def turn_side(lay, turned=None):
+    n, span = lay.slab, lay.slots * lay.head
+    outs = [((lay.zs, lay.width // lay.zs, lay.cols), BF)]
+    scratch = [pltpu.VMEM((n, span, lay.cols), BF)] * 2 + [pltpu.SemaphoreType.DMA((n,))] * 2
+
+    def build(peers, ins, outs, scratch):
+        return TurnBack(peers, outs[0], *scratch, ins[0] if ins else None)
+
+    operands = [] if turned is None else [turned]
+    return SideWork(operands, (False,) * len(operands), outs, (False,), scratch, build)
 
 
 def share_side(lay, a, points):
@@ -878,12 +902,12 @@
     def build_turn(peers, ins, outs, scratch):
         pieces = list(zip(ins, [scratch[3], *outs[1:]], counts))
         turning = Turn(peers, scratch[3], scratch[4], scratch[5], outs[0], *scratch[6:8])
-        return Paced(Both(RingGather(pieces, *scratch[:3]), turning), pace)
+        return Paced(Both(RingGather(pieces, *scratch[:3]), turning, False), pace)
 
     return SideWork(shards, (True,) * n, outs, (False,) + (True,) * (n - 1), sems + more, build_turn)
 
 
-def sum_side(pieces, pace, turned=None, cols=0):
+def sum_side(pieces, pace):
     zs = lax.axis_size("z")
     n = len(pieces)
     operands, outs, scratch = [], [], []
@@ -892,13 +916,6 @@
         outs.append((shape, BF))
         scratch.append(pltpu.VMEM((count, *shape), BF))
     scratch += [pltpu.SemaphoreType.DMA((n, zs - 1))] * 2
-    if turned is not None:
-        operands.append(turned)
-        slab = turned.shape[1] // cols
-        rows = turned.shape[1] // zs
-        outs.append(((zs, rows, cols), BF))
-        scratch += [pltpu.VMEM((slab, turned.shape[0], cols), BF)] * 2 + [pltpu.SemaphoreType.DMA((slab,))] * 2
-
     def build(peers, ins, outs, scratch):
         ins, made = list(ins), []
         for i, (part, shape, acc, first, count) in enumerate(pieces):
@@ -906,9 +923,7 @@
             acc_ref = None if acc is None else ins.pop(0)
             made.append((part_ref, acc_ref, scratch[i], outs[i], first, count))
         ring = RingSum(made, *scratch[n : n + 2])
-        if turned is None:
-            return Paced(ring, pace)
-        return Paced(SumAndTurn(ring, TurnBack(peers, ins.pop(0), outs[n], *scratch[n + 2 :])), pace)
+        return Paced(ring, pace)
 
     return SideWork(operands, (False,) * len(operands), outs, (False,) * len(outs), scratch, build)
 
@@ -1025,16 +1040,16 @@
 
 
 def feed_forward(side, *refs):
-    (src, mid, w_fc, w_proj, bias, vec) = refs[:6]
+    (src, mid, fc_packed, w_proj, bias, vec) = refs[:6]
     ins, refs = refs[6 : 6 + len(side.operands)], refs[6 + len(side.operands) :]
-    (normed_two, slope, activated, result, proj_out), refs = refs[:5], refs[5:]
+    (normed_two, slope, activated, result, proj_out, fc_out), refs = refs[:6], refs[6:]
     side_outs, refs = refs[: len(side.outs)], refs[len(side.outs) :]
-    gather_refs, reduce_refs, side_refs = refs[:5], refs[5 : 14 + 6], refs[14 + 6 :]
+    gather_refs, reduce_refs, side_refs = refs[:5], refs[5 : 14 + 8], refs[14 + 8 :]
     rows, width = src.shape
     peers = Peers()
     gather = Gather(peers, gather_refs[0], gather_refs[1:])
     reduce = Reduce(peers, *reduce_refs[:5], reduce_refs[5:9])
-    kept_sem, proj, proj_local, proj_send, proj_recv, proj_sem = reduce_refs[9:15]
+    kept_sem, proj, proj_local, proj_send, proj_recv, proj_sem, w_fc, fc_sem = reduce_refs[9:17]
     full = gather.full
     work = side.make(peers, ins, side_outs, side_refs)
     zs, z = lax.axis_size("z"), lax.axis_index("z")
@@ -1048,6 +1063,13 @@
     placed = [pltpu.make_async_copy(w_proj.at[b], proj.at[b], proj_local.at[i]) for i, b in enumerate(here)]
     for copy in placed:
         copy.start()
+    rows_of, units = fc_packed.shape[1], w_fc.shape[1]
+    for b in range(zs):
+        for c in range(2):
+            at = (b * 2 + c) * rows_of
+            w_fc[at : at + rows_of, :] = fc_packed[b, :, c * units : (c + 1) * units]
+    fc_kept = pltpu.make_async_copy(w_fc, fc_out, fc_sem)
+    fc_kept.start()
     before = None
     for k, chip in gather.arrivals():
         if k == 0:
@@ -1079,6 +1101,7 @@
     result[...] = out
     last.wait_send()
     proj_kept.wait()
+    fc_kept.wait()
     work.finish()
     gather.finish()
     reduce.finish()
@@ -1138,8 +1161,12 @@
         proj_terms()
     work.tick("proj")
     back = hidden[...]
-    for a, b in chunks(width, 512):
-        grad_fc[a:b, :] = dot(normed_two[:, a:b], back, 0, 0).astype(BF)
+    blocks, rows_of, units = grad_fc.shape[0], grad_fc.shape[1], back.shape[1]
+    for b in range(blocks):
+        at = b * 2 * rows_of
+        part = dot(normed_two[:, at : at + 2 * rows_of], back, 0, 0).astype(BF)
+        for c in range(2):
+            grad_fc[b, :, c * units : (c + 1) * units] = part[c * rows_of : (c + 1) * rows_of]
     work.tick("fc")
     unit_sums[...] = jnp.sum(back.astype(F32), axis=0, keepdims=True)
     own = src[...].astype(F32)
@@ -1162,7 +1189,7 @@
 def attention_backward(head, side, *refs):
     (src, grad_mid, h, w_qkv, w_out, qkv, attended, logs, normed, col, row, vec) = refs[:12]
     ins, refs = refs[12 : 12 + len(side.operands)], refs[12 + len(side.operands) :]
-    (grad_in, grad_qkv, grad_out, sums, head_sums), refs = refs[:5], refs[5:]
+    (grad_in, *grad_parts, grad_out, sums, head_sums), refs = refs[:7], refs[7:]
     side_outs, refs = refs[: len(side.outs)], refs[len(side.outs) :]
     gather_refs, reduce_refs, side_refs = refs[:5], refs[5 : 14 + 3], refs[14 + 3 :]
     joint, key_sum, value_sum = reduce_refs[9:12]
@@ -1219,10 +1246,13 @@
         before = k
     work.tick("sent")
     grads = joint[...]
+    grad_out[...] = dot(attended[...], full[...].reshape(tokens, width), 0, 0).astype(BF)
+    work.made(grad_out)
     for a, b in chunks(width, 512):
-        grad_qkv[a:b, :] = dot(normed[:, a:b], grads, 0, 0).astype(BF)
+        part = dot(normed[:, a:b], grads, 0, 0).astype(BF)
+        for i, grad in enumerate(grad_parts):
+            grad[a:b, :] = part[:, i * span : (i + 1) * span]
     work.tick("grad")
-    grad_out[...] = dot(attended[...], full[...].reshape(tokens, width), 0, 0).astype(BF)
     head_sums[...] = jnp.sum(grads.astype(F32), axis=0, keepdims=True)
     part, gain, shift = norm_back(h[...].astype(F32), vec[0:1, :], reduce.total())
     grad_in[...] = (grad_mid[...] + part).astype(BF)
@@ -1284,7 +1314,7 @@
 def run_feed_forward(name, side, *operands):
     src, mid, w_fc, w_proj, bias, vec = operands
     rows, width = src.shape
-    units = w_fc.shape[1]
+    units = w_fc.shape[2] // 2
     chips = lax.axis_size("section") * lax.axis_size("r")
     tokens = 2 * chips * rows
     outs = [
@@ -1293,10 +1323,11 @@
         ((tokens, units), BF),
         ((rows, width), BF),
         (w_proj.shape, BF),
+        ((width, units), BF),
     ]
     dma = pltpu.SemaphoreType.DMA
-    scratch = [dma, pltpu.VMEM(w_proj.shape, BF), dma((w_proj.shape[0],)), dma, dma, dma]
-    return call(functools.partial(feed_forward, side), name, outs, operands, side, (0, 4), scratch, (3,))
+    scratch = [dma, pltpu.VMEM(w_proj.shape, BF), dma((w_proj.shape[0],)), dma, dma, dma, pltpu.VMEM((width, units), BF), dma]
+    return call(functools.partial(feed_forward, side), name, outs, operands, side, (0, 4, 5), scratch, (3,))
 
 
 def run_feed_backward(name, side, *operands):
@@ -1308,7 +1339,7 @@
         ((rows, width), F32),
         ((rows, width), BF),
         ((zs, units // zs, width), BF),
-        ((width, units), BF),
+        ((zs, width // (2 * zs), 2 * units), BF),
         ((8, width), F32),
         ((1, units), F32),
     ]
@@ -1321,7 +1352,9 @@
     tokens, span = attended.shape
     outs = [
         ((rows, width), BF),
-        ((width, 3 * span), BF),
+        ((width, span), BF),
+        ((width, span), BF),
+        ((width, span), BF),
         ((span, width), BF),
         ((8, width), F32),
         ((1, 3 * span), F32),
@@ -1333,7 +1366,7 @@
 def start_kernel(sizes, *refs):
     block, span, half, seqs, micros = sizes
     (tiny, w_qkv, w_attn, w_fc, w_proj, inputs, cotangent), refs = refs[:7], refs[7:]
-    (qkv, wo, fc, (proj, qkv_full, w_out, h, g, row, *smalls)), refs = (refs[0:2], refs[2:4], refs[4:6], refs[6:18]), refs[18:]
+    (qkv, wo, fc, (proj, qkv_full, w_out, h, g, row, col, *smalls)), refs = (refs[0:2], refs[2:4], refs[4:6], refs[6:19]), refs[19:]
     tiny_out, stage, h_raw, g_raw, natural, proj_cut = refs[:6]
     cuts, lands, (wo_full, nat, land), refs = refs[6:9], refs[9:12], refs[12:15], refs[15:]
     z_send, z_recv, *sems = refs[:6]
@@ -1373,7 +1406,11 @@
             remote(came, came, all_send.at[a, i], all_recv.at[a, i], device).wait_recv()
         for layer in range(sections):
             for i in range(2 * rest):
-                shard[layer][i * block : (i + 1) * block, :] = lands[a][layer, i, :block, :]
+                rows_at, lanes_at = i * block, 0
+                if a == 2:
+                    rows_at, lanes_at = i % rest * block, i // rest * lands[a].shape[3]
+                to = shard[layer].at[rows_at : rows_at + block, lanes_at : lanes_at + lands[a].shape[3]]
+                to[...] = lands[a][layer, i, :block, :]
 
     cols = width // slab
     for t in range(slab):
@@ -1406,19 +1443,22 @@
     gather = Gather(peers, tiny_out, sems)
     gather.start(stage)
     settle(0, wo)
-    settle(1, qkv)
     turn = Turn(peers, wo_full, nat, land, w_out, turn_send, turn_recv)
     ring = RingGather([(wo[0], wo_full, zs - 1), (qkv[0], qkv_full, zs - 1)], ring_local, ring_send, ring_recv)
-    work = Both(ring, turn)
-    work.start()
+    work = Both(ring, turn, True)
+    ring.launch(0)
+    settle(1, qkv)
+    ring.launch(1)
     share(2)
     for d in range(1, sections):
         device, _ = peers.other(d, 0, 0)
         there = lax.rem(x + d, sections)
         send(remote(proj_cut.at[there], proj.at[x], far_send.at[d], far_recv.at[d], device))
     proj[x] = proj_cut[x]
+    work.tick()
     for _ in gather.arrivals():
         pass
+    work.tick()
 
     per_row, halves = sections * half // block, half // block
     for layer in range(sections):
@@ -1448,7 +1488,8 @@
                 at = ((a * rest + r) * 2 + c) * rows
                 line = tiny_out[r, 0, c * 2 + a, pl.ds(8 + per_row + z // seqs, 1), :rows]
                 row[:, at : at + rows] = line.astype(jnp.int32)
-    work.tick()
+                col[at : at + rows, :] = jnp.broadcast_to(line, (8, rows)).T[:, :1].astype(jnp.int32)
+    work.tick(2)
     settle(2, fc)
     work.tick()
     for i, (raw, ordered) in enumerate([(h_raw, h), (g_raw, g)]):
@@ -1473,22 +1514,22 @@
     vmem, hbm = pl.BlockSpec(memory_space=pltpu.VMEM), pl.BlockSpec(memory_space=pl.ANY)
     units = lay.units // n
     widths = [lay.cols, 3 * span, units]
-    flat = inputs.shape[2:]
-    outs = [((rows, m), BF) for m in (3 * span, lay.cols, units) for _ in range(sections)]
+    flat = (lay.rows, lay.width)
+    outs = [(a, BF) for a in ((rows, 3 * span), (rows, lay.cols), (rows // 2, 2 * units)) for _ in range(sections)]
     outs += [((sections, lay.half, lay.width), BF), ((zs, rows, 3 * span), BF), ((span, lay.width), BF)]
-    outs += [(flat, BF), (flat, BF), ((1, lay.tokens), jnp.int32)]
+    outs += [(flat, BF), (flat, BF), ((1, lay.tokens), jnp.int32), ((lay.tokens, 1), jnp.int32)]
     outs += [((8, lay.width), F32), ((1, 3 * span), F32), ((1, units), F32)] * sections
     dma = pltpu.SemaphoreType.DMA
     return pl.pallas_call(
         functools.partial(start_kernel, (block, span, lay.half, lay.seqs, lay.micros)),
         out_shape=[jax.ShapeDtypeStruct(*o) for o in outs],
         in_specs=[vmem] * 7,
-        out_specs=[vmem] * (1 + 3 * sections) + [hbm] + [vmem] * (4 + 3 * sections),
+        out_specs=[vmem] * (1 + 3 * sections) + [hbm] + [vmem] * (5 + 3 * sections),
         scratch_shapes=[
             pltpu.VMEM((chips, 2, zs, *tiny.shape), F32),
             pltpu.VMEM((zs, *tiny.shape), F32),
-            pltpu.VMEM(flat, BF),
-            pltpu.VMEM(flat, BF),
+            pltpu.VMEM(flat[::-1], BF),
+            pltpu.VMEM(flat[::-1], BF),
             pltpu.VMEM((8, n * span), F32),
             pltpu.VMEM((sections, lay.half, lay.width), BF),
         ]
@@ -1509,18 +1550,18 @@
 
 def end_kernel(sizes, *refs):
     block, width, units, seqs = sizes
-    (part, turned, qkv_one, wo_one, fc_zero, fc_one, proj_zero, proj_one), refs = refs[:8], refs[8:]
+    parts, (q_one, k_one, v_one, wo_one), (fc_zero, fc_one, proj_zero, proj_one), refs = refs[:4], refs[4:8], refs[8:12], refs[12:]
     sums, (last_rows, *ready), refs = refs[:8], refs[8:15], refs[15:]
     (out_qkv, out_wo, out_fc, out_proj, out_small, section_out, section_grad, home, out_rows), refs = refs[:9], refs[9:]
-    (qkv_total, wo_part, wo_total, wo_cut, wo_back, proj_both, proj_land), refs = refs[:7], refs[7:]
-    stages, lands, refs = refs[:3], refs[3:6], refs[6:]
-    (small_land, small_sum, z_land, came_qkv, came_wo, small, natural, rows_buf), refs = refs[:8], refs[8:]
-    all_send, all_recv, far_send, far_recv, z_send, z_recv, turn_send, turn_recv, ring_send, ring_recv, late_send, late_recv, *route_sems, rows_sem = refs
+    totals, (proj_both, proj_land), refs = refs[:4], refs[4:6], refs[6:]
+    stages, lands, refs = refs[:5], refs[5:10], refs[10:]
+    (small_land, small_sum, z_land), came, (small, natural, rows_buf), refs = refs[:3], refs[3:7], refs[7:10], refs[10:]
+    all_send, all_recv, far_send, far_recv, z_send, z_recv, ring_send, ring_recv, late_send, late_recv, *route_sems, rows_sem = refs
     peers = Peers()
     zs, z = lax.axis_size("z"), lax.axis_index("z")
     x, rest, slab = peers.x, peers.rest, 2 * peers.chips
     spot = peers.c * rest + peers.r
-    span, cols = turned.shape[0], wo_total.shape[1]
+    span, cols = q_one.shape[1], wo_one.shape[1]
     half, wide = proj_zero.shape[0], rest * block
     _, me = peers.other(0, 0, 0)
     offsets = peers.offsets()
@@ -1533,8 +1574,10 @@
         copy.start()
         sent.append(copy)
 
-    ring = RingSum([(part, None, came_qkv, qkv_total, 0, zs - 1)], ring_send, ring_recv)
+    pieces = [(parts[p], None, came[p], totals[p], 0, zs - 1) for p in range(4)]
+    ring = RingSum(pieces[:2], ring_send, ring_recv)
     ring.start()
+    route.start()
 
     def restore(first_crossed, second, first_home, out):
         whole = lax.rem(z, 2) == x
@@ -1550,10 +1593,35 @@
             for c in range(2):
                 for k in range(zs):
                     at, of = (c * zs + k) * wide, (k * 2 + c) * wide
-                    out[micro, :, at : at + wide] = rows_buf[micro, :, of : of + wide]
-
-    turn = TurnBack(peers, turned, wo_part, wo_cut, wo_back, turn_send, turn_recv)
-    turn.start()
+                    out[micro, at : at + wide, :] = rows_buf[micro, :, of : of + wide].astype(F32).T.astype(BF)
+
+    def cut(a, totals):
+        for layer, total in enumerate(totals):
+            for i in range(2 * rest):
+                wide_at, rows_at = 0, i * block
+                if a == 0:
+                    wide_at, rows_at = i // rest * stages[a].shape[3], i % rest * block
+                stages[a][layer, i, :block, :] = total[rows_at : rows_at + block, wide_at : wide_at + stages[a].shape[3]]
+        for i, place in offsets:
+            device, t = peers.other(*place)
+            src = stages[a].at[device["section"], device["dp"] * rest + device["r"]]
+            line = a + a // 3
+            send(remote(src, lands[a].at[me], all_send.at[line, i], all_recv.at[line, i], device))
+        lands[a][me] = stages[a][x, spot]
+
+    def settle(a, land):
+        for i, place in offsets:
+            device, t = peers.other(*(-d for d in place))
+            came = land.at[t]
+            remote(came, came, all_send.at[a, i], all_recv.at[a, i], device).wait_recv()
+
+    cut(0, (fc_zero, fc_one))
+    proj_both[0] = proj_zero[...]
+    proj_both[1] = proj_one[...]
+    device, _ = peers.other(1, 0, 0)
+    send(remote(proj_both.at[1 - x], proj_land.at[x], far_send, far_recv, device))
+    proj_land[x] = proj_both[x]
+    ring.tick(2)
     small[...] = jnp.zeros_like(small)
     halves = half // block
     for layer in range(2):
@@ -1584,33 +1652,15 @@
         send(remote(small.at[t], small_land.at[me], all_send.at[3, i], all_recv.at[3, i], device))
     small_land[me] = small[me]
 
-    def cut(a, totals):
-        for layer, total in enumerate(totals):
-            for i in range(2 * rest):
-                stages[a][layer, i, :block, :] = total[i * block : (i + 1) * block, :]
-        for i, place in offsets:
-            device, t = peers.other(*place)
-            src = stages[a].at[device["section"], device["dp"] * rest + device["r"]]
-            send(remote(src, lands[a].at[me], all_send.at[a, i], all_recv.at[a, i], device))
-        lands[a][me] = stages[a][x, spot]
-
-    def settle(a, land):
-        for i, place in offsets:
-            device, t = peers.other(*(-d for d in place))
-            came = land.at[t]
-            remote(came, came, all_send.at[a, i], all_recv.at[a, i], device).wait_recv()
-
-    route.start()
-    cut(0, (fc_zero, fc_one))
-    proj_both[0] = proj_zero[...]
-    proj_both[1] = proj_one[...]
-    device, _ = peers.other(1, 0, 0)
-    send(remote(proj_both.at[1 - x], proj_land.at[x], far_send, far_recv, device))
-    proj_land[x] = proj_both[x]
-
-    turn.finish()
-    wo_ring = RingSum([(wo_part, None, came_wo, wo_total, 0, zs - 1)], late_send, late_recv)
-    wo_ring.start()
+    ring.tick(2)
+    late_ring = RingSum(pieces[2:], late_send, late_recv)
+    late_ring.start()
+    settle(0, lands[0])
+    for t in range(slab):
+        h, c, r = t // (2 * rest), t // rest % 2, t % rest
+        for k in range(zs):
+            at = ((c * zs + k) * rest + r) * (units // (2 * zs * rest)) + h * half
+            out_fc[:, at : at + half] = lands[0][t, :block, k * half : (k + 1) * half]
     settle(3, small_land)
     total = small_land[0]
     for t in range(1, slab):
@@ -1620,80 +1670,77 @@
         there = lax.rem(z + k, zs)
         send(remote(small_sum.at[there], z_land.at[z], z_send.at[k], z_recv.at[k], {"z": there}))
     z_land[z] = small_sum[z]
-    ring.tick()
-    wo_ring.tick()
+    ring.finish()
+    cut(1, (totals[0], q_one))
+    cut(2, (totals[1], k_one))
+    late_ring.tick(2)
     route.arrived()
     across.tick("middle")
-    settle(0, lands[0])
-    for t in range(slab):
-        h, c, r = t // (2 * rest), t // rest % 2, t % rest
-        for k in range(zs):
-            at = ((c * zs + k) * rest + r) * (units // (2 * zs * rest)) + h * half
-            out_fc[:, at : at + half] = lands[0][t, :block, k * half : (k + 1) * half]
-    ring.tick()
-    wo_ring.tick()
     restore(ready[1], ready[2:4], ready[0], section_out)
-    came = proj_land.at[1 - x]
-    remote(came, came, far_send, far_recv, device).wait_recv()
+    came_proj = proj_land.at[1 - x]
+    remote(came_proj, came_proj, far_send, far_recv, device).wait_recv()
     for h in range(2):
         for c in range(2):
             for k in range(zs):
                 at, of = (c * zs + k) * wide, (k * 2 + c) * wide
                 out_proj[h * half : (h + 1) * half, at : at + wide] = proj_land[h, :, of : of + wide]
+    late_ring.tick(2)
     for k in range(1, zs):
-        came = z_land.at[lax.rem(z + zs - k, zs)]
-        remote(came, came, z_send.at[k], z_recv.at[k], {"z": lax.rem(z + k, zs)}).wait_recv()
+        block_in = z_land.at[lax.rem(z + zs - k, zs)]
+        remote(block_in, block_in, z_send.at[k], z_recv.at[k], {"z": lax.rem(z + k, zs)}).wait_recv()
     total = z_land[0]
     for k in range(1, zs):
         total = total + z_land[k]
     out_small[...] = total
-    wo_ring.finish()
-    cut(2, (wo_total, wo_one))
-    ring.finish()
-    cut(1, (qkv_total, qkv_one))
-    settle(2, lands[2])
+
+    def place(p):
+        for t in range(slab):
+            count = min(span, width - t * span)
+            if count > 0:
+                at = p * width + t * span
+                out_qkv[:, at : at + count] = lands[1 + p][t, :block, :count]
+
+    for p in range(2):
+        settle(1 + p, lands[1 + p])
+        place(p)
+    late_ring.finish()
+    cut(3, (totals[2], v_one))
+    cut(4, (totals[3], wo_one))
+    route.sent()
+    across.finish()
+    restore(out_rows, ready[4:], home, section_grad)
+    settle(4, lands[3])
+    place(2)
+    settle(5, lands[4])
     for t in range(slab):
         big, off = divmod(t * cols, wide)
         at = (big % 2 * zs + big // 2) * wide + off
-        out_wo[:, at : at + cols] = lands[2][t, :block, :]
-    settle(1, lands[1])
-    for t in range(slab):
-        count = min(span, width - t * span)
-        for p in range(3):
-            if count > 0:
-                at = p * width + t * span
-                out_qkv[:, at : at + count] = lands[1][t, :block, p * span : p * span + count]
-    route.sent()
-    across.finish()
-    restore(out_rows, ready[4:], home, section_grad)
+        out_wo[:, at : at + cols] = lands[4][t, :block, :]
     for copy in sent:
         copy.wait_send()
 
 
-def run_end(name, lay, part, turned, qkv_one, wo_one, fcs, projs, sums, last_rows, ready):
+def run_end(name, lay, parts, ones, fcs, projs, sums, last_rows, ready):
     zs, n = lay.zs, lay.slab
     span, width, block = lay.slots * lay.head, lay.width, lay.block
-    rows = part.shape[1]
+    rows = parts[0].shape[1]
     spots = lay.cores * lay.rest
     tall = -(-block // 16) * 16
     vmem = pl.BlockSpec(memory_space=pltpu.VMEM)
     dma = pltpu.SemaphoreType.DMA
-    widths = [fcs[0].shape[1], part.shape[2], lay.cols]
+    widths = [fcs[0].shape[1] // 2, span, span, span, lay.cols]
     half = projs[0].shape[0]
     tile = (-(-(8 + lay.unit_block // block) // 8) * 8, 128)
     outs = [(block, 3 * width), (block, width), (block, lay.units), (lay.unit_block, width), tile]
     return pl.pallas_call(
         functools.partial(end_kernel, (block, width, lay.units, lay.seqs)),
         out_shape=[jax.ShapeDtypeStruct(o, BF) for o in outs[:4]] + [jax.ShapeDtypeStruct(outs[4], F32)]
-        + [jax.ShapeDtypeStruct((lay.micros, *last_rows.shape), BF)] * 4,
-        in_specs=[vmem] * 16 + [pl.BlockSpec(memory_space=pl.ANY)] * 7,
+        + [jax.ShapeDtypeStruct((lay.micros, lay.width, lay.rows), BF)] * 2
+        + [jax.ShapeDtypeStruct((lay.micros, *last_rows.shape), BF)] * 2,
+        in_specs=[vmem] * 20 + [pl.BlockSpec(memory_space=pl.ANY)] * 7,
         out_specs=[vmem] * 7 + [pl.BlockSpec(memory_space=pl.ANY)] * 2,
         scratch_shapes=[
-            pltpu.VMEM((rows, part.shape[2]), BF),
-            pltpu.VMEM((zs, rows, lay.cols), BF),
-            pltpu.VMEM((rows, lay.cols), BF),
-            pltpu.VMEM((n, span, lay.cols), BF),
-            pltpu.VMEM((n, span, lay.cols), BF),
+            *[pltpu.VMEM((rows, a.shape[2]), BF) for a in parts],
             pltpu.VMEM((2, half, width), BF),
             pltpu.VMEM((2, half, width), BF),
         ]
@@ -1703,20 +1750,18 @@
             pltpu.VMEM((n, zs, *tile), F32),
             pltpu.VMEM((zs, *tile), F32),
             pltpu.VMEM((zs, *tile), F32),
-            pltpu.VMEM((zs - 1, rows, part.shape[2]), BF),
-            pltpu.VMEM((zs - 1, rows, lay.cols), BF),
+            *[pltpu.VMEM((zs - 1, rows, a.shape[2]), BF) for a in parts],
             pltpu.VMEM((n, zs, *tile), F32),
             pltpu.VMEM((8, n * span), F32),
             pltpu.VMEM((lay.micros, *last_rows.shape), BF),
         ]
-        + [dma((4, n))] * 2
+        + [dma((6, n))] * 2
         + [dma] * 2
         + [dma((zs,))] * 2
-        + [dma((n,))] * 2
         + [dma((2, zs - 1))] * 4
         + [dma, dma, dma((lay.micros,)), dma, dma, dma],
         compiler_params=pltpu.CompilerParams(collective_id=name, has_side_effects=True, vmem_limit_bytes=60 * 2**20),
-    )(part, turned, qkv_one, wo_one, *fcs, *projs, *sums, last_rows, *ready)
+    )(*parts, *ones, *fcs, *projs, *sums, last_rows, *ready)
 
 
 class Rings:
@@ -1730,13 +1775,13 @@
         _, acc, steps = self.state.get((kind, layer), (None, None, 0))
         self.state[kind, layer] = (part, acc, steps)
 
-    def side(self, plan, pace, makes={}, turned=None, cols=0):
+    def side(self, plan, pace, makes={}):
         pieces = []
         for kind, layer, count in plan:
             part, acc, steps = self.state.get((kind, layer), (None, None, 0))
             shape = makes[kind] if part is None else part.shape[1:]
             pieces.append((part, shape, acc, steps, count))
-        return sum_side(pieces, pace, turned, cols)
+        return sum_side(pieces, pace)
 
     def done(self, plan, outs):
         for (kind, layer, count), acc in zip(plan, outs):
@@ -1758,12 +1803,11 @@
     places = jnp.pad(positions.astype(F32), ((0, 0), (0, 128 - lay.rows)))
     small = jnp.concatenate([small, places])
     small = jnp.pad(small, ((0, -small.shape[0] % 8), (0, 0)))
-    *cut, proj_cut, w_qkv, w_out, h, g, row, vec_0, bias_0, unit_0, vec_1, bias_1, unit_1 = run_start(
-        0, lay, small, w_qkv[0], w_attn_out[0], w_fc[0], w_proj[0], inputs, cotangent
+    *cut, proj_cut, w_qkv, w_out, h, g, row, col, vec_0, bias_0, unit_0, vec_1, bias_1, unit_1 = run_start(
+        0, lay, small, w_qkv[0], w_attn_out[0], w_fc[0], w_proj[0], jnp.swapaxes(inputs, 2, 3), jnp.swapaxes(cotangent, 2, 3)
     )
     qkv_cut, wo_cut, fc_cut = cut[0:2], cut[2:4], cut[4:6]
     smalls = [(vec_0, bias_0, unit_0), (vec_1, bias_1, unit_1)]
-    col = row.reshape(lay.tokens, 1)
     outs, keeps, params = [], [], []
     for layer in range(lay.sections):
         last = layer == lay.sections - 1
@@ -1784,12 +1828,11 @@
             row,
             vec,
         )
-        w_fc = w_fc.reshape(width, -1)
         if last:
             side = route_side(lay, outs[0], "start")
         else:
-            side = gather_side([wo_cut[layer + 1], qkv_cut[layer + 1]], {"k3": 2}, turn=span)
-        (full_two, slope, activated, result, w_proj), later = run_feed_forward(
+            side = gather_side([wo_cut[layer + 1], qkv_cut[layer + 1]], {"k3": 2, "sent": 1}, turn=span)
+        (full_two, slope, activated, result, w_proj, w_fc), later = run_feed_forward(
             2 + 2 * layer, side, normed_two, mid, w_fc, w_proj, unit, vec
         )
         params.append((w_qkv, w_out, w_fc, w_proj.reshape(-1, width)))
@@ -1805,30 +1848,27 @@
     plans = {
         ("feed", 1): [("proj", 1, 3)],
         ("attention", 1): [("fc", 1, 3)],
-        ("feed", 0): [("qkv", 1, 3), ("proj", 0, 1)],
+        ("feed", 0): [("q", 1, 3), ("k", 1, 3), ("v", 1, 3), ("proj", 0, 1)],
         ("attention", 0): [("fc", 0, 3), ("proj", 0, 2), ("out", 1, 3)],
     }
     paces = {
         ("feed", 1): {"proj": 1, "fc": 1},
         ("attention", 1): {"k2": 1, "grad": 1},
-        ("feed", 0): {"k2": 1, "fc": 1, "launch": "fc"},
+        ("feed", 0): {"k3": 3},
         ("attention", 0): {"k3": 3},
     }
     crossed = {}
     sums = [None] * lay.sections
-    grad_out = None
     for layer in reversed(range(lay.sections)):
         w_qkv, w_out, w_fc, w_proj = params[layer]
         vec = smalls[layer][0]
         h, full, qkv, attended, logs, mid, full_two, slope, activated = keeps[layer]
         full, full_two = (a.reshape(lay.tokens, width) for a in (full, full_two))
         name = 1 + 4 * lay.sections - 2 * layer
-        side = rings.side(plans["feed", layer], paces["feed", layer], {"proj": (lay.half, width)}, grad_out, lay.cols)
-        late = grad_out is None
-        if late:
-            side = both_sides(side, route_side(lay, outs[1], "start"), across_side(0, home))
-        else:
-            side = both_sides(side, route_side(lay, g, "fc"))
+        side = rings.side(plans["feed", layer], paces["feed", layer], {"proj": (lay.half, width)})
+        late = layer == lay.sections - 1
+        turn = SideWork() if late else turn_side(lay, grad_out)
+        side = both_sides(side, turn, across_side(0 if late else 1, home), route_side(lay, outs[1] if late else g, "start"))
         (grad_mid, attn_rows, grad_proj, grad_fc, feed_sums, unit_sums), done = run_feed_backward(
             name, side, g, mid, w_fc, w_proj, slope, activated, full_two, vec, *([branch] if late else [])
         )
@@ -1836,26 +1876,29 @@
         rings.put("fc", layer, grad_fc)
         rings.done(plans["feed", layer], done)
         if late:
-            crossed["out", 0] = (home, done[-1])
-            home = done[-2]
+            crossed["out", 0] = (home, done[-2])
         else:
-            home = done[-1]
-            rings.put("out", layer + 1, done[-2])
-        side = both_sides(rings.side(plans["attention", layer], paces["attention", layer]), across_side(1, home))
-        (g, grad_qkv, grad_out, attn_sums, head_sums), done = run_attention_backward(
+            crossed["out", 1] = (home, done[-2])
+            rings.put("out", 1, done[-3])
+        home = done[-1]
+        side = rings.side(plans["attention", layer], paces["attention", layer])
+        if not late:
+            side = both_sides(side, turn_side(lay), across_side(1, home))
+        (g, *grad_parts, grad_out, attn_sums, head_sums), done = run_attention_backward(
             name + 1, lay.head, side, attn_rows, grad_mid, h, w_qkv, w_out, qkv, attended, logs, full, col, row, vec
         )
         rings.done(plans["attention", layer], done)
-        crossed["out" if late else "grad", 1] = (home, done[-1])
-        rings.put("qkv", layer, grad_qkv)
+        if not late:
+            rings.put("out", layer, done[-2])
+            crossed["grad", 1] = (home, done[-1])
+        for kind, part in zip("qkv", grad_parts):
+            rings.put(kind, layer, part)
         sums[layer] = (feed_sums, attn_sums, head_sums, unit_sums)
     out_qkv, out_attn, out_fc, out_proj, rows, section_out, section_grad, *_ = run_end(
         3 + 4 * lay.sections,
         lay,
-        rings.state["qkv", 0][0],
-        grad_out,
-        rings.state["qkv", 1][1],
-        rings.state["out", 1][1],
+        [rings.state[kind, 0][0] for kind in ("q", "k", "v", "out")],
+        [rings.state[kind, 1][1] for kind in ("q", "k", "v", "out")],
         [rings.state["fc", layer][1] for layer in range(2)],
         [rings.state["proj", layer][1] for layer in range(2)],
         [a for layer in range(2) for a in sums[layer]],
@@ -1864,8 +1907,8 @@
     )
     cols = rows[:8, :block].T
     return (
-        section_out[None, :, None],
-        section_grad[None, :, None],
+        jnp.swapaxes(section_out, 1, 2)[None, :, None],
+        jnp.swapaxes(section_grad, 1, 2)[None, :, None],
         out_qkv.astype(F32)[None],
         out_attn.astype(F32)[None],
         out_fc.astype(F32)[None],

time: 842 us -> 811 us (0.963)
  Pallas kernels: 805 us -> 778 us
    pallas_call x8, Pallas kernels: 614 us -> 595 us  [call(): pl.pallas_call(body, out_shape=[jax.ShapeDtypeStruct(*o) for o in (*outs,...]
    unnamed x18 -> x16, local copies, waits for them, and re-layouts: 18.3 us -> 11.3 us
where the time goes in v8:
time: 811 us; the launch traced here: 799 us
  Pallas kernels  778 us (96%)
  local copies, waits for them, and re-layouts  14.7 us (2%)
    pallas_call x8, Pallas kernels, call(): pl.pallas_call(body, out_shape=[jax.ShapeDtypeStruct(*o) for o in (*outs,...  595 us
    pallas_call x1, Pallas kernels, run_end(): pl.pallas_call(functools.partial(end_kernel, (block, width, lay.units, la...  94.6 us
    pallas_call x1, Pallas kernels, run_start(): pl.pallas_call(functools.partial(start_kernel, (block, span, lay.half, la...  88.1 us

profile of v8, /device:TPU:3, one launch (start us, length us, event | category | flops | bytes accessed | tf_op | source)
XLA Modules:
  0.0 799.1 jit_solution(18179777673500352895)
XLA Ops:
  0.6 0.7 convert_element_type.20
  1.3 0.7 convert_reduce_fusion
  2.0 0.1 reshape.80
  2.1 0.7 convert_bitcast_fusion
  2.9 0.6 pad.9.refs_0_
  3.5 88.1 %shard_map.169 = (bf16[400,768]{1,0:T(8,128)(2,1)}, bf16[400,768]{1,0:T(8,128)(2,1)}, bf16[400,200]{1,0:T(8,128)(2,1)}, bf16[400,200]{1,0:T(8,128)(2,1)}, bf16[2...) custom-call(f32[16,128]{1,0:T(8,128)} %pad.9.refs_0_, ...), custom_call_target="tpu_custom_call" | custom-call | tf_op jit(solution)/shard_map/pallas_call | solution.py:1523
  91.6 77.7 %shard_map.170 = (bf16[4,2,128,1600]{3,2,1,0:T(8,128)(2,1)}, bf16[1024,768]{1,0:T(8,128)(2,1)}, bf16[1024,256]{1,0:T(8,128)(2,1)}, f32[8,1024]{1,0:T(8,128)}, f3...) custom-call(bf16[128,1600]{1,0:T(8,128)(2,1)} %get-tuple-element.106, ...), custom_call_target="tpu_custom_call" | custom-call | tf_op jit(solution)/shard_map/pallas_call | solution.py:1284
  169.4 82.0 %shard_map.171 = (bf16[4,2,128,1600]{3,2,1,0:T(8,128)(2,1)}, bf16[1024,800]{1,0:T(8,128)(2,1)}, bf16[1024,800]{1,0:T(8,128)(2,1)}, bf16[128,1600]{1,0:T(8,128)(2...) custom-call(bf16[128,1600]{1,0:T(8,128)(2,1)} %get-tuple-element.115, ...), custom_call_target="tpu_custom_call" | custom-call | tf_op jit(solution)/shard_map/pallas_call | solution.py:1284
  251.4 78.2 %shard_map.172 = (bf16[4,2,128,1600]{3,2,1,0:T(8,128)(2,1)}, bf16[1024,768]{1,0:T(8,128)(2,1)}, bf16[1024,256]{1,0:T(8,128)(2,1)}, f32[8,1024]{1,0:T(8,128)}, f3...) custom-call(bf16[128,1600]{1,0:T(8,128)(2,1)} %get-tuple-element.122, ...), custom_call_target="tpu_custom_call" | custom-call | tf_op jit(solution)/shard_map/pallas_call | solution.py:1284
  329.6 57.7 %shard_map.173 = (bf16[4,2,128,1600]{3,2,1,0:T(8,128)(2,1)}, bf16[1024,800]{1,0:T(8,128)(2,1)}, bf16[1024,800]{1,0:T(8,128)(2,1)}, bf16[128,1600]{1,0:T(8,128)(2...) custom-call(bf16[128,1600]{1,0:T(8,128)(2,1)} %get-tuple-element.129.refs_0_, ...), custom_call_target="tpu_custom_call" | custom-call | tf_op jit(solution)/shard_map/pallas_call | solution.py:1284
  387.3 71.7 %shard_map.174 = (f32[128,1600]{1,0:T(8,128)}, bf16[128,1600]{1,0:T(8,128)(2,1)}, bf16[4,200,1600]{2,1,0:T(8,128)(2,1)}, bf16[4,200,1600]{2,1,0:T(8,128)(2,1)}, ...) custom-call(bf16[128,1600]{1,0:T(8,128)(2,1)} %get-tuple-element.105, ...), custom_call_target="tpu_custom_call" | custom-call | tf_op jit(solution)/shard_map/pallas_call | solution.py:1284
  459.0 59.9 %shard_map.175 = (bf16[128,1600]{1,0:T(8,128)(2,1)}, bf16[1600,256]{1,0:T(8,128)(2,1)}, bf16[1600,256]{1,0:T(8,128)(2,1)}, bf16[1600,256]{1,0:T(8,128)(2,1)}, bf...) custom-call(bf16[128,1600]{1,0:T(8,128)(2,1)} %get-tuple-element.141.refs_0_, ...), custom_call_target="tpu_custom_call" | custom-call | tf_op jit(solution)/shard_map/pallas_call | solution.py:1284
  518.9 77.8 %shard_map.176 = (f32[128,1600]{1,0:T(8,128)}, bf16[128,1600]{1,0:T(8,128)(2,1)}, bf16[4,200,1600]{2,1,0:T(8,128)(2,1)}, bf16[4,200,1600]{2,1,0:T(8,128)(2,1)}, ...) custom-call(bf16[128,1600]{1,0:T(8,128)(2,1)} %get-tuple-element.148, ...), custom_call_target="tpu_custom_call" | custom-call | tf_op jit(solution)/shard_map/pallas_call | solution.py:1284
  596.7 90.5 %shard_map.177 = (bf16[128,1600]{1,0:T(8,128)(2,1)}, bf16[1600,256]{1,0:T(8,128)(2,1)}, bf16[1600,256]{1,0:T(8,128)(2,1)}, bf16[1600,256]{1,0:T(8,128)(2,1)}, bf...) custom-call(bf16[128,1600]{1,0:T(8,128)(2,1)} %get-tuple-element.159, ...), custom_call_target="tpu_custom_call" | custom-call | tf_op jit(solution)/shard_map/pallas_call | solution.py:1284
  687.2 94.6 %shard_map.178 = (bf16[100,4800]{1,0:T(8,128)(2,1)}, bf16[100,1600]{1,0:T(8,128)(2,1)}, bf16[100,6400]{1,0:T(8,128)(2,1)}, bf16[400,1600]{1,0:T(8,128)(2,1)}, f3...) custom-call(bf16[4,400,256]{2,1,0:T(8,128)(2,1)} %bitcast.65, ...), custom_call_target="tpu_custom_call" | custom-call | tf_op jit(solution)/shard_map/pallas_call | solution.py:1735
  781.7 0.0 copy-start.2
  781.7 0.8 slice.40
  782.5 0.7 slice_bitcast_fusion.1
  783.2 0.7 reshape.79
  783.9 0.6 slice_bitcast_fusion.2
  784.4 0.6 copy.24
  785.0 1.0 bitcast_convert_fusion.3
  786.0 1.5 copy.22
  787.6 0.0 copy-done.2
  787.6 0.1 bitcast_convert_fusion.2
  787.7 0.0 copy-start.1
  787.7 3.3 copy.21
  791.0 0.2 bitcast_convert_fusion.1
  791.2 4.1 copy.23
  795.3 1.7 bitcast_convert_fusion
  797.0 0.9 copy.27
  797.8 0.9 copy.28
  (13 shorter events, 0.1 us)
Async XLA Ops:
  781.7 5.8 copy-start.2
  787.7 3.3 copy-start.1
  791.2 4.1 copy-start
  795.3 1.7 copy-start.4
  795.3 2.6 copy-start.3

commit v9 on v8

--- a/solution.py
+++ b/solution.py
@@ -361,6 +361,18 @@
             copy.wait_send()
 
 
+GROUPS = 5
+
+
+def groups_of(rows, start, count):
+    tall, at = rows // GROUPS, start
+    while at < start + count:
+        group, row = divmod(at, tall)
+        some = min(tall - row, start + count - at)
+        yield at - start, group, row, some
+        at += some
+
+
 class TurnBack:
     def __init__(self, peers, part, pieces, came, send, recv, given=None):
         self.given = given
@@ -402,7 +414,7 @@
             device, t = self.peers.other(*(-d for d in place))
             block = self.came.at[t]
             remote(block, block, self.send_sem.at[i], self.recv_sem.at[i], device).wait_recv()
-        zs, rows, _ = self.part.shape
+        zs, rows, cols = self.part.shape[0], self.part.shape[1] * GROUPS, self.came.shape[2]
         wide, span = rows // 2, self.came.shape[1]
         for c in range(2):
             for k in range(zs):
@@ -410,7 +422,9 @@
                 while done < wide:
                     t, row = divmod(at + done, span)
                     count = min(wide - done, span - row)
-                    self.part[k, c * wide + done : c * wide + done + count, :] = self.came[t, row : row + count, :]
+                    for first, group, to, some in groups_of(rows, c * wide + done, count):
+                        lanes = slice(group * cols, (group + 1) * cols)
+                        self.part[k, to : to + some, lanes] = self.came[t, row + first : row + first + some, :]
                     done += count
         for copy in self.sent:
             copy.wait_send()
@@ -423,12 +437,14 @@
         self.sent = []
 
     def start(self):
-        zs, rows, cols = self.full.shape
+        zs, rows, cols = self.full.shape[0], self.full.shape[1] * GROUPS, self.nat.shape[1]
         part, span = rows // 2, self.w_out.shape[0]
         for c in range(2):
             for z in range(zs):
                 at = (c * zs + z) * part
-                self.nat[at : at + part, :] = self.full[z, c * part : (c + 1) * part, :]
+                for first, group, row, some in groups_of(rows, c * part, part):
+                    lanes = slice(group * cols, (group + 1) * cols)
+                    self.nat[at + first : at + first + some, :] = self.full[z, row : row + some, lanes]
         used = zs * rows
         if used < self.nat.shape[0]:
             self.nat[used:, :] = jnp.zeros((self.nat.shape[0] - used, cols), BF)
@@ -829,7 +845,7 @@
 
 def turn_side(lay, turned=None):
     n, span = lay.slab, lay.slots * lay.head
-    outs = [((lay.zs, lay.width // lay.zs, lay.cols), BF)]
+    outs = [((lay.zs, lay.width // lay.zs // GROUPS, GROUPS * lay.cols), BF)]
     scratch = [pltpu.VMEM((n, span, lay.cols), BF)] * 2 + [pltpu.SemaphoreType.DMA((n,))] * 2
 
     def build(peers, ins, outs, scratch):
@@ -891,7 +907,7 @@
 
         return SideWork(shards, (True,) * n, outs, (True,) * n, sems, build)
     slab = 2 * lax.axis_size("section") * lax.axis_size("r")
-    cols = shards[0].shape[1]
+    cols = shards[0].shape[1] // GROUPS
     outs[0] = ((turn, slab * cols), BF)
     more = [
         pltpu.VMEM((zs, *shards[0].shape), BF),
@@ -1406,6 +1422,11 @@
             remote(came, came, all_send.at[a, i], all_recv.at[a, i], device).wait_recv()
         for layer in range(sections):
             for i in range(2 * rest):
+                if a == 0:
+                    for first, group, row, some in groups_of(2 * rest * block, i * block, block):
+                        to = shard[layer].at[row : row + some, group * cols : (group + 1) * cols]
+                        to[...] = lands[a][layer, i, first : first + some, :]
+                    continue
                 rows_at, lanes_at = i * block, 0
                 if a == 2:
                     rows_at, lanes_at = i % rest * block, i // rest * lands[a].shape[3]
@@ -1515,7 +1536,7 @@
     units = lay.units // n
     widths = [lay.cols, 3 * span, units]
     flat = (lay.rows, lay.width)
-    outs = [(a, BF) for a in ((rows, 3 * span), (rows, lay.cols), (rows // 2, 2 * units)) for _ in range(sections)]
+    outs = [(a, BF) for a in ((rows, 3 * span), (rows // GROUPS, GROUPS * lay.cols), (rows // 2, 2 * units)) for _ in range(sections)]
     outs += [((sections, lay.half, lay.width), BF), ((zs, rows, 3 * span), BF), ((span, lay.width), BF)]
     outs += [(flat, BF), (flat, BF), ((1, lay.tokens), jnp.int32), ((lay.tokens, 1), jnp.int32)]
     outs += [((8, lay.width), F32), ((1, 3 * span), F32), ((1, units), F32)] * sections
@@ -1535,7 +1556,7 @@
         ]
         + [pltpu.VMEM((n, tall, m), BF) for m in widths]
         + [pltpu.VMEM((sections, spots, tall, m), BF) for m in widths]
-        + [pltpu.VMEM((zs, rows, lay.cols), BF), pltpu.VMEM((n * span, lay.cols), BF), pltpu.VMEM((n, span, lay.cols), BF)]
+        + [pltpu.VMEM((zs, rows // GROUPS, GROUPS * lay.cols), BF), pltpu.VMEM((n * span, lay.cols), BF), pltpu.VMEM((n, span, lay.cols), BF)]
         + [dma((zs,))] * 2
         + [dma((chips,))] * 4
         + [dma((3, n))] * 2
@@ -1561,7 +1582,7 @@
     zs, z = lax.axis_size("z"), lax.axis_index("z")
     x, rest, slab = peers.x, peers.rest, 2 * peers.chips
     spot = peers.c * rest + peers.r
-    span, cols = q_one.shape[1], wo_one.shape[1]
+    span, cols = q_one.shape[1], wo_one.shape[1] // GROUPS
     half, wide = proj_zero.shape[0], rest * block
     _, me = peers.other(0, 0, 0)
     offsets = peers.offsets()
@@ -1598,6 +1619,11 @@
     def cut(a, totals):
         for layer, total in enumerate(totals):
             for i in range(2 * rest):
+                if a == 4:
+                    for first, group, row, some in groups_of(2 * rest * block, i * block, block):
+                        lanes = slice(group * cols, (group + 1) * cols)
+                        stages[a][layer, i, first : first + some, :] = total[row : row + some, lanes]
+                    continue
                 wide_at, rows_at = 0, i * block
                 if a == 0:
                     wide_at, rows_at = i // rest * stages[a].shape[3], i % rest * block
@@ -1660,7 +1686,7 @@
         h, c, r = t // (2 * rest), t // rest % 2, t % rest
         for k in range(zs):
             at = ((c * zs + k) * rest + r) * (units // (2 * zs * rest)) + h * half
-            out_fc[:, at : at + half] = lands[0][t, :block, k * half : (k + 1) * half]
+            out_fc[:, 0, at : at + half] = lands[0][t, :block, k * half : (k + 1) * half].astype(F32)
     settle(3, small_land)
     total = small_land[0]
     for t in range(1, slab):
@@ -1698,7 +1724,7 @@
             count = min(span, width - t * span)
             if count > 0:
                 at = p * width + t * span
-                out_qkv[:, at : at + count] = lands[1 + p][t, :block, :count]
+                out_qkv[:, 0, at : at + count] = lands[1 + p][t, :block, :count].astype(F32)
 
     for p in range(2):
         settle(1 + p, lands[1 + p])
@@ -1715,7 +1741,7 @@
     for t in range(slab):
         big, off = divmod(t * cols, wide)
         at = (big % 2 * zs + big // 2) * wide + off
-        out_wo[:, at : at + cols] = lands[4][t, :block, :]
+        out_wo[:, 0, at : at + cols] = lands[4][t, :block, :].astype(F32)
     for copy in sent:
         copy.wait_send()
 
@@ -1723,7 +1749,6 @@
 def run_end(name, lay, parts, ones, fcs, projs, sums, last_rows, ready):
     zs, n = lay.zs, lay.slab
     span, width, block = lay.slots * lay.head, lay.width, lay.block
-    rows = parts[0].shape[1]
     spots = lay.cores * lay.rest
     tall = -(-block // 16) * 16
     vmem = pl.BlockSpec(memory_space=pltpu.VMEM)
@@ -1731,16 +1756,16 @@
     widths = [fcs[0].shape[1] // 2, span, span, span, lay.cols]
     half = projs[0].shape[0]
     tile = (-(-(8 + lay.unit_block // block) // 8) * 8, 128)
-    outs = [(block, 3 * width), (block, width), (block, lay.units), (lay.unit_block, width), tile]
+    outs = [(block, 1, 3 * width), (block, 1, width), (block, 1, lay.units), (lay.unit_block, width), tile]
     return pl.pallas_call(
         functools.partial(end_kernel, (block, width, lay.units, lay.seqs)),
-        out_shape=[jax.ShapeDtypeStruct(o, BF) for o in outs[:4]] + [jax.ShapeDtypeStruct(outs[4], F32)]
+        out_shape=[jax.ShapeDtypeStruct(o, BF if i == 3 else F32) for i, o in enumerate(outs)]
         + [jax.ShapeDtypeStruct((lay.micros, lay.width, lay.rows), BF)] * 2
         + [jax.ShapeDtypeStruct((lay.micros, *last_rows.shape), BF)] * 2,
         in_specs=[vmem] * 20 + [pl.BlockSpec(memory_space=pl.ANY)] * 7,
         out_specs=[vmem] * 7 + [pl.BlockSpec(memory_space=pl.ANY)] * 2,
         scratch_shapes=[
-            *[pltpu.VMEM((rows, a.shape[2]), BF) for a in parts],
+            *[pltpu.VMEM(a.shape[1:], BF) for a in parts],
             pltpu.VMEM((2, half, width), BF),
             pltpu.VMEM((2, half, width), BF),
         ]
@@ -1750,7 +1775,7 @@
             pltpu.VMEM((n, zs, *tile), F32),
             pltpu.VMEM((zs, *tile), F32),
             pltpu.VMEM((zs, *tile), F32),
-            *[pltpu.VMEM((zs - 1, rows, a.shape[2]), BF) for a in parts],
+            *[pltpu.VMEM((zs - 1, *a.shape[1:]), BF) for a in parts],
             pltpu.VMEM((n, zs, *tile), F32),
             pltpu.VMEM((8, n * span), F32),
             pltpu.VMEM((lay.micros, *last_rows.shape), BF),
@@ -1909,9 +1934,9 @@
     return (
         jnp.swapaxes(section_out, 1, 2)[None, :, None],
         jnp.swapaxes(section_grad, 1, 2)[None, :, None],
-        out_qkv.astype(F32)[None],
-        out_attn.astype(F32)[None],
-        out_fc.astype(F32)[None],
+        jnp.swapaxes(out_qkv, 0, 1),
+        jnp.swapaxes(out_attn, 0, 1),
+        jnp.swapaxes(out_fc, 0, 1),
         out_proj.astype(F32)[None],
         cols[None, :, :2],
         cols[None, :, 2:],

time: 811 us -> 796 us (0.982)
  Pallas kernels: 778 us -> 767 us
where the time goes in v9:
time: 796 us; the launch traced here: 783 us
  Pallas kernels  767 us (96%)
  local copies, waits for them, and re-layouts  9.97 us (1%)
    pallas_call x8, Pallas kernels, call(): pl.pallas_call(body, out_shape=[jax.ShapeDtypeStruct(*o) for o in (*outs,...  593 us
    pallas_call x1, Pallas kernels, run_end(): pl.pallas_call(functools.partial(end_kernel, (block, width, lay.units, la...  87.1 us
    pallas_call x1, Pallas kernels, run_start(): pl.pallas_call(functools.partial(start_kernel, (block, span, lay.half, la...  86.1 us

profile of v9, /device:TPU:3, one launch (start us, length us, event | category | flops | bytes accessed | tf_op | source)
XLA Modules:
  0.0 783.0 jit_solution(12225629889696595301)
XLA Ops:
  0.6 0.7 convert_element_type.17
  1.3 0.7 convert_reduce_fusion
  2.0 0.1 reshape.80
  2.1 0.7 convert_bitcast_fusion
  2.9 0.6 pad.9.refs_0_
  3.5 86.1 %shard_map.169 = (bf16[400,768]{1,0:T(8,128)(2,1)}, bf16[400,768]{1,0:T(8,128)(2,1)}, bf16[80,1000]{1,0:T(8,128)(2,1)}, bf16[80,1000]{1,0:T(8,128)(2,1)}, bf16[2...) custom-call(f32[16,128]{1,0:T(8,128)} %pad.9.refs_0_, ...), custom_call_target="tpu_custom_call" | custom-call | tf_op jit(solution)/shard_map/pallas_call | solution.py:1544
  89.6 80.6 %shard_map.170 = (bf16[4,2,128,1600]{3,2,1,0:T(8,128)(2,1)}, bf16[1024,768]{1,0:T(8,128)(2,1)}, bf16[1024,256]{1,0:T(8,128)(2,1)}, f32[8,1024]{1,0:T(8,128)}, f3...) custom-call(bf16[128,1600]{1,0:T(8,128)(2,1)} %get-tuple-element.106, ...), custom_call_target="tpu_custom_call" | custom-call | tf_op jit(solution)/shard_map/pallas_call | solution.py:1300
  170.2 74.8 %shard_map.171 = (bf16[4,2,128,1600]{3,2,1,0:T(8,128)(2,1)}, bf16[1024,800]{1,0:T(8,128)(2,1)}, bf16[1024,800]{1,0:T(8,128)(2,1)}, bf16[128,1600]{1,0:T(8,128)(2...) custom-call(bf16[128,1600]{1,0:T(8,128)(2,1)} %get-tuple-element.115, ...), custom_call_target="tpu_custom_call" | custom-call | tf_op jit(solution)/shard_map/pallas_call | solution.py:1300
  245.1 78.7 %shard_map.172 = (bf16[4,2,128,1600]{3,2,1,0:T(8,128)(2,1)}, bf16[1024,768]{1,0:T(8,128)(2,1)}, bf16[1024,256]{1,0:T(8,128)(2,1)}, f32[8,1024]{1,0:T(8,128)}, f3...) custom-call(bf16[128,1600]{1,0:T(8,128)(2,1)} %get-tuple-element.122, ...), custom_call_target="tpu_custom_call" | custom-call | tf_op jit(solution)/shard_map/pallas_call | solution.py:1300
  323.8 56.8 %shard_map.173 = (bf16[4,2,128,1600]{3,2,1,0:T(8,128)(2,1)}, bf16[1024,800]{1,0:T(8,128)(2,1)}, bf16[1024,800]{1,0:T(8,128)(2,1)}, bf16[128,1600]{1,0:T(8,128)(2...) custom-call(bf16[128,1600]{1,0:T(8,128)(2,1)} %get-tuple-element.129.refs_0_, ...), custom_call_target="tpu_custom_call" | custom-call | tf_op jit(solution)/shard_map/pallas_call | solution.py:1300
  380.6 65.2 %shard_map.174 = (f32[128,1600]{1,0:T(8,128)}, bf16[128,1600]{1,0:T(8,128)(2,1)}, bf16[4,200,1600]{2,1,0:T(8,128)(2,1)}, bf16[4,200,1600]{2,1,0:T(8,128)(2,1)}, ...) custom-call(bf16[128,1600]{1,0:T(8,128)(2,1)} %get-tuple-element.105, ...), custom_call_target="tpu_custom_call" | custom-call | tf_op jit(solution)/shard_map/pallas_call | solution.py:1300
  445.8 67.1 %shard_map.175 = (bf16[128,1600]{1,0:T(8,128)(2,1)}, bf16[1600,256]{1,0:T(8,128)(2,1)}, bf16[1600,256]{1,0:T(8,128)(2,1)}, bf16[1600,256]{1,0:T(8,128)(2,1)}, bf...) custom-call(bf16[128,1600]{1,0:T(8,128)(2,1)} %get-tuple-element.141.refs_0_, ...), custom_call_target="tpu_custom_call" | custom-call | tf_op jit(solution)/shard_map/pallas_call | solution.py:1300
  512.9 78.1 %shard_map.176 = (f32[128,1600]{1,0:T(8,128)}, bf16[128,1600]{1,0:T(8,128)(2,1)}, bf16[4,200,1600]{2,1,0:T(8,128)(2,1)}, bf16[4,200,1600]{2,1,0:T(8,128)(2,1)}, ...) custom-call(bf16[128,1600]{1,0:T(8,128)(2,1)} %get-tuple-element.148, ...), custom_call_target="tpu_custom_call" | custom-call | tf_op jit(solution)/shard_map/pallas_call | solution.py:1300
  591.0 92.1 %shard_map.177 = (bf16[128,1600]{1,0:T(8,128)(2,1)}, bf16[1600,256]{1,0:T(8,128)(2,1)}, bf16[1600,256]{1,0:T(8,128)(2,1)}, bf16[1600,256]{1,0:T(8,128)(2,1)}, bf...) custom-call(bf16[128,1600]{1,0:T(8,128)(2,1)} %get-tuple-element.159, ...), custom_call_target="tpu_custom_call" | custom-call | tf_op jit(solution)/shard_map/pallas_call | solution.py:1300
  683.1 87.1 %shard_map.178 = (f32[100,1,4800]{2,1,0:T(1,128)}, f32[100,1,1600]{2,1,0:T(1,128)}, f32[100,1,6400]{2,1,0:T(1,128)}, bf16[400,1600]{1,0:T(8,128)(2,1)}, f32[16,1...) custom-call(bf16[4,400,256]{2,1,0:T(8,128)(2,1)} %bitcast.65, ...), custom_call_target="tpu_custom_call" | custom-call | tf_op jit(solution)/shard_map/pallas_call | solution.py:1760
  770.2 0.0 copy-start.3
  770.2 0.8 slice.40
  771.0 0.7 slice_bitcast_fusion.1
  771.7 0.7 reshape.79
  772.3 0.6 slice_bitcast_fusion.2
  772.9 0.6 copy.21
  773.5 3.1 bitcast_convert_fusion
  776.6 0.0 copy-done.3
  776.6 0.9 copy.27
  777.5 0.0 copy-done.2
  777.5 0.9 copy.28
  778.4 0.0 copy-done.1
  778.4 1.3 copy.29
  779.7 0.0 copy-done.4
  779.7 0.8 copy.30
  780.5 0.6 copy-done
  781.1 1.5 copy.31
  (10 shorter events, 0.1 us)
Async XLA Ops:
  770.2 6.4 copy-start.3
  773.5 4.0 copy-start.2
  773.5 4.9 copy-start.1
  777.5 2.2 copy-start.4
  778.4 2.7 copy-start

commit v10 on v9

--- a/solution.py
+++ b/solution.py
@@ -801,6 +801,28 @@
             self.copy.wait()
 
 
+class Store:
+    def __init__(self, far, near, sem):
+        self.copy = pltpu.make_async_copy(near, far, sem)
+        self.near, self.gone = near, False
+        self.shape, self.at = near.shape, near.at
+
+    def __getitem__(self, index):
+        return self.near[index]
+
+    def __setitem__(self, index, value):
+        self.near[index] = value
+
+    def flush(self):
+        self.gone = True
+        self.copy.start()
+
+    def finish(self):
+        if not self.gone:
+            self.flush()
+        self.copy.wait()
+
+
 def far(ref):
     return ref.far if isinstance(ref, Fetch) else ref
 
@@ -1015,6 +1037,7 @@
     work.tick("qkv")
     kept = pltpu.make_async_copy(full, normed, kept_sem)
     kept.start()
+    qkv.flush()
     scale = head ** (-0.5)
     order = list(range(1, peers.chips)) + [0]
     before = None
@@ -1042,6 +1065,7 @@
             reduce.push(before)
         work.tick("q%d" % order.index(k))
         before = k
+    attended.flush()
     reduce.push(before)
     out = h[...].astype(F32) + (reduce.total() + vec[4:5, :])
     mid[...] = out
@@ -1111,6 +1135,8 @@
         before = k
     kept = pltpu.make_async_copy(full, normed_two, kept_sem)
     kept.start()
+    slope.flush()
+    activated.flush()
     reduce.push(before)
     work.tick("sent")
     out = (mid[...] + (reduce.total() + vec[5:6, :])).astype(BF)
@@ -1150,6 +1176,7 @@
         branch = full[...].reshape(tokens, width)
         for b in range(grad_proj.shape[0]):
             grad_proj[b] = dot(activated[:, b * half : (b + 1) * half], branch, 0, 0).astype(BF)
+        grad_proj.flush()
         work.made(grad_proj)
 
     if ready:
@@ -1183,6 +1210,7 @@
         part = dot(normed_two[:, at : at + 2 * rows_of], back, 0, 0).astype(BF)
         for c in range(2):
             grad_fc[b, :, c * units : (c + 1) * units] = part[c * rows_of : (c + 1) * rows_of]
+    grad_fc.flush()
     work.tick("fc")
     unit_sums[...] = jnp.sum(back.astype(F32), axis=0, keepdims=True)
     own = src[...].astype(F32)
@@ -1263,11 +1291,14 @@
     work.tick("sent")
     grads = joint[...]
     grad_out[...] = dot(attended[...], full[...].reshape(tokens, width), 0, 0).astype(BF)
+    grad_out.flush()
     work.made(grad_out)
     for a, b in chunks(width, 512):
         part = dot(normed[:, a:b], grads, 0, 0).astype(BF)
         for i, grad in enumerate(grad_parts):
             grad[a:b, :] = part[:, i * span : (i + 1) * span]
+    for grad in grad_parts:
+        grad.flush()
     work.tick("grad")
     head_sums[...] = jnp.sum(grads.astype(F32), axis=0, keepdims=True)
     part, gain, shift = norm_back(h[...].astype(F32), vec[0:1, :], reduce.total())
@@ -1280,7 +1311,7 @@
     reduce.finish()
 
 
-def call(kernel, name, outs, operands, side, kept, scratch, keep=()):
+def call(kernel, name, outs, operands, side, kept, scratch, keep=(), early=()):
     chips = lax.axis_size("section") * lax.axis_size("r")
     rows, width = operands[0].shape
     vmem, hbm = pl.BlockSpec(memory_space=pltpu.VMEM), pl.BlockSpec(memory_space=pl.ANY)
@@ -1290,21 +1321,28 @@
 
     def body(*refs):
         refs = list(refs)
-        near, sems = refs[-1 - len(fetched) : -1], refs[-1]
+        count = len(fetched) + len(early)
+        near, sems = refs[-1 - count : -1], refs[-1]
         for k, i in enumerate(fetched):
             refs[i] = Fetch(refs[i], near[k], sems.at[k])
-        kernel(*refs[: -1 - len(fetched)])
+        for k, i in enumerate(early):
+            k += len(fetched)
+            refs[len(every) + i] = Store(refs[len(every) + i], near[k], sems.at[k])
+        kernel(*refs[: -1 - count])
         for i in fetched:
             refs[i].finish()
+        for i in early:
+            refs[len(every) + i].finish()
 
     out = pl.pallas_call(
         body,
         out_shape=[jax.ShapeDtypeStruct(*o) for o in (*outs, *side.outs)],
         in_specs=[hbm] * len(every),
-        out_specs=[hbm if i in kept else vmem for i in range(len(outs))] + [hbm if i else vmem for i in side.out_hbm],
+        out_specs=[hbm if i in kept or i in early else vmem for i in range(len(outs))] + [hbm if i else vmem for i in side.out_hbm],
         scratch_shapes=work
         + [pltpu.VMEM(every[i].shape, every[i].dtype) for i in fetched]
-        + [pltpu.SemaphoreType.DMA((len(fetched),))],
+        + [pltpu.VMEM(*outs[i]) for i in early]
+        + [pltpu.SemaphoreType.DMA((len(fetched) + len(early),))],
         compiler_params=pltpu.CompilerParams(collective_id=name, has_side_effects=True, vmem_limit_bytes=60 * 2**20),
     )(*every)
     return out[: len(outs)], out[len(outs) :]
@@ -1324,7 +1362,7 @@
         ((rows, width), F32),
         ((rows, width), BF),
     ]
-    return call(functools.partial(attention_forward, head, side), name, outs, operands, side, (0,), [pltpu.SemaphoreType.DMA])
+    return call(functools.partial(attention_forward, head, side), name, outs, operands, side, (0,), [pltpu.SemaphoreType.DMA], (), (1, 2))
 
 
 def run_feed_forward(name, side, *operands):
@@ -1343,7 +1381,7 @@
     ]
     dma = pltpu.SemaphoreType.DMA
     scratch = [dma, pltpu.VMEM(w_proj.shape, BF), dma((w_proj.shape[0],)), dma, dma, dma, pltpu.VMEM((width, units), BF), dma]
-    return call(functools.partial(feed_forward, side), name, outs, operands, side, (0, 4, 5), scratch, (3,))
+    return call(functools.partial(feed_forward, side), name, outs, operands, side, (0, 4, 5), scratch, (3,), (1, 2))
 
 
 def run_feed_backward(name, side, *operands):
@@ -1359,7 +1397,7 @@
         ((8, width), F32),
         ((1, units), F32),
     ]
-    return call(functools.partial(feed_backward, side, len(given)), name, outs, operands, side, (), [pltpu.VMEM((tokens, units), BF)])
+    return call(functools.partial(feed_backward, side, len(given)), name, outs, operands, side, (), [pltpu.VMEM((tokens, units), BF)], (), (2, 3))
 
 
 def run_attention_backward(name, head, side, *operands):
@@ -1376,7 +1414,7 @@
         ((1, 3 * span), F32),
     ]
     scratch = [pltpu.VMEM((tokens, 3 * span), BF), pltpu.VMEM((tokens, span), F32), pltpu.VMEM((tokens, span), F32)]
-    return call(functools.partial(attention_backward, head, side), name, outs, operands, side, (), scratch)
+    return call(functools.partial(attention_backward, head, side), name, outs, operands, side, (), scratch, (), (1, 2, 3, 4))
 
 
 def start_kernel(sizes, *refs):
@@ -1570,6 +1608,11 @@
 
 
 def end_kernel(sizes, *refs):
+    count = 20
+    refs = list(refs)
+    near, sems = refs[-1 - count : -1], refs[-1]
+    fetched = [Fetch(refs[i], near[i], sems.at[i]) for i in range(count)]
+    refs = fetched + refs[count : -1 - count]
     block, width, units, seqs = sizes
     parts, (q_one, k_one, v_one, wo_one), (fc_zero, fc_one, proj_zero, proj_one), refs = refs[:4], refs[4:8], refs[8:12], refs[12:]
     sums, (last_rows, *ready), refs = refs[:8], refs[8:15], refs[15:]
@@ -1734,6 +1777,8 @@
     cut(4, (totals[3], wo_one))
     route.sent()
     across.finish()
+    for operand in fetched:
+        operand.finish()
     restore(out_rows, ready[4:], home, section_grad)
     settle(4, lands[3])
     place(2)
@@ -1762,7 +1807,7 @@
         out_shape=[jax.ShapeDtypeStruct(o, BF if i == 3 else F32) for i, o in enumerate(outs)]
         + [jax.ShapeDtypeStruct((lay.micros, lay.width, lay.rows), BF)] * 2
         + [jax.ShapeDtypeStruct((lay.micros, *last_rows.shape), BF)] * 2,
-        in_specs=[vmem] * 20 + [pl.BlockSpec(memory_space=pl.ANY)] * 7,
+        in_specs=[pl.BlockSpec(memory_space=pl.ANY)] * 27,
         out_specs=[vmem] * 7 + [pl.BlockSpec(memory_space=pl.ANY)] * 2,
         scratch_shapes=[
             *[pltpu.VMEM(a.shape[1:], BF) for a in parts],
@@ -1784,7 +1829,9 @@
         + [dma] * 2
         + [dma((zs,))] * 2
         + [dma((2, zs - 1))] * 4
-        + [dma, dma, dma((lay.micros,)), dma, dma, dma],
+        + [dma, dma, dma((lay.micros,)), dma, dma, dma]
+        + [pltpu.VMEM(a.shape, a.dtype) for a in (*parts, *ones, *fcs, *projs, *sums)]
+        + [dma((20,))],
         compiler_params=pltpu.CompilerParams(collective_id=name, has_side_effects=True, vmem_limit_bytes=60 * 2**20),
     )(*parts, *ones, *fcs, *projs, *sums, last_rows, *ready)
 

time: 796 us -> 784 us (0.985)
  Pallas kernels: 767 us -> 755 us
    pallas_call x8, Pallas kernels: 593 us -> 584 us  [call(): pl.pallas_call(body, out_shape=[jax.ShapeDtypeStruct(*o) for o in (*outs,...]
where the time goes in v10:
time: 784 us; the launch traced here: 771 us
  Pallas kernels  755 us (96%)
  local copies, waits for them, and re-layouts  9.97 us (1%)
    pallas_call x8, Pallas kernels, call(): pl.pallas_call(body, out_shape=[jax.ShapeDtypeStruct(*o) for o in (*outs,...  584 us
    pallas_call x1, Pallas kernels, run_start(): pl.pallas_call(functools.partial(start_kernel, (block, span, lay.half, la...  86.1 us
    pallas_call x1, Pallas kernels, run_end(): pl.pallas_call(functools.partial(end_kernel, (block, width, lay.units, la...  84.7 us

profile of v10, /device:TPU:3, one launch (start us, length us, event | category | flops | bytes accessed | tf_op | source)
XLA Modules:
  0.0 771.4 jit_solution(17171881244812961727)
XLA Ops:
  0.6 0.7 convert_element_type.17
  1.3 0.7 convert_reduce_fusion
  2.0 0.1 reshape.80
  2.1 0.7 convert_bitcast_fusion
  2.9 0.6 pad.9.refs_0_
  3.5 86.1 %shard_map.169 = (bf16[400,768]{1,0:T(8,128)(2,1)}, bf16[400,768]{1,0:T(8,128)(2,1)}, bf16[80,1000]{1,0:T(8,128)(2,1)}, bf16[80,1000]{1,0:T(8,128)(2,1)}, bf16[2...) custom-call(f32[16,128]{1,0:T(8,128)} %pad.9.refs_0_, ...), custom_call_target="tpu_custom_call" | custom-call | tf_op jit(solution)/shard_map/pallas_call | solution.py:1582
  89.6 79.9 %shard_map.170 = (bf16[4,2,128,1600]{3,2,1,0:T(8,128)(2,1)}, bf16[1024,768]{1,0:T(8,128)(2,1)}, bf16[1024,256]{1,0:T(8,128)(2,1)}, f32[8,1024]{1,0:T(8,128)}, f3...) custom-call(bf16[128,1600]{1,0:T(8,128)(2,1)} %get-tuple-element.106, ...), custom_call_target="tpu_custom_call" | custom-call | tf_op jit(solution)/shard_map/pallas_call | solution.py:1337
  169.5 73.7 %shard_map.171 = (bf16[4,2,128,1600]{3,2,1,0:T(8,128)(2,1)}, bf16[1024,800]{1,0:T(8,128)(2,1)}, bf16[1024,800]{1,0:T(8,128)(2,1)}, bf16[128,1600]{1,0:T(8,128)(2...) custom-call(bf16[128,1600]{1,0:T(8,128)(2,1)} %get-tuple-element.115, ...), custom_call_target="tpu_custom_call" | custom-call | tf_op jit(solution)/shard_map/pallas_call | solution.py:1337
  243.2 78.1 %shard_map.172 = (bf16[4,2,128,1600]{3,2,1,0:T(8,128)(2,1)}, bf16[1024,768]{1,0:T(8,128)(2,1)}, bf16[1024,256]{1,0:T(8,128)(2,1)}, f32[8,1024]{1,0:T(8,128)}, f3...) custom-call(bf16[128,1600]{1,0:T(8,128)(2,1)} %get-tuple-element.122, ...), custom_call_target="tpu_custom_call" | custom-call | tf_op jit(solution)/shard_map/pallas_call | solution.py:1337
  321.3 55.6 %shard_map.173 = (bf16[4,2,128,1600]{3,2,1,0:T(8,128)(2,1)}, bf16[1024,800]{1,0:T(8,128)(2,1)}, bf16[1024,800]{1,0:T(8,128)(2,1)}, bf16[128,1600]{1,0:T(8,128)(2...) custom-call(bf16[128,1600]{1,0:T(8,128)(2,1)} %get-tuple-element.129.refs_0_, ...), custom_call_target="tpu_custom_call" | custom-call | tf_op jit(solution)/shard_map/pallas_call | solution.py:1337
  376.9 63.5 %shard_map.174 = (f32[128,1600]{1,0:T(8,128)}, bf16[128,1600]{1,0:T(8,128)(2,1)}, bf16[4,200,1600]{2,1,0:T(8,128)(2,1)}, bf16[4,200,1600]{2,1,0:T(8,128)(2,1)}, ...) custom-call(bf16[128,1600]{1,0:T(8,128)(2,1)} %get-tuple-element.105, ...), custom_call_target="tpu_custom_call" | custom-call | tf_op jit(solution)/shard_map/pallas_call | solution.py:1337
  440.5 66.1 %shard_map.175 = (bf16[128,1600]{1,0:T(8,128)(2,1)}, bf16[1600,256]{1,0:T(8,128)(2,1)}, bf16[1600,256]{1,0:T(8,128)(2,1)}, bf16[1600,256]{1,0:T(8,128)(2,1)}, bf...) custom-call(bf16[128,1600]{1,0:T(8,128)(2,1)} %get-tuple-element.141.refs_0_, ...), custom_call_target="tpu_custom_call" | custom-call | tf_op jit(solution)/shard_map/pallas_call | solution.py:1337
  506.5 76.2 %shard_map.176 = (f32[128,1600]{1,0:T(8,128)}, bf16[128,1600]{1,0:T(8,128)(2,1)}, bf16[4,200,1600]{2,1,0:T(8,128)(2,1)}, bf16[4,200,1600]{2,1,0:T(8,128)(2,1)}, ...) custom-call(bf16[128,1600]{1,0:T(8,128)(2,1)} %get-tuple-element.148, ...), custom_call_target="tpu_custom_call" | custom-call | tf_op jit(solution)/shard_map/pallas_call | solution.py:1337
  582.8 91.2 %shard_map.177 = (bf16[128,1600]{1,0:T(8,128)(2,1)}, bf16[1600,256]{1,0:T(8,128)(2,1)}, bf16[1600,256]{1,0:T(8,128)(2,1)}, bf16[1600,256]{1,0:T(8,128)(2,1)}, bf...) custom-call(bf16[128,1600]{1,0:T(8,128)(2,1)} %get-tuple-element.159, ...), custom_call_target="tpu_custom_call" | custom-call | tf_op jit(solution)/shard_map/pallas_call | solution.py:1337
  673.9 84.7 %shard_map.178 = (f32[100,1,4800]{2,1,0:T(1,128)}, f32[100,1,1600]{2,1,0:T(1,128)}, f32[100,1,6400]{2,1,0:T(1,128)}, bf16[400,1600]{1,0:T(8,128)(2,1)}, f32[16,1...) custom-call(bf16[4,400,256]{2,1,0:T(8,128)(2,1)} %bitcast.65, ...), custom_call_target="tpu_custom_call" | custom-call | tf_op jit(solution)/shard_map/pallas_call | solution.py:1805
  758.6 0.0 copy-start.3
  758.7 0.8 slice.40
  759.4 0.7 slice_bitcast_fusion.1
  760.1 0.7 reshape.79
  760.8 0.6 slice_bitcast_fusion.2
  761.3 0.6 copy.21
  761.9 3.1 bitcast_convert_fusion
  765.1 0.0 copy-done.3
  765.1 0.9 copy.27
  766.0 0.0 copy-done.2
  766.0 0.9 copy.28
  766.8 0.0 copy-done.1
  766.9 1.3 copy.29
  768.1 0.0 copy-done.4
  768.1 0.8 copy.30
  769.0 0.6 copy-done
  769.6 1.5 copy.31
  (10 shorter events, 0.1 us)
Async XLA Ops:
  758.6 6.4 copy-start.3
  761.9 4.0 copy-start.2
  761.9 4.9 copy-start.1
  766.0 2.2 copy-start.4
  766.8 2.7 copy-start
